TPU v7x, 128 devices: a whole 4x4x4 slice. The times are simulated.
128 devices in a mesh: dp: 32 (over y, x, core), tensor: 4 (over z).
Axes of the slice: x: 4, y: 4, z: 4, core: 2. Of those that a mesh axis runs over, the one named last changes fastest.
Arguments:
- tokens: bfloat16 [32768, 1536], P(('dp', 'tensor')), may hold values from -6 to 6
- cotangent: bfloat16 [32768, 1536], P(('dp', 'tensor')), may hold values from -6 to 6
- segments: int32 [32768], replicated, may hold values from 0 to 32767, as said below
- adapter_ids: int32 [16], replicated, may hold values from 0 to 7
- norm_gains: float32 [2, 1536], replicated, may hold values from 0.5 to 1.5
- q_weight: bfloat16 [1536, 1536], P('dp', 'tensor'), may hold values from -0.15625 to 0.15625
- kv_weight: bfloat16 [2, 1536, 128], P(None, 'dp'), may hold values from -0.15625 to 0.15625
- out_weight: bfloat16 [1536, 1536], P('tensor', 'dp'), may hold values from -0.625 to 0.625
- gate_up_weight: bfloat16 [2, 1536, 4608], P(None, 'dp', 'tensor'), may hold values from -0.15625 to 0.15625
- down_weight: bfloat16 [4608, 1536], P('tensor', 'dp'), may hold values from -0.125 to 0.125
- wide_adapters: bfloat16 [7, 1536, 128], P(None, 'dp'), may hold values from -0.359375 to 0.359375
- kv_adapter: bfloat16 [2, 128, 128], replicated, may hold values from -0.59765625 to 0.59765625
- q_adapter: bfloat16 [128, 1536], P(None, 'tensor'), may hold values from -0.59765625 to 0.59765625
- out_adapter: bfloat16 [1536, 128], P('tensor'), may hold values from -0.625 to 0.625
- gate_up_adapter: bfloat16 [2, 128, 4608], P(None, None, 'tensor'), may hold values from -0.59765625 to 0.59765625
- down_adapter: bfloat16 [4608, 128], P('tensor'), may hold values from -0.375 to 0.375
Outputs:
- block_output: bfloat16 [32768, 1536], P(('dp', 'tensor'))
- input_grad: float32 [32768, 1536], P(('dp', 'tensor'))
- wide_grad: float32 [7, 1536, 128], P(None, ('dp', 'tensor'))
- kv_adapter_grad: float32 [2, 128, 128], P(None, ('dp', 'tensor'))
- q_adapter_grad: float32 [128, 1536], P(None, 'tensor')
- out_adapter_grad: float32 [1536, 128], P('tensor')
- gate_up_adapter_grad: float32 [2, 128, 4608], P(None, None, 'tensor')
- down_adapter_grad: float32 [4608, 128], P('tensor')
Inputs may be any that keep to these rules, and one draw needn't show every extreme that they name: `segments`: A token's segment number is the index of the first token of its document, so the numbers never fall; a new document begins at the first token of each sequence of 2048 tokens, each sequence holds one document of exactly 1537 tokens that begins among its first 256 tokens, and the last token of all is a document of its own.
All inputs are finite; a program needn't handle non-finite values.
Results may differ from a plain program's by a relative error of at most 0.025.
Values may be sent and summed in bfloat16 or wider, within the bound.
No kernel may reach another device: no remote copies, remote signals or barrier semaphores. Data moves between devices by JAX's collectives and lax.ppermute only.
A program may use at most 192 MiB of HBM per device.

v0:
```python
from functools import partial

import jax
import jax.numpy as jnp
from jax import lax
from jax.sharding import PartitionSpec as P

HD = 128
WINDOW = 1024
RANK = 16


epsilon = 1e-06
highest = lax.Precision.HIGHEST
masked_score = -1e30


def shifted_2(value, axis, steps):
    count = lax.axis_size(axis)
    first, last = (max(0, -steps), min(count, count - steps))
    return lax.ppermute(value, axis, [(source, source + steps) for source in range(first, last)])


def matmul(left_side, right_side):
    return jnp.dot(left_side, right_side, preferred_element_type=jnp.float32)


def exact_product(left_side, right_side):
    return jnp.dot(left_side, right_side, preferred_element_type=jnp.float32, precision=highest)


def rms_norm(vector, gain_row):
    return (
        vector * lax.rsqrt(jnp.mean(vector * vector, axis=-1, keepdims=True) + epsilon) * gain_row
    )


def rope_tables(positions, head_width):
    half_width = head_width // 2
    frequency = 10000.0 ** (-(jnp.arange(half_width).astype(jnp.float32) / half_width))
    angles = positions.astype(jnp.float32)[:, None] * frequency[None, :]
    return (jnp.cos(angles), jnp.sin(angles))


def rotate(vector, cosine_table, sine_table):
    half_width = vector.shape[-1] // 2
    first_half = vector[..., :half_width]
    second_half = vector[..., half_width:]
    return jnp.concatenate(
        [
            first_half * cosine_table - second_half * sine_table,
            second_half * cosine_table + first_half * sine_table,
        ],
        axis=-1,
    )


def unrotate(gradient, cosine_table, sine_table):
    half_width = gradient.shape[-1] // 2
    first_half = gradient[..., :half_width]
    second_half = gradient[..., half_width:]
    return jnp.concatenate(
        [
            first_half * cosine_table + second_half * sine_table,
            second_half * cosine_table - first_half * sine_table,
        ],
        axis=-1,
    )


def round_trip(vector):
    return lax.optimization_barrier(vector.astype(jnp.bfloat16)).astype(jnp.float32)


def gelu_tanh(vector):
    return jax.nn.gelu(vector, approximate=True)


def on_device(
    tokens,
    cotangent,
    segments,
    adapter_ids,
    norm_gains,
    q_weight,
    kv_weight,
    out_weight,
    gate_up_weight,
    down_weight,
    wide_adapters,
    kv_adapter,
    q_adapter,
    out_adapter,
    gate_up_adapter,
    down_adapter,
):
    tok_rows = tokens.shape[0]
    tensor_count = lax.axis_size("tensor")
    group_rows = tok_rows * tensor_count
    seq_length = 2 * group_rows
    window = WINDOW
    head_width = HD
    rank_width = RANK
    block_rows = min(512, group_rows)
    block_count = group_rows // block_rows
    score_scale = head_width ** (-0.5)
    group_index = lax.axis_index("dp")
    adapter = lax.dynamic_index_in_dim(adapter_ids, group_index // 2, keepdims=False)
    column = adapter * rank_width

    def take_cols(matrix):
        return lax.dynamic_slice_in_dim(matrix, column, rank_width, matrix.ndim - 1)

    def take_rows(matrix):
        return lax.dynamic_slice_in_dim(matrix, column, rank_width, matrix.ndim - 2)

    w_query, w_keyval, w_output, w_gateup, w_down, wide_full = (
        lax.all_gather(q_weight, "dp", axis=0, tiled=True),
        lax.all_gather(kv_weight, "dp", axis=1, tiled=True),
        lax.all_gather(out_weight, "dp", axis=1, tiled=True),
        lax.all_gather(gate_up_weight, "dp", axis=1, tiled=True),
        lax.all_gather(down_weight, "dp", axis=1, tiled=True),
        lax.all_gather(wide_adapters, "dp", axis=1, tiled=True),
    )
    wide_cols = take_cols(wide_full)
    inputs = tokens.astype(jnp.float32)
    normed_one = rms_norm(inputs, norm_gains[0]).astype(jnp.bfloat16)
    tokens_one = lax.all_gather(normed_one, "tensor", axis=0, tiled=True)
    rank_attn = jnp.einsum(
        "td,jdr->jtr", tokens_one, wide_cols[:3], preferred_element_type=jnp.float32
    ).astype(jnp.bfloat16)
    query_lin = matmul(tokens_one, w_query) + matmul(rank_attn[0], take_rows(q_adapter))
    keyval_lin = jnp.einsum(
        "td,jdh->jth", tokens_one, w_keyval, preferred_element_type=jnp.float32
    ) + jnp.einsum(
        "jtr,jrh->jth", rank_attn[1:], take_rows(kv_adapter), preferred_element_type=jnp.float32
    )
    head_count = query_lin.shape[1] // head_width
    positions = group_index * group_rows + jnp.arange(group_rows)
    cosine_table, sine_table = rope_tables(positions % seq_length, head_width)
    queries = rotate(
        query_lin.reshape(group_rows, head_count, head_width),
        cosine_table[:, None, :],
        sine_table[:, None, :],
    ).astype(jnp.bfloat16)
    key_rows = rotate(keyval_lin[0], cosine_table, sine_table).astype(jnp.bfloat16)
    values = keyval_lin[1].astype(jnp.bfloat16)
    earlier = shifted_2(jnp.stack([key_rows, values]), "dp", 1)
    all_keys = jnp.concatenate([earlier[0], key_rows])
    all_values = jnp.concatenate([earlier[1], values])
    key_pos = group_index * group_rows - window + jnp.arange(window + group_rows)
    padded_seg = jnp.concatenate([jnp.full((window,), -1, jnp.int32), segments])
    key_seg = lax.dynamic_slice_in_dim(padded_seg, group_index * group_rows, window + group_rows, 0)
    key_seq = jnp.floor_divide(key_pos, seq_length)

    def block_scores(begin_row):
        query_block = lax.dynamic_slice_in_dim(queries, begin_row, block_rows, 0)
        key_block = lax.dynamic_slice_in_dim(all_keys, begin_row, block_rows + window, 0)
        value_block = lax.dynamic_slice_in_dim(all_values, begin_row, block_rows + window, 0)
        query_seg = lax.dynamic_slice_in_dim(key_seg, begin_row + window, block_rows, 0)
        near_seg = lax.dynamic_slice_in_dim(key_seg, begin_row, block_rows + window, 0)
        query_seq = lax.dynamic_slice_in_dim(key_seq, begin_row + window, block_rows, 0)
        near_seq = lax.dynamic_slice_in_dim(key_seq, begin_row, block_rows + window, 0)
        distance = (
            jnp.arange(block_rows)[:, None] + window - jnp.arange(block_rows + window)[None, :]
        )
        allowed = (
            (distance >= 0)
            & (distance <= window)
            & (query_seg[:, None] == near_seg[None, :])
            & (query_seq[:, None] == near_seq[None, :])
        )
        raw_scores = (
            jnp.einsum("bhd,kd->hbk", query_block, key_block, preferred_element_type=jnp.float32)
            * score_scale
        )
        return (
            jnp.where(allowed[None], raw_scores, masked_score),
            query_block,
            key_block,
            value_block,
        )

    def forward_block(begin_row):
        scores, query_block, key_block, value_block = block_scores(begin_row)
        top_score = jnp.max(scores, axis=-1, keepdims=True)
        shifted = jnp.exp(scores - top_score)
        row_total = jnp.sum(shifted, axis=-1, keepdims=True)
        probs_low = (shifted / row_total).astype(jnp.bfloat16)
        mixed_block = jnp.einsum(
            "hbk,kd->bhd", probs_low, value_block, preferred_element_type=jnp.float32
        )
        return (
            mixed_block.astype(jnp.bfloat16).reshape(block_rows, head_count * head_width),
            (top_score + jnp.log(row_total))[..., 0],
        )

    begins = jnp.arange(block_count) * block_rows
    mixed_blocks, log_totals = lax.map(forward_block, begins)
    mixed_heads = mixed_blocks.reshape(group_rows, head_count * head_width)
    out_down = take_cols(out_adapter)
    rank_out = matmul(mixed_heads, out_down)
    out_up = wide_cols[5].astype(jnp.float32).T
    part_rows = mixed_heads
    part_rank = rank_out
    branch = lax.psum_scatter(
        (matmul(part_rows, w_output) + exact_product(part_rank, out_up)).astype(jnp.bfloat16),
        "tensor",
        scatter_dimension=0,
        tiled=True,
    ).astype(jnp.float32)
    residual = inputs + branch
    normed_two = rms_norm(residual, norm_gains[1]).astype(jnp.bfloat16)
    tokens_two = lax.all_gather(normed_two, "tensor", axis=0, tiled=True)
    rank_ffn = jnp.einsum(
        "td,jdr->jtr", tokens_two, wide_cols[3:5], preferred_element_type=jnp.float32
    ).astype(jnp.bfloat16)
    gate_up = jnp.einsum(
        "td,jdf->jtf", tokens_two, w_gateup, preferred_element_type=jnp.float32
    ) + jnp.einsum(
        "jtr,jrf->jtf", rank_ffn, take_rows(gate_up_adapter), preferred_element_type=jnp.float32
    )
    activated, gelu_pull = jax.vjp(gelu_tanh, gate_up[0])
    hidden = (activated * gate_up[1]).astype(jnp.bfloat16)
    down_low = take_cols(down_adapter)
    rank_down = matmul(hidden, down_low)
    down_up = wide_cols[6].astype(jnp.float32).T
    part_rows = hidden
    part_rank = rank_down
    ffn_out = lax.psum_scatter(
        (matmul(part_rows, w_down) + exact_product(part_rank, down_up)).astype(jnp.bfloat16),
        "tensor",
        scatter_dimension=0,
        tiled=True,
    ).astype(jnp.float32)
    block_output = (residual + ffn_out).astype(jnp.bfloat16)
    w_query, w_keyval, w_output, w_gateup, w_down, wide_full = (
        lax.all_gather(q_weight, "dp", axis=0, tiled=True),
        lax.all_gather(kv_weight, "dp", axis=1, tiled=True),
        lax.all_gather(out_weight, "dp", axis=1, tiled=True),
        lax.all_gather(gate_up_weight, "dp", axis=1, tiled=True),
        lax.all_gather(down_weight, "dp", axis=1, tiled=True),
        lax.all_gather(wide_adapters, "dp", axis=1, tiled=True),
    )
    wide_cols = take_cols(wide_full)
    grad_ffn = lax.all_gather(cotangent, "tensor", axis=0, tiled=True)
    grad_rank_down = exact_product(grad_ffn, wide_cols[6].astype(jnp.float32)).astype(jnp.bfloat16)
    grad_hidden = round_trip(matmul(grad_ffn, w_down.T) + matmul(grad_rank_down, down_low.T))
    grad_gate = gelu_pull(grad_hidden * gate_up[1])[0]
    grad_gateup = jnp.stack([grad_gate, grad_hidden * activated]).astype(jnp.bfloat16)
    gateup_up_grad = jnp.einsum(
        "jtr,jtf->jrf", rank_ffn, grad_gateup, preferred_element_type=jnp.float32
    )
    grad_rank_ffn = jnp.einsum(
        "jtf,jrf->jtr", grad_gateup, take_rows(gate_up_adapter), preferred_element_type=jnp.float32
    )
    ffn_in_grad = jnp.einsum(
        "td,jtr->jdr",
        tokens_two,
        grad_rank_ffn,
        precision=highest,
        preferred_element_type=jnp.float32,
    )
    down_low_grad = matmul(hidden.T, grad_rank_down)
    down_up_grad = exact_product(grad_ffn.T, rank_down)
    ffn_in_wide = wide_cols[3:5].astype(jnp.float32)
    part_rank = grad_rank_ffn
    grad_two = lax.psum_scatter(
        (
            jnp.einsum("jtf,jdf->td", grad_gateup, w_gateup, preferred_element_type=jnp.float32)
            + jnp.einsum(
                "jtr,jdr->td",
                part_rank,
                ffn_in_wide,
                precision=highest,
                preferred_element_type=jnp.float32,
            )
        ).astype(jnp.bfloat16),
        "tensor",
        scatter_dimension=0,
        tiled=True,
    ).astype(jnp.float32)
    norm_pull_two = jax.vjp(partial(rms_norm, gain_row=norm_gains[1]), residual)[1]
    grad_residual = cotangent.astype(jnp.float32) + norm_pull_two(grad_two)[0]
    grad_attn = lax.all_gather(grad_residual.astype(jnp.bfloat16), "tensor", axis=0, tiled=True)
    grad_rank_out = exact_product(grad_attn, wide_cols[5].astype(jnp.float32)).astype(jnp.bfloat16)
    grad_mixed = (matmul(grad_attn, w_output.T) + matmul(grad_rank_out, out_down.T)).astype(
        jnp.bfloat16
    )
    out_down_grad = matmul(mixed_heads.T, grad_rank_out)
    out_up_grad = exact_product(grad_attn.T, rank_out)
    grad_heads = grad_mixed.reshape(group_rows, head_count, head_width)

    def backward_block(carried, block_index):
        key_grads, value_grads = carried
        begin_row = block_index * block_rows
        scores, query_block, key_block, value_block = block_scores(begin_row)
        log_total = lax.dynamic_index_in_dim(log_totals, block_index, keepdims=False)
        probs = jnp.exp(scores - log_total[..., None])
        grad_block = lax.dynamic_slice_in_dim(grad_heads, begin_row, block_rows, 0)
        grad_probs = jnp.einsum(
            "bhd,kd->hbk", grad_block, value_block, preferred_element_type=jnp.float32
        )
        value_part = jnp.einsum(
            "hbk,bhd->kd",
            probs.astype(jnp.bfloat16),
            grad_block,
            preferred_element_type=jnp.float32,
        )
        centred = jnp.sum(probs * grad_probs, axis=-1, keepdims=True)
        grad_scores = (probs * (grad_probs - centred)).astype(jnp.bfloat16)
        query_part = (
            jnp.einsum("hbk,kd->bhd", grad_scores, key_block, preferred_element_type=jnp.float32)
            * score_scale
        )
        key_part = (
            jnp.einsum("hbk,bhd->kd", grad_scores, query_block, preferred_element_type=jnp.float32)
            * score_scale
        )
        key_span = block_rows + window
        key_grads = lax.dynamic_update_slice_in_dim(
            key_grads,
            lax.dynamic_slice_in_dim(key_grads, begin_row, key_span, 0) + key_part,
            begin_row,
            0,
        )
        value_grads = lax.dynamic_update_slice_in_dim(
            value_grads,
            lax.dynamic_slice_in_dim(value_grads, begin_row, key_span, 0) + value_part,
            begin_row,
            0,
        )
        return ((key_grads, value_grads), query_part)

    zero_grads = jnp.zeros((window + group_rows, head_width), jnp.float32)
    (key_grads, value_grads), query_parts = lax.scan(
        backward_block, (zero_grads, zero_grads), jnp.arange(block_count)
    )
    returned = shifted_2(
        jnp.stack([key_grads[:window], value_grads[:window]]).astype(jnp.bfloat16), "dp", -1
    ).astype(jnp.float32)
    key_own = key_grads[window:].at[group_rows - window :].add(returned[0])
    value_own = value_grads[window:].at[group_rows - window :].add(returned[1])
    grad_query = unrotate(
        query_parts.reshape(group_rows, head_count, head_width),
        cosine_table[:, None, :],
        sine_table[:, None, :],
    )
    grad_query = grad_query.reshape(group_rows, head_count * head_width).astype(jnp.bfloat16)
    grad_key = unrotate(key_own, cosine_table, sine_table)
    keyval_grad = jnp.stack([grad_key, value_own])
    q_up_grad = matmul(rank_attn[0].T, grad_query)
    kv_up_grad = jnp.einsum(
        "jtr,jth->jrh",
        rank_attn[1:],
        keyval_grad,
        precision=highest,
        preferred_element_type=jnp.float32,
    )
    kv_up_wide = take_rows(kv_adapter).astype(jnp.float32)
    grad_rank_attn = jnp.concatenate(
        [
            matmul(grad_query, take_rows(q_adapter).T)[None],
            jnp.einsum(
                "jth,jrh->jtr",
                keyval_grad,
                kv_up_wide,
                precision=highest,
                preferred_element_type=jnp.float32,
            ),
        ]
    )
    attn_in_grad = jnp.einsum(
        "td,jtr->jdr",
        tokens_one,
        grad_rank_attn,
        precision=highest,
        preferred_element_type=jnp.float32,
    )
    keyval_wide = w_keyval.astype(jnp.float32)
    attn_in_wide = wide_cols[:3].astype(jnp.float32)
    part_rank = grad_rank_attn
    grad_one = lax.psum_scatter(
        (
            matmul(grad_query, w_query.T)
            + jnp.einsum(
                "jth,jdh->td",
                keyval_grad,
                keyval_wide,
                precision=highest,
                preferred_element_type=jnp.float32,
            )
            + jnp.einsum(
                "jtr,jdr->td",
                part_rank,
                attn_in_wide,
                precision=highest,
                preferred_element_type=jnp.float32,
            )
        ).astype(jnp.bfloat16),
        "tensor",
        scatter_dimension=0,
        tiled=True,
    ).astype(jnp.float32)
    norm_pull_one = jax.vjp(partial(rms_norm, gain_row=norm_gains[0]), inputs)[1]
    input_grad = grad_residual + norm_pull_one(grad_one)[0]
    adapter_width = wide_adapters.shape[2]
    wide_term = jnp.concatenate([attn_in_grad, ffn_in_grad, out_up_grad[None], down_up_grad[None]])
    kv_grad_full = lax.dynamic_update_slice_in_dim(
        jnp.zeros((2, adapter_width, head_width), jnp.float32), kv_up_grad, column, 1
    )
    wide_grad_full = lax.dynamic_update_slice_in_dim(
        jnp.zeros((7, wide_full.shape[1], adapter_width), jnp.float32), wide_term, column, 2
    )
    wide_grad, kv_adapter_grad = (
        lax.psum_scatter(wide_grad_full, ("dp", "tensor"), scatter_dimension=1, tiled=True),
        lax.psum_scatter(kv_grad_full, ("dp", "tensor"), scatter_dimension=1, tiled=True),
    )
    q_grad_full = lax.dynamic_update_slice_in_dim(
        jnp.zeros((adapter_width, q_up_grad.shape[1]), jnp.float32), q_up_grad, column, 0
    )
    gateup_grad_full = lax.dynamic_update_slice_in_dim(
        jnp.zeros((2, adapter_width, gateup_up_grad.shape[2]), jnp.float32),
        gateup_up_grad,
        column,
        1,
    )
    out_grad_full = lax.dynamic_update_slice_in_dim(
        jnp.zeros((out_down_grad.shape[0], adapter_width), jnp.float32), out_down_grad, column, 1
    )
    down_grad_full = lax.dynamic_update_slice_in_dim(
        jnp.zeros((down_low_grad.shape[0], adapter_width), jnp.float32), down_low_grad, column, 1
    )
    q_adapter_grad, gate_up_adapter_grad, out_adapter_grad, down_adapter_grad = (
        lax.psum(q_grad_full.astype(jnp.bfloat16), "dp").astype(jnp.float32),
        lax.psum(gateup_grad_full.astype(jnp.bfloat16), "dp").astype(jnp.float32),
        lax.psum(out_grad_full.astype(jnp.bfloat16), "dp").astype(jnp.float32),
        lax.psum(down_grad_full.astype(jnp.bfloat16), "dp").astype(jnp.float32),
    )
    return (
        block_output,
        input_grad,
        wide_grad,
        kv_adapter_grad,
        q_adapter_grad,
        out_adapter_grad,
        gate_up_adapter_grad,
        down_adapter_grad,
    )


def solution(mesh):
    return jax.shard_map(
        on_device,
        mesh=mesh,
        in_specs=(
            P(("dp", "tensor"), None),
            P(("dp", "tensor"), None),
            P(),
            P(),
            P(),
            P("dp", "tensor"),
            P(None, "dp", None),
            P("tensor", "dp"),
            P(None, "dp", "tensor"),
            P("tensor", "dp"),
            P(None, "dp", None),
            P(),
            P(None, "tensor"),
            P("tensor", None),
            P(None, None, "tensor"),
            P("tensor", None),
        ),
        out_specs=(
            P(("dp", "tensor"), None),
            P(("dp", "tensor"), None),
            P(None, ("dp", "tensor"), None),
            P(None, ("dp", "tensor"), None),
            P(None, "tensor"),
            P("tensor", None),
            P(None, None, "tensor"),
            P("tensor", None),
        ),
        check_vma=False,
    )
```

profile of v0, /device:TPU:1, one launch (start us, length us, event | category | flops | bytes accessed | tf_op | source)
XLA Modules:
  0.0 1234.0 jit_solution(8690871494552823852)
XLA Ops:
  15.8 26.7 %all_gather.37 = bf16[2,1536,128]{2,1,0:T(8,128)(2,1)S(1)} all-gather(bf16[2,48,128]{2,1,0:T(8,128)(2,1)S(1)} %copy-done.60), channel_id=1, replica_groups=mesh['dp'=32,'tensor'=4] {'dp'}, dimensions={1}, use_global_device_ids=true | all-gather | bytes 811008 | tf_op jit(solution)/shard_map/all_gather | solution.py:119
  42.5 14.4 %all-gather.14.cloned.1.call-done = bf16[1536,384]{1,0:T(8,128)(2,1)} async-done(((bf16[48,384]{1,0:T(8,128)(2,1)}), bf16[1536,384]{1,0:T(8,128)(2,1)}) %all-gather.14.cloned.1.call-update) | async-done | bytes 1179664 | tf_op jit(solution)/shard_map/all_gather | solution.py:118
  56.9 41.0 %all-gather.10.cloned.1.call-done = bf16[1024,1536]{1,0:T(8,128)(2,1)} async-done(((bf16[256,1536]{1,0:T(8,128)(2,1)}), bf16[1024,1536]{1,0:T(8,128)(2,1)}) %all-gather.10.cloned.1.call-update) | async-done | bytes 3145744 | tf_op jit(solution)/shard_map/all_gather | solution.py:128
  103.7 41.7 %all-gather.12.cloned.1.call-done = bf16[7,1536,128]{2,1,0:T(8,128)(2,1)} async-done(((bf16[7,48,128]{2,1,0:T(8,128)(2,1)}), bf16[7,1536,128]{2,1,0:T(8,128)(2,1)}) %all-gather.12.cloned.1.call-update) | async-done | bytes 2752528 | tf_op jit(solution)/shard_map/all_gather | solution.py:123
  171.6 33.6 %while.34 = (s32[]{:T(128)}, bf16[2,512,384]{2,1,0:T(8,128)(2,1)}, f32[2,3,512]{2,1,0:T(4,128)S(1)}, s32[2]{0:T(128)S(1)}, bf16[2048,128]{0,1:T(8,128)(2,1)S(1)}...) while((s32[]{:T(128)}, bf16[2,512,384]{2,1,0:T(8,128)(2,1)}, ...), condition=%wide.region_4.5_spmd, body=%wide.region_1.4_spmd.sunk | while | flops 1242758144 | bytes 34716428 | solution.py:199
  221.2 38.6 %reduce-scatter.6.cloned.1.call-done = bf16[256,1536]{1,0:T(8,128)(2,1)} async-done(((bf16[1024,1536]{1,0:T(8,128)(2,1)}), bf16[256,1536]{1,0:T(8,128)(2,1)}) %reduce-scatter.6.cloned.1.call-update) | async-done | bytes 786448 | tf_op jit(solution)/shard_map/reduce_scatter | solution.py:206
  264.4 36.2 %all-gather.24.cloned.1.call-done = bf16[1024,1536]{1,0:T(8,128)(2,1)} async-done(((bf16[256,1536]{1,0:T(8,128)(2,1)}), bf16[1024,1536]{1,0:T(8,128)(2,1)}) %all-gather.24.cloned.1.call-update) | async-done | bytes 3145744 | tf_op jit(solution)/shard_map/all_gather | solution.py:246
  303.8 45.1 %all-gather.22.cloned.1.call-done = bf16[1152,1536]{0,1:T(8,128)(2,1)} async-done(((bf16[1152,48]{0,1:T(8,128)(2,1)}), bf16[1152,1536]{0,1:T(8,128)(2,1)}) %all-gather.22.cloned.1.call-update) | async-done | bytes 3538960 | tf_op jit(solution)/shard_map/all_gather | solution.py:122
  358.4 31.6 %all-gather.18.cloned.1.call-done = bf16[1024,1536]{1,0:T(8,128)(2,1)} async-done(((bf16[256,1536]{1,0:T(8,128)(2,1)}), bf16[1024,1536]{1,0:T(8,128)(2,1)}) %all-gather.18.cloned.1.call-update) | async-done | bytes 3145744 | tf_op jit(solution)/shard_map/all_gather | solution.py:214
  393.4 49.8 %all-gather.20.cloned.1.call-done = bf16[2,1536,1152]{2,1,0:T(8,128)(2,1)} async-done(((bf16[2,48,1152]{2,1,0:T(8,128)(2,1)}), bf16[2,1536,1152]{2,1,0:T(8,128)(2,1)}) %all-gather.20.cloned.1.call-update) | async-done | bytes 7077904 | tf_op jit(solution)/shard_map/all_gather | solution.py:121
  443.2 10.5 fusion.71
  470.3 8.5 fusion.57
  478.9 37.3 %reduce-scatter.10.cloned.1.call-done = bf16[256,1536]{1,0:T(8,128)(2,1)} async-done(((bf16[1024,1536]{1,0:T(8,128)(2,1)}), bf16[256,1536]{1,0:T(8,128)(2,1)}) %reduce-scatter.10.cloned.1.call-update) | async-done | bytes 786448 | tf_op jit(solution)/shard_map/reduce_scatter | solution.py:268
  532.0 28.1 %all-gather.26.cloned.1.call-done = bf16[1024,1536]{1,0:T(8,128)(2,1)} async-done(((bf16[256,1536]{1,0:T(8,128)(2,1)}), bf16[1024,1536]{1,0:T(8,128)(2,1)}) %all-gather.26.cloned.1.call-update) | async-done | bytes 3145744 | tf_op jit(solution)/shard_map/all_gather | solution.py:285
  568.3 95.6 %while.35 = (s32[]{:T(128)}, f32[2048,128]{0,1:T(8,128)}, f32[2048,128]{0,1:T(8,128)}, f32[2,512,3,128]{3,1,0,2:T(8,128)}, s32[2]{0:T(128)S(1)}, /*index=5*/s32[...) while((s32[]{:T(128)}, f32[2048,128]{0,1:T(8,128)}, ...), condition=%wide.region_12.13_spmd, body=%wide.region_10.12_spmd.sunk | while | flops 3048209408 | bytes 101143464 | solution.py:336
  579.7 7.5 fusion.274
  587.2 11.0 fusion.276
  627.4 7.5 fusion.274
  634.9 11.0 fusion.276
  686.3 9.1 fusion.120
  696.0 8.0 fusion.100
  739.7 249.3 %dynamic_update_slice.51 = f32[7,1536,128]{2,0,1:T(8,128)} dynamic-update-slice(f32[7,1536,128]{2,0,1:T(8,128)} %broadcast_in_dim.131, f32[7,1536,16]{2,0,1:T(8,128)} %copy.92, s32[]{:T(128)} %constant.267.clone.1, s32[]{:T(128)} %constant.267.clone.1, s32[]{:T(128)S(6)} %select_n.116) | dynamic-update-slice | bytes 1376260 | tf_op jit(solution)/shard_map/dynamic_update_slice | solution.py:412
  999.2 11.7 reduce-scatter.8.cloned.1.call-done
  1015.0 212.3 %reduce-scatter.14.cloned.1.call-done = f32[7,12,128]{2,0,1:T(8,128)} async-done(((f32[7,1536,128]{2,0,1:T(8,128)}), f32[7,12,128]{2,0,1:T(8,128)}) %reduce-scatter.14.cloned.1.call-update) | async-done | bytes 43024 | tf_op jit(solution)/shard_map/reduce_scatter | solution.py:416
  (367 shorter events, 267.9 us)
Async XLA Ops:
  7.2 446.5 %copy-start = (bf16[2,128,1152]{2,1,0:T(8,128)(2,1)S(1)}, bf16[2,128,1152]{2,1,0:T(8,128)(2,1)}, u32[]{:S(2)}) copy-start(bf16[2,128,1152]{2,1,0:T(8,128)(2,1)} %param.42) | copy-start | bytes 1769476
  7.2 49.7 %all-gather.14.cloned.1.call-start = ((), (), s32[]{:S(2)}) async-start(), calls=%async_computation.7 | async-start | bytes 1216512 | tf_op jit(solution)/shard_map/all_gather | solution.py:118
  7.9 89.9 %all-gather.10.cloned.1.call-start = ((), (), s32[]{:S(2)}) async-start(), calls=%async_computation.5 | async-start | bytes 3932160 | tf_op jit(solution)/shard_map/all_gather | solution.py:128
  8.8 252.4 %copy-start.46 = (f32[1536]{0:T(1024)}, f32[1536]{0:T(1024)S(1)}, u32[]{:S(2)}) copy-start(f32[1536]{0:T(1024)S(1)} %get-tuple-element.389) | copy-start | bytes 18436
  13.1 132.3 %all-gather.12.cloned.1.call-start = ((), (), s32[]{:S(2)}) async-start(), calls=%async_computation.6 | async-start | bytes 2838528 | tf_op jit(solution)/shard_map/all_gather | solution.py:123
  13.8 199.2 %all-gather.16.cloned.1.call-start = ((), (), s32[]{:S(2)}) async-start(), calls=%async_computation.8 | async-start | bytes 1216512 | tf_op jit(solution)/shard_map/all_gather | solution.py:120
  14.4 245.4 %reduce-scatter.6.cloned.1.call-start = ((), (), s32[]{:S(2)}) async-start(), calls=%async_computation.9 | async-start | bytes 3932160 | tf_op jit(solution)/shard_map/reduce_scatter | solution.py:206
  14.5 143.1 %copy-start.72 = (f32[64]{0:T(128)}, f32[64]{0:T(128)S(1)}, u32[]{:S(2)}) copy-start(f32[64]{0:T(128)S(1)} %negate_power_fusion) | copy-start | bytes 772
  14.5 143.1 %copy-start.58 = (f32[1024]{0:T(1024)}, f32[1024]{0:T(1024)S(1)}, u32[]{:S(2)}) copy-start(f32[1024]{0:T(1024)S(1)} %fusion.157) | copy-start | bytes 12292
  42.5 59.2 %copy-start.27 = (bf16[2,1536,128]{2,1,0:T(8,128)(2,1)}, bf16[2,1536,128]{2,1,0:T(8,128)(2,1)S(1)}, u32[]{:S(2)}) copy-start(bf16[2,1536,128]{2,1,0:T(8,128)(2,1)S(1)} %all_gather.37) | copy-start | bytes 2359300
  162.2 8.9 collective-permute-start
  219.8 80.8 %all-gather.24.cloned.1.call-start = ((), (), s32[]{:S(2)}) async-start(), calls=%async_computation.14 | async-start | bytes 3932160 | tf_op jit(solution)/shard_map/all_gather | solution.py:246
  220.4 128.6 %all-gather.22.cloned.1.call-start = ((), (), s32[]{:S(2)}) async-start(), calls=%async_computation.12 | async-start | bytes 3649536 | tf_op jit(solution)/shard_map/all_gather | solution.py:122
  221.1 168.9 %all-gather.18.cloned.1.call-start = ((), (), s32[]{:S(2)}) async-start(), calls=%async_computation.10 | async-start | bytes 3932160 | tf_op jit(solution)/shard_map/all_gather | solution.py:214
  263.6 179.6 %all-gather.20.cloned.1.call-start = ((), (), s32[]{:S(2)}) async-start(), calls=%async_computation.11 | async-start | bytes 7299072 | tf_op jit(solution)/shard_map/all_gather | solution.py:121
  264.3 251.8 %reduce-scatter.10.cloned.1.call-start = ((), (), s32[]{:S(2)}) async-start(), calls=%async_computation.15 | async-start | bytes 3932160 | tf_op jit(solution)/shard_map/reduce_scatter | solution.py:268
  478.8 81.3 %all-gather.26.cloned.1.call-start = ((), (), s32[]{:S(2)}) async-start(), calls=%async_computation.16 | async-start | bytes 3932160 | tf_op jit(solution)/shard_map/all_gather | solution.py:285
  520.7 468.4 %all-reduce.8.cloned.1.call-start = ((), (), s32[]{:S(2)}) async-start(), calls=%async_computation.20 | async-start | bytes 2162688 | tf_op jit(solution)/shard_map/psum | solution.py:435
  670.6 10.8 collective-permute-start.1
  680.4 316.0 %all-reduce.6.cloned.1.call-start = ((), (), s32[]{:S(2)}) async-start(), calls=%async_computation.19 | async-start | bytes 262144
  695.5 302.2 %reduce-scatter.12.cloned.1.call-start = ((), (), s32[]{:S(2)}) async-start(), calls=%async_computation.17 | async-start | bytes 3932160 | tf_op jit(solution)/shard_map/reduce_scatter | solution.py:383
  707.5 303.4 %reduce-scatter.8.cloned.1.call-start = ((), (), s32[]{:S(2)}) async-start(), calls=%async_computation.13 | async-start | bytes 3932160 | tf_op jit(solution)/shard_map/reduce_scatter | solution.py:230
  722.5 504.8 %reduce-scatter.14.cloned.1.call-start = ((), (), s32[]{:S(2)}) async-start(), calls=%async_computation.18 | async-start | bytes 6340608 | tf_op jit(solution)/shard_map/reduce_scatter | solution.py:416
  999.2 228.2 %copy-start.1 = (bf16[2,128,1152]{2,1,0:T(8,128)(2,1)S(1)}, bf16[2,128,1152]{2,1,0:T(8,128)(2,1)}, u32[]{:S(2)}) copy-start(bf16[2,128,1152]{2,1,0:T(8,128)(2,1)} %param.42) | copy-start | bytes 1769476
  (73 other events, 1034.7 us)
Sparse Core Ops, SparseCore 0:
  10.4 46.4 all-gather.13
  59.1 38.6 all-gather.9
  100.2 45.0 all-gather.11
  147.6 42.0 all-gather.15
  219.9 39.8 reduce-scatter.5
  261.3 39.2 all-gather.23
  302.9 45.9 all-gather.21
  351.2 38.7 all-gather.17
  392.4 50.7 all-gather.19
  478.9 37.1 reduce-scatter.9
  520.8 39.2 all-gather.25
  680.5 104.8 all-reduce.7
  790.2 141.7 all-reduce.5
  934.4 35.8 reduce-scatter.11
  972.6 38.1 reduce-scatter.7
  1017.0 210.3 reduce-scatter.13
where the time goes:
time: 1240 us; the launch traced here: 1230 us
  waiting for transfers between devices  594 us (48%)
  local copies, waits for them, and re-layouts  303 us (24%)
  matrix products  199 us (16%)
  other arithmetic  74.7 us (6%)
  blocking collectives  26.7 us (2%)
  between operations  16 us (1%)
  loops' own time  13.4 us (1%)
    dynamic_update_slice x1, local copies, waits for them, and re-layouts, on_device(): lax.dynamic_update_slice_in_dim(jnp.zeros((7, wide_full.shape[1], adapter...  249 us
    reduce_scatter x1, waiting for transfers between devices, on_device(): lax.psum_scatter(wide_grad_full, ('dp', 'tensor'), scatter_dimension=1, t...  212 us
    all_gather x1, waiting for transfers between devices, on_device(): lax.all_gather(gate_up_weight, 'dp', axis=1, tiled=True)  49.8 us
    dot_general x15, matrix products, matmul(): return jnp.dot(left_side, right_side, preferred_element_type=jnp.float32)  45.8 us
    all_gather x1, waiting for transfers between devices, on_device(): lax.all_gather(down_weight, 'dp', axis=1, tiled=True)  45.1 us
    all_gather x1, waiting for transfers between devices, on_device(): lax.all_gather(wide_adapters, 'dp', axis=1, tiled=True)  41.7 us
    all_gather x1, waiting for transfers between devices, on_device(): tokens_one = lax.all_gather(normed_one, 'tensor', axis=0, tiled=True)  41 us
    reduce_scatter x1, waiting for transfers between devices, on_device(): lax.psum_scatter((matmul(part_rows, w_output) + exact_product(part_rank,...  38.6 us
  transfers between devices with their start and end apart: 18, of which 13 were waited for; matrix products, arithmetic and copies ran while one was open for 34% of the time, Pallas kernels for 0%

commit v1 on v0

v1 whole, which is shorter than its diff:
```python
import jax
import jax.numpy as jnp
from jax import lax
from jax.experimental import pallas as pl
from jax.experimental.pallas import tpu as pltpu
from jax.sharding import PartitionSpec as P

HD = 128
WINDOW = 1024
RANK = 16
LANES = 128
EPS = 1e-06
MASKED = -1e30
SCALE = HD ** (-0.5)
GELU_C = 0.7978845608028654
GELU_A = 0.044715
VMEM_LIMIT = 58 * 1024 * 1024
BF = jnp.bfloat16
F32 = jnp.float32
BOTH = ("dp", "tensor")

SLOT_Q, SLOT_K, SLOT_V, SLOT_G, SLOT_U, SLOT_O, SLOT_D = range(7)


def rows_of(slot):
    return slice(slot * RANK, (slot + 1) * RANK)


def mm(a, b):
    return lax.dot_general(a, b, (((1,), (0,)), ((), ())), preferred_element_type=F32)


def mm_nt(a, b):
    return lax.dot_general(a, b, (((1,), (1,)), ((), ())), preferred_element_type=F32)


def rope(v, cos, sin):
    return v * cos + pltpu.roll(v, HD // 2, 1) * sin


def rope_back(g, cos, sin):
    return g * cos - pltpu.roll(g, HD // 2, 1) * sin


def flat(ref):
    block = ref[...]
    return block.reshape(block.shape[0] * block.shape[2], block.shape[3])


def rms(v, gain):
    return v * lax.rsqrt(jnp.mean(v * v, axis=-1, keepdims=True) + EPS) * gain


def rms_back(v, gain, grad):
    inv = lax.rsqrt(jnp.mean(v * v, axis=-1, keepdims=True) + EPS)
    scaled = grad * gain
    dot = jnp.mean(v * scaled, axis=-1, keepdims=True)
    return inv * scaled - v * (inv * inv * inv * dot)


def pre_kernel(
    x_ref, gain_ref, a_ref, kvw_ref, bkv_ref, cos_ref, sin_ref, wq_ref, bq_ref,
    n1_ref, r1_ref, kv_ref, q_ref,
):
    @pl.when(pl.program_id(0) == 0)
    def _():
        n1 = rms(x_ref[...].astype(F32), gain_ref[...]).astype(BF)
        n1_ref[...] = n1
        r1 = mm(n1, a_ref[...]).astype(BF)
        r1_ref[...] = r1
        key = mm(n1, kvw_ref[0]) + mm(r1, bkv_ref[0])
        kv_ref[:, :HD] = rope(key, cos_ref[...], sin_ref[...]).astype(BF)
        kv_ref[:, HD:] = (mm(n1, kvw_ref[1]) + mm(r1, bkv_ref[1])).astype(BF)

    lin = mm(n1_ref[...], flat(wq_ref)) + mm(r1_ref[...], bq_ref[0])
    for h in range(lin.shape[1] // HD):
        part = slice(h * HD, (h + 1) * HD)
        q_ref[:, part] = rope(lin[:, part], cos_ref[...], sin_ref[...]).astype(BF)


def fill_bias(bias_ref, kseg_ref, qseg_ref):
    shape = bias_ref.shape
    key = lax.broadcasted_iota(jnp.int32, shape, 0)
    query = lax.broadcasted_iota(jnp.int32, shape, 1)
    allowed = (key >= query) & (key <= query + WINDOW) & (kseg_ref[...] == qseg_ref[...])
    bias_ref[...] = jnp.where(allowed, 0.0, MASKED)


def attn_kernel(
    kv_ref, kseg_ref, qseg_ref, x_ref, gain_ref, a_ref, q_ref, wo_ref, bo_ref,
    mixed_ref, lse_ref, res_ref, n2_ref, r2_ref, ro_ref,
    bias_ref, s_ref, p_ref, acc_ref, vt_ref, rank_ref,
):
    step = pl.program_id(0)
    rows = q_ref.shape[0]
    chunks = kv_ref.shape[0] // rows

    @pl.when(step == 0)
    def _():
        fill_bias(bias_ref, kseg_ref, qseg_ref)
        vt_ref[...] = kv_ref[:, HD:].astype(F32).T.astype(BF)
        acc_ref[...] = jnp.zeros_like(acc_ref)
        rank_ref[...] = jnp.zeros_like(rank_ref)

    for h in range(q_ref.shape[1] // HD):
        part = slice(h * HD, (h + 1) * HD)
        query = q_ref[:, part]
        top = jnp.full((1, rows), MASKED, F32)
        for c in range(chunks):
            span = slice(c * rows, (c + 1) * rows)
            s = mm_nt(kv_ref[span, :HD], query) * SCALE + bias_ref[span]
            s_ref[span] = s
            top = jnp.maximum(top, jnp.max(s, axis=0, keepdims=True))
        total = jnp.zeros((1, rows), F32)
        for c in range(chunks):
            span = slice(c * rows, (c + 1) * rows)
            p = jnp.exp(s_ref[span] - top)
            total = total + jnp.sum(p, axis=0, keepdims=True)
            p_ref[span] = p.astype(BF)
        out = mm(vt_ref[...], p_ref[...]) / total
        mixed_ref[:, part] = out.T.astype(BF)
        lse_ref[0, h : h + 1] = top + jnp.log(total)

    mixed = mixed_ref[...]
    acc_ref[...] += mm_nt(mixed, flat(wo_ref))
    rank_ref[...] += mm_nt(mixed, bo_ref[0])

    @pl.when(step == pl.num_programs(0) - 1)
    def _():
        ro = rank_ref[...].astype(BF)
        ro_ref[...] = ro
        res = x_ref[...].astype(F32) + (acc_ref[...] + mm_nt(ro, a_ref[...]))
        res_ref[...] = res
        n2 = rms(res, gain_ref[...]).astype(BF)
        n2_ref[...] = n2
        r2_ref[...] = mm(n2, a_ref[...]).astype(BF)


def ffn_kernel(
    res_ref, n2_ref, r2_ref, cot_ref, gain_ref, a_ref,
    g_ref, u_ref, d_ref, bg_ref, bu_ref, bd_ref,
    out_ref, gres_ref, gb_ref, wide_ref, gbg_ref, gbu_ref, gbd_ref,
    ffn_ref, g2_ref, rd_ref, gr_ref, r2t_ref, grd_ref, grdt_ref,
):
    step = pl.program_id(0)

    @pl.when(step == 0)
    def _():
        ffn_ref[...] = jnp.zeros_like(ffn_ref)
        g2_ref[...] = jnp.zeros_like(g2_ref)
        rd_ref[...] = jnp.zeros_like(rd_ref)
        gr_ref[...] = jnp.zeros_like(gr_ref)
        r2t_ref[...] = r2_ref[...].astype(F32).T.astype(BF)
        grd = mm(cot_ref[...], a_ref[...]).astype(BF)
        grd_ref[...] = grd
        grdt_ref[...] = grd.astype(F32).T.astype(BF)

    n2, r2, cot = n2_ref[...], r2_ref[...], cot_ref[...]
    w_g, w_u, w_d = flat(g_ref), flat(u_ref), flat(d_ref)
    gate = mm(n2, w_g) + mm(r2, bg_ref[0])
    up = mm(n2, w_u) + mm(r2, bu_ref[0])
    grad_hidden = (mm(cot, w_d) + mm(grd_ref[...], bd_ref[0])).astype(BF).astype(F32)
    square = gate * gate
    th = jnp.tanh(GELU_C * (gate + GELU_A * square * gate))
    half = 0.5 * (1.0 + th)
    act = gate * half
    slope = half + 0.5 * gate * (1.0 - th * th) * (GELU_C * (1.0 + 3.0 * GELU_A * square))
    hidden = (act * up).astype(BF)
    grad_gate = (grad_hidden * up * slope).astype(BF)
    grad_up = (grad_hidden * act).astype(BF)
    ffn_ref[...] += mm_nt(hidden, w_d)
    rd_ref[...] += mm_nt(hidden, bd_ref[0])
    g2_ref[...] += mm_nt(grad_gate, w_g) + mm_nt(grad_up, w_u)
    gr_ref[...] += mm_nt(grad_gate, bg_ref[0]) + mm_nt(grad_up, bu_ref[0])
    gbg_ref[0] = mm(r2t_ref[rows_of(SLOT_G)], grad_gate).astype(BF)
    gbu_ref[0] = mm(r2t_ref[rows_of(SLOT_U)], grad_up).astype(BF)
    gbd_ref[0] = mm(grdt_ref[rows_of(SLOT_D)], hidden).astype(BF)

    @pl.when(step == pl.num_programs(0) - 1)
    def _():
        rd = rd_ref[...].astype(BF)
        gr = gr_ref[...].astype(BF)
        res = res_ref[...]
        out_ref[...] = (res + (ffn_ref[...] + mm_nt(rd, a_ref[...]))).astype(BF)
        grad_two = g2_ref[...] + mm_nt(gr, a_ref[...])
        grad_res = cot_ref[...].astype(F32) + rms_back(res, gain_ref[...], grad_two)
        gres_ref[...] = grad_res
        gb_ref[...] = grad_res.astype(BF)
        wide_ref[...] = mm(gr_ref[...].T.astype(BF), n2) + mm(rd_ref[...].T.astype(BF), cot)


def attn_back_kernel(
    kv_ref, kseg_ref, qseg_ref, gb_ref, a_ref, r1_ref, ro_ref, cos_ref, sin_ref,
    q_ref, mixed_ref, lse_ref, wo_ref, bo_ref, wq_ref, bq_ref,
    dkv_ref, g1_ref, gr_ref, wide_ref, gbo_ref, gbq_ref,
    bias_ref, ds_ref, dk_ref, dv_ref, kt_ref, r1t_ref, gro_ref, grot_ref, gq_ref, gm_ref,
):
    step = pl.program_id(0)
    rows = q_ref.shape[0]
    chunks = kv_ref.shape[0] // rows

    @pl.when(step == 0)
    def _():
        fill_bias(bias_ref, kseg_ref, qseg_ref)
        kt_ref[...] = kv_ref[:, :HD].astype(F32).T.astype(BF)
        r1t_ref[...] = r1_ref[...].astype(F32).T.astype(BF)
        gro = mm(gb_ref[...], a_ref[...]).astype(BF)
        gro_ref[...] = gro
        grot_ref[...] = gro.astype(F32).T.astype(BF)
        dk_ref[...] = jnp.zeros_like(dk_ref)
        dv_ref[...] = jnp.zeros_like(dv_ref)
        g1_ref[...] = jnp.zeros_like(g1_ref)
        gr_ref[...] = jnp.zeros_like(gr_ref)

    gm_ref[...] = (mm(gb_ref[...], flat(wo_ref)) + mm(gro_ref[...], bo_ref[0])).astype(BF)
    gbo_ref[0] = mm(grot_ref[rows_of(SLOT_O)], mixed_ref[...]).astype(BF)
    for h in range(q_ref.shape[1] // HD):
        part = slice(h * HD, (h + 1) * HD)
        query, grad = q_ref[:, part], gm_ref[:, part]
        delta = grad.astype(F32) * mixed_ref[:, part].astype(F32)
        delta = jnp.sum(delta.T, axis=0, keepdims=True)
        lse = lse_ref[0, h : h + 1]
        for c in range(chunks):
            span = slice(c * rows, (c + 1) * rows)
            s = mm_nt(kv_ref[span, :HD], query) * SCALE + bias_ref[span]
            p = jnp.exp(s - lse)
            dp = mm_nt(kv_ref[span, HD:], grad)
            ds = (p * (dp - delta)).astype(BF)
            ds_ref[span] = ds
            dk_ref[span] += mm(ds, query)
            dv_ref[span] += mm(p.astype(BF), grad)
        dq = mm(kt_ref[...], ds_ref[...]) * SCALE
        gq_ref[:, part] = rope_back(dq.T, cos_ref[...], sin_ref[...]).astype(BF)

    gq = gq_ref[...]
    gbq_ref[0] = mm(r1t_ref[rows_of(SLOT_Q)], gq).astype(BF)
    gr_ref[...] += mm_nt(gq, bq_ref[0])
    g1_ref[...] += mm_nt(gq, flat(wq_ref))

    @pl.when(step == pl.num_programs(0) - 1)
    def _():
        dkv_ref[:, :HD] = (dk_ref[...] * SCALE).astype(BF)
        dkv_ref[:, HD:] = dv_ref[...].astype(BF)
        wide_ref[...] = mm(ro_ref[...].astype(F32).T.astype(BF), gb_ref[...])


def final_kernel(
    x_ref, gain_ref, a_ref, n1_ref, r1_ref, kvw_ref, bkv_ref, cos_ref, sin_ref,
    gkv_ref, g1_ref, gr_ref, gres_ref, widef_ref, wideo_ref,
    grad_ref, wide_ref, kvg_ref,
):
    gk = rope_back(gkv_ref[:, :HD].astype(F32), cos_ref[...], sin_ref[...]).astype(BF)
    gv = gkv_ref[:, HD:].astype(BF)
    gr = gr_ref[...] + mm_nt(gk, bkv_ref[0]) + mm_nt(gv, bkv_ref[1])
    wide = mm(gr.T.astype(BF), n1_ref[...]) + widef_ref[...] + wideo_ref[...]
    wide_ref[...] = wide.T.astype(BF)
    r1t = r1_ref[...].astype(F32).T.astype(BF)
    kvg_ref[0] = mm(r1t[rows_of(SLOT_K)], gk).astype(BF)
    kvg_ref[1] = mm(r1t[rows_of(SLOT_V)], gv).astype(BF)
    g1 = g1_ref[...] + mm_nt(gk, kvw_ref[0]) + mm_nt(gv, kvw_ref[1])
    g1 = g1 + mm_nt(gr.astype(BF), a_ref[...])
    x = x_ref[...].astype(F32)
    grad_ref[...] = gres_ref[...] + rms_back(x, gain_ref[...], g1)


def whole(array):
    rank = len(array.shape)
    return pl.BlockSpec(array.shape, lambda *_: (0,) * rank)


def out_whole(shape):
    rank = len(shape)
    return pl.BlockSpec(shape, lambda *_: (0,) * rank)


def call(kernel, name, steps, args, specs, outs, out_specs, scratch, flops, nbytes):
    return pl.pallas_call(
        kernel,
        name=name,
        grid=(steps,),
        in_specs=specs,
        out_specs=out_specs,
        out_shape=outs,
        scratch_shapes=scratch,
        compiler_params=pltpu.CompilerParams(
            dimension_semantics=("arbitrary",), vmem_limit_bytes=VMEM_LIMIT
        ),
        cost_estimate=pl.CostEstimate(flops=flops, bytes_accessed=nbytes, transcendentals=0),
    )(*args)


def on_device(
    tokens, cotangent, segments, adapter_ids, norm_gains, q_weight, kv_weight, out_weight,
    gate_up_weight, down_weight, wide_adapters, kv_adapter, q_adapter, out_adapter,
    gate_up_adapter, down_adapter,
):
    rows, width = tokens.shape
    dp_count, tensor_count = lax.axis_size("dp"), lax.axis_size("tensor")
    devices = dp_count * tensor_count
    group_rows = rows * tensor_count
    seq_length = 2 * group_rows
    shard_rows = q_weight.shape[0]
    q_cols, ff_cols = q_weight.shape[1], gate_up_weight.shape[2]
    pack_cols = 3 * ff_cols + 2 * q_cols
    seqs = adapter_ids.shape[0]
    adapters = wide_adapters.shape[2] // RANK
    q_block = 3 * ff_cols // q_cols
    dp = lax.axis_index("dp")
    tensor = lax.axis_index("tensor")
    adapter = lax.dynamic_index_in_dim(adapter_ids, dp // 2, keepdims=False)
    column = adapter * RANK

    def sds(shape, dtype):
        return jax.ShapeDtypeStruct(shape, dtype)

    pack = jnp.concatenate(
        [gate_up_weight[0], gate_up_weight[1], down_weight.T, q_weight, out_weight.T], axis=1
    )
    weights = lax.all_gather(pack, BOTH, axis=0, tiled=False)
    weights = weights.reshape(dp_count, tensor_count, shard_rows, pack_cols)
    kv_full = lax.all_gather(kv_weight, "dp", axis=1, tiled=True)

    wide = wide_adapters.reshape(7, shard_rows, adapters, RANK)
    wide = jnp.take(wide, adapter_ids, axis=2).transpose(2, 1, 0, 3)
    wide = wide.reshape(seqs, shard_rows, 7 * RANK)
    wide = jnp.pad(wide, ((0, 0), (0, 0), (0, LANES - 7 * RANK)))
    wide = jnp.repeat(wide, dp_count // seqs, axis=0)
    a_all = lax.all_to_all(wide, "dp", 0, 0, tiled=True).reshape(width, LANES)

    def take_rows(matrix):
        return lax.dynamic_slice_in_dim(matrix, column, RANK, matrix.ndim - 2)

    def take_cols(matrix):
        return lax.dynamic_slice_in_dim(matrix, column, RANK, matrix.ndim - 1)

    gu_rows = take_rows(gate_up_adapter)
    b_own = jnp.concatenate(
        [gu_rows[0], gu_rows[1], take_cols(down_adapter).T, take_rows(q_adapter), take_cols(out_adapter).T],
        axis=1,
    )
    b_all = lax.all_gather(b_own, "tensor", axis=0, tiled=False)

    def in_slot(block, slot):
        pads = [(0, 0)] * block.ndim
        pads[-2] = (slot * RANK, LANES - (slot + 1) * RANK)
        return jnp.pad(block, pads)

    f1, f2, f3 = ff_cols, 2 * ff_cols, 3 * ff_cols
    b_pad = jnp.concatenate(
        [
            in_slot(b_all[:, :, :f1], SLOT_G),
            in_slot(b_all[:, :, f1:f2], SLOT_U),
            in_slot(b_all[:, :, f2:f3], SLOT_D),
            in_slot(b_all[:, :, f3 : f3 + q_cols], SLOT_Q),
            in_slot(b_all[:, :, f3 + q_cols :], SLOT_O),
        ],
        axis=2,
    )
    kv_rows = take_rows(kv_adapter)
    b_kv = jnp.stack([in_slot(kv_rows[0], SLOT_K), in_slot(kv_rows[1], SLOT_V)])

    start = dp * group_rows + tensor * rows
    positions = (start + jnp.arange(rows)) % seq_length
    half = HD // 2
    frequency = 10000.0 ** (-(jnp.arange(half).astype(F32) / half))
    angles = positions.astype(F32)[:, None] * frequency[None, :]
    cos, sin = jnp.cos(angles), jnp.sin(angles)
    cos = jnp.concatenate([cos, cos], axis=1)
    sin = jnp.concatenate([-sin, sin], axis=1)

    padded = jnp.concatenate([jnp.full((WINDOW,), -1, jnp.int32), segments])
    kseg = lax.dynamic_slice_in_dim(padded, start, WINDOW + rows, 0)
    qseg = kseg[WINDOW:].reshape(1, rows)
    kseg = kseg.reshape(WINDOW + rows, 1)
    span = WINDOW + rows

    gain_one, gain_two = norm_gains[0:1], norm_gains[1:2]

    def weight_spec(cols, block):
        return pl.BlockSpec((dp_count, 1, shard_rows, cols), lambda t: (0, t, 0, block))

    def adapter_spec(cols, block):
        return pl.BlockSpec((1, LANES, cols), lambda t: (t, 0, block))

    def token_cols(cols):
        return pl.BlockSpec((rows, cols), lambda t: (0, t))

    def by_step(*shape):
        return pl.BlockSpec((1,) + shape, lambda t: (t,) + (0,) * len(shape))

    heads_cols = tensor_count * q_cols
    q_spec, qb_spec = weight_spec(q_cols, q_block), adapter_spec(q_cols, q_block)
    o_spec, ob_spec = weight_spec(q_cols, q_block + 1), adapter_spec(q_cols, q_block + 1)

    args = (tokens, gain_one, a_all, kv_full, b_kv, cos, sin, weights, b_pad)
    normed_one, rank_one, kv_own, queries = call(
        pre_kernel, "qkv", tensor_count, args,
        [whole(v) for v in args[:7]] + [q_spec, qb_spec],
        (sds((rows, width), BF), sds((rows, LANES), BF), sds((rows, 2 * HD), BF), sds((rows, heads_cols), BF)),
        (out_whole((rows, width)), out_whole((rows, LANES)), out_whole((rows, 2 * HD)), token_cols(q_cols)),
        [], 2 * rows * width * (heads_cols + 384), 2 * width * heads_cols,
    )

    kv_half = lax.all_gather(kv_own, "tensor", axis=0, tiled=True)
    kv_prev = lax.ppermute(kv_half, "dp", [(2 * s, 2 * s + 1) for s in range(dp_count // 2)])
    kv_window = lax.dynamic_slice_in_dim(jnp.concatenate([kv_prev, kv_half]), tensor * rows, span, 0)

    args = (kv_window, kseg, qseg, tokens, gain_two, a_all, queries, weights, b_pad)
    mixed, lse, residual, normed_two, rank_two, rank_out = call(
        attn_kernel, "attention", tensor_count, args,
        [whole(v) for v in args[:6]] + [token_cols(q_cols), o_spec, ob_spec],
        (
            sds((rows, heads_cols), BF), sds((tensor_count, 8, rows), F32), sds((rows, width), F32),
            sds((rows, width), BF), sds((rows, LANES), BF), sds((rows, LANES), BF),
        ),
        (
            token_cols(q_cols), by_step(8, rows), out_whole((rows, width)),
            out_whole((rows, width)), out_whole((rows, LANES)), out_whole((rows, LANES)),
        ),
        [
            pltpu.VMEM((span, rows), F32), pltpu.VMEM((span, rows), F32), pltpu.VMEM((span, rows), BF),
            pltpu.VMEM((rows, width), F32), pltpu.VMEM((HD, span), BF), pltpu.VMEM((rows, LANES), F32),
        ],
        2 * rows * heads_cols * (2 * span + width), 2 * width * heads_cols,
    )

    args = (residual, normed_two, rank_two, cotangent, gain_two, a_all, weights, weights, weights, b_pad, b_pad, b_pad)
    block_output, grad_residual, grad_branch, wide_ffn, grad_bg, grad_bu, grad_bd = call(
        ffn_kernel, "feed_forward", tensor_count, args,
        [whole(v) for v in args[:6]]
        + [weight_spec(ff_cols, j) for j in range(3)]
        + [adapter_spec(ff_cols, j) for j in range(3)],
        (sds((rows, width), BF), sds((rows, width), F32), sds((rows, width), BF), sds((LANES, width), F32))
        + (sds((tensor_count, RANK, ff_cols), BF),) * 3,
        (out_whole((rows, width)), out_whole((rows, width)), out_whole((rows, width)), out_whole((LANES, width)))
        + (by_step(RANK, ff_cols),) * 3,
        [
            pltpu.VMEM((rows, width), F32), pltpu.VMEM((rows, width), F32),
            pltpu.VMEM((rows, LANES), F32), pltpu.VMEM((rows, LANES), F32),
            pltpu.VMEM((LANES, rows), BF), pltpu.VMEM((rows, LANES), BF), pltpu.VMEM((LANES, rows), BF),
        ],
        12 * rows * width * tensor_count * ff_cols, 6 * width * tensor_count * ff_cols,
    )

    args = (
        kv_window, kseg, qseg, grad_branch, a_all, rank_one, rank_out, cos, sin,
        queries, mixed, lse, weights, b_pad, weights, b_pad,
    )
    dkv, grad_one, grad_rank, wide_out, grad_bo, grad_bq = call(
        attn_back_kernel, "attention_back", tensor_count, args,
        [whole(v) for v in args[:9]]
        + [token_cols(q_cols), token_cols(q_cols), by_step(8, rows), o_spec, ob_spec, q_spec, qb_spec],
        (
            sds((span, 2 * HD), BF), sds((rows, width), F32), sds((rows, LANES), F32), sds((LANES, width), F32),
            sds((tensor_count, RANK, q_cols), BF), sds((tensor_count, RANK, q_cols), BF),
        ),
        (
            out_whole((span, 2 * HD)), out_whole((rows, width)), out_whole((rows, LANES)), out_whole((LANES, width)),
            by_step(RANK, q_cols), by_step(RANK, q_cols),
        ),
        [
            pltpu.VMEM((span, rows), F32), pltpu.VMEM((span, rows), BF),
            pltpu.VMEM((span, HD), F32), pltpu.VMEM((span, HD), F32), pltpu.VMEM((HD, span), BF),
            pltpu.VMEM((LANES, rows), BF), pltpu.VMEM((rows, LANES), BF), pltpu.VMEM((LANES, rows), BF),
            pltpu.VMEM((rows, q_cols), BF), pltpu.VMEM((rows, q_cols), BF),
        ],
        2 * rows * heads_cols * (5 * span + 2 * width), 4 * width * heads_cols,
    )

    placed = lax.dynamic_update_slice_in_dim(jnp.zeros((seq_length, 2 * HD), BF), dkv, tensor * rows, 0)
    returned = lax.ppermute(placed[:group_rows], "dp", [(2 * s + 1, 2 * s) for s in range(dp_count // 2)])
    gathered = placed[group_rows:].astype(F32) + returned.astype(F32)
    grad_kv = lax.psum_scatter(gathered.astype(BF), "tensor", scatter_dimension=0, tiled=True)

    args = (
        tokens, gain_one, a_all, normed_one, rank_one, kv_full, b_kv, cos, sin,
        grad_kv, grad_one, grad_rank, grad_residual, wide_ffn, wide_out,
    )
    input_grad, wide_term, kv_term = call(
        final_kernel, "input_gradient", 1, args, [whole(v) for v in args],
        (sds((rows, width), F32), sds((width, LANES), BF), sds((2, RANK, HD), BF)),
        (out_whole((rows, width)), out_whole((width, LANES)), out_whole((2, RANK, HD))),
        [], 2 * rows * width * 640, 8 * rows * width,
    )

    own_rows = width // devices
    kv_rows_out = jnp.tile(kv_term.transpose(1, 0, 2), (devices // RANK, 1, 1))
    payload = jnp.concatenate(
        [wide_term.reshape(devices, own_rows, LANES), kv_rows_out, jnp.zeros((devices, 2, LANES), BF)], axis=1
    )
    received = lax.all_to_all(payload, BOTH, 0, 0, tiled=True)
    sent_rows = own_rows + 4
    source_adapter = jnp.repeat(adapter_ids, devices // seqs)
    pick = (jnp.arange(adapters)[:, None] == source_adapter[None, :]).astype(BF)
    summed = mm(pick, received.reshape(devices, sent_rows * LANES)).reshape(adapters, sent_rows, LANES)
    wide_grad = summed[:, :own_rows, : 7 * RANK].reshape(adapters, own_rows, 7, RANK)
    wide_grad = wide_grad.transpose(2, 1, 0, 3).reshape(7, own_rows, adapters * RANK)
    own_row = dp * tensor_count + tensor
    kv_adapter_grad = lax.dynamic_index_in_dim(
        summed[:, own_rows : own_rows + 2], own_row // RANK, 0, keepdims=False
    ).reshape(2, 1, HD)

    pick_dp = (jnp.arange(adapters)[:, None] == jnp.repeat(adapter_ids, dp_count // seqs)[None, :]).astype(BF)

    def by_adapter(terms):
        own = lax.psum_scatter(terms, "tensor", scatter_dimension=0, tiled=True)
        every = lax.all_gather(own.reshape(RANK, -1), "dp", axis=0, tiled=False)
        cols = every.shape[2]
        return mm(pick_dp, every.reshape(dp_count, RANK * cols)).reshape(adapters * RANK, cols)

    early = by_adapter(jnp.concatenate([grad_bg, grad_bu, grad_bd, grad_bo], axis=2))
    q_adapter_grad = by_adapter(grad_bq)
    gate_up_adapter_grad = jnp.stack([early[:, :f1], early[:, f1:f2]])
    down_adapter_grad = early[:, f2:f3].T
    out_adapter_grad = early[:, f3:].T
    return (
        block_output, input_grad, wide_grad, kv_adapter_grad,
        q_adapter_grad, out_adapter_grad, gate_up_adapter_grad, down_adapter_grad,
    )


def solution(mesh):
    return jax.shard_map(
        on_device,
        mesh=mesh,
        in_specs=(
            P(BOTH, None), P(BOTH, None), P(), P(), P(), P("dp", "tensor"), P(None, "dp", None),
            P("tensor", "dp"), P(None, "dp", "tensor"), P("tensor", "dp"), P(None, "dp", None), P(),
            P(None, "tensor"), P("tensor", None), P(None, None, "tensor"), P("tensor", None),
        ),
        out_specs=(
            P(BOTH, None), P(BOTH, None), P(None, BOTH, None), P(None, BOTH, None),
            P(None, "tensor"), P("tensor", None), P(None, None, "tensor"), P("tensor", None),
        ),
        check_vma=False,
    )
```

time: 1240 us -> 410 us (0.33)
  waiting for transfers between devices: 594 us -> 143 us
  local copies, waits for them, and re-layouts: 303 us -> 35.5 us
  matrix products: 199 us -> 2.33 us
  Pallas kernels: 0 us -> 96.5 us
  other arithmetic: 74.7 us -> 10.8 us
  blocking collectives: 26.7 us -> 83.8 us
  starting transfers between devices: 7.4 us -> 22 us
  loops' own time: 13.4 us -> 0 us
    dynamic_update_slice x18 -> x1, local copies, waits for them, and re-layouts: 266 us -> 1.14 us  [on_device(): lax.dynamic_update_slice_in_dim(jnp.zeros((seq_length, 2 * HD), BF), dkv,...]
    reduce_scatter x5 -> x3, waiting for transfers between devices: 300 us -> 40.5 us  [the longest x1 24.2 us: on_device(): lax.psum_scatter(gathered.astype(BF), 'tensor', scatter_dimension=0, tile...]
    dot_general x51 -> x3, matrix products: 199 us -> 2.33 us  [mm(): lax.dot_general(a, b, (((1,), (0,)), ((), ())), preferred_element_type=F32)]
    all_gather x9 -> x2, waiting for transfers between devices: 288 us -> 97.5 us  [the longest x1 77.6 us: on_device(): weights = lax.all_gather(pack, BOTH, axis=0, tiled=False)]
    pallas_call x0 -> x5, Pallas kernels: none -> 96.5 us  [call(): pl.pallas_call(kernel, name=name, grid=(steps,), in_specs=specs, out_spec...]
    all_gather x1 -> x4, blocking collectives: 26.7 us -> 83.8 us  [the longest x1 30.2 us: by_adapter(): every = lax.all_gather(own.reshape(RANK, -1), 'dp', axis=0, tiled=False)]
    convert_element_type x12 -> x2, other arithmetic: 38.3 us -> 0.93 us  [the longest x1 0.92 us: on_device(): gathered.astype(BF)]
    all_to_all x0 -> x2, starting transfers between devices: none -> 18.1 us  [the longest x1 9.55 us: on_device(): received = lax.all_to_all(payload, BOTH, 0, 0, tiled=True)]
  transfers between devices with their start and end apart: 18 -> 9, of which waited for: 13 -> 7; matrix products, arithmetic and copies ran while one was open for 34% -> 6% of each run, Pallas kernels for 0% -> 1%
where the time goes in v1:
time: 410 us; the launch traced here: 408 us
  waiting for transfers between devices  143 us (35%)
  Pallas kernels  96.5 us (24%)
  blocking collectives  83.8 us (20%)
  local copies, waits for them, and re-layouts  35.5 us (9%)
  starting transfers between devices  22 us (5%)
  between operations  14.8 us (4%)
  other arithmetic  10.8 us (3%)
    pallas_call x5, Pallas kernels, call(): pl.pallas_call(kernel, name=name, grid=(steps,), in_specs=specs, out_spec...  96.5 us
    all_gather x1, waiting for transfers between devices, on_device(): weights = lax.all_gather(pack, BOTH, axis=0, tiled=False)  77.6 us
    all_gather x1, blocking collectives, by_adapter(): every = lax.all_gather(own.reshape(RANK, -1), 'dp', axis=0, tiled=False)  30.2 us
    all_gather x1, blocking collectives, on_device(): kv_full = lax.all_gather(kv_weight, 'dp', axis=1, tiled=True)  30.1 us
    reduce_scatter x1, waiting for transfers between devices, on_device(): lax.psum_scatter(gathered.astype(BF), 'tensor', scatter_dimension=0, tile...  24.2 us
    all_gather x1, waiting for transfers between devices, by_adapter(): every = lax.all_gather(own.reshape(RANK, -1), 'dp', axis=0, tiled=False)  19.9 us
    unnamed x44, local copies, waits for them, and re-layouts  18.6 us
    reduce_scatter x2, waiting for transfers between devices, by_adapter(): own = lax.psum_scatter(terms, 'tensor', scatter_dimension=0, tiled=True)  16.3 us
  transfers between devices with their start and end apart: 9, of which 7 were waited for; matrix products, arithmetic and copies ran while one was open for 6% of the time, Pallas kernels for 1%

profile of v1, /device:TPU:1, one launch (start us, length us, event | category | flops | bytes accessed | tf_op | source)
XLA Modules:
  0.0 408.3 jit_solution(7214558808118848326)
XLA Ops:
  16.0 8.6 %all-to-all-start = ((bf16[32,48,128]{2,1,0:T(8,128)(2,1)}), bf16[32,48,128]{2,1,0:T(8,128)(2,1)S(1)}, u32[]{:S(2)}, u32[]{:S(2)}) async-start(bf16[32,48,128]{2,1,0:T(8,128)(2,1)} %bitcast.3), calls=%async_computation | async-start | bytes 786432 | tf_op jit(solution)/shard_map/all_to_all | solution.py:328
  31.5 13.2 %all-gather.1 = bf16[64,4224]{1,0:T(8,128)(2,1)S(1)} all-gather(bf16[16,4224]{1,0:T(8,128)(2,1)S(1)} %constant_dynamic-update-slice_fusion.1), channel_id=3, replica_groups=mesh['dp'=32,'tensor'=4] {'tensor'}, dimensions={0}, use_global_device_ids=true | all-gather | bytes 675840 | tf_op jit(solution)/shard_map/all_gather | solution.py:341
  49.9 30.1 %all_gather.24.kvw_ref = bf16[2,1536,128]{2,1,0:T(8,128)(2,1)} all-gather(bf16[2,48,128]{2,1,0:T(8,128)(2,1)S(1)} %copy-done.9), channel_id=1, replica_groups=mesh['dp'=32,'tensor'=4] {'dp'}, dimensions={1}, use_global_device_ids=true | all-gather | bytes 811008 | tf_op jit(solution)/shard_map/all_gather | solution.py:321
  80.6 77.6 %all-gather.7.cloned.1.call-done = bf16[6144,4224]{1,0:T(8,128)(2,1)} async-done(((bf16[48,4224]{1,0:T(8,128)(2,1)}), bf16[6144,4224]{1,0:T(8,128)(2,1)}) %all-gather.7.cloned.1.call-update) | async-done | bytes 51904528 | tf_op jit(solution)/shard_map/all_gather | solution.py:319
  158.2 7.5 %qkv.1 = (bf16[256,1536]{1,0:T(8,128)(2,1)}, bf16[256,128]{1,0:T(8,128)(2,1)}, bf16[256,256]{1,0:T(8,128)(2,1)}, bf16[256,1536]{1,0:T(8,128)(2,1)}) custom-call(bf16[256,1536]{1,0:T(8,128)(2,1)} %x_ref.5, f32[1,1536]{1,0:T(1,128)} %get-tuple-element.103.gain_ref, bf16[1536,128]{1,0:T(8,128)(2,1)} %bitcast.80, bf16[2,1536,128]{2,1,0:T(8,128)(2,1)} %all_gather.24.kvw_ref, ...), custom_call_target="tpu_custom_call" | custom-call | flops 1509949440 | bytes 4718592 | tf_op jit(solution)/shard_map/qkv/pallas_call | solution.py:277
  165.8 10.3 %all_gather.29 = bf16[1024,256]{1,0:T(8,128)(2,1)S(1)} all-gather(bf16[256,256]{1,0:T(8,128)(2,1)} %get-tuple-element.34), channel_id=1, replica_groups=mesh['dp'=32,'tensor'=4] {'tensor'}, dimensions={0}, use_global_device_ids=true | all-gather | bytes 655360 | tf_op jit(solution)/shard_map/all_gather | solution.py:404
  179.2 2.5 collective-permute-done
  181.7 2.2 fusion.kv_ref
  183.9 16.6 %attention.1 = (bf16[256,1536]{1,0:T(8,128)(2,1)}, f32[4,8,256]{2,1,0:T(8,128)}, f32[256,1536]{1,0:T(8,128)}, bf16[256,1536]{1,0:T(8,128)(2,1)}, bf16[256,128]{1,0:T(8,128)(2,1)}, /*index=5*/bf16[256,128]{1,0:T(8,128)(2,1)}) custom-call(bf16[1280,256]{1,0:T(8,128)(2,1)} %fusion.kv_ref, s32[1280,1]{1,0:T(8,128)} %reshape.132.kseg_ref, s32[1,256]{1,0:T(1,128)} %bitcast.95, ...), custom_call_target="tpu_custom_call" | custom-call | flops 3221225472 | bytes 4718592 | tf_op jit(solution)/shard_map/attention/pallas_call | solution.py:277
  200.5 39.2 %feed_forward.1 = (bf16[256,1536]{1,0:T(8,128)(2,1)}, f32[256,1536]{1,0:T(8,128)}, bf16[256,1536]{1,0:T(8,128)(2,1)}, f32[128,1536]{1,0:T(8,128)}, bf16[4,16,115...) custom-call(f32[256,1536]{1,0:T(8,128)} %get-tuple-element.36.res_ref, ...), custom_call_target="tpu_custom_call" | custom-call | flops 21743271936 | bytes 42467328 | tf_op jit(solution)/shard_map/feed_forward/pallas_call | solution.py:277
  239.7 27.1 %attention_back.1 = (bf16[1280,256]{1,0:T(8,128)(2,1)}, f32[256,1536]{1,0:T(8,128)}, f32[256,128]{1,0:T(8,128)}, f32[128,1536]{1,0:T(8,128)}, bf16[4,16,384]{2,1,0:T(8,128)(2,1)}, /*index=5*/bf16[4,16,384]{2,1,0:T(8,128)(2,1)}) custom-call(bf16[1280,256]{1,0:T(8,128)(2,1)} %fusion.kv_ref, s32[1280,1]{1,0:T(8,128)} %reshape.132.kseg_ref, s32[1,256]{1,0:T(1,128)} %bitcast.96, ...), custom_call_target="tpu_custom_call" | custom-call | flops 7449083904 | bytes 9437184 | tf_op jit(solution)/shard_map/attention_back/pallas_call | solution.py:277
  269.8 2.4 collective-permute-start.1
  275.3 13.2 %reduce-scatter.8.cloned.1.call-done = bf16[1,16,3840]{2,1,0:T(8,128)(2,1)} async-done(((bf16[4,16,3840]{2,1,0:T(8,128)(2,1)}), bf16[1,16,3840]{2,1,0:T(8,128)(2,1)}) %reduce-scatter.8.cloned.1.call-update) | async-done | bytes 122896 | tf_op jit(solution)/shard_map/reduce_scatter | solution.py:506
  288.6 24.2 %reduce-scatter.4.cloned.1.call-done.gkv_ref = bf16[256,256]{1,0:T(8,128)(2,1)} async-done(((bf16[1024,256]{1,0:T(8,128)(2,1)}), bf16[256,256]{1,0:T(8,128)(2,1)}) %reduce-scatter.4.cloned.1.call-update) | async-done | bytes 131088 | tf_op jit(solution)/shard_map/reduce_scatter | solution.py:473
  312.8 6.1 %input_gradient.1 = (f32[256,1536]{1,0:T(8,128)}, bf16[1536,128]{1,0:T(8,128)(2,1)}, bf16[2,16,128]{2,1,0:T(8,128)(2,1)}) custom-call(bf16[256,1536]{1,0:T(8,128)(2,1)} %x_ref.5, f32[1,1536]{1,0:T(1,128)} %get-tuple-element.103.gain_ref, bf16[1536,128]{1,0:T(8,128)(2,1)} %bitcast.84, bf16[256,1536]{1,0:T(8,128)(2,1)} %get-tuple-element.40.n1_ref, ...), custom_call_target="tpu_custom_call" | custom-call | flops 503316480 | bytes 3145728 | tf_op jit(solution)/shard_map/input_gradient/pallas_call | solution.py:277
  321.8 9.5 %all-to-all-start.1 = ((bf16[128,16,128]{2,1,0:T(8,128)(2,1)}), bf16[128,16,128]{2,1,0:T(8,128)(2,1)S(1)}, u32[]{:S(2)}, u32[]{:S(2)}) async-start(bf16[128,16,128]{2,1,0:T(8,128)(2,1)} %maximum_maximum_fusion), calls=%async_computation.2 | async-start | bytes 1048576 | tf_op jit(solution)/shard_map/all_to_all | solution.py:491
  331.7 3.0 reduce-scatter.6.cloned.1.call-done
  334.7 30.2 %all_gather.30 = bf16[32,16,384]{2,1,0:T(8,128)(2,1)S(1)} all-gather(bf16[1,16,384]{2,1,0:T(8,128)(2,1)} %reduce-scatter.6.cloned.1.call-done), channel_id=1, replica_groups=mesh['dp'=32,'tensor'=4] {'dp'}, dimensions={0}, use_global_device_ids=true | all-gather | bytes 405504 | tf_op jit(solution)/shard_map/all_gather | solution.py:507
  368.2 19.9 %all-gather.5.cloned.1.call-done = bf16[32,16,3840]{2,1,0:T(8,128)(2,1)} async-done(((bf16[1,16,3840]{2,1,0:T(8,128)(2,1)}), bf16[32,16,3840]{2,1,0:T(8,128)(2,1)}) %all-gather.5.cloned.1.call-update) | async-done | bytes 3932176 | tf_op jit(solution)/shard_map/all_gather | solution.py:507
  388.1 3.3 copy.72
  391.4 1.9 fusion.6
  393.3 1.9 reshape.118
  397.9 1.7 copy.65
  399.6 2.2 pad_maximum_fusion
  (109 shorter events, 39.0 us)
Async XLA Ops:
  7.2 18.7 %copy-start = (bf16[1152,128]{1,0:T(8,128)(2,1)S(1)}, bf16[1152,128]{1,0:T(8,128)(2,1)}, u32[]{:S(2)}) copy-start(bf16[1152,128]{1,0:T(8,128)(2,1)} %param.31) | copy-start | bytes 884740
  7.2 7.6 %copy-start.11 = (s32[16]{0:T(128)S(1)}, s32[16]{0:T(128)}, u32[]{:S(2)}) copy-start(s32[16]{0:T(128)} %param.19) | copy-start | bytes 196
  7.2 151.0 %all-gather.7.cloned.1.call-start = ((), (), s32[]{:S(2)}) async-start(), calls=%async_computation.9 | async-start | bytes 52310016 | tf_op jit(solution)/shard_map/all_gather | solution.py:319
  10.8 15.4 %copy-start.8 = (bf16[384,128]{1,0:T(8,128)(2,1)S(1)}, bf16[384,128]{1,0:T(8,128)(2,1)}, u32[]{:S(2)}) copy-start(bf16[384,128]{1,0:T(8,128)(2,1)} %param.29) | copy-start | bytes 294916
  11.6 0.7 copy-start.3
  16.0 64.6 %all-to-all-start = ((bf16[32,48,128]{2,1,0:T(8,128)(2,1)}), bf16[32,48,128]{2,1,0:T(8,128)(2,1)S(1)}, u32[]{:S(2)}, u32[]{:S(2)}) async-start(bf16[32,48,128]{2,1,0:T(8,128)(2,1)} %bitcast.3), calls=%async_computation | async-start | bytes 786432 | tf_op jit(solution)/shard_map/all_to_all | solution.py:328
  24.6 263.9 %reduce-scatter.8.cloned.1.call-start = ((), (), s32[]{:S(2)}) async-start(), calls=%async_computation.7 | async-start | bytes 614400 | tf_op jit(solution)/shard_map/reduce_scatter | solution.py:506
  29.4 20.5 %copy-start.9 = (bf16[2,48,128]{2,1,0:T(8,128)(2,1)S(1)}, bf16[2,48,128]{2,1,0:T(8,128)(2,1)}, u32[]{:S(2)}) copy-start(bf16[2,48,128]{2,1,0:T(8,128)(2,1)} %param.22) | copy-start | bytes 73732
  30.6 49.4 %copy-start.10 = (f32[2,1536]{1,0:T(2,128)S(1)}, f32[2,1536]{1,0:T(2,128)}, u32[]{:S(2)}) copy-start(f32[2,1536]{1,0:T(2,128)} %param.20) | copy-start | bytes 36868
  80.6 77.6 %copy-start.2 = (bf16[32,48,128]{2,1,0:T(8,128)(2,1)}, bf16[32,48,128]{2,1,0:T(8,128)(2,1)S(1)}, u32[]{:S(2)}) copy-start(bf16[32,48,128]{2,1,0:T(8,128)(2,1)S(1)} %all-to-all-done) | copy-start | bytes 1179652
  158.2 19.1 %copy-start.4 = (s32[32768]{0:T(1024)S(1)}, s32[32768]{0:T(1024)}, u32[]{:S(2)}) copy-start(s32[32768]{0:T(1024)} %param.18) | copy-start | bytes 393220
  176.1 5.6 %collective-permute-start = (bf16[1024,256]{1,0:T(8,128)(2,1)S(1)}, bf16[1024,256]{1,0:T(8,128)(2,1)S(1)}, u32[]{:S(2)}, u32[]{:S(2)}) collective-permute-start(bf16[1024,256]{1,0:T(8,128)(2,1)S(1)} %all_gather.29), channel_id=1, source_target_pairs={{0,4},{8,12},{16,20},{24,28},{32,36},{40,44},{48,52},{56,60},{64,6... | collective-permute-start | bytes 1572872 | tf_op jit(solution)/shard_map/ppermute | solution.py:405
  239.7 27.1 %copy-start.5 = (bf16[4,16,1152]{2,1,0:T(8,128)(2,1)S(1)}, bf16[4,16,1152]{2,1,0:T(8,128)(2,1)}, u32[]{:S(2)}) copy-start(bf16[4,16,1152]{2,1,0:T(8,128)(2,1)} %get-tuple-element.56) | copy-start | bytes 442372
  239.7 27.1 %copy-start.6 = (bf16[4,16,1152]{2,1,0:T(8,128)(2,1)S(1)}, bf16[4,16,1152]{2,1,0:T(8,128)(2,1)}, u32[]{:S(2)}) copy-start(bf16[4,16,1152]{2,1,0:T(8,128)(2,1)} %get-tuple-element.57) | copy-start | bytes 442372
  239.7 27.1 %copy-start.7 = (bf16[4,16,1152]{2,1,0:T(8,128)(2,1)S(1)}, bf16[4,16,1152]{2,1,0:T(8,128)(2,1)}, u32[]{:S(2)}) copy-start(bf16[4,16,1152]{2,1,0:T(8,128)(2,1)} %get-tuple-element.58) | copy-start | bytes 442372
  268.5 44.3 %reduce-scatter.4.cloned.1.call-start = ((), (), s32[]{:S(2)}) async-start(), calls=%async_computation.5 | async-start | bytes 655360 | tf_op jit(solution)/shard_map/reduce_scatter | solution.py:473
  269.8 3.9 collective-permute-start.1
  274.6 60.1 %reduce-scatter.6.cloned.1.call-start = ((), (), s32[]{:S(2)}) async-start(), calls=%async_computation.6 | async-start | bytes 61440 | tf_op jit(solution)/shard_map/reduce_scatter | solution.py:506
  275.2 112.9 %all-gather.5.cloned.1.call-start = ((), (), s32[]{:S(2)}) async-start(), calls=%async_computation.8 | async-start | bytes 4055040 | tf_op jit(solution)/shard_map/all_gather | solution.py:507
  321.8 44.2 %all-to-all-start.1 = ((bf16[128,16,128]{2,1,0:T(8,128)(2,1)}), bf16[128,16,128]{2,1,0:T(8,128)(2,1)S(1)}, u32[]{:S(2)}, u32[]{:S(2)}) async-start(bf16[128,16,128]{2,1,0:T(8,128)(2,1)} %maximum_maximum_fusion), calls=%async_computation.2 | async-start | bytes 1048576 | tf_op jit(solution)/shard_map/all_to_all | solution.py:491
  393.3 8.4 %copy-start.1 = (bf16[1152,128]{1,0:T(8,128)(2,1)S(1)}, bf16[1152,128]{1,0:T(8,128)(2,1)}, u32[]{:S(2)}) copy-start(bf16[1152,128]{1,0:T(8,128)(2,1)} %param.31) | copy-start | bytes 884740
Sparse Core Ops, SparseCore 0:
  12.5 145.6 all-gather.6
  268.6 19.8 reduce-scatter.7
  291.6 21.1 reduce-scatter.3
  315.1 19.5 reduce-scatter.5
  336.8 51.2 all-gather.4

commit v2 on v1

--- a/solution.py
+++ b/solution.py
@@ -59,7 +59,7 @@
 
 
 def pre_kernel(
-    x_ref, gain_ref, a_ref, kvw_ref, bkv_ref, cos_ref, sin_ref, wq_ref, bq_ref,
+    x_ref, gain_ref, a_ref, wk_ref, wv_ref, bkv_ref, cos_ref, sin_ref, wq_ref, bq_ref,
     n1_ref, r1_ref, kv_ref, q_ref,
 ):
     @pl.when(pl.program_id(0) == 0)
@@ -68,9 +68,9 @@
         n1_ref[...] = n1
         r1 = mm(n1, a_ref[...]).astype(BF)
         r1_ref[...] = r1
-        key = mm(n1, kvw_ref[0]) + mm(r1, bkv_ref[0])
+        key = mm(n1, wk_ref[...]) + mm(r1, bkv_ref[0])
         kv_ref[:, :HD] = rope(key, cos_ref[...], sin_ref[...]).astype(BF)
-        kv_ref[:, HD:] = (mm(n1, kvw_ref[1]) + mm(r1, bkv_ref[1])).astype(BF)
+        kv_ref[:, HD:] = (mm(n1, wv_ref[...]) + mm(r1, bkv_ref[1])).astype(BF)
 
     lin = mm(n1_ref[...], flat(wq_ref)) + mm(r1_ref[...], bq_ref[0])
     for h in range(lin.shape[1] // HD):
@@ -88,8 +88,8 @@
 
 def attn_kernel(
     kv_ref, kseg_ref, qseg_ref, x_ref, gain_ref, a_ref, q_ref, wo_ref, bo_ref,
-    mixed_ref, lse_ref, res_ref, n2_ref, r2_ref, ro_ref,
-    bias_ref, s_ref, p_ref, acc_ref, vt_ref, rank_ref,
+    mixed_ref, p_ref, res_ref, n2_ref, r2_ref, ro_ref,
+    bias_ref, s_ref, acc_ref, vt_ref, rank_ref,
 ):
     step = pl.program_id(0)
     rows = q_ref.shape[0]
@@ -116,10 +116,12 @@
             span = slice(c * rows, (c + 1) * rows)
             p = jnp.exp(s_ref[span] - top)
             total = total + jnp.sum(p, axis=0, keepdims=True)
-            p_ref[span] = p.astype(BF)
-        out = mm(vt_ref[...], p_ref[...]) / total
-        mixed_ref[:, part] = out.T.astype(BF)
-        lse_ref[0, h : h + 1] = top + jnp.log(total)
+            s_ref[span] = p
+        inv = 1.0 / total
+        for c in range(chunks):
+            span = slice(c * rows, (c + 1) * rows)
+            p_ref[h, span] = (s_ref[span] * inv).astype(BF)
+        mixed_ref[:, part] = mm(vt_ref[...], p_ref[h]).T.astype(BF)
 
     mixed = mixed_ref[...]
     acc_ref[...] += mm_nt(mixed, flat(wo_ref))
@@ -137,9 +139,9 @@
 
 
 def ffn_kernel(
-    res_ref, n2_ref, r2_ref, cot_ref, gain_ref, a_ref,
+    res_ref, n2_ref, r2_ref, cot_ref, gain_ref, mixed_ref, ro_ref, a_ref,
     g_ref, u_ref, d_ref, bg_ref, bu_ref, bd_ref,
-    out_ref, gres_ref, gb_ref, wide_ref, gbg_ref, gbu_ref, gbd_ref,
+    out_ref, gres_ref, gb_ref, wide_ref, gro_ref, gbo_ref, gbg_ref, gbu_ref, gbd_ref,
     ffn_ref, g2_ref, rd_ref, gr_ref, r2t_ref, grd_ref, grdt_ref,
 ):
     step = pl.program_id(0)
@@ -185,15 +187,23 @@
         grad_two = g2_ref[...] + mm_nt(gr, a_ref[...])
         grad_res = cot_ref[...].astype(F32) + rms_back(res, gain_ref[...], grad_two)
         gres_ref[...] = grad_res
-        gb_ref[...] = grad_res.astype(BF)
-        wide_ref[...] = mm(gr_ref[...].T.astype(BF), n2) + mm(rd_ref[...].T.astype(BF), cot)
+        grad_branch = grad_res.astype(BF)
+        gb_ref[...] = grad_branch
+        gro = mm(grad_branch, a_ref[...])
+        gro_ref[...] = gro.astype(BF)
+        grot = gro.T[rows_of(SLOT_O)].astype(BF)
+        cols = gbo_ref.shape[2]
+        for t in range(gbo_ref.shape[0]):
+            gbo_ref[t] = mm(grot, mixed_ref[:, t * cols : (t + 1) * cols]).astype(BF)
+        wide = mm(gr_ref[...].T.astype(BF), n2) + mm(rd_ref[...].T.astype(BF), cot)
+        wide_ref[...] = wide + mm(ro_ref[...].astype(F32).T.astype(BF), grad_branch)
 
 
 def attn_back_kernel(
-    kv_ref, kseg_ref, qseg_ref, gb_ref, a_ref, r1_ref, ro_ref, cos_ref, sin_ref,
-    q_ref, mixed_ref, lse_ref, wo_ref, bo_ref, wq_ref, bq_ref,
-    dkv_ref, g1_ref, gr_ref, wide_ref, gbo_ref, gbq_ref,
-    bias_ref, ds_ref, dk_ref, dv_ref, kt_ref, r1t_ref, gro_ref, grot_ref, gq_ref, gm_ref,
+    kv_ref, gb_ref, gro_ref, r1_ref, cos_ref, sin_ref,
+    q_ref, mixed_ref, p_ref, wo_ref, bo_ref, wq_ref, bq_ref,
+    dkv_ref, g1_ref, gr_ref, gbq_ref,
+    ds_ref, dk_ref, dv_ref, kt_ref, r1t_ref, gq_ref, gm_ref,
 ):
     step = pl.program_id(0)
     rows = q_ref.shape[0]
@@ -201,34 +211,27 @@
 
     @pl.when(step == 0)
     def _():
-        fill_bias(bias_ref, kseg_ref, qseg_ref)
         kt_ref[...] = kv_ref[:, :HD].astype(F32).T.astype(BF)
         r1t_ref[...] = r1_ref[...].astype(F32).T.astype(BF)
-        gro = mm(gb_ref[...], a_ref[...]).astype(BF)
-        gro_ref[...] = gro
-        grot_ref[...] = gro.astype(F32).T.astype(BF)
         dk_ref[...] = jnp.zeros_like(dk_ref)
         dv_ref[...] = jnp.zeros_like(dv_ref)
         g1_ref[...] = jnp.zeros_like(g1_ref)
         gr_ref[...] = jnp.zeros_like(gr_ref)
 
     gm_ref[...] = (mm(gb_ref[...], flat(wo_ref)) + mm(gro_ref[...], bo_ref[0])).astype(BF)
-    gbo_ref[0] = mm(grot_ref[rows_of(SLOT_O)], mixed_ref[...]).astype(BF)
     for h in range(q_ref.shape[1] // HD):
         part = slice(h * HD, (h + 1) * HD)
         query, grad = q_ref[:, part], gm_ref[:, part]
         delta = grad.astype(F32) * mixed_ref[:, part].astype(F32)
         delta = jnp.sum(delta.T, axis=0, keepdims=True)
-        lse = lse_ref[0, h : h + 1]
         for c in range(chunks):
             span = slice(c * rows, (c + 1) * rows)
-            s = mm_nt(kv_ref[span, :HD], query) * SCALE + bias_ref[span]
-            p = jnp.exp(s - lse)
+            p = p_ref[h, span]
             dp = mm_nt(kv_ref[span, HD:], grad)
-            ds = (p * (dp - delta)).astype(BF)
+            ds = (p.astype(F32) * (dp - delta)).astype(BF)
             ds_ref[span] = ds
             dk_ref[span] += mm(ds, query)
-            dv_ref[span] += mm(p.astype(BF), grad)
+            dv_ref[span] += mm(p, grad)
         dq = mm(kt_ref[...], ds_ref[...]) * SCALE
         gq_ref[:, part] = rope_back(dq.T, cos_ref[...], sin_ref[...]).astype(BF)
 
@@ -241,23 +244,25 @@
     def _():
         dkv_ref[:, :HD] = (dk_ref[...] * SCALE).astype(BF)
         dkv_ref[:, HD:] = dv_ref[...].astype(BF)
-        wide_ref[...] = mm(ro_ref[...].astype(F32).T.astype(BF), gb_ref[...])
 
 
 def final_kernel(
-    x_ref, gain_ref, a_ref, n1_ref, r1_ref, kvw_ref, bkv_ref, cos_ref, sin_ref,
-    gkv_ref, g1_ref, gr_ref, gres_ref, widef_ref, wideo_ref,
+    x_ref, gain_ref, a_ref, wk_ref, wv_ref, n1_ref, r1_ref, bkv_ref, cos_ref, sin_ref,
+    own_ref, back1_ref, back2_ref, back3_ref, back4_ref, g1_ref, gr_ref, gres_ref, widef_ref,
     grad_ref, wide_ref, kvg_ref,
 ):
-    gk = rope_back(gkv_ref[:, :HD].astype(F32), cos_ref[...], sin_ref[...]).astype(BF)
-    gv = gkv_ref[:, HD:].astype(BF)
+    gkv = own_ref[...].astype(F32)
+    for back_ref in (back1_ref, back2_ref, back3_ref, back4_ref):
+        gkv = gkv + back_ref[...].astype(F32)
+    gk = rope_back(gkv[:, :HD], cos_ref[...], sin_ref[...]).astype(BF)
+    gv = gkv[:, HD:].astype(BF)
     gr = gr_ref[...] + mm_nt(gk, bkv_ref[0]) + mm_nt(gv, bkv_ref[1])
-    wide = mm(gr.T.astype(BF), n1_ref[...]) + widef_ref[...] + wideo_ref[...]
+    wide = mm(gr.T.astype(BF), n1_ref[...]) + widef_ref[...]
     wide_ref[...] = wide.T.astype(BF)
     r1t = r1_ref[...].astype(F32).T.astype(BF)
     kvg_ref[0] = mm(r1t[rows_of(SLOT_K)], gk).astype(BF)
     kvg_ref[1] = mm(r1t[rows_of(SLOT_V)], gv).astype(BF)
-    g1 = g1_ref[...] + mm_nt(gk, kvw_ref[0]) + mm_nt(gv, kvw_ref[1])
+    g1 = g1_ref[...] + mm_nt(gk, wk_ref[...]) + mm_nt(gv, wv_ref[...])
     g1 = g1 + mm_nt(gr.astype(BF), a_ref[...])
     x = x_ref[...].astype(F32)
     grad_ref[...] = gres_ref[...] + rms_back(x, gain_ref[...], g1)
@@ -318,14 +323,15 @@
     )
     weights = lax.all_gather(pack, BOTH, axis=0, tiled=False)
     weights = weights.reshape(dp_count, tensor_count, shard_rows, pack_cols)
-    kv_full = lax.all_gather(kv_weight, "dp", axis=1, tiled=True)
 
     wide = wide_adapters.reshape(7, shard_rows, adapters, RANK)
     wide = jnp.take(wide, adapter_ids, axis=2).transpose(2, 1, 0, 3)
     wide = wide.reshape(seqs, shard_rows, 7 * RANK)
     wide = jnp.pad(wide, ((0, 0), (0, 0), (0, LANES - 7 * RANK)))
     wide = jnp.repeat(wide, dp_count // seqs, axis=0)
-    a_all = lax.all_to_all(wide, "dp", 0, 0, tiled=True).reshape(width, LANES)
+    shared = jnp.broadcast_to(kv_weight[:, None], (2, dp_count, shard_rows, HD))
+    wide = jnp.concatenate([wide, shared[0], shared[1]], axis=2)
+    a_all = lax.all_to_all(wide, "dp", 0, 0, tiled=True).reshape(width, 3 * LANES)
 
     def take_rows(matrix):
         return lax.dynamic_slice_in_dim(matrix, column, RANK, matrix.ndim - 2)
@@ -392,47 +398,73 @@
     q_spec, qb_spec = weight_spec(q_cols, q_block), adapter_spec(q_cols, q_block)
     o_spec, ob_spec = weight_spec(q_cols, q_block + 1), adapter_spec(q_cols, q_block + 1)
 
-    args = (tokens, gain_one, a_all, kv_full, b_kv, cos, sin, weights, b_pad)
+    def lane_block(block):
+        return pl.BlockSpec((width, LANES), lambda *_: (0, block))
+
+    a_spec, wk_spec, wv_spec = lane_block(0), lane_block(1), lane_block(2)
+
+    def wholes(*arrays):
+        return [whole(v) for v in arrays]
+
+    args = (tokens, gain_one, a_all, a_all, a_all, b_kv, cos, sin, weights, b_pad)
     normed_one, rank_one, kv_own, queries = call(
         pre_kernel, "qkv", tensor_count, args,
-        [whole(v) for v in args[:7]] + [q_spec, qb_spec],
+        wholes(tokens, gain_one) + [a_spec, wk_spec, wv_spec] + wholes(b_kv, cos, sin) + [q_spec, qb_spec],
         (sds((rows, width), BF), sds((rows, LANES), BF), sds((rows, 2 * HD), BF), sds((rows, heads_cols), BF)),
         (out_whole((rows, width)), out_whole((rows, LANES)), out_whole((rows, 2 * HD)), token_cols(q_cols)),
         [], 2 * rows * width * (heads_cols + 384), 2 * width * heads_cols,
     )
 
-    kv_half = lax.all_gather(kv_own, "tensor", axis=0, tiled=True)
-    kv_prev = lax.ppermute(kv_half, "dp", [(2 * s, 2 * s + 1) for s in range(dp_count // 2)])
-    kv_window = lax.dynamic_slice_in_dim(jnp.concatenate([kv_prev, kv_half]), tensor * rows, span, 0)
+    parts = seq_length // rows
+    reach = WINDOW // rows
+
+    def moved(value, steps):
+        pairs = [
+            (s * parts + c, s * parts + c + steps)
+            for s in range(devices // parts) for c in range(parts) if 0 <= c + steps < parts
+        ]
+        return lax.ppermute(value, BOTH, pairs)
+
+    kv_window = jnp.concatenate([moved(kv_own, d) for d in range(reach, 0, -1)] + [kv_own])
 
     args = (kv_window, kseg, qseg, tokens, gain_two, a_all, queries, weights, b_pad)
-    mixed, lse, residual, normed_two, rank_two, rank_out = call(
+    q_heads = q_cols // HD
+    mixed, probs, residual, normed_two, rank_two, rank_out = call(
         attn_kernel, "attention", tensor_count, args,
-        [whole(v) for v in args[:6]] + [token_cols(q_cols), o_spec, ob_spec],
+        wholes(*args[:5]) + [a_spec, token_cols(q_cols), o_spec, ob_spec],
         (
-            sds((rows, heads_cols), BF), sds((tensor_count, 8, rows), F32), sds((rows, width), F32),
+            sds((rows, heads_cols), BF), sds((tensor_count * q_heads, span, rows), BF), sds((rows, width), F32),
             sds((rows, width), BF), sds((rows, LANES), BF), sds((rows, LANES), BF),
         ),
         (
-            token_cols(q_cols), by_step(8, rows), out_whole((rows, width)),
+            token_cols(q_cols), pl.BlockSpec((q_heads, span, rows), lambda t: (t, 0, 0)), out_whole((rows, width)),
             out_whole((rows, width)), out_whole((rows, LANES)), out_whole((rows, LANES)),
         ),
         [
-            pltpu.VMEM((span, rows), F32), pltpu.VMEM((span, rows), F32), pltpu.VMEM((span, rows), BF),
+            pltpu.VMEM((span, rows), F32), pltpu.VMEM((span, rows), F32),
             pltpu.VMEM((rows, width), F32), pltpu.VMEM((HD, span), BF), pltpu.VMEM((rows, LANES), F32),
         ],
         2 * rows * heads_cols * (2 * span + width), 2 * width * heads_cols,
     )
 
-    args = (residual, normed_two, rank_two, cotangent, gain_two, a_all, weights, weights, weights, b_pad, b_pad, b_pad)
-    block_output, grad_residual, grad_branch, wide_ffn, grad_bg, grad_bu, grad_bd = call(
+    args = (
+        residual, normed_two, rank_two, cotangent, gain_two, mixed, rank_out, a_all,
+        weights, weights, weights, b_pad, b_pad, b_pad,
+    )
+    block_output, grad_residual, grad_branch, wide_ffn, grad_ro, grad_bo, grad_bg, grad_bu, grad_bd = call(
         ffn_kernel, "feed_forward", tensor_count, args,
-        [whole(v) for v in args[:6]]
+        wholes(*args[:7]) + [a_spec]
         + [weight_spec(ff_cols, j) for j in range(3)]
         + [adapter_spec(ff_cols, j) for j in range(3)],
-        (sds((rows, width), BF), sds((rows, width), F32), sds((rows, width), BF), sds((LANES, width), F32))
+        (
+            sds((rows, width), BF), sds((rows, width), F32), sds((rows, width), BF), sds((LANES, width), F32),
+            sds((rows, LANES), BF), sds((tensor_count, RANK, q_cols), BF),
+        )
         + (sds((tensor_count, RANK, ff_cols), BF),) * 3,
-        (out_whole((rows, width)), out_whole((rows, width)), out_whole((rows, width)), out_whole((LANES, width)))
+        (
+            out_whole((rows, width)), out_whole((rows, width)), out_whole((rows, width)), out_whole((LANES, width)),
+            out_whole((rows, LANES)), out_whole((tensor_count, RANK, q_cols)),
+        )
         + (by_step(RANK, ff_cols),) * 3,
         [
             pltpu.VMEM((rows, width), F32), pltpu.VMEM((rows, width), F32),
@@ -443,41 +475,43 @@
     )
 
     args = (
-        kv_window, kseg, qseg, grad_branch, a_all, rank_one, rank_out, cos, sin,
-        queries, mixed, lse, weights, b_pad, weights, b_pad,
-    )
-    dkv, grad_one, grad_rank, wide_out, grad_bo, grad_bq = call(
+        kv_window, grad_branch, grad_ro, rank_one, cos, sin,
+        queries, mixed, probs, weights, b_pad, weights, b_pad,
+    )
+    dkv, grad_one, grad_rank, grad_bq = call(
         attn_back_kernel, "attention_back", tensor_count, args,
-        [whole(v) for v in args[:9]]
-        + [token_cols(q_cols), token_cols(q_cols), by_step(8, rows), o_spec, ob_spec, q_spec, qb_spec],
+        wholes(*args[:6])
+        + [
+            token_cols(q_cols), token_cols(q_cols), pl.BlockSpec((q_heads, span, rows), lambda t: (t, 0, 0)),
+            o_spec, ob_spec, q_spec, qb_spec,
+        ],
         (
-            sds((span, 2 * HD), BF), sds((rows, width), F32), sds((rows, LANES), F32), sds((LANES, width), F32),
-            sds((tensor_count, RANK, q_cols), BF), sds((tensor_count, RANK, q_cols), BF),
+            sds((span, 2 * HD), BF), sds((rows, width), F32), sds((rows, LANES), F32),
+            sds((tensor_count, RANK, q_cols), BF),
         ),
         (
-            out_whole((span, 2 * HD)), out_whole((rows, width)), out_whole((rows, LANES)), out_whole((LANES, width)),
-            by_step(RANK, q_cols), by_step(RANK, q_cols),
+            out_whole((span, 2 * HD)), out_whole((rows, width)), out_whole((rows, LANES)), by_step(RANK, q_cols),
         ),
         [
-            pltpu.VMEM((span, rows), F32), pltpu.VMEM((span, rows), BF),
+            pltpu.VMEM((span, rows), BF),
             pltpu.VMEM((span, HD), F32), pltpu.VMEM((span, HD), F32), pltpu.VMEM((HD, span), BF),
-            pltpu.VMEM((LANES, rows), BF), pltpu.VMEM((rows, LANES), BF), pltpu.VMEM((LANES, rows), BF),
+            pltpu.VMEM((LANES, rows), BF),
             pltpu.VMEM((rows, q_cols), BF), pltpu.VMEM((rows, q_cols), BF),
         ],
-        2 * rows * heads_cols * (5 * span + 2 * width), 4 * width * heads_cols,
-    )
-
-    placed = lax.dynamic_update_slice_in_dim(jnp.zeros((seq_length, 2 * HD), BF), dkv, tensor * rows, 0)
-    returned = lax.ppermute(placed[:group_rows], "dp", [(2 * s + 1, 2 * s) for s in range(dp_count // 2)])
-    gathered = placed[group_rows:].astype(F32) + returned.astype(F32)
-    grad_kv = lax.psum_scatter(gathered.astype(BF), "tensor", scatter_dimension=0, tiled=True)
-
+        2 * rows * heads_cols * (4 * span + 2 * width), 4 * width * heads_cols,
+    )
+
+    backs = [
+        moved(dkv[(reach - d) * rows : (reach - d + 1) * rows], -d) for d in range(1, reach + 1)
+    ]
     args = (
-        tokens, gain_one, a_all, normed_one, rank_one, kv_full, b_kv, cos, sin,
-        grad_kv, grad_one, grad_rank, grad_residual, wide_ffn, wide_out,
+        tokens, gain_one, a_all, a_all, a_all, normed_one, rank_one, b_kv, cos, sin,
+        dkv, *backs, grad_one, grad_rank, grad_residual, wide_ffn,
     )
     input_grad, wide_term, kv_term = call(
-        final_kernel, "input_gradient", 1, args, [whole(v) for v in args],
+        final_kernel, "input_gradient", 1, args,
+        wholes(*args[:2]) + [a_spec, wk_spec, wv_spec] + wholes(*args[5:10])
+        + [pl.BlockSpec((rows, 2 * HD), lambda *_: (reach, 0))] + wholes(*args[11:]),
         (sds((rows, width), F32), sds((width, LANES), BF), sds((2, RANK, HD), BF)),
         (out_whole((rows, width)), out_whole((width, LANES)), out_whole((2, RANK, HD))),
         [], 2 * rows * width * 640, 8 * rows * width,
@@ -500,16 +534,15 @@
         summed[:, own_rows : own_rows + 2], own_row // RANK, 0, keepdims=False
     ).reshape(2, 1, HD)
 
+    early = jnp.concatenate([grad_bg, grad_bu, grad_bd, grad_bo], axis=2)
+    early = lax.psum_scatter(early, "tensor", scatter_dimension=0, tiled=True).reshape(RANK, -1)
+    early = lax.all_gather(early, "dp", axis=0, tiled=False)
     pick_dp = (jnp.arange(adapters)[:, None] == jnp.repeat(adapter_ids, dp_count // seqs)[None, :]).astype(BF)
-
-    def by_adapter(terms):
-        own = lax.psum_scatter(terms, "tensor", scatter_dimension=0, tiled=True)
-        every = lax.all_gather(own.reshape(RANK, -1), "dp", axis=0, tiled=False)
-        cols = every.shape[2]
-        return mm(pick_dp, every.reshape(dp_count, RANK * cols)).reshape(adapters * RANK, cols)
-
-    early = by_adapter(jnp.concatenate([grad_bg, grad_bu, grad_bd, grad_bo], axis=2))
-    q_adapter_grad = by_adapter(grad_bq)
+    early = mm(pick_dp, early.reshape(dp_count, -1)).reshape(adapters * RANK, f3 + q_cols)
+
+    late = jnp.broadcast_to(grad_bq[None], (dp_count, tensor_count, RANK, q_cols))
+    late = lax.all_to_all(late.reshape(devices, RANK, q_cols), BOTH, 0, 0, tiled=True)
+    q_adapter_grad = mm(pick, late.reshape(devices, RANK * q_cols)).reshape(adapters * RANK, q_cols)
     gate_up_adapter_grad = jnp.stack([early[:, :f1], early[:, f1:f2]])
     down_adapter_grad = early[:, f2:f3].T
     out_adapter_grad = early[:, f3:].T

time: 410 us -> 391 us (0.954)
  blocking collectives: 83.8 us -> 35.5 us
  waiting for transfers between devices: 143 us -> 163 us
  starting transfers between devices: 22 us -> 32.4 us
    all_gather x3 -> x0, blocking collectives: 70.6 us -> none  [the longest x1 30.2 us: by_adapter(): every = lax.all_gather(own.reshape(RANK, -1), 'dp', axis=0, tiled=False)]
    all_gather x1, waiting for transfers between devices: 77.6 us -> 111 us  [on_device(): weights = lax.all_gather(pack, BOTH, axis=0, tiled=False)]
    all_to_all x2, waiting for transfers between devices: 0.01 us -> 22.3 us  [the longest x1 22.3 us: on_device(): lax.all_to_all(late.reshape(devices, RANK, q_cols), BOTH, 0, 0, tiled=True)]
    all_to_all x0 -> x1, blocking collectives: none -> 21.5 us  [on_device(): received = lax.all_to_all(payload, BOTH, 0, 0, tiled=True)]
    reduce_scatter x3 -> x1, waiting for transfers between devices: 40.5 us -> 19.2 us  [on_device(): lax.psum_scatter(early, 'tensor', scatter_dimension=0, tiled=True)]
    all_gather x1, waiting for transfers between devices: 19.9 us -> 0.01 us  [on_device(): early = lax.all_gather(early, 'dp', axis=0, tiled=False)]
    ppermute x2 -> x8, starting transfers between devices: 3.69 us -> 19.3 us  [moved(): return lax.ppermute(value, BOTH, pairs)]
    ppermute x2 -> x8, waiting for transfers between devices: 4.01 us -> 10.3 us  [moved(): return lax.ppermute(value, BOTH, pairs)]
  transfers between devices with their start and end apart: 9 -> 13, of which waited for: 7 -> 7; matrix products, arithmetic and copies ran while one was open for 6% -> 7% of each run, Pallas kernels for 1% -> 8%
where the time goes in v2:
time: 391 us; the launch traced here: 390 us
  waiting for transfers between devices  163 us (42%)
  Pallas kernels  96.8 us (25%)
  local copies, waits for them, and re-layouts  38.1 us (10%)
  blocking collectives  35.5 us (9%)
  starting transfers between devices  32.4 us (8%)
  between operations  14.9 us (4%)
  other arithmetic  7.23 us (2%)
    all_gather x1, waiting for transfers between devices, on_device(): weights = lax.all_gather(pack, BOTH, axis=0, tiled=False)  111 us
    pallas_call x5, Pallas kernels, call(): pl.pallas_call(kernel, name=name, grid=(steps,), in_specs=specs, out_spec...  96.8 us
    all_to_all x1, waiting for transfers between devices, on_device(): lax.all_to_all(late.reshape(devices, RANK, q_cols), BOTH, 0, 0, tiled=True)  22.3 us
    all_to_all x1, blocking collectives, on_device(): received = lax.all_to_all(payload, BOTH, 0, 0, tiled=True)  21.5 us
    unnamed x58, local copies, waits for them, and re-layouts  20.6 us
    ppermute x8, starting transfers between devices, moved(): return lax.ppermute(value, BOTH, pairs)  19.3 us
    reduce_scatter x1, waiting for transfers between devices, on_device(): lax.psum_scatter(early, 'tensor', scatter_dimension=0, tiled=True)  19.2 us
    all_gather x1, blocking collectives, on_device(): b_all = lax.all_gather(b_own, 'tensor', axis=0, tiled=False)  14 us
  transfers between devices with their start and end apart: 13, of which 7 were waited for; matrix products, arithmetic and copies ran while one was open for 7% of the time, Pallas kernels for 8%

profile of v2, /device:TPU:1, one launch (start us, length us, event | category | flops | bytes accessed | tf_op | source)
XLA Modules:
  0.0 390.3 jit_solution(585579233983229597)
XLA Ops:
  16.5 8.7 %all-to-all-start = ((bf16[32,48,384]{2,1,0:T(8,128)(2,1)}), bf16[32,48,384]{2,1,0:T(8,128)(2,1)S(1)}, u32[]{:S(2)}, u32[]{:S(2)}) async-start(bf16[32,48,384]{2,1,0:T(8,128)(2,1)} %pad_maximum_fusion), calls=%async_computation | async-start | bytes 2359296 | tf_op jit(solution)/shard_map/all_to_all | solution.py:334
  30.1 14.0 %all-gather.1 = bf16[64,4224]{1,0:T(8,128)(2,1)S(1)} all-gather(bf16[16,4224]{1,0:T(8,128)(2,1)S(1)} %constant_dynamic-update-slice_fusion.2), channel_id=3, replica_groups=mesh['dp'=32,'tensor'=4] {'tensor'}, dimensions={0}, use_global_device_ids=true | all-gather | bytes 675840 | tf_op jit(solution)/shard_map/all_gather | solution.py:347
  52.0 110.9 %all-gather.7.cloned.1.call-done = bf16[6144,4224]{1,0:T(8,128)(2,1)} async-done(((bf16[48,4224]{1,0:T(8,128)(2,1)}), bf16[6144,4224]{1,0:T(8,128)(2,1)}) %all-gather.7.cloned.1.call-update) | async-done | bytes 51904528 | tf_op jit(solution)/shard_map/all_gather | solution.py:324
  163.0 7.5 %qkv.1 = (bf16[256,1536]{1,0:T(8,128)(2,1)}, bf16[256,128]{1,0:T(8,128)(2,1)}, bf16[256,256]{1,0:T(8,128)(2,1)}, bf16[256,1536]{1,0:T(8,128)(2,1)}) custom-call(bf16[256,1536]{1,0:T(8,128)(2,1)} %x_ref.5, f32[1,1536]{1,0:T(1,128)} %get-tuple-element.109.gain_ref, bf16[1536,384]{1,0:T(8,128)(2,1)} %bitcast.84, bf16[1536,384]{1,0:T(8,128)(2,1)} %bitcast.85, ...), custom_call_target="tpu_custom_call" | custom-call | flops 1509949440 | bytes 4718592 | tf_op jit(solution)/shard_map/qkv/pallas_call | solution.py:282
  172.0 3.6 collective-permute-start.1
  177.4 1.9 collective-permute-start.2
  179.3 1.9 collective-permute-start.3
  181.3 4.1 %collective-permute-done.2 = bf16[256,256]{1,0:T(8,128)(2,1)S(1)} collective-permute-done((bf16[256,256]{1,0:T(8,128)(2,1)}, bf16[256,256]{1,0:T(8,128)(2,1)S(1)}, u32[]{:S(2)}, u32[]{:S(2)}) %collective-permute-start.2) | collective-permute-done | bytes 131104 | tf_op jit(solution)/shard_map/ppermute | solution.py:426
  187.9 19.0 %attention.1 = (bf16[256,1536]{1,0:T(8,128)(2,1)}, bf16[12,1280,256]{2,1,0:T(8,128)(2,1)}, f32[256,1536]{1,0:T(8,128)}, bf16[256,1536]{1,0:T(8,128)(2,1)}, bf16[...) custom-call(bf16[1280,256]{1,0:T(8,128)(2,1)} %copy-done.3, s32[1280,1]{1,0:T(8,128)} %reshape.142.kseg_ref, ...), custom_call_target="tpu_custom_call" | custom-call | flops 3221225472 | bytes 4718592 | tf_op jit(solution)/shard_map/attention/pallas_call | solution.py:282
  206.9 40.4 %feed_forward.1 = (bf16[256,1536]{1,0:T(8,128)(2,1)}, f32[256,1536]{1,0:T(8,128)}, bf16[256,1536]{1,0:T(8,128)(2,1)}, f32[128,1536]{1,0:T(8,128)}, bf16[256,128]...) custom-call(f32[256,1536]{1,0:T(8,128)} %get-tuple-element.36.res_re, ...), custom_call_target="tpu_custom_call" | custom-call | flops 21743271936 | bytes 42467328 | tf_op jit(solution)/shard_map/feed_forward/pallas_call | solution.py:282
  247.3 1.9 pad_maximum_fusion.2
  249.2 19.2 %reduce-scatter.2.cloned.1.call-done = bf16[1,16,3840]{2,1,0:T(8,128)(2,1)} async-done(((bf16[4,16,3840]{2,1,0:T(8,128)(2,1)}), bf16[1,16,3840]{2,1,0:T(8,128)(2,1)}) %reduce-scatter.2.cloned.1.call-update) | async-done | bytes 122896 | tf_op jit(solution)/shard_map/reduce_scatter | solution.py:538
  268.5 23.8 %attention_back.1 = (bf16[1280,256]{1,0:T(8,128)(2,1)}, f32[256,1536]{1,0:T(8,128)}, f32[256,128]{1,0:T(8,128)}, bf16[4,16,384]{2,1,0:T(8,128)(2,1)}) custom-call(bf16[1280,256]{1,0:T(8,128)(2,1)} %copy-done.3, bf16[256,1536]{1,0:T(8,128)(2,1)} %get-tuple-element.44.gb_ref, bf16[256,128]{1,0:T(8,128)(2,1)} %get-tuple-element.45.gro_ref, ...), custom_call_target="tpu_custom_call" | custom-call | flops 6442450944 | bytes 9437184 | tf_op jit(solution)/shard_map/attention_back/pallas_call | solution.py:282
  293.4 4.4 %collective-permute-start.4 = (bf16[256,256]{1,0:T(8,128)(2,1)S(1)}, bf16[256,256]{1,0:T(8,128)(2,1)S(1)}, u32[]{:S(2)}, u32[]{:S(2)}) collective-permute-start(bf16[256,256]{1,0:T(8,128)(2,1)S(1)} %get-tuple-element.98), channel_id=1, source_target_pairs={{1,0},{2,1},{3,2},{4,3},{5,4},{6,5},{7,6},{9,8},{10,9},{11,10},{12... | collective-permute-start | bytes 393224 | tf_op jit(solution)/shard_map/ppermute | solution.py:426
  297.8 2.8 collective-permute-start.5
  300.6 1.9 collective-permute-start.6
  303.9 2.1 collective-permute-done.5.back2_ref
  306.1 2.5 collective-permute-done.6.back3_ref
  309.2 6.1 %input_gradient.1 = (f32[256,1536]{1,0:T(8,128)}, bf16[1536,128]{1,0:T(8,128)(2,1)}, bf16[2,16,128]{2,1,0:T(8,128)(2,1)}) custom-call(bf16[256,1536]{1,0:T(8,128)(2,1)} %x_ref.5, f32[1,1536]{1,0:T(1,128)} %get-tuple-element.109.gain_ref, bf16[1536,384]{1,0:T(8,128)(2,1)} %bitcast.89, bf16[1536,384]{1,0:T(8,128)(2,1)} %bitcast.90, ...), custom_call_target="tpu_custom_call" | custom-call | flops 503316480 | bytes 3145728 | tf_op jit(solution)/shard_map/input_gradient/pallas_call | solution.py:282
  317.5 21.5 %all_to_all.15 = bf16[128,16,128]{2,1,0:T(8,128)(2,1)S(1)} all-to-all(bf16[128,16,128]{2,1,0:T(8,128)(2,1)S(1)} %maximum_maximum_fusion), channel_id=1, replica_groups=mesh['dp'=32,'tensor'=4] {'dp','tensor'}, dimensions={0} | all-to-all | bytes 1048576 | tf_op jit(solution)/shard_map/all_to_all | solution.py:525
  340.4 4.3 %all-to-all-start.2 = ((bf16[128,16,384]{2,1,0:T(8,128)(2,1)}), bf16[128,16,384]{2,1,0:T(8,128)(2,1)S(1)}, u32[]{:S(2)}, u32[]{:S(2)}) async-start(bf16[128,16,384]{2,1,0:T(8,128)(2,1)} %bitcast.31), calls=%async_computation.2 | async-start | bytes 3145728 | tf_op jit(solution)/shard_map/all_to_all | solution.py:544
  347.3 22.3 %all-to-all-done.2 = bf16[128,16,384]{2,1,0:T(8,128)(2,1)S(1)} async-done(((bf16[128,16,384]{2,1,0:T(8,128)(2,1)}), bf16[128,16,384]{2,1,0:T(8,128)(2,1)S(1)}, u32[]{:S(2)}, u32[]{:S(2)}) %all-to-all-start.2) | async-done | bytes 1572896 | tf_op jit(solution)/shard_map/all_to_all | solution.py:544
  371.1 3.3 copy.69
  374.4 2.0 fusion.6
  (129 shorter events, 45.2 us)
Async XLA Ops:
  7.2 19.4 %copy-start = (bf16[1152,128]{1,0:T(8,128)(2,1)S(1)}, bf16[1152,128]{1,0:T(8,128)(2,1)}, u32[]{:S(2)}) copy-start(bf16[1152,128]{1,0:T(8,128)(2,1)} %param.31) | copy-start | bytes 884740
  7.2 155.8 %all-gather.7.cloned.1.call-start = ((), (), s32[]{:S(2)}) async-start(), calls=%async_computation.6 | async-start | bytes 52310016 | tf_op jit(solution)/shard_map/all_gather | solution.py:324
  9.1 5.7 %copy-start.16 = (s32[16]{0:T(128)S(1)}, s32[16]{0:T(128)}, u32[]{:S(2)}) copy-start(s32[16]{0:T(128)} %param.19) | copy-start | bytes 196
  16.5 10.4 %copy-start.12 = (bf16[384,128]{1,0:T(8,128)(2,1)S(1)}, bf16[384,128]{1,0:T(8,128)(2,1)}, u32[]{:S(2)}) copy-start(bf16[384,128]{1,0:T(8,128)(2,1)} %param.29) | copy-start | bytes 294916
  16.5 35.5 %all-to-all-start = ((bf16[32,48,384]{2,1,0:T(8,128)(2,1)}), bf16[32,48,384]{2,1,0:T(8,128)(2,1)S(1)}, u32[]{:S(2)}, u32[]{:S(2)}) async-start(bf16[32,48,384]{2,1,0:T(8,128)(2,1)} %pad_maximum_fusion), calls=%async_computation | async-start | bytes 2359296 | tf_op jit(solution)/shard_map/all_to_all | solution.py:334
  25.2 243.2 %reduce-scatter.2.cloned.1.call-start = ((), (), s32[]{:S(2)}) async-start(), calls=%async_computation.4 | async-start | bytes 614400 | tf_op jit(solution)/shard_map/reduce_scatter | solution.py:538
  45.9 5.5 %copy-start.15 = (f32[2,1536]{1,0:T(2,128)S(1)}, f32[2,1536]{1,0:T(2,128)}, u32[]{:S(2)}) copy-start(f32[2,1536]{1,0:T(2,128)} %param.20) | copy-start | bytes 36868
  52.0 110.9 %copy-start.2 = (bf16[32,48,384]{2,1,0:T(8,128)(2,1)}, bf16[32,48,384]{2,1,0:T(8,128)(2,1)S(1)}, u32[]{:S(2)}) copy-start(bf16[32,48,384]{2,1,0:T(8,128)(2,1)S(1)} %all-to-all-done) | copy-start | bytes 3538948
  163.0 9.0 %copy-start.6 = (s32[32768]{0:T(1024)S(1)}, s32[32768]{0:T(1024)}, u32[]{:S(2)}) copy-start(s32[32768]{0:T(1024)} %param.18) | copy-start | bytes 393220
  170.5 16.5 %copy-start.11 = (bf16[256,256]{1,0:T(8,128)(2,1)S(1)}, bf16[256,256]{1,0:T(8,128)(2,1)}, u32[]{:S(2)}) copy-start(bf16[256,256]{1,0:T(8,128)(2,1)} %get-tuple-element.34) | copy-start | bytes 393220
  170.5 10.7 %collective-permute-start = (bf16[256,256]{1,0:T(8,128)(2,1)}, bf16[256,256]{1,0:T(8,128)(2,1)S(1)}, u32[]{:S(2)}, u32[]{:S(2)}) collective-permute-start(bf16[256,256]{1,0:T(8,128)(2,1)} %get-tuple-element.34), channel_id=1, source_target_pairs={{0,4},{1,5},{2,6},{3,7},{8,12},{9,13},{10,14},{11,15},{16,20},{17,... | collective-permute-start | bytes 393224 | tf_op jit(solution)/shard_map/ppermute | solution.py:426
  172.0 9.2 %collective-permute-start.1 = (bf16[256,256]{1,0:T(8,128)(2,1)}, bf16[256,256]{1,0:T(8,128)(2,1)S(1)}, u32[]{:S(2)}, u32[]{:S(2)}) collective-permute-start(bf16[256,256]{1,0:T(8,128)(2,1)} %get-tuple-element.34), channel_id=1, source_target_pairs={{0,3},{1,4},{2,5},{3,6},{4,7},{8,11},{9,12},{10,13},{11,14},{12,15... | collective-permute-start | bytes 393224 | tf_op jit(solution)/shard_map/ppermute | solution.py:426
  177.4 8.0 %collective-permute-start.2 = (bf16[256,256]{1,0:T(8,128)(2,1)}, bf16[256,256]{1,0:T(8,128)(2,1)S(1)}, u32[]{:S(2)}, u32[]{:S(2)}) collective-permute-start(bf16[256,256]{1,0:T(8,128)(2,1)} %get-tuple-element.34), channel_id=1, source_target_pairs={{0,2},{1,3},{2,4},{3,5},{4,6},{5,7},{8,10},{9,11},{10,12},{11,13},... | collective-permute-start | bytes 393224 | tf_op jit(solution)/shard_map/ppermute | solution.py:426
  179.3 7.7 %collective-permute-start.3 = (bf16[256,256]{1,0:T(8,128)(2,1)}, bf16[256,256]{1,0:T(8,128)(2,1)S(1)}, u32[]{:S(2)}, u32[]{:S(2)}) collective-permute-start(bf16[256,256]{1,0:T(8,128)(2,1)} %get-tuple-element.34), channel_id=1, source_target_pairs={{0,1},{1,2},{2,3},{3,4},{4,5},{5,6},{6,7},{8,9},{9,10},{10,11},{11... | collective-permute-start | bytes 393224 | tf_op jit(solution)/shard_map/ppermute | solution.py:426
  249.2 121.9 %all-gather.5.cloned.1.call-start = ((), (), s32[]{:S(2)}) async-start(), calls=%async_computation.5 | async-start | bytes 4055040 | tf_op jit(solution)/shard_map/all_gather | solution.py:539
  293.4 10.5 %collective-permute-start.4 = (bf16[256,256]{1,0:T(8,128)(2,1)S(1)}, bf16[256,256]{1,0:T(8,128)(2,1)S(1)}, u32[]{:S(2)}, u32[]{:S(2)}) collective-permute-start(bf16[256,256]{1,0:T(8,128)(2,1)S(1)} %get-tuple-element.98), channel_id=1, source_target_pairs={{1,0},{2,1},{3,2},{4,3},{5,4},{6,5},{7,6},{9,8},{10,9},{11,10},{12... | collective-permute-start | bytes 393224 | tf_op jit(solution)/shard_map/ppermute | solution.py:426
  297.8 8.3 %collective-permute-start.5 = (bf16[256,256]{1,0:T(8,128)(2,1)S(1)}, bf16[256,256]{1,0:T(8,128)(2,1)S(1)}, u32[]{:S(2)}, u32[]{:S(2)}) collective-permute-start(bf16[256,256]{1,0:T(8,128)(2,1)S(1)} %get-tuple-element.97), channel_id=1, source_target_pairs={{2,0},{3,1},{4,2},{5,3},{6,4},{7,5},{10,8},{11,9},{12,10},{13,11},... | collective-permute-start | bytes 393224 | tf_op jit(solution)/shard_map/ppermute | solution.py:426
  300.6 7.9 %collective-permute-start.6 = (bf16[256,256]{1,0:T(8,128)(2,1)S(1)}, bf16[256,256]{1,0:T(8,128)(2,1)S(1)}, u32[]{:S(2)}, u32[]{:S(2)}) collective-permute-start(bf16[256,256]{1,0:T(8,128)(2,1)S(1)} %get-tuple-element.96), channel_id=1, source_target_pairs={{3,0},{4,1},{5,2},{6,3},{7,4},{11,8},{12,9},{13,10},{14,11},{15,12... | collective-permute-start | bytes 393224 | tf_op jit(solution)/shard_map/ppermute | solution.py:426
  302.5 6.0 %collective-permute-start.7 = (bf16[256,256]{1,0:T(8,128)(2,1)S(1)}, bf16[256,256]{1,0:T(8,128)(2,1)S(1)}, u32[]{:S(2)}, u32[]{:S(2)}) collective-permute-start(bf16[256,256]{1,0:T(8,128)(2,1)S(1)} %get-tuple-element.95), channel_id=1, source_target_pairs={{4,0},{5,1},{6,2},{7,3},{12,8},{13,9},{14,10},{15,11},{20,16},{21,... | collective-permute-start | bytes 393224 | tf_op jit(solution)/shard_map/ppermute | solution.py:426
  303.9 4.6 %copy-start.7 = (bf16[256,256]{1,0:T(8,128)(2,1)}, bf16[256,256]{1,0:T(8,128)(2,1)S(1)}, u32[]{:S(2)}) copy-start(bf16[256,256]{1,0:T(8,128)(2,1)S(1)} %collective-permute-done.4.back1_ref) | copy-start | bytes 393220
  315.4 23.6 %copy-start.13 = (bf16[4,16,384]{2,1,0:T(8,128)(2,1)S(1)}, bf16[4,16,384]{2,1,0:T(8,128)(2,1)}, u32[]{:S(2)}) copy-start(bf16[4,16,384]{2,1,0:T(8,128)(2,1)} %get-tuple-element.55) | copy-start | bytes 147460
  340.4 29.3 %all-to-all-start.2 = ((bf16[128,16,384]{2,1,0:T(8,128)(2,1)}), bf16[128,16,384]{2,1,0:T(8,128)(2,1)S(1)}, u32[]{:S(2)}, u32[]{:S(2)}) async-start(bf16[128,16,384]{2,1,0:T(8,128)(2,1)} %bitcast.31), calls=%async_computation.2 | async-start | bytes 3145728 | tf_op jit(solution)/shard_map/all_to_all | solution.py:544
  378.8 4.9 %copy-start.1 = (bf16[1152,128]{1,0:T(8,128)(2,1)S(1)}, bf16[1152,128]{1,0:T(8,128)(2,1)}, u32[]{:S(2)}) copy-start(bf16[1152,128]{1,0:T(8,128)(2,1)} %param.31) | copy-start | bytes 884740
  379.8 2.9 copy-start.4
  (6 other events, 6.5 us)
Sparse Core Ops, SparseCore 0:
  12.5 150.4 all-gather.6
  249.3 19.0 reduce-scatter.1
  270.9 47.2 all-gather.4

commit v3 on v2

--- a/solution.py
+++ b/solution.py
@@ -58,12 +58,24 @@
     return inv * scaled - v * (inv * inv * inv * dot)
 
 
-def pre_kernel(
-    x_ref, gain_ref, a_ref, wk_ref, wv_ref, bkv_ref, cos_ref, sin_ref, wq_ref, bq_ref,
-    n1_ref, r1_ref, kv_ref, q_ref,
-):
-    @pl.when(pl.program_id(0) == 0)
-    def _():
+def pre_kernel(place_ref, x_ref, gain_ref, a_ref, wk_ref, wv_ref, bkv_ref, cos_ref, sin_ref, bq_ref, *rest):
+    pieces, (n1_ref, r1_ref, kv_ref, q_ref, wq_ref) = rest[:-5], rest[-5:]
+    y_count = len(pieces) // 2
+    x_count, tensor_count, shard_rows, _ = pieces[0].shape
+    step = pl.program_id(0)
+
+    @pl.when(step == 0)
+    def _():
+        my_y, my_x, my_core, my_z = (place_ref[axis] for axis in range(4))
+        for number, piece in enumerate(pieces):
+            y = lax.rem(my_y + number % y_count, y_count)
+            core = my_core if number < y_count else 1 - my_core
+            for away_x in range(x_count):
+                x = lax.rem(my_x + away_x, x_count)
+                row = pl.multiple_of(((y * x_count + x) * 2 + core) * shard_rows, 16)
+                for away_z in range(tensor_count):
+                    z = lax.rem(my_z + away_z, tensor_count)
+                    wq_ref[z, pl.ds(row, shard_rows)] = piece[away_x, away_z]
         n1 = rms(x_ref[...].astype(F32), gain_ref[...]).astype(BF)
         n1_ref[...] = n1
         r1 = mm(n1, a_ref[...]).astype(BF)
@@ -72,7 +84,7 @@
         kv_ref[:, :HD] = rope(key, cos_ref[...], sin_ref[...]).astype(BF)
         kv_ref[:, HD:] = (mm(n1, wv_ref[...]) + mm(r1, bkv_ref[1])).astype(BF)
 
-    lin = mm(n1_ref[...], flat(wq_ref)) + mm(r1_ref[...], bq_ref[0])
+    lin = mm(n1_ref[...], wq_ref[step]) + mm(r1_ref[...], bq_ref[0])
     for h in range(lin.shape[1] // HD):
         part = slice(h * HD, (h + 1) * HD)
         q_ref[:, part] = rope(lin[:, part], cos_ref[...], sin_ref[...]).astype(BF)
@@ -86,11 +98,7 @@
     bias_ref[...] = jnp.where(allowed, 0.0, MASKED)
 
 
-def attn_kernel(
-    kv_ref, kseg_ref, qseg_ref, x_ref, gain_ref, a_ref, q_ref, wo_ref, bo_ref,
-    mixed_ref, p_ref, res_ref, n2_ref, r2_ref, ro_ref,
-    bias_ref, s_ref, acc_ref, vt_ref, rank_ref,
-):
+def attn_kernel(kv_ref, kseg_ref, qseg_ref, q_ref, mixed_ref, p_ref, bias_ref, s_ref, vt_ref):
     step = pl.program_id(0)
     rows = q_ref.shape[0]
     chunks = kv_ref.shape[0] // rows
@@ -99,8 +107,6 @@
     def _():
         fill_bias(bias_ref, kseg_ref, qseg_ref)
         vt_ref[...] = kv_ref[:, HD:].astype(F32).T.astype(BF)
-        acc_ref[...] = jnp.zeros_like(acc_ref)
-        rank_ref[...] = jnp.zeros_like(rank_ref)
 
     for h in range(q_ref.shape[1] // HD):
         part = slice(h * HD, (h + 1) * HD)
@@ -123,6 +129,17 @@
             p_ref[h, span] = (s_ref[span] * inv).astype(BF)
         mixed_ref[:, part] = mm(vt_ref[...], p_ref[h]).T.astype(BF)
 
+
+def out_kernel(
+    x_ref, gain_ref, a_ref, mixed_ref, wo_ref, bo_ref, res_ref, n2_ref, r2_ref, ro_ref, acc_ref, rank_ref,
+):
+    step = pl.program_id(0)
+
+    @pl.when(step == 0)
+    def _():
+        acc_ref[...] = jnp.zeros_like(acc_ref)
+        rank_ref[...] = jnp.zeros_like(rank_ref)
+
     mixed = mixed_ref[...]
     acc_ref[...] += mm_nt(mixed, flat(wo_ref))
     rank_ref[...] += mm_nt(mixed, bo_ref[0])
@@ -238,7 +255,7 @@
     gq = gq_ref[...]
     gbq_ref[0] = mm(r1t_ref[rows_of(SLOT_Q)], gq).astype(BF)
     gr_ref[...] += mm_nt(gq, bq_ref[0])
-    g1_ref[...] += mm_nt(gq, flat(wq_ref))
+    g1_ref[...] += mm_nt(gq, wq_ref[0])
 
     @pl.when(step == pl.num_programs(0) - 1)
     def _():
@@ -268,6 +285,49 @@
     grad_ref[...] = gres_ref[...] + rms_back(x, gain_ref[...], g1)
 
 
+def sum_hidden_kernel(ids_ref, terms_ref, gu_ref, down_ref, out_ref, acc_ref):
+    acc_ref[...] = jnp.zeros_like(acc_ref)
+    for s in range(terms_ref.shape[0] // 2):
+        acc_ref[ids_ref[s]] += terms_ref[2 * s].astype(F32) + terms_ref[2 * s + 1].astype(F32)
+    adapters, rank, cols = acc_ref.shape
+    ff = gu_ref.shape[2]
+
+    def taken(first, last):
+        return acc_ref[:, :, first:last].reshape(adapters * rank, last - first)
+
+    gu_ref[0] = taken(0, ff)
+    gu_ref[1] = taken(ff, 2 * ff)
+    down_ref[...] = taken(2 * ff, 3 * ff).T
+    out_ref[...] = taken(3 * ff, cols).T
+
+
+def sum_wide_kernel(ids_ref, own_ref, terms_ref, wide_ref, kv_ref, q_ref, acc_ref):
+    acc_ref[...] = jnp.zeros_like(acc_ref)
+    seqs, parts = terms_ref.shape[:2]
+    for s in range(seqs):
+        term = terms_ref[s, 0].astype(F32)
+        for part in range(1, parts):
+            term = term + terms_ref[s, part].astype(F32)
+        acc_ref[ids_ref[s]] += term
+    adapters, rank, _ = acc_ref.shape
+    q_ref[...] = acc_ref[:, :, LANES:].reshape(q_ref.shape)
+    lane = lax.broadcasted_iota(jnp.int32, (rank, LANES), 1) // RANK
+    slots, own_rows = wide_ref.shape[:2]
+    for j in range(slots):
+        total = jnp.zeros((rank, LANES), F32)
+        for a in range(adapters):
+            turned = pltpu.roll(acc_ref[a, :, :LANES], ((a - j) * RANK) % LANES, 1)
+            total = jnp.where(lane == a, turned, total)
+        wide_ref[j] = total[:own_rows]
+    mine = acc_ref[own_ref[0], :, :LANES]
+    for j in range(2):
+        kv_ref[j] = mine[own_rows + j : own_rows + j + 1]
+
+
+def scalars():
+    return pl.BlockSpec(memory_space=pltpu.SMEM)
+
+
 def whole(array):
     rank = len(array.shape)
     return pl.BlockSpec(array.shape, lambda *_: (0,) * rank)
@@ -306,10 +366,10 @@
     seq_length = 2 * group_rows
     shard_rows = q_weight.shape[0]
     q_cols, ff_cols = q_weight.shape[1], gate_up_weight.shape[2]
-    pack_cols = 3 * ff_cols + 2 * q_cols
+    pack_cols = 3 * ff_cols + q_cols
     seqs = adapter_ids.shape[0]
     adapters = wide_adapters.shape[2] // RANK
-    q_block = 3 * ff_cols // q_cols
+    o_block = 3 * ff_cols // q_cols
     dp = lax.axis_index("dp")
     tensor = lax.axis_index("tensor")
     adapter = lax.dynamic_index_in_dim(adapter_ids, dp // 2, keepdims=False)
@@ -319,10 +379,33 @@
         return jax.ShapeDtypeStruct(shape, dtype)
 
     pack = jnp.concatenate(
-        [gate_up_weight[0], gate_up_weight[1], down_weight.T, q_weight, out_weight.T], axis=1
+        [gate_up_weight[0], gate_up_weight[1], down_weight.T, out_weight.T], axis=1
     )
     weights = lax.all_gather(pack, BOTH, axis=0, tiled=False)
     weights = weights.reshape(dp_count, tensor_count, shard_rows, pack_cols)
+
+    chips = dp_count // 2
+    x_count = 4 if chips % 4 == 0 else chips
+    y_count = chips // x_count
+    my_core, my_x, my_y = dp % 2, (dp // 2) % x_count, dp // (2 * x_count)
+
+    def from_z(value, away):
+        return lax.ppermute(value, "tensor", [((z + away) % tensor_count, z) for z in range(tensor_count)])
+
+    def from_dp(value, away_y, away_x, away_core):
+        pairs = []
+        for y in range(y_count):
+            for x in range(x_count):
+                for c in range(2):
+                    source = (((y + away_y) % y_count) * x_count + (x + away_x) % x_count) * 2 + (c ^ away_core)
+                    pairs.append((source, (y * x_count + x) * 2 + c))
+        return lax.ppermute(value, "dp", pairs)
+
+    q_z = jnp.stack([q_weight] + [from_z(q_weight, d) for d in range(1, tensor_count)])
+    q_x = jnp.stack([q_z] + [from_dp(q_z, 0, d, 0) for d in range(1, x_count)])
+    q_y = [q_x] + [from_dp(q_x, d, 0, 0) for d in range(1, y_count)]
+    q_pieces = q_y + [from_dp(piece, 0, 0, 1) for piece in q_y]
+    place = jnp.stack([my_y, my_x, my_core, tensor]).astype(jnp.int32)
 
     wide = wide_adapters.reshape(7, shard_rows, adapters, RANK)
     wide = jnp.take(wide, adapter_ids, axis=2).transpose(2, 1, 0, 3)
@@ -341,7 +424,7 @@
 
     gu_rows = take_rows(gate_up_adapter)
     b_own = jnp.concatenate(
-        [gu_rows[0], gu_rows[1], take_cols(down_adapter).T, take_rows(q_adapter), take_cols(out_adapter).T],
+        [gu_rows[0], gu_rows[1], take_cols(down_adapter).T, take_cols(out_adapter).T, take_rows(q_adapter)],
         axis=1,
     )
     b_all = lax.all_gather(b_own, "tensor", axis=0, tiled=False)
@@ -357,8 +440,8 @@
             in_slot(b_all[:, :, :f1], SLOT_G),
             in_slot(b_all[:, :, f1:f2], SLOT_U),
             in_slot(b_all[:, :, f2:f3], SLOT_D),
-            in_slot(b_all[:, :, f3 : f3 + q_cols], SLOT_Q),
-            in_slot(b_all[:, :, f3 + q_cols :], SLOT_O),
+            in_slot(b_all[:, :, f3 : f3 + q_cols], SLOT_O),
+            in_slot(b_all[:, :, f3 + q_cols :], SLOT_Q),
         ],
         axis=2,
     )
@@ -395,8 +478,8 @@
         return pl.BlockSpec((1,) + shape, lambda t: (t,) + (0,) * len(shape))
 
     heads_cols = tensor_count * q_cols
-    q_spec, qb_spec = weight_spec(q_cols, q_block), adapter_spec(q_cols, q_block)
-    o_spec, ob_spec = weight_spec(q_cols, q_block + 1), adapter_spec(q_cols, q_block + 1)
+    o_spec, ob_spec = weight_spec(q_cols, o_block), adapter_spec(q_cols, o_block)
+    q_spec, qb_spec = by_step(width, q_cols), adapter_spec(q_cols, o_block + 1)
 
     def lane_block(block):
         return pl.BlockSpec((width, LANES), lambda *_: (0, block))
@@ -406,12 +489,19 @@
     def wholes(*arrays):
         return [whole(v) for v in arrays]
 
-    args = (tokens, gain_one, a_all, a_all, a_all, b_kv, cos, sin, weights, b_pad)
-    normed_one, rank_one, kv_own, queries = call(
+    args = (place, tokens, gain_one, a_all, a_all, a_all, b_kv, cos, sin, b_pad, *q_pieces)
+    normed_one, rank_one, kv_own, queries, w_query = call(
         pre_kernel, "qkv", tensor_count, args,
-        wholes(tokens, gain_one) + [a_spec, wk_spec, wv_spec] + wholes(b_kv, cos, sin) + [q_spec, qb_spec],
-        (sds((rows, width), BF), sds((rows, LANES), BF), sds((rows, 2 * HD), BF), sds((rows, heads_cols), BF)),
-        (out_whole((rows, width)), out_whole((rows, LANES)), out_whole((rows, 2 * HD)), token_cols(q_cols)),
+        [scalars()] + wholes(tokens, gain_one) + [a_spec, wk_spec, wv_spec] + wholes(b_kv, cos, sin) + [qb_spec]
+        + wholes(*q_pieces),
+        (
+            sds((rows, width), BF), sds((rows, LANES), BF), sds((rows, 2 * HD), BF), sds((rows, heads_cols), BF),
+            sds((tensor_count, width, q_cols), BF),
+        ),
+        (
+            out_whole((rows, width)), out_whole((rows, LANES)), out_whole((rows, 2 * HD)), token_cols(q_cols),
+            out_whole((tensor_count, width, q_cols)),
+        ),
         [], 2 * rows * width * (heads_cols + 384), 2 * width * heads_cols,
     )
 
@@ -427,24 +517,26 @@
 
     kv_window = jnp.concatenate([moved(kv_own, d) for d in range(reach, 0, -1)] + [kv_own])
 
-    args = (kv_window, kseg, qseg, tokens, gain_two, a_all, queries, weights, b_pad)
+    args = (kv_window, kseg, qseg, queries)
     q_heads = q_cols // HD
-    mixed, probs, residual, normed_two, rank_two, rank_out = call(
+    p_spec = pl.BlockSpec((q_heads, span, rows), lambda t: (t, 0, 0))
+    mixed, probs = call(
         attn_kernel, "attention", tensor_count, args,
-        wholes(*args[:5]) + [a_spec, token_cols(q_cols), o_spec, ob_spec],
-        (
-            sds((rows, heads_cols), BF), sds((tensor_count * q_heads, span, rows), BF), sds((rows, width), F32),
-            sds((rows, width), BF), sds((rows, LANES), BF), sds((rows, LANES), BF),
-        ),
-        (
-            token_cols(q_cols), pl.BlockSpec((q_heads, span, rows), lambda t: (t, 0, 0)), out_whole((rows, width)),
-            out_whole((rows, width)), out_whole((rows, LANES)), out_whole((rows, LANES)),
-        ),
-        [
-            pltpu.VMEM((span, rows), F32), pltpu.VMEM((span, rows), F32),
-            pltpu.VMEM((rows, width), F32), pltpu.VMEM((HD, span), BF), pltpu.VMEM((rows, LANES), F32),
-        ],
-        2 * rows * heads_cols * (2 * span + width), 2 * width * heads_cols,
+        wholes(*args[:3]) + [token_cols(q_cols)],
+        (sds((rows, heads_cols), BF), sds((tensor_count * q_heads, span, rows), BF)),
+        (token_cols(q_cols), p_spec),
+        [pltpu.VMEM((span, rows), F32), pltpu.VMEM((span, rows), F32), pltpu.VMEM((HD, span), BF)],
+        4 * rows * heads_cols * span, 2 * rows * heads_cols * span // HD,
+    )
+
+    args = (tokens, gain_two, a_all, mixed, weights, b_pad)
+    residual, normed_two, rank_two, rank_out = call(
+        out_kernel, "out_projection", tensor_count, args,
+        wholes(*args[:2]) + [a_spec, token_cols(q_cols), o_spec, ob_spec],
+        (sds((rows, width), F32), sds((rows, width), BF), sds((rows, LANES), BF), sds((rows, LANES), BF)),
+        (out_whole((rows, width)), out_whole((rows, width)), out_whole((rows, LANES)), out_whole((rows, LANES))),
+        [pltpu.VMEM((rows, width), F32), pltpu.VMEM((rows, LANES), F32)],
+        2 * rows * heads_cols * width, 2 * width * heads_cols,
     )
 
     args = (
@@ -476,13 +568,13 @@
 
     args = (
         kv_window, grad_branch, grad_ro, rank_one, cos, sin,
-        queries, mixed, probs, weights, b_pad, weights, b_pad,
+        queries, mixed, probs, weights, b_pad, w_query, b_pad,
     )
     dkv, grad_one, grad_rank, grad_bq = call(
         attn_back_kernel, "attention_back", tensor_count, args,
         wholes(*args[:6])
         + [
-            token_cols(q_cols), token_cols(q_cols), pl.BlockSpec((q_heads, span, rows), lambda t: (t, 0, 0)),
+            token_cols(q_cols), token_cols(q_cols), p_spec,
             o_spec, ob_spec, q_spec, qb_spec,
         ],
         (
@@ -517,35 +609,38 @@
         [], 2 * rows * width * 640, 8 * rows * width,
     )
 
-    own_rows = width // devices
-    kv_rows_out = jnp.tile(kv_term.transpose(1, 0, 2), (devices // RANK, 1, 1))
-    payload = jnp.concatenate(
-        [wide_term.reshape(devices, own_rows, LANES), kv_rows_out, jnp.zeros((devices, 2, LANES), BF)], axis=1
-    )
-    received = lax.all_to_all(payload, BOTH, 0, 0, tiled=True)
-    sent_rows = own_rows + 4
-    source_adapter = jnp.repeat(adapter_ids, devices // seqs)
-    pick = (jnp.arange(adapters)[:, None] == source_adapter[None, :]).astype(BF)
-    summed = mm(pick, received.reshape(devices, sent_rows * LANES)).reshape(adapters, sent_rows, LANES)
-    wide_grad = summed[:, :own_rows, : 7 * RANK].reshape(adapters, own_rows, 7, RANK)
-    wide_grad = wide_grad.transpose(2, 1, 0, 3).reshape(7, own_rows, adapters * RANK)
-    own_row = dp * tensor_count + tensor
-    kv_adapter_grad = lax.dynamic_index_in_dim(
-        summed[:, own_rows : own_rows + 2], own_row // RANK, 0, keepdims=False
-    ).reshape(2, 1, HD)
-
     early = jnp.concatenate([grad_bg, grad_bu, grad_bd, grad_bo], axis=2)
     early = lax.psum_scatter(early, "tensor", scatter_dimension=0, tiled=True).reshape(RANK, -1)
+    early, grad_bq = lax.optimization_barrier((early, grad_bq))
     early = lax.all_gather(early, "dp", axis=0, tiled=False)
-    pick_dp = (jnp.arange(adapters)[:, None] == jnp.repeat(adapter_ids, dp_count // seqs)[None, :]).astype(BF)
-    early = mm(pick_dp, early.reshape(dp_count, -1)).reshape(adapters * RANK, f3 + q_cols)
-
-    late = jnp.broadcast_to(grad_bq[None], (dp_count, tensor_count, RANK, q_cols))
-    late = lax.all_to_all(late.reshape(devices, RANK, q_cols), BOTH, 0, 0, tiled=True)
-    q_adapter_grad = mm(pick, late.reshape(devices, RANK * q_cols)).reshape(adapters * RANK, q_cols)
-    gate_up_adapter_grad = jnp.stack([early[:, :f1], early[:, f1:f2]])
-    down_adapter_grad = early[:, f2:f3].T
-    out_adapter_grad = early[:, f3:].T
+    gate_up_adapter_grad, down_adapter_grad, out_adapter_grad = pl.pallas_call(
+        sum_hidden_kernel,
+        name="sum_hidden",
+        in_specs=[scalars()] + wholes(early),
+        out_specs=(out_whole((2, LANES, ff_cols)), out_whole((ff_cols, LANES)), out_whole((q_cols, LANES))),
+        out_shape=(sds((2, LANES, ff_cols), F32), sds((ff_cols, LANES), F32), sds((q_cols, LANES), F32)),
+        scratch_shapes=[pltpu.VMEM((adapters, RANK, f3 + q_cols), F32)],
+        compiler_params=pltpu.CompilerParams(vmem_limit_bytes=VMEM_LIMIT),
+    )(adapter_ids, early)
+
+    own_rows = width // devices
+    kv_terms = jnp.tile(kv_term.transpose(1, 0, 2), (devices // RANK, 1, 1))
+    owned = jnp.concatenate(
+        [wide_term.reshape(devices, own_rows, LANES), kv_terms, jnp.zeros((devices, 2, LANES), BF)], axis=1
+    )
+    every = jnp.broadcast_to(grad_bq[None], (dp_count, tensor_count, RANK, q_cols)).reshape(devices, RANK, q_cols)
+    terms = lax.all_to_all(jnp.concatenate([owned, every], axis=2), BOTH, 0, 0, tiled=True)
+    terms = terms.reshape(seqs, devices // seqs, RANK, LANES + q_cols)
+    own_adapter = ((dp * tensor_count + tensor) // RANK).astype(jnp.int32).reshape(1)
+    wide_grad, kv_adapter_grad, q_adapter_grad = pl.pallas_call(
+        sum_wide_kernel,
+        name="sum_wide",
+        in_specs=[scalars(), scalars()] + wholes(terms),
+        out_specs=(out_whole((7, own_rows, LANES)), out_whole((2, 1, HD)), out_whole((LANES, q_cols))),
+        out_shape=(sds((7, own_rows, LANES), F32), sds((2, 1, HD), F32), sds((LANES, q_cols), F32)),
+        scratch_shapes=[pltpu.VMEM((adapters, RANK, LANES + q_cols), F32)],
+        compiler_params=pltpu.CompilerParams(vmem_limit_bytes=VMEM_LIMIT),
+    )(adapter_ids, own_adapter, terms)
     return (
         block_output, input_grad, wide_grad, kv_adapter_grad,
         q_adapter_grad, out_adapter_grad, gate_up_adapter_grad, down_adapter_grad,

time: 391 us -> 344 us (0.88)
  waiting for transfers between devices: 163 us -> 109 us
  starting transfers between devices: 32.4 us -> 62.3 us
  blocking collectives: 35.5 us -> 11.9 us
  local copies, waits for them, and re-layouts: 38.1 us -> 24.3 us
  Pallas kernels: 96.8 us -> 110 us
    all_gather x1, waiting for transfers between devices: 111 us -> 32.2 us  [on_device(): weights = lax.all_gather(pack, BOTH, axis=0, tiled=False)]
    ppermute x0 -> x13, starting transfers between devices: none -> 27.2 us  [the longest x10 21.8 us: from_dp(): return lax.ppermute(value, 'dp', pairs)]
    ppermute x0 -> x13, waiting for transfers between devices: none -> 26.6 us  [the longest x10 26.6 us: from_dp(): return lax.ppermute(value, 'dp', pairs)]
    all_to_all x1 -> x0, blocking collectives: 21.5 us -> none  [on_device(): received = lax.all_to_all(payload, BOTH, 0, 0, tiled=True)]
    reduce_scatter x1, waiting for transfers between devices: 19.2 us -> 0.02 us  [on_device(): lax.psum_scatter(early, 'tensor', scatter_dimension=0, tiled=True)]
    all_to_all x1, waiting for transfers between devices: 22.3 us -> 36.7 us  [on_device(): lax.all_to_all(jnp.concatenate([owned, every], axis=2), BOTH, 0, 0, tiled...]
    unnamed x58 -> x55, local copies, waits for them, and re-layouts: 20.6 us -> 12.8 us
    pallas_call x0 -> x2, Pallas kernels: none -> 7.23 us  [the longest x1 4.51 us: on_device(): pl.pallas_call(sum_hidden_kernel, name='sum_hidden', in_specs=[scalars()]...]
  transfers between devices with their start and end apart: 13 -> 26, of which waited for: 7 -> 12; matrix products, arithmetic and copies ran while one was open for 7% -> 8% of each run, Pallas kernels for 8% -> 17%
where the time goes in v3:
time: 344 us; the launch traced here: 343 us
  Pallas kernels  110 us (32%)
  waiting for transfers between devices  109 us (32%)
  starting transfers between devices  62.3 us (18%)
  local copies, waits for them, and re-layouts  24.3 us (7%)
  between operations  15 us (4%)
  blocking collectives  11.9 us (3%)
  other arithmetic  10.4 us (3%)
    pallas_call x6, Pallas kernels, call(): pl.pallas_call(kernel, name=name, grid=(steps,), in_specs=specs, out_spec...  103 us
    all_to_all x1, waiting for transfers between devices, on_device(): lax.all_to_all(jnp.concatenate([owned, every], axis=2), BOTH, 0, 0, tiled...  36.7 us
    all_gather x1, waiting for transfers between devices, on_device(): weights = lax.all_gather(pack, BOTH, axis=0, tiled=False)  32.2 us
    ppermute x10, waiting for transfers between devices, from_dp(): return lax.ppermute(value, 'dp', pairs)  26.6 us
    ppermute x10, starting transfers between devices, from_dp(): return lax.ppermute(value, 'dp', pairs)  21.8 us
    ppermute x8, starting transfers between devices, moved(): return lax.ppermute(value, BOTH, pairs)  20.1 us
    ppermute x8, waiting for transfers between devices, moved(): return lax.ppermute(value, BOTH, pairs)  13.8 us
    unnamed x55, local copies, waits for them, and re-layouts  12.8 us
  transfers between devices with their start and end apart: 26, of which 12 were waited for; matrix products, arithmetic and copies ran while one was open for 8% of the time, Pallas kernels for 17%

profile of v3, /device:TPU:1, one launch (start us, length us, event | category | flops | bytes accessed | tf_op | source)
XLA Modules:
  0.0 343.0 jit_solution(17612981159504282147)
XLA Ops:
  10.0 4.7 %collective-permute-start = (bf16[48,384]{1,0:T(8,128)(2,1)}, bf16[48,384]{1,0:T(8,128)(2,1)S(1)}, u32[]{:S(2)}, u32[]{:S(2)}) collective-permute-start(bf16[48,384]{1,0:T(8,128)(2,1)} %param.21), channel_id=1, source_target_pairs={{1,0},{2,1},{3,2},{0,3},{5,4},{6,5},{7,6},{4,7},{9,8},{10,9},{11,1... | collective-permute-start | bytes 110600 | tf_op jit(solution)/shard_map/ppermute | solution.py:393
  19.5 8.6 %all-to-all-start = ((bf16[32,48,384]{2,1,0:T(8,128)(2,1)}), bf16[32,48,384]{2,1,0:T(8,128)(2,1)S(1)}, u32[]{:S(2)}, u32[]{:S(2)}) async-start(bf16[32,48,384]{2,1,0:T(8,128)(2,1)} %pad_maximum_fusion.1), calls=%async_computation | async-start | bytes 2359296 | tf_op jit(solution)/shard_map/all_to_all | solution.py:417
  32.3 11.9 %all-gather = bf16[64,4224]{1,0:T(8,128)(2,1)S(1)} all-gather(bf16[16,4224]{1,0:T(8,128)(2,1)S(1)} %constant_dynamic-update-slice_fusion), channel_id=2, replica_groups=mesh['dp'=32,'tensor'=4] {'tensor'}, dimensions={0}, use_global_device_ids=true | all-gather | bytes 675840 | tf_op jit(solution)/shard_map/all_gather | solution.py:430
  57.3 4.6 %collective-permute-start.6 = (bf16[4,4,48,384]{3,2,1,0:T(8,128)(2,1)S(1)}, bf16[4,4,48,384]{3,2,1,0:T(8,128)(2,1)S(1)}, u32[]{:S(2)}, u32[]{:S(2)}) collective-permute-start(bf16[4,4,48,384]{3,2,1,0:T(8,128)(2,1)S(1)} %pad_maximum_fusion.2.rest_0_), channel_id=1, source_target_pairs={{32,0},{36,4},{40,8},{44,12},{48,16},{52,20},{56,24},{60,28},{64,3... | collective-permute-start | bytes 1769480 | tf_op jit(solution)/shard_map/ppermute | solution.py:402
  65.2 5.3 %collective-permute-start.9 = (bf16[4,4,48,384]{3,2,1,0:T(8,128)(2,1)S(1)}, bf16[4,4,48,384]{3,2,1,0:T(8,128)(2,1)}, u32[]{:S(2)}, u32[]{:S(2)}) collective-permute-start(bf16[4,4,48,384]{3,2,1,0:T(8,128)(2,1)S(1)} %pad_maximum_fusion.2.rest_0_), channel_id=1, source_target_pairs={{4,0},{0,4},{12,8},{8,12},{20,16},{16,20},{28,24},{24,28},{36,32},... | collective-permute-start | bytes 1769480 | tf_op jit(solution)/shard_map/ppermute | solution.py:402
  70.5 12.5 %collective-permute-done.6.rest_1_ = bf16[4,4,48,384]{3,2,1,0:T(8,128)(2,1)S(1)} collective-permute-done((bf16[4,4,48,384]{3,2,1,0:T(8,128)(2,1)S(1)}, bf16[4,4,48,384]{3,2,1,0:T(8,128)(2,1)S(1)}, u32[]{:S(2)}, u32[]{:S(2)}) %collective-permute-start.6) | collective-permute-done | bytes 589856 | tf_op jit(solution)/shard_map/ppermute | solution.py:402
  83.0 4.9 %collective-permute-start.10 = (bf16[4,4,48,384]{3,2,1,0:T(8,128)(2,1)S(1)}, bf16[4,4,48,384]{3,2,1,0:T(8,128)(2,1)}, u32[]{:S(2)}, u32[]{:S(2)}) collective-permute-start(bf16[4,4,48,384]{3,2,1,0:T(8,128)(2,1)S(1)} %collective-permute-done.6.rest_1_), channel_id=1, source_target_pairs={{4,0},{0,4},{12,8},{8,12},{20,16},{16,20},{28,24},{24,28},{36,32},... | collective-permute-start | bytes 1769480 | tf_op jit(solution)/shard_map/ppermute | solution.py:402
  89.1 9.1 %collective-permute-done.8.rest_3_ = bf16[4,4,48,384]{3,2,1,0:T(8,128)(2,1)} collective-permute-done((bf16[4,4,48,384]{3,2,1,0:T(8,128)(2,1)S(1)}, bf16[4,4,48,384]{3,2,1,0:T(8,128)(2,1)}, u32[]{:S(2)}, u32[]{:S(2)}) %collective-permute-start.8) | collective-permute-done | bytes 589856 | tf_op jit(solution)/shard_map/ppermute | solution.py:402
  102.9 11.2 %qkv.1 = (bf16[256,1536]{1,0:T(8,128)(2,1)}, bf16[256,128]{1,0:T(8,128)(2,1)}, bf16[256,256]{1,0:T(8,128)(2,1)}, bf16[256,1536]{1,0:T(8,128)(2,1)}, bf16[4,1536,384]{2,1,0:T(8,128)(2,1)}) custom-call(s32[4]{0:T(128)} %pad_add_fusion.place_ref, bf16[256,1536]{1,0:T(8,128)(2,1)} %x_ref.5, f32[1,1536]{1,0:T(1,128)} %get-tuple-element.119.gain_ref, ...), custom_call_target="tpu_custom_call" | custom-call | flops 1509949440 | bytes 4718592 | tf_op jit(solution)/shard_map/qkv/pallas_call | solution.py:342
  115.5 4.2 %collective-permute-start.14 = (bf16[256,256]{1,0:T(8,128)(2,1)}, bf16[256,256]{1,0:T(8,128)(2,1)S(1)}, u32[]{:S(2)}, u32[]{:S(2)}) collective-permute-start(bf16[256,256]{1,0:T(8,128)(2,1)} %get-tuple-element.43), channel_id=1, source_target_pairs={{0,3},{1,4},{2,5},{3,6},{4,7},{8,11},{9,12},{10,13},{11,14},{12,15... | collective-permute-start | bytes 393224 | tf_op jit(solution)/shard_map/ppermute | solution.py:516
  125.5 7.5 %collective-permute-done.15 = bf16[256,256]{1,0:T(8,128)(2,1)S(1)} collective-permute-done((bf16[256,256]{1,0:T(8,128)(2,1)}, bf16[256,256]{1,0:T(8,128)(2,1)S(1)}, u32[]{:S(2)}, u32[]{:S(2)}) %collective-permute-start.15) | collective-permute-done | bytes 131104 | tf_op jit(solution)/shard_map/ppermute | solution.py:516
  136.9 13.9 %attention.1 = (bf16[256,1536]{1,0:T(8,128)(2,1)}, bf16[12,1280,256]{2,1,0:T(8,128)(2,1)}) custom-call(bf16[1280,256]{1,0:T(8,128)(2,1)} %copy-done.5, s32[1280,1]{1,0:T(8,128)} %reshape.117.kseg_ref, s32[1,256]{1,0:T(1,128)} %bitcast.93, bf16[256,1536]{1,0:T(8,128)(2,1)} %get-tuple-element.44.q_ref), custom_call_target="tpu_custom_call" | custom-call | flops 2013265920 | bytes 7864320 | tf_op jit(solution)/shard_map/attention/pallas_call | solution.py:342
  150.8 32.2 %all-gather.6.cloned.1.call-done = bf16[6144,3840]{1,0:T(8,128)(2,1)} async-done(((bf16[48,3840]{1,0:T(8,128)(2,1)}), bf16[6144,3840]{1,0:T(8,128)(2,1)}) %all-gather.6.cloned.1.call-update) | async-done | bytes 47185936 | tf_op jit(solution)/shard_map/all_gather | solution.py:384
  183.1 7.7 %out_projection.1 = (f32[256,1536]{1,0:T(8,128)}, bf16[256,1536]{1,0:T(8,128)(2,1)}, bf16[256,128]{1,0:T(8,128)(2,1)}, bf16[256,128]{1,0:T(8,128)(2,1)}) custom-call(bf16[256,1536]{1,0:T(8,128)(2,1)} %x_ref.5, f32[1,1536]{1,0:T(1,128)} %get-tuple-element.120.gain_ref, bf16[1536,384]{1,0:T(8,128)(2,1)} %bitcast.68, ...), custom_call_target="tpu_custom_call" | custom-call | flops 1207959552 | bytes 4718592 | tf_op jit(solution)/shard_map/out_projection/pallas_call | solution.py:342
  190.7 40.1 %feed_forward.1 = (bf16[256,1536]{1,0:T(8,128)(2,1)}, f32[256,1536]{1,0:T(8,128)}, bf16[256,1536]{1,0:T(8,128)(2,1)}, f32[128,1536]{1,0:T(8,128)}, bf16[256,128]...) custom-call(f32[256,1536]{1,0:T(8,128)} %get-tuple-element.46.res_re, ...), custom_call_target="tpu_custom_call" | custom-call | flops 21743271936 | bytes 42467328 | tf_op jit(solution)/shard_map/feed_forward/pallas_call | solution.py:342
  232.8 23.7 %attention_back.1 = (bf16[1280,256]{1,0:T(8,128)(2,1)}, f32[256,1536]{1,0:T(8,128)}, f32[256,128]{1,0:T(8,128)}, bf16[4,16,384]{2,1,0:T(8,128)(2,1)}) custom-call(bf16[1280,256]{1,0:T(8,128)(2,1)} %copy-done.5, bf16[256,1536]{1,0:T(8,128)(2,1)} %get-tuple-element.53.gb_ref, bf16[256,128]{1,0:T(8,128)(2,1)} %get-tuple-element.54.gro_ref, ...), custom_call_target="tpu_custom_call" | custom-call | flops 6442450944 | bytes 9437184 | tf_op jit(solution)/shard_map/attention_back/pallas_call | solution.py:342
  257.6 4.3 %collective-permute-start.17 = (bf16[256,256]{1,0:T(8,128)(2,1)S(1)}, bf16[256,256]{1,0:T(8,128)(2,1)S(1)}, u32[]{:S(2)}, u32[]{:S(2)}) collective-permute-start(bf16[256,256]{1,0:T(8,128)(2,1)S(1)} %get-tuple-element.105), channel_id=1, source_target_pairs={{1,0},{2,1},{3,2},{4,3},{5,4},{6,5},{7,6},{9,8},{10,9},{11,10},{12... | collective-permute-start | bytes 393224 | tf_op jit(solution)/shard_map/ppermute | solution.py:516
  262.0 3.1 collective-permute-start.18
  269.2 3.2 collective-permute-done.19.back3_ref
  273.1 6.1 %input_gradient.1 = (f32[256,1536]{1,0:T(8,128)}, bf16[1536,128]{1,0:T(8,128)(2,1)}, bf16[2,16,128]{2,1,0:T(8,128)(2,1)}) custom-call(bf16[256,1536]{1,0:T(8,128)(2,1)} %x_ref.5, f32[1,1536]{1,0:T(1,128)} %get-tuple-element.119.gain_ref, bf16[1536,384]{1,0:T(8,128)(2,1)} %bitcast.70, bf16[1536,384]{1,0:T(8,128)(2,1)} %bitcast.71, ...), custom_call_target="tpu_custom_call" | custom-call | flops 503316480 | bytes 3145728 | tf_op jit(solution)/shard_map/input_gradient/pallas_call | solution.py:342
  283.3 6.3 %all-to-all-start.1 = ((bf16[128,16,512]{2,1,0:T(8,128)(2,1)}), bf16[128,16,512]{2,1,0:T(8,128)(2,1)S(1)}, u32[]{:S(2)}, u32[]{:S(2)}) async-start(bf16[128,16,512]{2,1,0:T(8,128)(2,1)} %pad_maximum_fusion), calls=%async_computation.2 | async-start | bytes 4194304 | tf_op jit(solution)/shard_map/all_to_all | solution.py:632
  289.7 36.7 %all-to-all-done.1 = bf16[128,16,512]{2,1,0:T(8,128)(2,1)S(1)} async-done(((bf16[128,16,512]{2,1,0:T(8,128)(2,1)}), bf16[128,16,512]{2,1,0:T(8,128)(2,1)S(1)}, u32[]{:S(2)}, u32[]{:S(2)}) %all-to-all-start.1) | async-done | bytes 2097184 | tf_op jit(solution)/shard_map/all_to_all | solution.py:632
  327.7 2.7 sum_wide.1
  331.9 4.5 %sum_hidden.1 = (f32[2,128,1152]{2,1,0:T(8,128)}, f32[1152,128]{1,0:T(8,128)}, f32[384,128]{1,0:T(8,128)}) custom-call(s32[16]{0:T(128)} %ids_ref.3, bf16[32,16,3840]{2,1,0:T(8,128)(2,1)} %bitcast.76), custom_call_target="tpu_custom_call" | custom-call | tf_op jit(solution)/shard_map/sum_hidden/pallas_call | solution.py:616
  (139 shorter events, 59.2 us)
Async XLA Ops:
  7.2 175.9 %all-gather.6.cloned.1.call-start = ((), (), s32[]{:S(2)}) async-start(), calls=%async_computation.4 | async-start | bytes 47554560 | tf_op jit(solution)/shard_map/all_gather | solution.py:384
  10.0 37.2 %collective-permute-start = (bf16[48,384]{1,0:T(8,128)(2,1)}, bf16[48,384]{1,0:T(8,128)(2,1)S(1)}, u32[]{:S(2)}, u32[]{:S(2)}) collective-permute-start(bf16[48,384]{1,0:T(8,128)(2,1)} %param.21), channel_id=1, source_target_pairs={{1,0},{2,1},{3,2},{0,3},{5,4},{6,5},{7,6},{4,7},{9,8},{10,9},{11,1... | collective-permute-start | bytes 110600 | tf_op jit(solution)/shard_map/ppermute | solution.py:393
  14.6 32.5 %collective-permute-start.1 = (bf16[48,384]{1,0:T(8,128)(2,1)}, bf16[48,384]{1,0:T(8,128)(2,1)S(1)}, u32[]{:S(2)}, u32[]{:S(2)}) collective-permute-start(bf16[48,384]{1,0:T(8,128)(2,1)} %param.21), channel_id=1, source_target_pairs={{2,0},{3,1},{0,2},{1,3},{6,4},{7,5},{4,6},{5,7},{10,8},{11,9},{8,1... | collective-permute-start | bytes 110600 | tf_op jit(solution)/shard_map/ppermute | solution.py:393
  14.6 32.5 %collective-permute-start.2 = (bf16[48,384]{1,0:T(8,128)(2,1)}, bf16[48,384]{1,0:T(8,128)(2,1)S(1)}, u32[]{:S(2)}, u32[]{:S(2)}) collective-permute-start(bf16[48,384]{1,0:T(8,128)(2,1)} %param.21), channel_id=1, source_target_pairs={{3,0},{0,1},{1,2},{2,3},{7,4},{4,5},{5,6},{6,7},{11,8},{8,9},{9,10... | collective-permute-start | bytes 110600 | tf_op jit(solution)/shard_map/ppermute | solution.py:393
  19.5 82.4 %all-to-all-start = ((bf16[32,48,384]{2,1,0:T(8,128)(2,1)}), bf16[32,48,384]{2,1,0:T(8,128)(2,1)S(1)}, u32[]{:S(2)}, u32[]{:S(2)}) async-start(bf16[32,48,384]{2,1,0:T(8,128)(2,1)} %pad_maximum_fusion.1), calls=%async_computation | async-start | bytes 2359296 | tf_op jit(solution)/shard_map/all_to_all | solution.py:417
  28.1 228.3 %reduce-scatter.2.cloned.1.call-start = ((), (), s32[]{:S(2)}) async-start(), calls=%async_computation.3 | async-start | bytes 614400 | tf_op jit(solution)/shard_map/reduce_scatter | solution.py:613
  49.6 5.6 %collective-permute-start.4 = (bf16[4,48,384]{2,1,0:T(8,128)(2,1)S(1)}, bf16[4,48,384]{2,1,0:T(8,128)(2,1)S(1)}, u32[]{:S(2)}, u32[]{:S(2)}) collective-permute-start(bf16[4,48,384]{2,1,0:T(8,128)(2,1)S(1)} %get-tuple-element.114), channel_id=1, source_target_pairs={{16,0},{20,4},{24,8},{28,12},{0,16},{4,20},{8,24},{12,28},{48,32},... | collective-permute-start | bytes 442376 | tf_op jit(solution)/shard_map/ppermute | solution.py:402
  50.4 6.8 %collective-permute-start.5 = (bf16[4,48,384]{2,1,0:T(8,128)(2,1)S(1)}, bf16[4,48,384]{2,1,0:T(8,128)(2,1)S(1)}, u32[]{:S(2)}, u32[]{:S(2)}) collective-permute-start(bf16[4,48,384]{2,1,0:T(8,128)(2,1)S(1)} %get-tuple-element.114), channel_id=1, source_target_pairs={{24,0},{28,4},{0,8},{4,12},{8,16},{12,20},{16,24},{20,28},{56,32},... | collective-permute-start | bytes 442376 | tf_op jit(solution)/shard_map/ppermute | solution.py:402
  57.3 25.7 %collective-permute-start.6 = (bf16[4,4,48,384]{3,2,1,0:T(8,128)(2,1)S(1)}, bf16[4,4,48,384]{3,2,1,0:T(8,128)(2,1)S(1)}, u32[]{:S(2)}, u32[]{:S(2)}) collective-permute-start(bf16[4,4,48,384]{3,2,1,0:T(8,128)(2,1)S(1)} %pad_maximum_fusion.2.rest_0_), channel_id=1, source_target_pairs={{32,0},{36,4},{40,8},{44,12},{48,16},{52,20},{56,24},{60,28},{64,3... | collective-permute-start | bytes 1769480 | tf_op jit(solution)/shard_map/ppermute | solution.py:402
  61.9 26.0 %collective-permute-start.7 = (bf16[4,4,48,384]{3,2,1,0:T(8,128)(2,1)S(1)}, bf16[4,4,48,384]{3,2,1,0:T(8,128)(2,1)S(1)}, u32[]{:S(2)}, u32[]{:S(2)}) collective-permute-start(bf16[4,4,48,384]{3,2,1,0:T(8,128)(2,1)S(1)} %pad_maximum_fusion.2.rest_0_), channel_id=1, source_target_pairs={{64,0},{68,4},{72,8},{76,12},{80,16},{84,20},{88,24},{92,28},{96,3... | collective-permute-start | bytes 1769480 | tf_op jit(solution)/shard_map/ppermute | solution.py:402
  61.9 36.3 %collective-permute-start.8 = (bf16[4,4,48,384]{3,2,1,0:T(8,128)(2,1)S(1)}, bf16[4,4,48,384]{3,2,1,0:T(8,128)(2,1)}, u32[]{:S(2)}, u32[]{:S(2)}) collective-permute-start(bf16[4,4,48,384]{3,2,1,0:T(8,128)(2,1)S(1)} %pad_maximum_fusion.2.rest_0_), channel_id=1, source_target_pairs={{96,0},{100,4},{104,8},{108,12},{112,16},{116,20},{120,24},{124,28... | collective-permute-start | bytes 1769480 | tf_op jit(solution)/shard_map/ppermute | solution.py:402
  65.2 36.7 %collective-permute-start.9 = (bf16[4,4,48,384]{3,2,1,0:T(8,128)(2,1)S(1)}, bf16[4,4,48,384]{3,2,1,0:T(8,128)(2,1)}, u32[]{:S(2)}, u32[]{:S(2)}) collective-permute-start(bf16[4,4,48,384]{3,2,1,0:T(8,128)(2,1)S(1)} %pad_maximum_fusion.2.rest_0_), channel_id=1, source_target_pairs={{4,0},{0,4},{12,8},{8,12},{20,16},{16,20},{28,24},{24,28},{36,32},... | collective-permute-start | bytes 1769480 | tf_op jit(solution)/shard_map/ppermute | solution.py:402
  83.0 18.9 %collective-permute-start.10 = (bf16[4,4,48,384]{3,2,1,0:T(8,128)(2,1)S(1)}, bf16[4,4,48,384]{3,2,1,0:T(8,128)(2,1)}, u32[]{:S(2)}, u32[]{:S(2)}) collective-permute-start(bf16[4,4,48,384]{3,2,1,0:T(8,128)(2,1)S(1)} %collective-permute-done.6.rest_1_), channel_id=1, source_target_pairs={{4,0},{0,4},{12,8},{8,12},{20,16},{16,20},{28,24},{24,28},{36,32},... | collective-permute-start | bytes 1769480 | tf_op jit(solution)/shard_map/ppermute | solution.py:402
  87.8 14.1 %collective-permute-start.11 = (bf16[4,4,48,384]{3,2,1,0:T(8,128)(2,1)S(1)}, bf16[4,4,48,384]{3,2,1,0:T(8,128)(2,1)}, u32[]{:S(2)}, u32[]{:S(2)}) collective-permute-start(bf16[4,4,48,384]{3,2,1,0:T(8,128)(2,1)S(1)} %collective-permute-done.7.rest_2_), channel_id=1, source_target_pairs={{4,0},{0,4},{12,8},{8,12},{20,16},{16,20},{28,24},{24,28},{36,32},... | collective-permute-start | bytes 1769480 | tf_op jit(solution)/shard_map/ppermute | solution.py:402
  114.1 11.3 %collective-permute-start.13 = (bf16[256,256]{1,0:T(8,128)(2,1)}, bf16[256,256]{1,0:T(8,128)(2,1)S(1)}, u32[]{:S(2)}, u32[]{:S(2)}) collective-permute-start(bf16[256,256]{1,0:T(8,128)(2,1)} %get-tuple-element.43), channel_id=1, source_target_pairs={{0,4},{1,5},{2,6},{3,7},{8,12},{9,13},{10,14},{11,15},{16,20},{17,... | collective-permute-start | bytes 393224 | tf_op jit(solution)/shard_map/ppermute | solution.py:516
  115.5 10.1 %collective-permute-start.14 = (bf16[256,256]{1,0:T(8,128)(2,1)}, bf16[256,256]{1,0:T(8,128)(2,1)S(1)}, u32[]{:S(2)}, u32[]{:S(2)}) collective-permute-start(bf16[256,256]{1,0:T(8,128)(2,1)} %get-tuple-element.43), channel_id=1, source_target_pairs={{0,3},{1,4},{2,5},{3,6},{4,7},{8,11},{9,12},{10,13},{11,14},{12,15... | collective-permute-start | bytes 393224 | tf_op jit(solution)/shard_map/ppermute | solution.py:516
  121.4 11.6 %collective-permute-start.15 = (bf16[256,256]{1,0:T(8,128)(2,1)}, bf16[256,256]{1,0:T(8,128)(2,1)S(1)}, u32[]{:S(2)}, u32[]{:S(2)}) collective-permute-start(bf16[256,256]{1,0:T(8,128)(2,1)} %get-tuple-element.43), channel_id=1, source_target_pairs={{0,2},{1,3},{2,4},{3,5},{4,6},{5,7},{8,10},{9,11},{10,12},{11,13},... | collective-permute-start | bytes 393224 | tf_op jit(solution)/shard_map/ppermute | solution.py:516
  123.3 11.9 %collective-permute-start.16 = (bf16[256,256]{1,0:T(8,128)(2,1)}, bf16[256,256]{1,0:T(8,128)(2,1)S(1)}, u32[]{:S(2)}, u32[]{:S(2)}) collective-permute-start(bf16[256,256]{1,0:T(8,128)(2,1)} %get-tuple-element.43), channel_id=1, source_target_pairs={{0,1},{1,2},{2,3},{3,4},{4,5},{5,6},{6,7},{8,9},{9,10},{10,11},{11... | collective-permute-start | bytes 393224 | tf_op jit(solution)/shard_map/ppermute | solution.py:516
  232.7 99.2 %all-gather.8.cloned.1.call-start = ((), (), s32[]{:S(2)}) async-start(), calls=%async_computation.5 | async-start | bytes 4055040 | tf_op jit(solution)/shard_map/all_gather | solution.py:615
  257.6 10.7 %collective-permute-start.17 = (bf16[256,256]{1,0:T(8,128)(2,1)S(1)}, bf16[256,256]{1,0:T(8,128)(2,1)S(1)}, u32[]{:S(2)}, u32[]{:S(2)}) collective-permute-start(bf16[256,256]{1,0:T(8,128)(2,1)S(1)} %get-tuple-element.105), channel_id=1, source_target_pairs={{1,0},{2,1},{3,2},{4,3},{5,4},{6,5},{7,6},{9,8},{10,9},{11,10},{12... | collective-permute-start | bytes 393224 | tf_op jit(solution)/shard_map/ppermute | solution.py:516
  262.0 7.2 %collective-permute-start.18 = (bf16[256,256]{1,0:T(8,128)(2,1)S(1)}, bf16[256,256]{1,0:T(8,128)(2,1)S(1)}, u32[]{:S(2)}, u32[]{:S(2)}) collective-permute-start(bf16[256,256]{1,0:T(8,128)(2,1)S(1)} %get-tuple-element.104), channel_id=1, source_target_pairs={{2,0},{3,1},{4,2},{5,3},{6,4},{7,5},{10,8},{11,9},{12,10},{13,11},... | collective-permute-start | bytes 393224 | tf_op jit(solution)/shard_map/ppermute | solution.py:516
  265.0 7.4 %collective-permute-start.19 = (bf16[256,256]{1,0:T(8,128)(2,1)S(1)}, bf16[256,256]{1,0:T(8,128)(2,1)S(1)}, u32[]{:S(2)}, u32[]{:S(2)}) collective-permute-start(bf16[256,256]{1,0:T(8,128)(2,1)S(1)} %get-tuple-element.103), channel_id=1, source_target_pairs={{3,0},{4,1},{5,2},{6,3},{7,4},{11,8},{12,9},{13,10},{14,11},{15,12... | collective-permute-start | bytes 393224 | tf_op jit(solution)/shard_map/ppermute | solution.py:516
  267.0 5.4 %collective-permute-start.20 = (bf16[256,256]{1,0:T(8,128)(2,1)S(1)}, bf16[256,256]{1,0:T(8,128)(2,1)S(1)}, u32[]{:S(2)}, u32[]{:S(2)}) collective-permute-start(bf16[256,256]{1,0:T(8,128)(2,1)S(1)} %get-tuple-element.102), channel_id=1, source_target_pairs={{4,0},{5,1},{6,2},{7,3},{12,8},{13,9},{14,10},{15,11},{20,16},{21,... | collective-permute-start | bytes 393224 | tf_op jit(solution)/shard_map/ppermute | solution.py:516
  283.3 43.1 %all-to-all-start.1 = ((bf16[128,16,512]{2,1,0:T(8,128)(2,1)}), bf16[128,16,512]{2,1,0:T(8,128)(2,1)S(1)}, u32[]{:S(2)}, u32[]{:S(2)}) async-start(bf16[128,16,512]{2,1,0:T(8,128)(2,1)} %pad_maximum_fusion), calls=%async_computation.2 | async-start | bytes 4194304 | tf_op jit(solution)/shard_map/all_to_all | solution.py:632
  (21 other events, 242.0 us)
Sparse Core Ops, SparseCore 0:
  11.0 172.0 all-gather.5
  232.8 21.0 reduce-scatter.1
  256.6 62.1 all-gather.7

commit v4 on v2

v4 whole, which is shorter than its diff:
```python
import math

import jax
import jax.numpy as jnp
from jax import lax
from jax.experimental import pallas as pl
from jax.experimental.pallas import tpu as pltpu
from jax.sharding import Mesh, PartitionSpec as P

HD = 128
WINDOW = 1024
RANK = 16
LANES = 128
EPS = 1e-06
MASKED = -1e30
SCALE = HD ** (-0.5)
LOG2E = math.log2(math.e)
GELU_C = 0.7978845608028654
GELU_A = 0.044715
VMEM_LIMIT = 58 * 1024 * 1024
BF = jnp.bfloat16
F32 = jnp.float32
DP = ("y", "x", "core")
SEQ = ("core", "tensor")
ALL = ("y", "x", "core", "tensor")

SLOT_Q, SLOT_K, SLOT_V, SLOT_G, SLOT_U, SLOT_O, SLOT_D = range(7)


def rows_of(slot):
    return slice(slot * RANK, (slot + 1) * RANK)


def mm(a, b):
    return lax.dot_general(a, b, (((1,), (0,)), ((), ())), preferred_element_type=F32)


def mm_nt(a, b):
    return lax.dot_general(a, b, (((1,), (1,)), ((), ())), preferred_element_type=F32)


def turned(a):
    return a.astype(F32).T.astype(BF)


def rope(v, cos, sin):
    return v * cos + pltpu.roll(v, HD // 2, 1) * sin


def rope_back(g, cos, sin):
    return g * cos - pltpu.roll(g, HD // 2, 1) * sin


def flat(ref):
    block = ref[...]
    return block.reshape(block.shape[0] * block.shape[2], block.shape[3])


def rms(v, gain):
    return v * lax.rsqrt(jnp.mean(v * v, axis=-1, keepdims=True) + EPS) * gain


def rms_back(v, gain, grad):
    inv = lax.rsqrt(jnp.mean(v * v, axis=-1, keepdims=True) + EPS)
    scaled = grad * gain
    dot = jnp.mean(v * scaled, axis=-1, keepdims=True)
    return inv * scaled - v * (inv * inv * inv * dot)


def shared_kernel(x_ref, gain_ref, a_ref, wk_ref, wv_ref, bkv_ref, cos_ref, sin_ref, n1_ref, r1_ref, kv_ref):
    n1 = rms(x_ref[...].astype(F32), gain_ref[...]).astype(BF)
    n1_ref[...] = n1
    r1 = mm(n1, a_ref[...]).astype(BF)
    r1_ref[...] = r1
    key = mm(n1, wk_ref[...]) + mm(r1, bkv_ref[0])
    kv_ref[:, :HD] = rope(key, cos_ref[...], sin_ref[...]).astype(BF)
    kv_ref[:, HD:] = (mm(n1, wv_ref[...]) + mm(r1, bkv_ref[1])).astype(BF)


def fill_window(kv_ref, place_ref, seq_ref):
    rows = seq_ref.shape[1]
    reach = kv_ref.shape[0] // rows - 1
    own = place_ref[0] * (seq_ref.shape[0] // 2) + place_ref[1]
    for w in range(reach + 1):
        kv_ref[w * rows : (w + 1) * rows] = seq_ref[jnp.maximum(own - reach + w, 0)]


def attn_kernel(
    place_ref, seq_ref, kseg_ref, qseg_ref, n1_ref, r1_ref, cos_ref, sin_ref, x_ref, gain_ref, a_ref,
    wq_ref, bq_ref, wo_ref, bo_ref,
    q_ref, mixed_ref, p_ref, inv_ref, res_ref, n2_ref, r2_ref, ro_ref,
    bias_ref, s_ref, vt_ref, kv_ref, acc_ref, rank_ref,
):
    step = pl.program_id(0)
    rows = q_ref.shape[0]
    chunks = kv_ref.shape[0] // rows

    @pl.when(step == 0)
    def _():
        fill_window(kv_ref, place_ref, seq_ref)
        key = lax.broadcasted_iota(jnp.int32, bias_ref.shape, 0)
        query = lax.broadcasted_iota(jnp.int32, bias_ref.shape, 1)
        allowed = (key >= query) & (key <= query + WINDOW) & (kseg_ref[...] == qseg_ref[...])
        bias_ref[...] = jnp.where(allowed, 0.0, MASKED)
        vt_ref[...] = turned(kv_ref[:, HD:])
        acc_ref[...] = jnp.zeros_like(acc_ref)
        rank_ref[...] = jnp.zeros_like(rank_ref)

    lin = mm(n1_ref[...], flat(wq_ref)) + mm(r1_ref[...], bq_ref[0])
    for h in range(q_ref.shape[1] // HD):
        part = slice(h * HD, (h + 1) * HD)
        query = (rope(lin[:, part], cos_ref[...], sin_ref[...]) * (SCALE * LOG2E)).astype(BF)
        q_ref[:, part] = query
        top = jnp.full((1, rows), MASKED, F32)
        for c in range(chunks):
            span = slice(c * rows, (c + 1) * rows)
            s = mm_nt(kv_ref[span, :HD], query) + bias_ref[span]
            s_ref[span] = s
            top = jnp.maximum(top, jnp.max(s, axis=0, keepdims=True))
        total = jnp.zeros((1, rows), F32)
        for c in range(chunks):
            span = slice(c * rows, (c + 1) * rows)
            p = jnp.exp2(s_ref[span] - top)
            total = total + jnp.sum(p, axis=0, keepdims=True)
            p_ref[h, span] = p.astype(BF)
        inv = 1.0 / total
        inv_ref[0, h : h + 1] = inv
        mixed_ref[:, part] = (mm(vt_ref[...], p_ref[h]) * inv).T.astype(BF)

    mixed = mixed_ref[...]
    acc_ref[...] += mm_nt(mixed, flat(wo_ref))
    rank_ref[...] += mm_nt(mixed, bo_ref[0])

    @pl.when(step == pl.num_programs(0) - 1)
    def _():
        ro = rank_ref[...].astype(BF)
        ro_ref[...] = ro
        res = x_ref[...].astype(F32) + (acc_ref[...] + mm_nt(ro, a_ref[...]))
        res_ref[...] = res
        n2 = rms(res, gain_ref[...]).astype(BF)
        n2_ref[...] = n2
        r2_ref[...] = mm(n2, a_ref[...]).astype(BF)


def ffn_kernel(
    res_ref, n2_ref, r2_ref, cot_ref, gain_ref, mixed_ref, ro_ref, a_ref, b_ref, w_ref,
    out_ref, gres_ref, gb_ref, wide_ref, gro_ref, gbo_ref, gbh_ref,
    ffn_ref, g2_ref, rd_ref, gr_ref, r2t_ref, grd_ref, grdt_ref, wv_ref, sems,
):
    step = pl.program_id(0)
    last = pl.num_programs(0) - 1
    ff = b_ref.shape[2] // 3
    slot = lax.rem(step, 2)

    def copies(at, to):
        spans = (pl.ds(2 * ff, ff), pl.ds(0, 2 * ff))
        return [
            pltpu.make_async_copy(w_ref.at[:, at, :, cols], wv_ref.at[to, :, :, cols], sems.at[to, j])
            for j, cols in enumerate(spans)
        ]

    @pl.when(step == 0)
    def _():
        for copy in copies(0, 0):
            copy.start()
        ffn_ref[...] = jnp.zeros_like(ffn_ref)
        g2_ref[...] = jnp.zeros_like(g2_ref)
        rd_ref[...] = jnp.zeros_like(rd_ref)
        gr_ref[...] = jnp.zeros_like(gr_ref)
        r2t_ref[...] = turned(r2_ref[...])
        grd = mm(cot_ref[...], a_ref[...]).astype(BF)
        grd_ref[...] = grd
        grdt_ref[...] = turned(grd)

    @pl.when(step < last)
    def _():
        for copy in copies(step + 1, 1 - slot):
            copy.start()

    n2, r2, cot = n2_ref[...], r2_ref[...], cot_ref[...]
    b_gu, b_d = b_ref[0, :, : 2 * ff], b_ref[0, :, 2 * ff :]
    down, gate_up = copies(step, slot)
    rows_of_weight = wv_ref.shape[1] * wv_ref.shape[2]
    down.wait()
    w_d = wv_ref[slot, :, :, 2 * ff :].reshape(rows_of_weight, ff)
    grad_hidden = (mm(cot, w_d) + mm(grd_ref[...], b_d)).astype(BF).astype(F32)
    gate_up.wait()
    w_gu = wv_ref[slot, :, :, : 2 * ff].reshape(rows_of_weight, 2 * ff)
    lin = mm(n2, w_gu) + mm(r2, b_gu)
    gate, up = lin[:, :ff], lin[:, ff:]
    square = gate * gate
    th = jnp.tanh(GELU_C * (gate + GELU_A * square * gate))
    half = 0.5 * (1.0 + th)
    act = gate * half
    slope = half + 0.5 * gate * (1.0 - th * th) * (GELU_C * (1.0 + 3.0 * GELU_A * square))
    hidden = (act * up).astype(BF)
    grad_gate = (grad_hidden * up * slope).astype(BF)
    grad_up = (grad_hidden * act).astype(BF)
    grads = jnp.concatenate([grad_gate, grad_up], axis=1)
    ffn_ref[...] += mm_nt(hidden, w_d)
    rd_ref[...] += mm_nt(hidden, b_d)
    g2_ref[...] += mm_nt(grads, w_gu)
    gr_ref[...] += mm_nt(grads, b_gu)
    gbh_ref[0, :, :ff] = mm(r2t_ref[rows_of(SLOT_G)], grad_gate).astype(BF)
    gbh_ref[0, :, ff : 2 * ff] = mm(r2t_ref[rows_of(SLOT_U)], grad_up).astype(BF)
    gbh_ref[0, :, 2 * ff :] = mm(grdt_ref[rows_of(SLOT_D)], hidden).astype(BF)

    @pl.when(step == last)
    def _():
        rd = rd_ref[...].astype(BF)
        gr = gr_ref[...].astype(BF)
        res = res_ref[...]
        out_ref[...] = (res + (ffn_ref[...] + mm_nt(rd, a_ref[...]))).astype(BF)
        grad_two = g2_ref[...] + mm_nt(gr, a_ref[...])
        grad_res = cot_ref[...].astype(F32) + rms_back(res, gain_ref[...], grad_two)
        gres_ref[...] = grad_res
        grad_branch = grad_res.astype(BF)
        gb_ref[...] = grad_branch
        gro = mm(grad_branch, a_ref[...])
        gro_ref[...] = gro.astype(BF)
        grot = gro.T[rows_of(SLOT_O)].astype(BF)
        cols = gbo_ref.shape[2]
        for t in range(gbo_ref.shape[0]):
            gbo_ref[t] = mm(grot, mixed_ref[:, t * cols : (t + 1) * cols]).astype(BF)
        wide = mm(gr_ref[...].T.astype(BF), n2) + mm(rd_ref[...].T.astype(BF), cot)
        wide_ref[...] = wide + mm(turned(ro_ref[...]), grad_branch)


def attn_back_kernel(
    place_ref, seq_ref, gb_ref, gro_ref, r1_ref, cos_ref, sin_ref, cosw_ref, sinw_ref, a_ref, bkv_ref, widef_ref,
    n1a_ref, n1b_ref, n1c_ref, n1d_ref, n1e_ref,
    q_ref, mixed_ref, p_ref, inv_ref, wo_ref, bo_ref, wq_ref, bq_ref,
    dkv_ref, g1_ref, gr_ref, gbq_ref, wide_ref, kvg_ref,
    ds_ref, dk_ref, dv_ref, kt_ref, r1t_ref, gq_ref, gm_ref, kv_ref,
):
    step = pl.program_id(0)
    rows = q_ref.shape[0]
    chunks = kv_ref.shape[0] // rows

    @pl.when(step == 0)
    def _():
        fill_window(kv_ref, place_ref, seq_ref)
        kt_ref[...] = turned(kv_ref[:, :HD])
        r1t_ref[...] = turned(r1_ref[...])
        dk_ref[...] = jnp.zeros_like(dk_ref)
        dv_ref[...] = jnp.zeros_like(dv_ref)
        g1_ref[...] = jnp.zeros_like(g1_ref)
        gr_ref[...] = jnp.zeros_like(gr_ref)

    gm_ref[...] = (mm(gb_ref[...], flat(wo_ref)) + mm(gro_ref[...], bo_ref[0])).astype(BF)
    for h in range(q_ref.shape[1] // HD):
        part = slice(h * HD, (h + 1) * HD)
        query, grad = q_ref[:, part], gm_ref[:, part]
        delta = grad.astype(F32) * mixed_ref[:, part].astype(F32)
        delta = jnp.sum(delta.T, axis=0, keepdims=True)
        inv = inv_ref[0, h : h + 1]
        for c in range(chunks):
            span = slice(c * rows, (c + 1) * rows)
            p = p_ref[h, span].astype(F32) * inv
            dp = mm_nt(kv_ref[span, HD:], grad)
            ds = (p * (dp - delta)).astype(BF)
            ds_ref[span] = ds
            dk_ref[span] += mm(ds, query)
            dv_ref[span] += mm(p.astype(BF), grad)
        dq = mm(kt_ref[...], ds_ref[...]) * SCALE
        gq_ref[:, part] = rope_back(dq.T, cos_ref[...], sin_ref[...]).astype(BF)

    gq = gq_ref[...]
    gbq_ref[0] = mm(r1t_ref[rows_of(SLOT_Q)], gq).astype(BF)
    gr_ref[...] += mm_nt(gq, bq_ref[0])
    g1_ref[...] += mm_nt(gq, flat(wq_ref))

    @pl.when(step == pl.num_programs(0) - 1)
    def _():
        wide = widef_ref[...]
        kvg = [jnp.zeros((RANK, HD), F32), jnp.zeros((RANK, HD), F32)]
        n1_refs = (n1a_ref, n1b_ref, n1c_ref, n1d_ref, n1e_ref)
        for w, n1w_ref in enumerate(n1_refs):
            span = slice(w * rows, (w + 1) * rows)
            grad_key = dk_ref[span] * (1.0 / LOG2E)
            gv = dv_ref[span].astype(BF)
            dkv_ref[span, :HD] = grad_key.astype(BF)
            dkv_ref[span, HD:] = gv
            gk = rope_back(grad_key, cosw_ref[span], sinw_ref[span]).astype(BF)
            gr = mm_nt(gk, bkv_ref[0]) + mm_nt(gv, bkv_ref[1])
            if w == chunks - 1:
                gr = gr + gr_ref[...]
                r1t = r1t_ref[...]
            else:
                r1t = mm(n1w_ref[...], a_ref[...]).T.astype(BF)
            wide = wide + mm(gr.T.astype(BF), n1w_ref[...])
            kvg[0] = kvg[0] + mm(r1t[rows_of(SLOT_K)], gk)
            kvg[1] = kvg[1] + mm(r1t[rows_of(SLOT_V)], gv)
        wide_ref[...] = wide.T.astype(BF)
        kvg_ref[0] = kvg[0].astype(BF)
        kvg_ref[1] = kvg[1].astype(BF)


def input_kernel(
    x_ref, gain_ref, a_ref, wk_ref, wv_ref, bkv_ref, cos_ref, sin_ref,
    own_ref, back1_ref, back2_ref, back3_ref, back4_ref, gr_ref, g1_ref, gres_ref, grad_ref,
):
    gkv = own_ref[...].astype(F32)
    for back_ref in (back1_ref, back2_ref, back3_ref, back4_ref):
        gkv = gkv + back_ref[...].astype(F32)
    gk = rope_back(gkv[:, :HD], cos_ref[...], sin_ref[...]).astype(BF)
    gv = gkv[:, HD:].astype(BF)
    gr = gr_ref[...] + mm_nt(gk, bkv_ref[0]) + mm_nt(gv, bkv_ref[1])
    g1 = g1_ref[...] + mm_nt(gk, wk_ref[...]) + mm_nt(gv, wv_ref[...])
    g1 = g1 + mm_nt(gr.astype(BF), a_ref[...])
    x = x_ref[...].astype(F32)
    grad_ref[...] = gres_ref[...] + rms_back(x, gain_ref[...], g1)


def sum_hidden_kernel(ids_ref, terms_ref, gu_ref, down_ref, out_ref, acc_ref):
    acc_ref[...] = jnp.zeros_like(acc_ref)
    for s in range(terms_ref.shape[0] // 2):
        acc_ref[ids_ref[s]] += terms_ref[2 * s].astype(F32) + terms_ref[2 * s + 1].astype(F32)
    adapters, rank, cols = acc_ref.shape
    ff = gu_ref.shape[2]

    def taken(first, last):
        return acc_ref[:, :, first:last].reshape(adapters * rank, last - first)

    gu_ref[0] = taken(0, ff)
    gu_ref[1] = taken(ff, 2 * ff)
    down_ref[...] = taken(2 * ff, 3 * ff).T
    out_ref[...] = taken(3 * ff, cols).T


def sum_wide_kernel(ids_ref, own_ref, terms_ref, wide_ref, kv_ref, q_ref, acc_ref):
    acc_ref[...] = jnp.zeros_like(acc_ref)
    seqs, parts = terms_ref.shape[:2]
    for s in range(seqs):
        term = terms_ref[s, 0].astype(F32)
        for part in range(1, parts):
            term = term + terms_ref[s, part].astype(F32)
        acc_ref[ids_ref[s]] += term
    adapters, rank, _ = acc_ref.shape
    q_ref[...] = acc_ref[:, :, LANES:].reshape(q_ref.shape)
    lane = lax.broadcasted_iota(jnp.int32, (rank, LANES), 1) // RANK
    slots, own_rows = wide_ref.shape[:2]
    for j in range(slots):
        total = jnp.zeros((rank, LANES), F32)
        for a in range(adapters):
            moved = pltpu.roll(acc_ref[a, :, :LANES], ((a - j) * RANK) % LANES, 1)
            total = jnp.where(lane == a, moved, total)
        wide_ref[j] = total[:own_rows]
    mine = acc_ref[own_ref[0], :, :LANES]
    for j in range(2):
        kv_ref[j] = mine[own_rows + j : own_rows + j + 1]


def sds(shape, dtype):
    return jax.ShapeDtypeStruct(shape, dtype)


def scalars():
    return pl.BlockSpec(memory_space=pltpu.SMEM)


def whole(array):
    rank = len(array.shape)
    return pl.BlockSpec(array.shape, lambda *_: (0,) * rank)


def wholes(*arrays):
    return [whole(v) for v in arrays]


def by_step(*shape):
    return pl.BlockSpec((1,) + shape, lambda t: (t,) + (0,) * len(shape))


def call(kernel, name, steps, args, specs, outs, scratch, flops, nbytes):
    shapes = [shape for shape, _ in outs]
    return pl.pallas_call(
        kernel,
        name=name,
        grid=(steps,),
        in_specs=specs,
        out_specs=[whole(shape) if spec is None else spec for shape, spec in outs],
        out_shape=shapes,
        scratch_shapes=scratch,
        compiler_params=pltpu.CompilerParams(
            dimension_semantics=("arbitrary",), vmem_limit_bytes=VMEM_LIMIT
        ),
        cost_estimate=pl.CostEstimate(flops=flops, bytes_accessed=nbytes, transcendentals=0),
    )(*args)


def rope_tables(positions):
    half = HD // 2
    frequency = 10000.0 ** (-(jnp.arange(half).astype(F32) / half))
    angles = positions.astype(F32)[:, None] * frequency[None, :]
    cos, sin = jnp.cos(angles), jnp.sin(angles)
    return jnp.concatenate([cos, cos], axis=1), jnp.concatenate([-sin, sin], axis=1)


def on_device(
    tokens, cotangent, segments, adapter_ids, norm_gains, q_weight, kv_weight, out_weight,
    gate_up_weight, down_weight, wide_adapters, kv_adapter, q_adapter, out_adapter,
    gate_up_adapter, down_adapter,
):
    rows, width = tokens.shape
    tensor_count = lax.axis_size("tensor")
    dp_count = lax.axis_size("y") * lax.axis_size("x") * 2
    devices = dp_count * tensor_count
    group_rows = rows * tensor_count
    seq_length = 2 * group_rows
    shard_rows = q_weight.shape[0]
    q_cols, ff_cols = q_weight.shape[1], gate_up_weight.shape[2]
    heads_cols = tensor_count * q_cols
    seqs = adapter_ids.shape[0]
    adapters = wide_adapters.shape[2] // RANK
    dp = lax.axis_index(DP)
    tensor = lax.axis_index("tensor")
    place = jnp.stack([lax.axis_index("core"), tensor]).astype(jnp.int32)
    adapter = lax.dynamic_index_in_dim(adapter_ids, dp // 2, keepdims=False)
    column = adapter * RANK
    f3 = 3 * ff_cols

    pack = jnp.concatenate(
        [gate_up_weight[0], gate_up_weight[1], down_weight.T, q_weight, out_weight.T], axis=1
    )
    pack, wide_adapters = lax.optimization_barrier((pack, wide_adapters))
    weights = lax.all_gather(pack, ALL, axis=0, tiled=False)
    weights = weights.reshape(dp_count, tensor_count, shard_rows, f3 + 2 * q_cols)

    wide = wide_adapters.reshape(7, shard_rows, adapters, RANK)
    wide = jnp.take(wide, adapter_ids, axis=2).transpose(2, 1, 0, 3)
    wide = wide.reshape(seqs, shard_rows, 7 * RANK)
    wide = jnp.pad(wide, ((0, 0), (0, 0), (0, LANES - 7 * RANK)))
    wide = jnp.repeat(wide, dp_count // seqs, axis=0)
    shared = jnp.broadcast_to(kv_weight[:, None], (2, dp_count, shard_rows, HD))
    wide = jnp.concatenate([wide, shared[0], shared[1]], axis=2)
    a_all = lax.all_to_all(wide, DP, 0, 0, tiled=True).reshape(width, 3 * LANES)

    def take_rows(matrix):
        return lax.dynamic_slice_in_dim(matrix, column, RANK, matrix.ndim - 2)

    def take_cols(matrix):
        return lax.dynamic_slice_in_dim(matrix, column, RANK, matrix.ndim - 1)

    def in_slot(block, slot):
        pads = [(0, 0)] * block.ndim
        pads[-2] = (slot * RANK, LANES - (slot + 1) * RANK)
        return jnp.pad(block, pads)

    gu_rows = take_rows(gate_up_adapter)
    b_own = jnp.concatenate(
        [gu_rows[0], gu_rows[1], take_cols(down_adapter).T, take_rows(q_adapter), take_cols(out_adapter).T], axis=1
    )
    b_all = lax.all_gather(b_own, "tensor", axis=0, tiled=False)
    edges = [0, ff_cols, 2 * ff_cols, f3, f3 + q_cols, f3 + 2 * q_cols]
    b_pad = jnp.concatenate(
        [
            in_slot(b_all[:, :, first:last], slot)
            for first, last, slot in zip(edges, edges[1:], (SLOT_G, SLOT_U, SLOT_D, SLOT_Q, SLOT_O))
        ],
        axis=2,
    )
    kv_rows = take_rows(kv_adapter)
    b_kv = jnp.stack([in_slot(kv_rows[0], SLOT_K), in_slot(kv_rows[1], SLOT_V)])

    start = dp * group_rows + tensor * rows
    span = WINDOW + rows
    cos_window, sin_window = rope_tables((start - WINDOW + jnp.arange(span)) % seq_length)
    cos, sin = cos_window[WINDOW:], sin_window[WINDOW:]
    padded = jnp.concatenate([jnp.full((WINDOW,), -1, jnp.int32), segments])
    kseg = lax.dynamic_slice_in_dim(padded, start, span, 0)
    qseg = kseg[WINDOW:].reshape(1, rows)
    kseg = kseg.reshape(span, 1)

    gain_one, gain_two = norm_gains[0:1], norm_gains[1:2]
    q_block = f3 // q_cols

    def weight_spec(block):
        return pl.BlockSpec((dp_count, 1, shard_rows, q_cols), lambda t: (0, t, 0, block))

    def adapter_spec(block):
        return pl.BlockSpec((1, LANES, q_cols), lambda t: (t, 0, block))

    def lane_block(block):
        return pl.BlockSpec((width, LANES), lambda *_: (0, block))

    head_specs = [weight_spec(q_block), adapter_spec(q_block), weight_spec(q_block + 1), adapter_spec(q_block + 1)]
    q_spec, qb_spec, o_spec, ob_spec = head_specs
    a_spec, wk_spec, wv_spec = lane_block(0), lane_block(1), lane_block(2)
    token_cols = pl.BlockSpec((rows, q_cols), lambda t: (0, t))
    tok_bf, tok_f32, rank_bf = sds((rows, width), BF), sds((rows, width), F32), sds((rows, LANES), BF)

    args = (tokens, gain_one, a_all, a_all, a_all, b_kv, cos, sin)
    normed_one, rank_one, kv_own = call(
        shared_kernel, "keys_values", 1, args,
        wholes(*args[:2]) + [a_spec, wk_spec, wv_spec] + wholes(*args[5:]),
        [(tok_bf, None), (rank_bf, None), (sds((rows, 2 * HD), BF), None)],
        [], 2 * rows * width * 384, 6 * rows * width,
    )
    parts = seq_length // rows
    reach = WINDOW // rows
    kv_seq = lax.all_to_all(jnp.broadcast_to(kv_own[None], (parts, rows, 2 * HD)), SEQ, 0, 0, tiled=True)

    def moved(value, steps):
        return lax.ppermute(value, SEQ, [(c, c + steps) for c in range(parts) if 0 <= c + steps < parts])

    args = (
        place, kv_seq, kseg, qseg, normed_one, rank_one, cos, sin, tokens, gain_two, a_all,
        weights, b_pad, weights, b_pad,
    )
    heads = q_cols // HD
    p_spec = pl.BlockSpec((heads, span, rows), lambda t: (t, 0, 0))
    queries, mixed, probs, norms, residual, normed_two, rank_two, rank_out = call(
        attn_kernel, "attention", tensor_count, args,
        [scalars()] + wholes(*args[1:10]) + [a_spec] + head_specs,
        [
            (sds((rows, heads_cols), BF), token_cols), (sds((rows, heads_cols), BF), token_cols),
            (sds((tensor_count * heads, span, rows), BF), p_spec), (sds((tensor_count, 8, rows), F32), by_step(8, rows)),
            (tok_f32, None), (tok_bf, None), (rank_bf, None), (rank_bf, None),
        ],
        [
            pltpu.VMEM((span, rows), F32), pltpu.VMEM((span, rows), F32), pltpu.VMEM((HD, span), BF),
            pltpu.VMEM((span, 2 * HD), BF), pltpu.VMEM((rows, width), F32), pltpu.VMEM((rows, LANES), F32),
        ],
        4 * rows * heads_cols * (span + width), 4 * width * heads_cols,
    )

    sent_one, normed_two = lax.optimization_barrier((normed_one, normed_two))
    window_one = [moved(sent_one, d) for d in range(reach, 0, -1)]

    args = (
        residual, normed_two, rank_two, cotangent, gain_two, mixed, rank_out, a_all, b_pad, weights,
    )
    block_output, grad_residual, grad_branch, wide_ffn, grad_ro, grad_bo, grad_bh = call(
        ffn_kernel, "feed_forward", tensor_count, args,
        wholes(*args[:7]) + [a_spec, by_step(LANES, f3), pl.BlockSpec(memory_space=pl.ANY)],
        [
            (tok_bf, None), (tok_f32, None), (tok_bf, None), (sds((LANES, width), F32), None), (rank_bf, None),
            (sds((tensor_count, RANK, q_cols), BF), None), (sds((tensor_count, RANK, f3), BF), by_step(RANK, f3)),
        ],
        [
            pltpu.VMEM((rows, width), F32), pltpu.VMEM((rows, width), F32),
            pltpu.VMEM((rows, LANES), F32), pltpu.VMEM((rows, LANES), F32),
            pltpu.VMEM((LANES, rows), BF), pltpu.VMEM((rows, LANES), BF), pltpu.VMEM((LANES, rows), BF),
            pltpu.VMEM((2, dp_count, shard_rows, f3), BF), pltpu.SemaphoreType.DMA((2, 2)),
        ],
        12 * rows * width * tensor_count * ff_cols, 6 * width * tensor_count * ff_cols,
    )
    early = jnp.concatenate([grad_bh, grad_bo], axis=2)
    early = lax.psum_scatter(early, "tensor", scatter_dimension=0, tiled=True).reshape(RANK, -1)

    args = (
        place, kv_seq, grad_branch, grad_ro, rank_one, cos, sin, cos_window, sin_window, a_all, b_kv, wide_ffn,
        *window_one, normed_one, queries, mixed, probs, norms, weights, b_pad, weights, b_pad,
    )
    dkv, grad_one, grad_rank, grad_bq, wide_term, kv_term = call(
        attn_back_kernel, "attention_back", tensor_count, args,
        [scalars()] + wholes(*args[1:9]) + [a_spec] + wholes(*args[10:17])
        + [token_cols, token_cols, p_spec, by_step(8, rows), o_spec, ob_spec, q_spec, qb_spec],
        [
            (sds((span, 2 * HD), BF), None), (tok_f32, None), (sds((rows, LANES), F32), None),
            (sds((tensor_count, RANK, q_cols), BF), by_step(RANK, q_cols)),
            (sds((width, LANES), BF), None), (sds((2, RANK, HD), BF), None),
        ],
        [
            pltpu.VMEM((span, rows), BF),
            pltpu.VMEM((span, HD), F32), pltpu.VMEM((span, HD), F32), pltpu.VMEM((HD, span), BF),
            pltpu.VMEM((LANES, rows), BF),
            pltpu.VMEM((rows, q_cols), BF), pltpu.VMEM((rows, q_cols), BF), pltpu.VMEM((span, 2 * HD), BF),
        ],
        2 * rows * heads_cols * (4 * span + 2 * width), 4 * width * heads_cols,
    )

    own_rows = width // devices
    kv_terms = jnp.tile(kv_term.transpose(1, 0, 2), (devices // RANK, 1, 1))
    owned = jnp.concatenate(
        [wide_term.reshape(devices, own_rows, LANES), kv_terms, jnp.zeros((devices, 2, LANES), BF)], axis=1
    )
    every = jnp.broadcast_to(grad_bq[None], (dp_count, tensor_count, RANK, q_cols)).reshape(devices, RANK, q_cols)
    terms = lax.all_to_all(jnp.concatenate([owned, every], axis=2), ALL, 0, 0, tiled=True)
    terms = terms.reshape(seqs, parts, RANK, LANES + q_cols)

    backs = [moved(dkv[(reach - d) * rows : (reach - d + 1) * rows], -d) for d in range(1, reach + 1)]
    args = (
        tokens, gain_one, a_all, a_all, a_all, b_kv, cos, sin, dkv, *backs, grad_rank, grad_one, grad_residual,
    )
    (input_grad,) = call(
        input_kernel, "input_gradient", 1, args,
        wholes(*args[:2]) + [a_spec, wk_spec, wv_spec] + wholes(*args[5:8])
        + [pl.BlockSpec((rows, 2 * HD), lambda *_: (reach, 0))] + wholes(*args[9:]),
        [(tok_f32, None)], [], 2 * rows * width * 384, 16 * rows * width,
    )

    early, grad_one = lax.optimization_barrier((early, grad_one))
    early = lax.all_gather(early, DP, axis=0, tiled=False)
    gate_up_adapter_grad, down_adapter_grad, out_adapter_grad = call(
        sum_hidden_kernel, "sum_hidden", 1, (adapter_ids, early),
        [scalars()] + wholes(early),
        [(sds((2, LANES, ff_cols), F32), None), (sds((ff_cols, LANES), F32), None), (sds((q_cols, LANES), F32), None)],
        [pltpu.VMEM((adapters, RANK, f3 + q_cols), F32)], 0, 4 * LANES * f3,
    )
    own_adapter = ((dp * tensor_count + tensor) // RANK).astype(jnp.int32).reshape(1)
    wide_grad, kv_adapter_grad, q_adapter_grad = call(
        sum_wide_kernel, "sum_wide", 1, (adapter_ids, own_adapter, terms),
        [scalars(), scalars()] + wholes(terms),
        [(sds((7, own_rows, LANES), F32), None), (sds((2, 1, HD), F32), None), (sds((LANES, q_cols), F32), None)],
        [pltpu.VMEM((adapters, RANK, LANES + q_cols), F32)], 0, 4 * LANES * f3,
    )
    return (
        block_output, input_grad, wide_grad, kv_adapter_grad,
        q_adapter_grad, out_adapter_grad, gate_up_adapter_grad, down_adapter_grad,
    )


def solution(mesh):
    dp_count, tensor_count = mesh.shape["dp"], mesh.shape["tensor"]
    chips = dp_count // 2
    x_count = math.isqrt(chips)
    devices = mesh.devices.reshape(chips // x_count, x_count, 2, tensor_count)
    return jax.shard_map(
        on_device,
        mesh=Mesh(devices, ALL),
        in_specs=(
            P(ALL, None), P(ALL, None), P(), P(), P(), P(DP, "tensor"), P(None, DP, None),
            P("tensor", DP), P(None, DP, "tensor"), P("tensor", DP), P(None, DP, None), P(),
            P(None, "tensor"), P("tensor", None), P(None, None, "tensor"), P("tensor", None),
        ),
        out_specs=(
            P(ALL, None), P(ALL, None), P(None, ALL, None), P(None, ALL, None),
            P(None, "tensor"), P("tensor", None), P(None, None, "tensor"), P("tensor", None),
        ),
        check_vma=False,
    )
```

time: 391 us -> 348 us (0.89)
  waiting for transfers between devices: 163 us -> 128 us
  blocking collectives: 35.5 us -> 13.2 us
  starting transfers between devices: 32.4 us -> 43.7 us
  Pallas kernels: 96.8 us -> 105 us
  local copies, waits for them, and re-layouts: 38.1 us -> 29.9 us
  other arithmetic: 7.23 us -> 11.8 us
    all_to_all x1 -> x0, blocking collectives: 21.5 us -> none  [on_device(): received = lax.all_to_all(payload, BOTH, 0, 0, tiled=True)]
    all_gather x2, waiting for transfers between devices: 111 us -> 91.5 us  [the longest x1 91.5 us: on_device(): weights = lax.all_gather(pack, ALL, axis=0, tiled=False)]
    reduce_scatter x1, waiting for transfers between devices: 19.2 us -> 0.02 us  [on_device(): lax.psum_scatter(early, 'tensor', scatter_dimension=0, tiled=True)]
    ppermute x8, waiting for transfers between devices: 10.3 us -> 21.7 us  [moved(): lax.ppermute(value, SEQ, [(c, c + steps) for c in range(parts) if 0 <= c...]
    all_to_all x2 -> x3, starting transfers between devices: 13 us -> 23.6 us  [the longest x1 8.95 us: on_device(): lax.all_to_all(jnp.concatenate([owned, every], axis=2), ALL, 0, 0, tiled=...]
    pallas_call x5 -> x7, Pallas kernels: 96.8 us -> 105 us  [call(): pl.pallas_call(kernel, name=name, grid=(steps,), in_specs=specs, out_spec...]
    all_to_all x2 -> x3, waiting for transfers between devices: 22.3 us -> 15.1 us  [the longest x1 15.1 us: on_device(): lax.all_to_all(jnp.broadcast_to(kv_own[None], (parts, rows, 2 * HD)), SEQ...]
    reshape x7 -> x1, local copies, waits for them, and re-layouts: 5.59 us -> 1.07 us  [on_device(): kseg = kseg.reshape(span, 1)]
  transfers between devices with their start and end apart: 13 -> 14, of which waited for: 7 -> 5; matrix products, arithmetic and copies ran while one was open for 7% -> 9% of each run, Pallas kernels for 8% -> 23%
where the time goes in v4:
time: 348 us; the launch traced here: 346 us
  waiting for transfers between devices  128 us (37%)
  Pallas kernels  105 us (30%)
  starting transfers between devices  43.7 us (13%)
  local copies, waits for them, and re-layouts  29.9 us (9%)
  between operations  14.8 us (4%)
  blocking collectives  13.2 us (4%)
  other arithmetic  11.8 us (3%)
    pallas_call x7, Pallas kernels, call(): pl.pallas_call(kernel, name=name, grid=(steps,), in_specs=specs, out_spec...  105 us
    all_gather x1, waiting for transfers between devices, on_device(): weights = lax.all_gather(pack, ALL, axis=0, tiled=False)  91.5 us
    ppermute x8, waiting for transfers between devices, moved(): lax.ppermute(value, SEQ, [(c, c + steps) for c in range(parts) if 0 <= c...  21.7 us
    ppermute x8, starting transfers between devices, moved(): lax.ppermute(value, SEQ, [(c, c + steps) for c in range(parts) if 0 <= c...  19.8 us
    unnamed x52, local copies, waits for them, and re-layouts  16.8 us
    all_to_all x1, waiting for transfers between devices, on_device(): lax.all_to_all(jnp.broadcast_to(kv_own[None], (parts, rows, 2 * HD)), SEQ...  15.1 us
    all_gather x1, blocking collectives, on_device(): b_all = lax.all_gather(b_own, 'tensor', axis=0, tiled=False)  13.2 us
    all_to_all x1, starting transfers between devices, on_device(): lax.all_to_all(jnp.concatenate([owned, every], axis=2), ALL, 0, 0, tiled=...  8.95 us
  transfers between devices with their start and end apart: 14, of which 5 were waited for; matrix products, arithmetic and copies ran while one was open for 9% of the time, Pallas kernels for 23%

profile of v4, /device:TPU:1, one launch (start us, length us, event | category | flops | bytes accessed | tf_op | source)
XLA Modules:
  0.0 346.3 jit_solution(6364782191549460189)
XLA Ops:
  16.5 8.7 %all-to-all-start = ((bf16[32,48,384]{2,1,0:T(8,128)(2,1)}), bf16[32,48,384]{2,1,0:T(8,128)(2,1)S(1)}, u32[]{:S(2)}, u32[]{:S(2)}) async-start(bf16[32,48,384]{2,1,0:T(8,128)(2,1)} %pad_maximum_fusion.1), calls=%async_computation | async-start | bytes 2359296 | tf_op jit(solution)/shard_map/all_to_all | solution.py:437
  30.8 2.4 multiply_sine_fusion
  34.0 13.2 %all-gather.1 = bf16[64,4224]{1,0:T(8,128)(2,1)S(1)} all-gather(bf16[16,4224]{1,0:T(8,128)(2,1)S(1)} %constant_dynamic-update-slice_fusion.1), channel_id=3, replica_groups=mesh['y'=4,'x'=4,'core'=2,'tensor'=4] {'tensor'}, dimensions={0}, use_global_device_ids=true | all-gather | bytes 675840 | tf_op jit(solution)/shard_map/all_gather | solution.py:454
  50.1 3.3 keys_values.1
  53.4 2.0 broadcast_in_dim.53
  55.4 5.9 %all-to-all-start.1 = ((bf16[8,256,256]{2,1,0:T(8,128)(2,1)}), bf16[8,256,256]{2,1,0:T(8,128)(2,1)S(1)}, u32[]{:S(2)}, u32[]{:S(2)}) async-start(bf16[8,256,256]{2,1,0:T(8,128)(2,1)} %broadcast_in_dim.53), calls=%async_computation.1 | async-start | bytes 2097152 | tf_op jit(solution)/shard_map/all_to_all | solution.py:502
  67.6 15.1 %all-to-all-done.1.seq_ref = bf16[8,256,256]{2,1,0:T(8,128)(2,1)S(1)} async-done(((bf16[8,256,256]{2,1,0:T(8,128)(2,1)}), bf16[8,256,256]{2,1,0:T(8,128)(2,1)S(1)}, u32[]{:S(2)}, u32[]{:S(2)}) %all-to-all-start.1) | async-done | bytes 1048608 | tf_op jit(solution)/shard_map/all_to_all | solution.py:502
  82.7 91.5 %all-gather.6.cloned.1.call-done = bf16[6144,4224]{1,0:T(8,128)(2,1)} async-done(((bf16[48,4224]{1,0:T(8,128)(2,1)}), bf16[6144,4224]{1,0:T(8,128)(2,1)}) %all-gather.6.cloned.1.call-update) | async-done | bytes 51904528 | tf_op jit(solution)/shard_map/all_gather | solution.py:427
  174.2 20.8 %attention.1 = (bf16[256,1536]{1,0:T(8,128)(2,1)}, bf16[256,1536]{1,0:T(8,128)(2,1)}, bf16[12,1280,256]{2,1,0:T(8,128)(2,1)}, f32[4,8,256]{2,1,0:T(8,128)}, f32[...) custom-call(s32[2]{0:T(128)} %pad_add_fusion.place_ref, ...), custom_call_target="tpu_custom_call" | custom-call | flops 4429185024 | bytes 9437184 | tf_op jit(solution)/shard_map/attention/pallas_call | solution.py:377
  196.3 3.6 %collective-permute-start.1 = (bf16[256,1536]{1,0:T(8,128)(2,1)}, bf16[256,1536]{1,0:T(8,128)(2,1)}, u32[]{:S(2)}, u32[]{:S(2)}) collective-permute-start(bf16[256,1536]{1,0:T(8,128)(2,1)} %get-tuple-element.58.n1_ref.n1e_ref), channel_id=1, source_target_pairs={{0,3},{1,4},{2,5},{3,6},{4,7},{8,11},{9,12},{10,13},{11,14},{12,15... | collective-permute-start | bytes 2359304 | tf_op jit(solution)/shard_map/ppermute | solution.py:505
  199.9 1.9 collective-permute-start.2
  201.8 2.1 collective-permute-start.3
  203.9 39.7 %feed_forward.1 = (bf16[256,1536]{1,0:T(8,128)(2,1)}, f32[256,1536]{1,0:T(8,128)}, bf16[256,1536]{1,0:T(8,128)(2,1)}, f32[128,1536]{1,0:T(8,128)}, bf16[256,128]...) custom-call(f32[256,1536]{1,0:T(8,128)} %get-tuple-element.48.res_ref, ...), custom_call_target="tpu_custom_call" | custom-call | flops 21743271936 | bytes 42467328 | tf_op jit(solution)/shard_map/feed_forward/pallas_call | solution.py:377
  248.2 28.1 %attention_back.1 = (bf16[1280,256]{1,0:T(8,128)(2,1)}, f32[256,1536]{1,0:T(8,128)}, f32[256,128]{1,0:T(8,128)}, bf16[4,16,384]{2,1,0:T(8,128)(2,1)}, bf16[1536,...) custom-call(s32[2]{0:T(128)} %pad_add_fusion.place_ref, bf16[8,256,256]{2,1,0:T(8,128)(2,1)} %copy-done.3, ...), custom_call_target="tpu_custom_call" | custom-call | flops 6442450944 | bytes 9437184 | tf_op jit(solution)/shard_map/attention_back/pallas_call | solution.py:377
  279.3 2.1 pad_maximum_fusion
  281.3 8.9 %all-to-all-start.2 = ((bf16[128,16,512]{2,1,0:T(8,128)(2,1)}), bf16[128,16,512]{2,1,0:T(8,128)(2,1)S(1)}, u32[]{:S(2)}, u32[]{:S(2)}) async-start(bf16[128,16,512]{2,1,0:T(8,128)(2,1)} %pad_maximum_fusion), calls=%async_computation.2 | async-start | bytes 4194304 | tf_op jit(solution)/shard_map/all_to_all | solution.py:580
  291.0 5.4 %collective-permute-start.4 = (bf16[256,256]{1,0:T(8,128)(2,1)}, bf16[256,256]{1,0:T(8,128)(2,1)S(1)}, u32[]{:S(2)}, u32[]{:S(2)}) collective-permute-start(bf16[256,256]{1,0:T(8,128)(2,1)} %get-tuple-element.105), channel_id=1, source_target_pairs={{1,0},{2,1},{3,2},{4,3},{5,4},{6,5},{7,6},{9,8},{10,9},{11,10},{12... | collective-permute-start | bytes 393224 | tf_op jit(solution)/shard_map/ppermute | solution.py:505
  296.4 2.2 collective-permute-start.5
  301.9 9.9 %collective-permute-done.4.back1_ref = bf16[256,256]{1,0:T(8,128)(2,1)S(1)} collective-permute-done((bf16[256,256]{1,0:T(8,128)(2,1)}, bf16[256,256]{1,0:T(8,128)(2,1)S(1)}, u32[]{:S(2)}, u32[]{:S(2)}) %collective-permute-start.4) | collective-permute-done | bytes 131104 | tf_op jit(solution)/shard_map/ppermute | solution.py:505
  311.8 8.8 %collective-permute-done.5.back2_ref = bf16[256,256]{1,0:T(8,128)(2,1)S(1)} collective-permute-done((bf16[256,256]{1,0:T(8,128)(2,1)S(1)}, bf16[256,256]{1,0:T(8,128)(2,1)S(1)}, u32[]{:S(2)}, u32[]{:S(2)}) %collective-permute-start.5) | collective-permute-done | bytes 131104 | tf_op jit(solution)/shard_map/ppermute | solution.py:505
  320.6 3.0 collective-permute-done.6.back3_ref
  324.3 5.4 %input_gradient.1 = f32[256,1536]{1,0:T(8,128)} custom-call(bf16[256,1536]{1,0:T(8,128)(2,1)} %x_ref.5, f32[1,1536]{1,0:T(1,128)} %get-tuple-element.116.gain_ref, bf16[1536,384]{1,0:T(8,128)(2,1)} %bitcast.62, bf16[1536,384]{1,0:T(8,128)(2,1)} %bitcast.63, bf16[1536,384]{1,0:T(8,128)(2,1)} %bitcast.64, bf16[2,128,128]{2,1,0:T(8,128)(2,1)} %pad_maximum_fusion.5.bkv_ref, ...), custom_call_target="tpu_custom_call" | custom-call | flops 301989888 | bytes 6291456 | tf_op jit(solution)/shard_map/input_gradient/pallas_call | solution.py:377
  331.1 2.7 sum_wide.1
  335.3 4.5 %sum_hidden.1 = (f32[2,128,1152]{2,1,0:T(8,128)}, f32[1152,128]{1,0:T(8,128)}, f32[384,128]{1,0:T(8,128)}) custom-call(s32[16]{0:T(128)} %ids_ref.3, bf16[32,16,3840]{2,1,0:T(8,128)(2,1)} %bitcast.68), custom_call_target="tpu_custom_call" | custom-call | bytes 1769472 | tf_op jit(solution)/shard_map/sum_hidden/pallas_call | solution.py:377
  (110 shorter events, 40.2 us)
Async XLA Ops:
  7.2 19.4 %copy-start = (bf16[1152,128]{1,0:T(8,128)(2,1)S(1)}, bf16[1152,128]{1,0:T(8,128)(2,1)}, u32[]{:S(2)}) copy-start(bf16[1152,128]{1,0:T(8,128)(2,1)} %param.31) | copy-start | bytes 884740
  7.2 7.6 %copy-start.17 = (s32[16]{0:T(128)S(1)}, s32[16]{0:T(128)}, u32[]{:S(2)}) copy-start(s32[16]{0:T(128)} %ids_ref.3) | copy-start | bytes 196
  7.2 167.0 %all-gather.6.cloned.1.call-start = ((), (), s32[]{:S(2)}) async-start(), calls=%async_computation.5 | async-start | bytes 52310016 | tf_op jit(solution)/shard_map/all_gather | solution.py:427
  15.3 11.5 %copy-start.14 = (bf16[384,128]{1,0:T(8,128)(2,1)S(1)}, bf16[384,128]{1,0:T(8,128)(2,1)}, u32[]{:S(2)}) copy-start(bf16[384,128]{1,0:T(8,128)(2,1)} %param.29) | copy-start | bytes 294916
  16.5 11.3 %copy-start.8 = (s32[32768]{0:T(1024)S(1)}, s32[32768]{0:T(1024)}, u32[]{:S(2)}) copy-start(s32[32768]{0:T(1024)} %param.18) | copy-start | bytes 393220
  16.5 32.5 %all-to-all-start = ((bf16[32,48,384]{2,1,0:T(8,128)(2,1)}), bf16[32,48,384]{2,1,0:T(8,128)(2,1)S(1)}, u32[]{:S(2)}, u32[]{:S(2)}) async-start(bf16[32,48,384]{2,1,0:T(8,128)(2,1)} %pad_maximum_fusion.1), calls=%async_computation | async-start | bytes 2359296 | tf_op jit(solution)/shard_map/all_to_all | solution.py:437
  33.1 15.3 %copy-start.16 = (f32[2,1536]{1,0:T(2,128)S(1)}, f32[2,1536]{1,0:T(2,128)}, u32[]{:S(2)}) copy-start(f32[2,1536]{1,0:T(2,128)} %param.20) | copy-start | bytes 36868
  53.4 9.6 %copy-start.9 = (s32[32768]{0:T(1024)S(1)}, s32[32768]{0:T(1024)}, u32[]{:S(2)}) copy-start(s32[32768]{0:T(1024)} %param.18) | copy-start | bytes 393220
  55.4 27.3 %all-to-all-start.1 = ((bf16[8,256,256]{2,1,0:T(8,128)(2,1)}), bf16[8,256,256]{2,1,0:T(8,128)(2,1)S(1)}, u32[]{:S(2)}, u32[]{:S(2)}) async-start(bf16[8,256,256]{2,1,0:T(8,128)(2,1)} %broadcast_in_dim.53), calls=%async_computation.1 | async-start | bytes 2097152 | tf_op jit(solution)/shard_map/all_to_all | solution.py:502
  61.3 215.0 %reduce-scatter.2.cloned.1.call-start = ((), (), s32[]{:S(2)}) async-start(), calls=%async_computation.4 | async-start | bytes 614400 | tf_op jit(solution)/shard_map/reduce_scatter | solution.py:550
  82.7 91.5 %copy-start.3 = (bf16[8,256,256]{2,1,0:T(8,128)(2,1)}, bf16[8,256,256]{2,1,0:T(8,128)(2,1)S(1)}, u32[]{:S(2)}) copy-start(bf16[8,256,256]{2,1,0:T(8,128)(2,1)S(1)} %all-to-all-done.1.seq_ref) | copy-start | bytes 3145732
  195.0 52.3 %collective-permute-start = (bf16[256,1536]{1,0:T(8,128)(2,1)}, bf16[256,1536]{1,0:T(8,128)(2,1)S(1)}, u32[]{:S(2)}, u32[]{:S(2)}) collective-permute-start(bf16[256,1536]{1,0:T(8,128)(2,1)} %get-tuple-element.58.n1_ref.n1e_ref), channel_id=1, source_target_pairs={{0,4},{1,5},{2,6},{3,7},{8,12},{9,13},{10,14},{11,15},{16,20},{17,... | collective-permute-start | bytes 2359304 | tf_op jit(solution)/shard_map/ppermute | solution.py:505
  196.3 51.0 %collective-permute-start.1 = (bf16[256,1536]{1,0:T(8,128)(2,1)}, bf16[256,1536]{1,0:T(8,128)(2,1)}, u32[]{:S(2)}, u32[]{:S(2)}) collective-permute-start(bf16[256,1536]{1,0:T(8,128)(2,1)} %get-tuple-element.58.n1_ref.n1e_ref), channel_id=1, source_target_pairs={{0,3},{1,4},{2,5},{3,6},{4,7},{8,11},{9,12},{10,13},{11,14},{12,15... | collective-permute-start | bytes 2359304 | tf_op jit(solution)/shard_map/ppermute | solution.py:505
  199.9 47.4 %collective-permute-start.2 = (bf16[256,1536]{1,0:T(8,128)(2,1)}, bf16[256,1536]{1,0:T(8,128)(2,1)}, u32[]{:S(2)}, u32[]{:S(2)}) collective-permute-start(bf16[256,1536]{1,0:T(8,128)(2,1)} %get-tuple-element.58.n1_ref.n1e_ref), channel_id=1, source_target_pairs={{0,2},{1,3},{2,4},{3,5},{4,6},{5,7},{8,10},{9,11},{10,12},{11,13},... | collective-permute-start | bytes 2359304 | tf_op jit(solution)/shard_map/ppermute | solution.py:505
  201.8 45.5 %collective-permute-start.3 = (bf16[256,1536]{1,0:T(8,128)(2,1)}, bf16[256,1536]{1,0:T(8,128)(2,1)}, u32[]{:S(2)}, u32[]{:S(2)}) collective-permute-start(bf16[256,1536]{1,0:T(8,128)(2,1)} %get-tuple-element.58.n1_ref.n1e_ref), channel_id=1, source_target_pairs={{0,1},{1,2},{2,3},{3,4},{4,5},{5,6},{6,7},{8,9},{9,10},{10,11},{11... | collective-permute-start | bytes 2359304 | tf_op jit(solution)/shard_map/ppermute | solution.py:505
  245.6 89.7 %all-gather.8.cloned.1.call-start = ((), (), s32[]{:S(2)}) async-start(), calls=%async_computation.6 | async-start | bytes 4055040 | tf_op jit(solution)/shard_map/all_gather | solution.py:595
  281.3 9.0 %copy-start.5 = (bf16[1280,256]{1,0:T(8,128)(2,1)S(1)}, bf16[1280,256]{1,0:T(8,128)(2,1)}, u32[]{:S(2)}) copy-start(bf16[1280,256]{1,0:T(8,128)(2,1)} %get-tuple-element.62.own_ref) | copy-start | bytes 1966084
  281.3 48.4 %all-to-all-start.2 = ((bf16[128,16,512]{2,1,0:T(8,128)(2,1)}), bf16[128,16,512]{2,1,0:T(8,128)(2,1)S(1)}, u32[]{:S(2)}, u32[]{:S(2)}) async-start(bf16[128,16,512]{2,1,0:T(8,128)(2,1)} %pad_maximum_fusion), calls=%async_computation.2 | async-start | bytes 4194304 | tf_op jit(solution)/shard_map/all_to_all | solution.py:580
  291.0 20.8 %collective-permute-start.4 = (bf16[256,256]{1,0:T(8,128)(2,1)}, bf16[256,256]{1,0:T(8,128)(2,1)S(1)}, u32[]{:S(2)}, u32[]{:S(2)}) collective-permute-start(bf16[256,256]{1,0:T(8,128)(2,1)} %get-tuple-element.105), channel_id=1, source_target_pairs={{1,0},{2,1},{3,2},{4,3},{5,4},{6,5},{7,6},{9,8},{10,9},{11,10},{12... | collective-permute-start | bytes 393224 | tf_op jit(solution)/shard_map/ppermute | solution.py:505
  296.4 24.2 %collective-permute-start.5 = (bf16[256,256]{1,0:T(8,128)(2,1)S(1)}, bf16[256,256]{1,0:T(8,128)(2,1)S(1)}, u32[]{:S(2)}, u32[]{:S(2)}) collective-permute-start(bf16[256,256]{1,0:T(8,128)(2,1)S(1)} %get-tuple-element.104), channel_id=1, source_target_pairs={{2,0},{3,1},{4,2},{5,3},{6,4},{7,5},{10,8},{11,9},{12,10},{13,11},... | collective-permute-start | bytes 393224 | tf_op jit(solution)/shard_map/ppermute | solution.py:505
  298.6 25.0 %collective-permute-start.6 = (bf16[256,256]{1,0:T(8,128)(2,1)S(1)}, bf16[256,256]{1,0:T(8,128)(2,1)S(1)}, u32[]{:S(2)}, u32[]{:S(2)}) collective-permute-start(bf16[256,256]{1,0:T(8,128)(2,1)S(1)} %get-tuple-element.103), channel_id=1, source_target_pairs={{3,0},{4,1},{5,2},{6,3},{7,4},{11,8},{12,9},{13,10},{14,11},{15,12... | collective-permute-start | bytes 393224 | tf_op jit(solution)/shard_map/ppermute | solution.py:505
  300.6 23.0 %collective-permute-start.7 = (bf16[256,256]{1,0:T(8,128)(2,1)S(1)}, bf16[256,256]{1,0:T(8,128)(2,1)S(1)}, u32[]{:S(2)}, u32[]{:S(2)}) collective-permute-start(bf16[256,256]{1,0:T(8,128)(2,1)S(1)} %get-tuple-element.102), channel_id=1, source_target_pairs={{4,0},{5,1},{6,2},{7,3},{12,8},{13,9},{14,10},{15,11},{20,16},{21,... | collective-permute-start | bytes 393224 | tf_op jit(solution)/shard_map/ppermute | solution.py:505
  311.8 11.9 %copy-start.10 = (bf16[256,256]{1,0:T(8,128)(2,1)}, bf16[256,256]{1,0:T(8,128)(2,1)S(1)}, u32[]{:S(2)}) copy-start(bf16[256,256]{1,0:T(8,128)(2,1)S(1)} %collective-permute-done.4.back1_ref) | copy-start | bytes 393220
  331.1 8.7 %copy-start.1 = (bf16[1152,128]{1,0:T(8,128)(2,1)S(1)}, bf16[1152,128]{1,0:T(8,128)(2,1)}, u32[]{:S(2)}) copy-start(bf16[1152,128]{1,0:T(8,128)(2,1)} %param.31) | copy-start | bytes 884740
  (8 other events, 9.5 us)
Sparse Core Ops, SparseCore 0:
  12.5 161.6 all-gather.5
  245.7 20.4 reduce-scatter.1
  276.5 55.2 all-gather.7

commit v5 on v4

--- a/solution.py
+++ b/solution.py
@@ -1,3 +1,4 @@
+import functools
 import math
 
 import jax
@@ -22,6 +23,7 @@
 F32 = jnp.float32
 DP = ("y", "x", "core")
 SEQ = ("core", "tensor")
+PLANES = ("y", "x", "tensor")
 ALL = ("y", "x", "core", "tensor")
 
 SLOT_Q, SLOT_K, SLOT_V, SLOT_G, SLOT_U, SLOT_O, SLOT_D = range(7)
@@ -77,19 +79,11 @@
     kv_ref[:, HD:] = (mm(n1, wv_ref[...]) + mm(r1, bkv_ref[1])).astype(BF)
 
 
-def fill_window(kv_ref, place_ref, seq_ref):
-    rows = seq_ref.shape[1]
-    reach = kv_ref.shape[0] // rows - 1
-    own = place_ref[0] * (seq_ref.shape[0] // 2) + place_ref[1]
-    for w in range(reach + 1):
-        kv_ref[w * rows : (w + 1) * rows] = seq_ref[jnp.maximum(own - reach + w, 0)]
-
-
 def attn_kernel(
-    place_ref, seq_ref, kseg_ref, qseg_ref, n1_ref, r1_ref, cos_ref, sin_ref, x_ref, gain_ref, a_ref,
+    kv_ref, kseg_ref, qseg_ref, n1_ref, r1_ref, cos_ref, sin_ref, x_ref, gain_ref, a_ref,
     wq_ref, bq_ref, wo_ref, bo_ref,
     q_ref, mixed_ref, p_ref, inv_ref, res_ref, n2_ref, r2_ref, ro_ref,
-    bias_ref, s_ref, vt_ref, kv_ref, acc_ref, rank_ref,
+    bias_ref, s_ref, vt_ref, acc_ref, rank_ref, qs_ref,
 ):
     step = pl.program_id(0)
     rows = q_ref.shape[0]
@@ -97,7 +91,6 @@
 
     @pl.when(step == 0)
     def _():
-        fill_window(kv_ref, place_ref, seq_ref)
         key = lax.broadcasted_iota(jnp.int32, bias_ref.shape, 0)
         query = lax.broadcasted_iota(jnp.int32, bias_ref.shape, 1)
         allowed = (key >= query) & (key <= query + WINDOW) & (kseg_ref[...] == qseg_ref[...])
@@ -107,25 +100,32 @@
         rank_ref[...] = jnp.zeros_like(rank_ref)
 
     lin = mm(n1_ref[...], flat(wq_ref)) + mm(r1_ref[...], bq_ref[0])
-    for h in range(q_ref.shape[1] // HD):
+    heads = q_ref.shape[1] // HD
+    for h in range(heads):
         part = slice(h * HD, (h + 1) * HD)
         query = (rope(lin[:, part], cos_ref[...], sin_ref[...]) * (SCALE * LOG2E)).astype(BF)
         q_ref[:, part] = query
-        top = jnp.full((1, rows), MASKED, F32)
-        for c in range(chunks):
-            span = slice(c * rows, (c + 1) * rows)
-            s = mm_nt(kv_ref[span, :HD], query) + bias_ref[span]
-            s_ref[span] = s
-            top = jnp.maximum(top, jnp.max(s, axis=0, keepdims=True))
-        total = jnp.zeros((1, rows), F32)
-        for c in range(chunks):
-            span = slice(c * rows, (c + 1) * rows)
-            p = jnp.exp2(s_ref[span] - top)
-            total = total + jnp.sum(p, axis=0, keepdims=True)
-            p_ref[h, span] = p.astype(BF)
-        inv = 1.0 / total
-        inv_ref[0, h : h + 1] = inv
-        mixed_ref[:, part] = (mm(vt_ref[...], p_ref[h]) * inv).T.astype(BF)
+        qs_ref[h * rows : (h + 1) * rows] = query
+    queries = qs_ref[...]
+    top = jnp.full((1, heads * rows), MASKED, F32)
+    for c in range(chunks):
+        span = slice(c * rows, (c + 1) * rows)
+        s = mm_nt(kv_ref[span, :HD], queries)
+        bias = bias_ref[span]
+        s = jnp.concatenate([s[:, h * rows : (h + 1) * rows] + bias for h in range(heads)], axis=1)
+        s_ref[span] = s
+        top = jnp.maximum(top, jnp.max(s, axis=0, keepdims=True))
+    total = jnp.zeros((1, heads * rows), F32)
+    for c in range(chunks):
+        span = slice(c * rows, (c + 1) * rows)
+        p = jnp.exp2(s_ref[span] - top)
+        total = total + jnp.sum(p, axis=0, keepdims=True)
+        p_ref[0, span] = p.astype(BF)
+    inv = 1.0 / total
+    inv_ref[0, 0:1] = inv
+    out = mm(vt_ref[...], p_ref[0]) * inv
+    for h in range(heads):
+        mixed_ref[:, h * HD : (h + 1) * HD] = out[:, h * rows : (h + 1) * rows].T.astype(BF)
 
     mixed = mixed_ref[...]
     acc_ref[...] += mm_nt(mixed, flat(wo_ref))
@@ -148,16 +148,26 @@
     ffn_ref, g2_ref, rd_ref, gr_ref, r2t_ref, grd_ref, grdt_ref, wv_ref, sems,
 ):
     step = pl.program_id(0)
-    last = pl.num_programs(0) - 1
+    steps = pl.num_programs(0)
+    tensor_count = w_ref.shape[1]
     ff = b_ref.shape[2] // 3
+    part = ff // tensor_count
     slot = lax.rem(step, 2)
 
     def copies(at, to):
-        spans = (pl.ds(2 * ff, ff), pl.ds(0, 2 * ff))
-        return [
-            pltpu.make_async_copy(w_ref.at[:, at, :, cols], wv_ref.at[to, :, :, cols], sems.at[to, j])
-            for j, cols in enumerate(spans)
-        ]
+        moves = []
+        for kind in (2, 0, 1):
+            for t in range(tensor_count):
+                source = pl.multiple_of((kind * steps + at) * part, LANES)
+                target = (kind * tensor_count + t) * part
+                moves.append(
+                    pltpu.make_async_copy(
+                        w_ref.at[:, t, :, pl.ds(source, part)],
+                        wv_ref.at[to, :, :, pl.ds(target, part)],
+                        sems.at[to, len(moves)],
+                    )
+                )
+        return moves
 
     @pl.when(step == 0)
     def _():
@@ -172,19 +182,21 @@
         grd_ref[...] = grd
         grdt_ref[...] = turned(grd)
 
-    @pl.when(step < last)
+    @pl.when(step < steps - 1)
     def _():
         for copy in copies(step + 1, 1 - slot):
             copy.start()
 
     n2, r2, cot = n2_ref[...], r2_ref[...], cot_ref[...]
     b_gu, b_d = b_ref[0, :, : 2 * ff], b_ref[0, :, 2 * ff :]
-    down, gate_up = copies(step, slot)
+    arrivals = copies(step, slot)
     rows_of_weight = wv_ref.shape[1] * wv_ref.shape[2]
-    down.wait()
+    for copy in arrivals[:tensor_count]:
+        copy.wait()
     w_d = wv_ref[slot, :, :, 2 * ff :].reshape(rows_of_weight, ff)
     grad_hidden = (mm(cot, w_d) + mm(grd_ref[...], b_d)).astype(BF).astype(F32)
-    gate_up.wait()
+    for copy in arrivals[tensor_count:]:
+        copy.wait()
     w_gu = wv_ref[slot, :, :, : 2 * ff].reshape(rows_of_weight, 2 * ff)
     lin = mm(n2, w_gu) + mm(r2, b_gu)
     gate, up = lin[:, :ff], lin[:, ff:]
@@ -201,11 +213,16 @@
     rd_ref[...] += mm_nt(hidden, b_d)
     g2_ref[...] += mm_nt(grads, w_gu)
     gr_ref[...] += mm_nt(grads, b_gu)
-    gbh_ref[0, :, :ff] = mm(r2t_ref[rows_of(SLOT_G)], grad_gate).astype(BF)
-    gbh_ref[0, :, ff : 2 * ff] = mm(r2t_ref[rows_of(SLOT_U)], grad_up).astype(BF)
-    gbh_ref[0, :, 2 * ff :] = mm(grdt_ref[rows_of(SLOT_D)], hidden).astype(BF)
-
-    @pl.when(step == last)
+    terms = (
+        mm(r2t_ref[rows_of(SLOT_G)], grad_gate), mm(r2t_ref[rows_of(SLOT_U)], grad_up),
+        mm(grdt_ref[rows_of(SLOT_D)], hidden),
+    )
+    for kind, term in enumerate(terms):
+        target = pl.multiple_of((kind * steps + step) * part, LANES)
+        for t in range(tensor_count):
+            gbh_ref[t, :, pl.ds(target, part)] = term[:, t * part : (t + 1) * part].astype(BF)
+
+    @pl.when(step == steps - 1)
     def _():
         rd = rd_ref[...].astype(BF)
         gr = gr_ref[...].astype(BF)
@@ -227,11 +244,10 @@
 
 
 def attn_back_kernel(
-    place_ref, seq_ref, gb_ref, gro_ref, r1_ref, cos_ref, sin_ref, cosw_ref, sinw_ref, a_ref, bkv_ref, widef_ref,
-    n1a_ref, n1b_ref, n1c_ref, n1d_ref, n1e_ref,
+    kv_ref, gb_ref, gro_ref, r1_ref, cos_ref, sin_ref,
     q_ref, mixed_ref, p_ref, inv_ref, wo_ref, bo_ref, wq_ref, bq_ref,
-    dkv_ref, g1_ref, gr_ref, gbq_ref, wide_ref, kvg_ref,
-    ds_ref, dk_ref, dv_ref, kt_ref, r1t_ref, gq_ref, gm_ref, kv_ref,
+    dkv_ref, g1_ref, gr_ref, gbq_ref,
+    ds_ref, dk_ref, dv_ref, kt_ref, r1t_ref, gq_ref, gm_ref, qs_ref, gs_ref,
 ):
     step = pl.program_id(0)
     rows = q_ref.shape[0]
@@ -239,7 +255,6 @@
 
     @pl.when(step == 0)
     def _():
-        fill_window(kv_ref, place_ref, seq_ref)
         kt_ref[...] = turned(kv_ref[:, :HD])
         r1t_ref[...] = turned(r1_ref[...])
         dk_ref[...] = jnp.zeros_like(dk_ref)
@@ -248,22 +263,29 @@
         gr_ref[...] = jnp.zeros_like(gr_ref)
 
     gm_ref[...] = (mm(gb_ref[...], flat(wo_ref)) + mm(gro_ref[...], bo_ref[0])).astype(BF)
-    for h in range(q_ref.shape[1] // HD):
-        part = slice(h * HD, (h + 1) * HD)
-        query, grad = q_ref[:, part], gm_ref[:, part]
+    heads = q_ref.shape[1] // HD
+    deltas = []
+    for h in range(heads):
+        part, span = slice(h * HD, (h + 1) * HD), slice(h * rows, (h + 1) * rows)
+        grad = gm_ref[:, part]
+        qs_ref[span] = q_ref[:, part]
+        gs_ref[span] = grad
         delta = grad.astype(F32) * mixed_ref[:, part].astype(F32)
-        delta = jnp.sum(delta.T, axis=0, keepdims=True)
-        inv = inv_ref[0, h : h + 1]
-        for c in range(chunks):
-            span = slice(c * rows, (c + 1) * rows)
-            p = p_ref[h, span].astype(F32) * inv
-            dp = mm_nt(kv_ref[span, HD:], grad)
-            ds = (p * (dp - delta)).astype(BF)
-            ds_ref[span] = ds
-            dk_ref[span] += mm(ds, query)
-            dv_ref[span] += mm(p.astype(BF), grad)
-        dq = mm(kt_ref[...], ds_ref[...]) * SCALE
-        gq_ref[:, part] = rope_back(dq.T, cos_ref[...], sin_ref[...]).astype(BF)
+        deltas.append(jnp.sum(delta.T, axis=0, keepdims=True))
+    delta, inv = jnp.concatenate(deltas, axis=1), inv_ref[0, 0:1]
+    queries, grads = qs_ref[...], gs_ref[...]
+    for c in range(chunks):
+        span = slice(c * rows, (c + 1) * rows)
+        p = p_ref[0, span].astype(F32) * inv
+        dp = mm_nt(kv_ref[span, HD:], grads)
+        ds = (p * (dp - delta)).astype(BF)
+        ds_ref[span] = ds
+        dk_ref[span] += mm(ds, queries)
+        dv_ref[span] += mm(p.astype(BF), grads)
+    dq = mm(kt_ref[...], ds_ref[...]) * SCALE
+    for h in range(heads):
+        part, span = slice(h * HD, (h + 1) * HD), slice(h * rows, (h + 1) * rows)
+        gq_ref[:, part] = rope_back(dq[:, span].T, cos_ref[...], sin_ref[...]).astype(BF)
 
     gq = gq_ref[...]
     gbq_ref[0] = mm(r1t_ref[rows_of(SLOT_Q)], gq).astype(BF)
@@ -272,42 +294,43 @@
 
     @pl.when(step == pl.num_programs(0) - 1)
     def _():
-        wide = widef_ref[...]
-        kvg = [jnp.zeros((RANK, HD), F32), jnp.zeros((RANK, HD), F32)]
-        n1_refs = (n1a_ref, n1b_ref, n1c_ref, n1d_ref, n1e_ref)
-        for w, n1w_ref in enumerate(n1_refs):
-            span = slice(w * rows, (w + 1) * rows)
-            grad_key = dk_ref[span] * (1.0 / LOG2E)
-            gv = dv_ref[span].astype(BF)
-            dkv_ref[span, :HD] = grad_key.astype(BF)
-            dkv_ref[span, HD:] = gv
-            gk = rope_back(grad_key, cosw_ref[span], sinw_ref[span]).astype(BF)
-            gr = mm_nt(gk, bkv_ref[0]) + mm_nt(gv, bkv_ref[1])
-            if w == chunks - 1:
-                gr = gr + gr_ref[...]
-                r1t = r1t_ref[...]
-            else:
-                r1t = mm(n1w_ref[...], a_ref[...]).T.astype(BF)
-            wide = wide + mm(gr.T.astype(BF), n1w_ref[...])
-            kvg[0] = kvg[0] + mm(r1t[rows_of(SLOT_K)], gk)
-            kvg[1] = kvg[1] + mm(r1t[rows_of(SLOT_V)], gv)
-        wide_ref[...] = wide.T.astype(BF)
-        kvg_ref[0] = kvg[0].astype(BF)
-        kvg_ref[1] = kvg[1].astype(BF)
-
-
-def input_kernel(
-    x_ref, gain_ref, a_ref, wk_ref, wv_ref, bkv_ref, cos_ref, sin_ref,
-    own_ref, back1_ref, back2_ref, back3_ref, back4_ref, gr_ref, g1_ref, gres_ref, grad_ref,
+        dkv_ref[:, :HD] = (dk_ref[...] * (1.0 / LOG2E)).astype(BF)
+        dkv_ref[:, HD:] = dv_ref[...].astype(BF)
+
+
+def shared_back_kernel(
+    chips, core_ref, n1_ref, r1_ref, bkv_ref, cos_ref, sin_ref, own_ref, back1_ref, back2_ref, back3_ref, back4_ref,
+    gr_ref, widef_ref,
+    mine_ref, theirs_ref, gk_ref, gv_ref, grt_ref,
 ):
     gkv = own_ref[...].astype(F32)
     for back_ref in (back1_ref, back2_ref, back3_ref, back4_ref):
         gkv = gkv + back_ref[...].astype(F32)
     gk = rope_back(gkv[:, :HD], cos_ref[...], sin_ref[...]).astype(BF)
     gv = gkv[:, HD:].astype(BF)
+    gk_ref[...] = gk
+    gv_ref[...] = gv
     gr = gr_ref[...] + mm_nt(gk, bkv_ref[0]) + mm_nt(gv, bkv_ref[1])
-    g1 = g1_ref[...] + mm_nt(gk, wk_ref[...]) + mm_nt(gv, wv_ref[...])
-    g1 = g1 + mm_nt(gr.astype(BF), a_ref[...])
+    grt_ref[...] = gr.astype(BF)
+    wide = (mm(gr.T.astype(BF), n1_ref[...]) + widef_ref[...]).T.astype(BF)
+    share = mine_ref.shape[0] - 2 * RANK
+    wide = wide.reshape(chips, 2, share // chips, LANES)
+    first = core_ref[0] == 0
+    mine_ref[:share] = jnp.where(first, wide[:, 0], wide[:, 1]).reshape(share, LANES)
+    theirs_ref[:share] = jnp.where(first, wide[:, 1], wide[:, 0]).reshape(share, LANES)
+    r1t = turned(r1_ref[...])
+    for j, (slot, grad) in enumerate(((SLOT_K, gk), (SLOT_V, gv))):
+        term = mm(r1t[rows_of(slot)], grad).astype(BF)
+        rows = slice(share + j * RANK, share + (j + 1) * RANK)
+        mine_ref[rows] = term
+        theirs_ref[rows] = term
+
+
+def input_kernel(
+    x_ref, gain_ref, a_ref, wk_ref, wv_ref, gk_ref, gv_ref, gr_ref, g1_ref, gres_ref, grad_ref,
+):
+    g1 = g1_ref[...] + mm_nt(gk_ref[...], wk_ref[...]) + mm_nt(gv_ref[...], wv_ref[...])
+    g1 = g1 + mm_nt(gr_ref[...], a_ref[...])
     x = x_ref[...].astype(F32)
     grad_ref[...] = gres_ref[...] + rms_back(x, gain_ref[...], g1)
 
@@ -415,7 +438,7 @@
     adapters = wide_adapters.shape[2] // RANK
     dp = lax.axis_index(DP)
     tensor = lax.axis_index("tensor")
-    place = jnp.stack([lax.axis_index("core"), tensor]).astype(jnp.int32)
+    my_core = lax.axis_index("core")
     adapter = lax.dynamic_index_in_dim(adapter_ids, dp // 2, keepdims=False)
     column = adapter * RANK
     f3 = 3 * ff_cols
@@ -451,15 +474,6 @@
     b_own = jnp.concatenate(
         [gu_rows[0], gu_rows[1], take_cols(down_adapter).T, take_rows(q_adapter), take_cols(out_adapter).T], axis=1
     )
-    b_all = lax.all_gather(b_own, "tensor", axis=0, tiled=False)
-    edges = [0, ff_cols, 2 * ff_cols, f3, f3 + q_cols, f3 + 2 * q_cols]
-    b_pad = jnp.concatenate(
-        [
-            in_slot(b_all[:, :, first:last], slot)
-            for first, last, slot in zip(edges, edges[1:], (SLOT_G, SLOT_U, SLOT_D, SLOT_Q, SLOT_O))
-        ],
-        axis=2,
-    )
     kv_rows = take_rows(kv_adapter)
     b_kv = jnp.stack([in_slot(kv_rows[0], SLOT_K), in_slot(kv_rows[1], SLOT_V)])
 
@@ -484,7 +498,7 @@
     def lane_block(block):
         return pl.BlockSpec((width, LANES), lambda *_: (0, block))
 
-    head_specs = [weight_spec(q_block), adapter_spec(q_block), weight_spec(q_block + 1), adapter_spec(q_block + 1)]
+    head_specs = [weight_spec(q_block), adapter_spec(0), weight_spec(q_block + 1), adapter_spec(1)]
     q_spec, qb_spec, o_spec, ob_spec = head_specs
     a_spec, wk_spec, wv_spec = lane_block(0), lane_block(1), lane_block(2)
     token_cols = pl.BlockSpec((rows, q_cols), lambda t: (0, t))
@@ -499,50 +513,66 @@
     )
     parts = seq_length // rows
     reach = WINDOW // rows
-    kv_seq = lax.all_to_all(jnp.broadcast_to(kv_own[None], (parts, rows, 2 * HD)), SEQ, 0, 0, tiled=True)
 
     def moved(value, steps):
         return lax.ppermute(value, SEQ, [(c, c + steps) for c in range(parts) if 0 <= c + steps < parts])
 
+    def from_other_core(value):
+        return lax.ppermute(value, "core", [(0, 1), (1, 0)])
+
+    kv_window = jnp.concatenate([moved(kv_own, d) for d in range(reach, 0, -1)] + [kv_own])
+
+    b_own, kv_window = lax.optimization_barrier((b_own, kv_window))
+    b_all = lax.all_gather(b_own, "tensor", axis=0, tiled=False)
+    b_heads = jnp.concatenate(
+        [in_slot(b_all[:, :, f3 : f3 + q_cols], SLOT_Q), in_slot(b_all[:, :, f3 + q_cols :], SLOT_O)], axis=2
+    )
+    steps = 3
+    part_cols = ff_cols // steps
+    b_hidden = b_all[:, :, :f3].reshape(tensor_count, RANK, 3, steps, part_cols).transpose(3, 2, 1, 0, 4)
+    b_hidden = b_hidden.reshape(steps, 3, RANK, tensor_count * part_cols)
+    b_hidden = jnp.concatenate(
+        [in_slot(b_hidden[:, kind], slot) for kind, slot in enumerate((SLOT_G, SLOT_U, SLOT_D))], axis=2
+    )
+
     args = (
-        place, kv_seq, kseg, qseg, normed_one, rank_one, cos, sin, tokens, gain_two, a_all,
-        weights, b_pad, weights, b_pad,
+        kv_window, kseg, qseg, normed_one, rank_one, cos, sin, tokens, gain_two, a_all,
+        weights, b_heads, weights, b_heads,
     )
     heads = q_cols // HD
-    p_spec = pl.BlockSpec((heads, span, rows), lambda t: (t, 0, 0))
+    p_spec, norm_spec = by_step(span, heads * rows), by_step(8, heads * rows)
     queries, mixed, probs, norms, residual, normed_two, rank_two, rank_out = call(
         attn_kernel, "attention", tensor_count, args,
-        [scalars()] + wholes(*args[1:10]) + [a_spec] + head_specs,
+        wholes(*args[:9]) + [a_spec] + head_specs,
         [
             (sds((rows, heads_cols), BF), token_cols), (sds((rows, heads_cols), BF), token_cols),
-            (sds((tensor_count * heads, span, rows), BF), p_spec), (sds((tensor_count, 8, rows), F32), by_step(8, rows)),
+            (sds((tensor_count, span, heads * rows), BF), p_spec),
+            (sds((tensor_count, 8, heads * rows), F32), norm_spec),
             (tok_f32, None), (tok_bf, None), (rank_bf, None), (rank_bf, None),
         ],
         [
-            pltpu.VMEM((span, rows), F32), pltpu.VMEM((span, rows), F32), pltpu.VMEM((HD, span), BF),
-            pltpu.VMEM((span, 2 * HD), BF), pltpu.VMEM((rows, width), F32), pltpu.VMEM((rows, LANES), F32),
+            pltpu.VMEM((span, rows), F32), pltpu.VMEM((span, heads * rows), F32), pltpu.VMEM((HD, span), BF),
+            pltpu.VMEM((rows, width), F32), pltpu.VMEM((rows, LANES), F32), pltpu.VMEM((heads * rows, HD), BF),
         ],
         4 * rows * heads_cols * (span + width), 4 * width * heads_cols,
     )
 
-    sent_one, normed_two = lax.optimization_barrier((normed_one, normed_two))
-    window_one = [moved(sent_one, d) for d in range(reach, 0, -1)]
-
     args = (
-        residual, normed_two, rank_two, cotangent, gain_two, mixed, rank_out, a_all, b_pad, weights,
+        residual, normed_two, rank_two, cotangent, gain_two, mixed, rank_out, a_all, b_hidden, weights,
     )
     block_output, grad_residual, grad_branch, wide_ffn, grad_ro, grad_bo, grad_bh = call(
-        ffn_kernel, "feed_forward", tensor_count, args,
-        wholes(*args[:7]) + [a_spec, by_step(LANES, f3), pl.BlockSpec(memory_space=pl.ANY)],
+        ffn_kernel, "feed_forward", steps, args,
+        wholes(*args[:7]) + [a_spec, by_step(LANES, 3 * tensor_count * part_cols), pl.BlockSpec(memory_space=pl.ANY)],
         [
             (tok_bf, None), (tok_f32, None), (tok_bf, None), (sds((LANES, width), F32), None), (rank_bf, None),
-            (sds((tensor_count, RANK, q_cols), BF), None), (sds((tensor_count, RANK, f3), BF), by_step(RANK, f3)),
+            (sds((tensor_count, RANK, q_cols), BF), None), (sds((tensor_count, RANK, f3), BF), None),
         ],
         [
             pltpu.VMEM((rows, width), F32), pltpu.VMEM((rows, width), F32),
             pltpu.VMEM((rows, LANES), F32), pltpu.VMEM((rows, LANES), F32),
             pltpu.VMEM((LANES, rows), BF), pltpu.VMEM((rows, LANES), BF), pltpu.VMEM((LANES, rows), BF),
-            pltpu.VMEM((2, dp_count, shard_rows, f3), BF), pltpu.SemaphoreType.DMA((2, 2)),
+            pltpu.VMEM((2, dp_count, shard_rows, 3 * tensor_count * part_cols), BF),
+            pltpu.SemaphoreType.DMA((2, 3 * tensor_count)),
         ],
         12 * rows * width * tensor_count * ff_cols, 6 * width * tensor_count * ff_cols,
     )
@@ -550,44 +580,61 @@
     early = lax.psum_scatter(early, "tensor", scatter_dimension=0, tiled=True).reshape(RANK, -1)
 
     args = (
-        place, kv_seq, grad_branch, grad_ro, rank_one, cos, sin, cos_window, sin_window, a_all, b_kv, wide_ffn,
-        *window_one, normed_one, queries, mixed, probs, norms, weights, b_pad, weights, b_pad,
-    )
-    dkv, grad_one, grad_rank, grad_bq, wide_term, kv_term = call(
+        kv_window, grad_branch, grad_ro, rank_one, cos, sin, queries, mixed, probs, norms,
+        weights, b_heads, weights, b_heads,
+    )
+    dkv, grad_one, grad_rank, grad_bq = call(
         attn_back_kernel, "attention_back", tensor_count, args,
-        [scalars()] + wholes(*args[1:9]) + [a_spec] + wholes(*args[10:17])
-        + [token_cols, token_cols, p_spec, by_step(8, rows), o_spec, ob_spec, q_spec, qb_spec],
+        wholes(*args[:6]) + [token_cols, token_cols, p_spec, norm_spec, o_spec, ob_spec, q_spec, qb_spec],
         [
             (sds((span, 2 * HD), BF), None), (tok_f32, None), (sds((rows, LANES), F32), None),
             (sds((tensor_count, RANK, q_cols), BF), by_step(RANK, q_cols)),
-            (sds((width, LANES), BF), None), (sds((2, RANK, HD), BF), None),
         ],
         [
-            pltpu.VMEM((span, rows), BF),
+            pltpu.VMEM((span, heads * rows), BF),
             pltpu.VMEM((span, HD), F32), pltpu.VMEM((span, HD), F32), pltpu.VMEM((HD, span), BF),
-            pltpu.VMEM((LANES, rows), BF),
-            pltpu.VMEM((rows, q_cols), BF), pltpu.VMEM((rows, q_cols), BF), pltpu.VMEM((span, 2 * HD), BF),
+            pltpu.VMEM((LANES, rows), BF), pltpu.VMEM((rows, q_cols), BF), pltpu.VMEM((rows, q_cols), BF),
+            pltpu.VMEM((heads * rows, HD), BF), pltpu.VMEM((heads * rows, HD), BF),
         ],
         2 * rows * heads_cols * (4 * span + 2 * width), 4 * width * heads_cols,
     )
 
+    backs = [moved(dkv[(reach - d) * rows : (reach - d + 1) * rows], -d) for d in range(1, reach + 1)]
+    grad_bq = (grad_bq.astype(F32) + from_other_core(grad_bq).astype(F32)).astype(BF)
+    chips = dp_count // 2
+    share = width // 2 + 2 * RANK
+    args = (
+        my_core.astype(jnp.int32).reshape(1), normed_one, rank_one, b_kv, cos, sin, dkv, *backs, grad_rank, wide_ffn,
+    )
+    mine, theirs, grad_key, grad_value, grad_rank = call(
+        functools.partial(shared_back_kernel, chips), "shared_back", 1, args,
+        [scalars()] + wholes(*args[1:6]) + [pl.BlockSpec((rows, 2 * HD), lambda *_: (reach, 0))] + wholes(*args[7:]),
+        [
+            (sds((share, LANES), BF), None), (sds((share, LANES), BF), None),
+            (sds((rows, HD), BF), None), (sds((rows, HD), BF), None), (rank_bf, None),
+        ],
+        [], 4 * rows * width * LANES, 6 * rows * width,
+    )
+    mine = (mine.astype(F32) + from_other_core(theirs).astype(F32)).astype(BF)
+
     own_rows = width // devices
-    kv_terms = jnp.tile(kv_term.transpose(1, 0, 2), (devices // RANK, 1, 1))
+    planes = chips * tensor_count
+    kv_terms = mine[width // 2 :].reshape(2, RANK // (2 * tensor_count), 2, tensor_count, HD)
+    kv_terms = lax.dynamic_index_in_dim(kv_terms, my_core, 2, keepdims=False).transpose(1, 2, 0, 3)
+    kv_terms = jnp.tile(kv_terms.reshape(-1, 2, HD), (planes // (RANK // 2), 1, 1))
     owned = jnp.concatenate(
-        [wide_term.reshape(devices, own_rows, LANES), kv_terms, jnp.zeros((devices, 2, LANES), BF)], axis=1
-    )
-    every = jnp.broadcast_to(grad_bq[None], (dp_count, tensor_count, RANK, q_cols)).reshape(devices, RANK, q_cols)
-    terms = lax.all_to_all(jnp.concatenate([owned, every], axis=2), ALL, 0, 0, tiled=True)
-    terms = terms.reshape(seqs, parts, RANK, LANES + q_cols)
-
-    backs = [moved(dkv[(reach - d) * rows : (reach - d + 1) * rows], -d) for d in range(1, reach + 1)]
+        [mine[: width // 2].reshape(planes, own_rows, LANES), kv_terms, jnp.zeros((planes, 2, LANES), BF)], axis=1
+    )
+    every = jnp.broadcast_to(grad_bq[None], (chips, tensor_count, RANK, q_cols)).reshape(planes, RANK, q_cols)
+    terms = lax.all_to_all(jnp.concatenate([owned, every], axis=2), PLANES, 0, 0, tiled=True)
+    terms = terms.reshape(seqs, tensor_count, RANK, LANES + q_cols)
+
     args = (
-        tokens, gain_one, a_all, a_all, a_all, b_kv, cos, sin, dkv, *backs, grad_rank, grad_one, grad_residual,
+        tokens, gain_one, a_all, a_all, a_all, grad_key, grad_value, grad_rank, grad_one, grad_residual,
     )
     (input_grad,) = call(
         input_kernel, "input_gradient", 1, args,
-        wholes(*args[:2]) + [a_spec, wk_spec, wv_spec] + wholes(*args[5:8])
-        + [pl.BlockSpec((rows, 2 * HD), lambda *_: (reach, 0))] + wholes(*args[9:]),
+        wholes(*args[:2]) + [a_spec, wk_spec, wv_spec] + wholes(*args[5:]),
         [(tok_f32, None)], [], 2 * rows * width * 384, 16 * rows * width,
     )
 

time: 348 us -> 324 us (0.931)
  local copies, waits for them, and re-layouts: 29.9 us -> 20.9 us
  Pallas kernels: 105 us -> 96.5 us
  starting transfers between devices: 43.7 us -> 37.5 us
    all_to_all x1, waiting for transfers between devices: 0.01 us -> 13.3 us  [on_device(): a_all = lax.all_to_all(wide, DP, 0, 0, tiled=True).reshape(width, 3 * LANES)]
    all_gather x1, waiting for transfers between devices: 91.5 us -> 80 us  [on_device(): weights = lax.all_gather(pack, ALL, axis=0, tiled=False)]
    pallas_call x7 -> x8, Pallas kernels: 105 us -> 96.5 us  [call(): pl.pallas_call(kernel, name=name, grid=(steps,), in_specs=specs, out_spec...]
    all_to_all x2 -> x1, starting transfers between devices: 14.8 us -> 7.16 us  [on_device(): lax.all_to_all(jnp.concatenate([owned, every], axis=2), PLANES, 0, 0, til...]
    ppermute x8, waiting for transfers between devices: 21.7 us -> 14.8 us  [moved(): lax.ppermute(value, SEQ, [(c, c + steps) for c in range(parts) if 0 <= c...]
    unnamed x52 -> x48, local copies, waits for them, and re-layouts: 16.8 us -> 11.2 us
    all_to_all x2 -> x1, waiting for transfers between devices: 15.1 us -> 17.3 us  [on_device(): lax.all_to_all(jnp.concatenate([owned, every], axis=2), PLANES, 0, 0, til...]
  transfers between devices with their start and end apart: 14 -> 15, of which waited for: 5 -> 9; matrix products, arithmetic and copies ran while one was open for 9% -> 8% of each run, Pallas kernels for 23% -> 11%
where the time goes in v5:
time: 324 us; the launch traced here: 322 us
  waiting for transfers between devices  127 us (39%)
  Pallas kernels  96.5 us (30%)
  starting transfers between devices  37.5 us (12%)
  local copies, waits for them, and re-layouts  20.9 us (6%)
  between operations  15 us (5%)
  other arithmetic  13.3 us (4%)
  blocking collectives  11.5 us (4%)
    pallas_call x8, Pallas kernels, call(): pl.pallas_call(kernel, name=name, grid=(steps,), in_specs=specs, out_spec...  96.5 us
    all_gather x1, waiting for transfers between devices, on_device(): weights = lax.all_gather(pack, ALL, axis=0, tiled=False)  80 us
    ppermute x8, starting transfers between devices, moved(): lax.ppermute(value, SEQ, [(c, c + steps) for c in range(parts) if 0 <= c...  20.7 us
    all_to_all x1, waiting for transfers between devices, on_device(): lax.all_to_all(jnp.concatenate([owned, every], axis=2), PLANES, 0, 0, til...  17.3 us
    ppermute x8, waiting for transfers between devices, moved(): lax.ppermute(value, SEQ, [(c, c + steps) for c in range(parts) if 0 <= c...  14.8 us
    all_to_all x1, waiting for transfers between devices, on_device(): a_all = lax.all_to_all(wide, DP, 0, 0, tiled=True).reshape(width, 3 * LANES)  13.3 us
    all_gather x1, blocking collectives, on_device(): b_all = lax.all_gather(b_own, 'tensor', axis=0, tiled=False)  11.5 us
    unnamed x48, local copies, waits for them, and re-layouts  11.2 us
  transfers between devices with their start and end apart: 15, of which 9 were waited for; matrix products, arithmetic and copies ran while one was open for 8% of the time, Pallas kernels for 11%

profile of v5, /device:TPU:1, one launch (start us, length us, event | category | flops | bytes accessed | tf_op | source)
XLA Modules:
  0.0 321.5 jit_solution(8743326179263440060)
XLA Ops:
  16.5 8.7 %all-to-all-start = ((bf16[32,48,384]{2,1,0:T(8,128)(2,1)}), bf16[32,48,384]{2,1,0:T(8,128)(2,1)S(1)}, u32[]{:S(2)}, u32[]{:S(2)}) async-start(bf16[32,48,384]{2,1,0:T(8,128)(2,1)} %pad_maximum_fusion), calls=%async_computation | async-start | bytes 2359296 | tf_op jit(solution)/shard_map/all_to_all | solution.py:460
  30.8 2.4 fusion.9
  34.6 13.3 %all-to-all-done = bf16[32,48,384]{2,1,0:T(8,128)(2,1)S(1)} async-done(((bf16[32,48,384]{2,1,0:T(8,128)(2,1)}), bf16[32,48,384]{2,1,0:T(8,128)(2,1)S(1)}, u32[]{:S(2)}, u32[]{:S(2)}) %all-to-all-start) | async-done | bytes 1179680 | tf_op jit(solution)/shard_map/all_to_all | solution.py:460
  48.9 3.4 %keys_values.1 = (bf16[256,1536]{1,0:T(8,128)(2,1)}, bf16[256,128]{1,0:T(8,128)(2,1)}, bf16[256,256]{1,0:T(8,128)(2,1)}) custom-call(bf16[256,1536]{1,0:T(8,128)(2,1)} %x_ref.5, f32[1,1536]{1,0:T(1,128)} %get-tuple-element.122.gain_ref, bf16[1536,384]{1,0:T(8,128)(2,1)} %bitcast.69, bf16[1536,384]{1,0:T(8,128)(2,1)} %bitcast.70, bf16[1536,384]{1,0:T(8,128)(2,1)} %bitcast.71, ...), custom_call_target="tpu_custom_call" | custom-call | flops 301989888 | bytes 2359296 | tf_op jit(solution)/shard_map/keys_values/pallas_call | solution.py:400
  53.6 6.1 %collective-permute-start.1 = (bf16[256,256]{1,0:T(8,128)(2,1)}, bf16[256,256]{1,0:T(8,128)(2,1)S(1)}, u32[]{:S(2)}, u32[]{:S(2)}) collective-permute-start(bf16[256,256]{1,0:T(8,128)(2,1)} %get-tuple-element.47), channel_id=1, source_target_pairs={{0,3},{1,4},{2,5},{3,6},{4,7},{8,11},{9,12},{10,13},{11,14},{12,15... | collective-permute-start | bytes 393224 | tf_op jit(solution)/shard_map/ppermute | solution.py:518
  63.3 1.9 collective-permute-start.3
  66.1 6.9 %collective-permute-done.2 = bf16[256,256]{1,0:T(8,128)(2,1)S(1)} collective-permute-done((bf16[256,256]{1,0:T(8,128)(2,1)}, bf16[256,256]{1,0:T(8,128)(2,1)S(1)}, u32[]{:S(2)}, u32[]{:S(2)}) %collective-permute-start.2) | collective-permute-done | bytes 131104 | tf_op jit(solution)/shard_map/ppermute | solution.py:518
  73.0 2.2 collective-permute-done.3
  76.1 11.5 %all-gather.1 = bf16[64,4224]{1,0:T(8,128)(2,1)S(1)} all-gather(bf16[16,4224]{1,0:T(8,128)(2,1)S(1)} %constant_dynamic-update-slice_fusion), channel_id=3, replica_groups=mesh['y'=4,'x'=4,'core'=2,'tensor'=4] {'tensor'}, dimensions={0}, use_global_device_ids=true | all-gather | bytes 675840 | tf_op jit(solution)/shard_map/all_gather | solution.py:526
  89.4 2.4 fusion.5.b_ref
  91.8 80.0 %all-gather.6.cloned.1.call-done = bf16[6144,4224]{1,0:T(8,128)(2,1)} async-done(((bf16[48,4224]{1,0:T(8,128)(2,1)}), bf16[6144,4224]{1,0:T(8,128)(2,1)}) %all-gather.6.cloned.1.call-update) | async-done | bytes 51904528 | tf_op jit(solution)/shard_map/all_gather | solution.py:450
  171.8 18.8 %attention.1 = (bf16[256,1536]{1,0:T(8,128)(2,1)}, bf16[256,1536]{1,0:T(8,128)(2,1)}, bf16[4,1280,768]{2,1,0:T(8,128)(2,1)}, f32[4,8,768]{2,1,0:T(8,128)}, f32[2...) custom-call(bf16[1280,256]{1,0:T(8,128)(2,1)} %copy-done.4, ...), custom_call_target="tpu_custom_call" | custom-call | flops 4429185024 | bytes 9437184 | tf_op jit(solution)/shard_map/attention/pallas_call | solution.py:400
  190.6 39.0 %feed_forward.1 = (bf16[256,1536]{1,0:T(8,128)(2,1)}, f32[256,1536]{1,0:T(8,128)}, bf16[256,1536]{1,0:T(8,128)(2,1)}, f32[128,1536]{1,0:T(8,128)}, bf16[256,128]...) custom-call(f32[256,1536]{1,0:T(8,128)} %get-tuple-element.53.res_ref, ...), custom_call_target="tpu_custom_call" | custom-call | flops 21743271936 | bytes 42467328 | tf_op jit(solution)/shard_map/feed_forward/pallas_call | solution.py:400
  231.6 20.2 %attention_back.1 = (bf16[1280,256]{1,0:T(8,128)(2,1)}, f32[256,1536]{1,0:T(8,128)}, f32[256,128]{1,0:T(8,128)}, bf16[4,16,384]{2,1,0:T(8,128)(2,1)}) custom-call(bf16[1280,256]{1,0:T(8,128)(2,1)} %copy-done.4, bf16[256,1536]{1,0:T(8,128)(2,1)} %get-tuple-element.59.gb_ref, bf16[256,128]{1,0:T(8,128)(2,1)} %get-tuple-element.60.gro_ref, ...), custom_call_target="tpu_custom_call" | custom-call | flops 6442450944 | bytes 9437184 | tf_op jit(solution)/shard_map/attention_back/pallas_call | solution.py:400
  253.0 3.7 %collective-permute-start.4 = (bf16[256,256]{1,0:T(8,128)(2,1)S(1)}, bf16[256,256]{1,0:T(8,128)(2,1)S(1)}, u32[]{:S(2)}, u32[]{:S(2)}) collective-permute-start(bf16[256,256]{1,0:T(8,128)(2,1)S(1)} %get-tuple-element.111), channel_id=1, source_target_pairs={{1,0},{2,1},{3,2},{4,3},{5,4},{6,5},{7,6},{9,8},{10,9},{11,10},{12... | collective-permute-start | bytes 393224 | tf_op jit(solution)/shard_map/ppermute | solution.py:518
  256.7 2.6 collective-permute-start.5
  259.3 1.9 collective-permute-start.6
  264.2 3.4 %collective-permute-done.6.back3_ref = bf16[256,256]{1,0:T(8,128)(2,1)S(1)} collective-permute-done((bf16[256,256]{1,0:T(8,128)(2,1)S(1)}, bf16[256,256]{1,0:T(8,128)(2,1)S(1)}, u32[]{:S(2)}, u32[]{:S(2)}) %collective-permute-start.6) | collective-permute-done | bytes 131104 | tf_op jit(solution)/shard_map/ppermute | solution.py:518
  268.3 3.3 %shared_back.1 = (bf16[800,128]{1,0:T(8,128)(2,1)}, bf16[800,128]{1,0:T(8,128)(2,1)}, bf16[256,128]{1,0:T(8,128)(2,1)}, bf16[256,128]{1,0:T(8,128)(2,1)}, bf16[256,128]{1,0:T(8,128)(2,1)}) custom-call(s32[1]{0:T(128)} %bitcast.27.core_ref, bf16[256,1536]{1,0:T(8,128)(2,1)} %get-tuple-element.49.n1_ref, bf16[256,128]{1,0:T(8,128)(2,1)} %get-tuple-element.50.r1_ref, ...), custom_call_target="tpu_custom_call" | custom-call | flops 201326592 | bytes 2359296 | tf_op jit(solution)/shard_map/shared_back/pallas_call | solution.py:400
  276.2 7.2 %all-to-all-start.1 = ((bf16[64,16,512]{2,1,0:T(8,128)(2,1)}), bf16[64,16,512]{2,1,0:T(8,128)(2,1)S(1)}, u32[]{:S(2)}, u32[]{:S(2)}) async-start(bf16[64,16,512]{2,1,0:T(8,128)(2,1)} %pad_maximum_fusion.1), calls=%async_computation.1 | async-start | bytes 2097152 | tf_op jit(solution)/shard_map/all_to_all | solution.py:629
  283.4 5.2 %input_gradient.1 = f32[256,1536]{1,0:T(8,128)} custom-call(bf16[256,1536]{1,0:T(8,128)(2,1)} %x_ref.5, f32[1,1536]{1,0:T(1,128)} %get-tuple-element.122.gain_ref, bf16[1536,384]{1,0:T(8,128)(2,1)} %bitcast.74, bf16[1536,384]{1,0:T(8,128)(2,1)} %bitcast.75, bf16[1536,384]{1,0:T(8,128)(2,1)} %bitcast.76, bf16[256,128]{1,0:T(8,128)(2,1)} %get-tuple-element.67.gk_ref, ...), custom_call_target="tpu_custom_call" | custom-call | flops 301989888 | bytes 6291456 | tf_op jit(solution)/shard_map/input_gradient/pallas_call | solution.py:400
  288.5 17.3 %all-to-all-done.1 = bf16[64,16,512]{2,1,0:T(8,128)(2,1)S(1)} async-done(((bf16[64,16,512]{2,1,0:T(8,128)(2,1)}), bf16[64,16,512]{2,1,0:T(8,128)(2,1)S(1)}, u32[]{:S(2)}, u32[]{:S(2)}) %all-to-all-start.1) | async-done | bytes 1048608 | tf_op jit(solution)/shard_map/all_to_all | solution.py:629
  306.8 2.2 sum_wide.1
  310.5 4.5 %sum_hidden.1 = (f32[2,128,1152]{2,1,0:T(8,128)}, f32[1152,128]{1,0:T(8,128)}, f32[384,128]{1,0:T(8,128)}) custom-call(s32[16]{0:T(128)} %ids_ref.3, bf16[32,16,3840]{2,1,0:T(8,128)(2,1)} %bitcast.79), custom_call_target="tpu_custom_call" | custom-call | bytes 1769472 | tf_op jit(solution)/shard_map/sum_hidden/pallas_call | solution.py:400
  (117 shorter events, 38.5 us)
Async XLA Ops:
  7.2 19.4 %copy-start = (bf16[1152,128]{1,0:T(8,128)(2,1)S(1)}, bf16[1152,128]{1,0:T(8,128)(2,1)}, u32[]{:S(2)}) copy-start(bf16[1152,128]{1,0:T(8,128)(2,1)} %param.31) | copy-start | bytes 884740
  7.2 7.6 %copy-start.15 = (s32[16]{0:T(128)S(1)}, s32[16]{0:T(128)}, u32[]{:S(2)}) copy-start(s32[16]{0:T(128)} %ids_ref.3) | copy-start | bytes 196
  7.2 164.6 %all-gather.6.cloned.1.call-start = ((), (), s32[]{:S(2)}) async-start(), calls=%async_computation.4 | async-start | bytes 52310016 | tf_op jit(solution)/shard_map/all_gather | solution.py:450
  16.5 10.4 %copy-start.11 = (bf16[384,128]{1,0:T(8,128)(2,1)S(1)}, bf16[384,128]{1,0:T(8,128)(2,1)}, u32[]{:S(2)}) copy-start(bf16[384,128]{1,0:T(8,128)(2,1)} %param.29) | copy-start | bytes 294916
  16.5 31.4 %all-to-all-start = ((bf16[32,48,384]{2,1,0:T(8,128)(2,1)}), bf16[32,48,384]{2,1,0:T(8,128)(2,1)S(1)}, u32[]{:S(2)}, u32[]{:S(2)}) async-start(bf16[32,48,384]{2,1,0:T(8,128)(2,1)} %pad_maximum_fusion), calls=%async_computation | async-start | bytes 2359296 | tf_op jit(solution)/shard_map/all_to_all | solution.py:460
  25.2 226.5 %reduce-scatter.2.cloned.1.call-start = ((), (), s32[]{:S(2)}) async-start(), calls=%async_computation.3 | async-start | bytes 614400 | tf_op jit(solution)/shard_map/reduce_scatter | solution.py:580
  48.9 4.6 %copy-start.6 = (s32[32768]{0:T(1024)S(1)}, s32[32768]{0:T(1024)}, u32[]{:S(2)}) copy-start(s32[32768]{0:T(1024)} %param.18) | copy-start | bytes 393220
  52.3 13.0 %collective-permute-start = (bf16[256,256]{1,0:T(8,128)(2,1)}, bf16[256,256]{1,0:T(8,128)(2,1)S(1)}, u32[]{:S(2)}, u32[]{:S(2)}) collective-permute-start(bf16[256,256]{1,0:T(8,128)(2,1)} %get-tuple-element.47), channel_id=1, source_target_pairs={{0,4},{1,5},{2,6},{3,7},{8,12},{9,13},{10,14},{11,15},{16,20},{17,... | collective-permute-start | bytes 393224 | tf_op jit(solution)/shard_map/ppermute | solution.py:518
  53.6 12.4 %collective-permute-start.1 = (bf16[256,256]{1,0:T(8,128)(2,1)}, bf16[256,256]{1,0:T(8,128)(2,1)S(1)}, u32[]{:S(2)}, u32[]{:S(2)}) collective-permute-start(bf16[256,256]{1,0:T(8,128)(2,1)} %get-tuple-element.47), channel_id=1, source_target_pairs={{0,3},{1,4},{2,5},{3,6},{4,7},{8,11},{9,12},{10,13},{11,14},{12,15... | collective-permute-start | bytes 393224 | tf_op jit(solution)/shard_map/ppermute | solution.py:518
  61.4 11.5 %collective-permute-start.2 = (bf16[256,256]{1,0:T(8,128)(2,1)}, bf16[256,256]{1,0:T(8,128)(2,1)S(1)}, u32[]{:S(2)}, u32[]{:S(2)}) collective-permute-start(bf16[256,256]{1,0:T(8,128)(2,1)} %get-tuple-element.47), channel_id=1, source_target_pairs={{0,2},{1,3},{2,4},{3,5},{4,6},{5,7},{8,10},{9,11},{10,12},{11,13},... | collective-permute-start | bytes 393224 | tf_op jit(solution)/shard_map/ppermute | solution.py:518
  63.3 11.8 %collective-permute-start.3 = (bf16[256,256]{1,0:T(8,128)(2,1)}, bf16[256,256]{1,0:T(8,128)(2,1)S(1)}, u32[]{:S(2)}, u32[]{:S(2)}) collective-permute-start(bf16[256,256]{1,0:T(8,128)(2,1)} %get-tuple-element.47), channel_id=1, source_target_pairs={{0,1},{1,2},{2,3},{3,4},{4,5},{5,6},{6,7},{8,9},{9,10},{10,11},{11... | collective-permute-start | bytes 393224 | tf_op jit(solution)/shard_map/ppermute | solution.py:518
  76.1 12.3 %copy-start.4 = (bf16[1280,256]{1,0:T(8,128)(2,1)}, bf16[1280,256]{1,0:T(8,128)(2,1)S(1)}, u32[]{:S(2)}) copy-start(bf16[1280,256]{1,0:T(8,128)(2,1)S(1)} %constant_dynamic-update-slice_fusion.3.kv_ref) | copy-start | bytes 1966084
  231.5 79.0 %all-gather.8.cloned.1.call-start = ((), (), s32[]{:S(2)}) async-start(), calls=%async_computation.5 | async-start | bytes 4055040 | tf_op jit(solution)/shard_map/all_gather | solution.py:642
  251.8 20.6 %copy-start.12 = (bf16[4,16,384]{2,1,0:T(8,128)(2,1)S(1)}, bf16[4,16,384]{2,1,0:T(8,128)(2,1)}, u32[]{:S(2)}) copy-start(bf16[4,16,384]{2,1,0:T(8,128)(2,1)} %get-tuple-element.74) | copy-start | bytes 147460
  253.0 9.7 %collective-permute-start.4 = (bf16[256,256]{1,0:T(8,128)(2,1)S(1)}, bf16[256,256]{1,0:T(8,128)(2,1)S(1)}, u32[]{:S(2)}, u32[]{:S(2)}) collective-permute-start(bf16[256,256]{1,0:T(8,128)(2,1)S(1)} %get-tuple-element.111), channel_id=1, source_target_pairs={{1,0},{2,1},{3,2},{4,3},{5,4},{6,5},{7,6},{9,8},{10,9},{11,10},{12... | collective-permute-start | bytes 393224 | tf_op jit(solution)/shard_map/ppermute | solution.py:518
  256.7 7.5 %collective-permute-start.5 = (bf16[256,256]{1,0:T(8,128)(2,1)S(1)}, bf16[256,256]{1,0:T(8,128)(2,1)S(1)}, u32[]{:S(2)}, u32[]{:S(2)}) collective-permute-start(bf16[256,256]{1,0:T(8,128)(2,1)S(1)} %get-tuple-element.110), channel_id=1, source_target_pairs={{2,0},{3,1},{4,2},{5,3},{6,4},{7,5},{10,8},{11,9},{12,10},{13,11},... | collective-permute-start | bytes 393224 | tf_op jit(solution)/shard_map/ppermute | solution.py:518
  259.3 8.3 %collective-permute-start.6 = (bf16[256,256]{1,0:T(8,128)(2,1)S(1)}, bf16[256,256]{1,0:T(8,128)(2,1)S(1)}, u32[]{:S(2)}, u32[]{:S(2)}) collective-permute-start(bf16[256,256]{1,0:T(8,128)(2,1)S(1)} %get-tuple-element.109), channel_id=1, source_target_pairs={{3,0},{4,1},{5,2},{6,3},{7,4},{11,8},{12,9},{13,10},{14,11},{15,12... | collective-permute-start | bytes 393224 | tf_op jit(solution)/shard_map/ppermute | solution.py:518
  261.2 6.4 %collective-permute-start.7 = (bf16[256,256]{1,0:T(8,128)(2,1)S(1)}, bf16[256,256]{1,0:T(8,128)(2,1)S(1)}, u32[]{:S(2)}, u32[]{:S(2)}) collective-permute-start(bf16[256,256]{1,0:T(8,128)(2,1)S(1)} %get-tuple-element.108), channel_id=1, source_target_pairs={{4,0},{5,1},{6,2},{7,3},{12,8},{13,9},{14,10},{15,11},{20,16},{21,... | collective-permute-start | bytes 393224 | tf_op jit(solution)/shard_map/ppermute | solution.py:518
  262.5 9.8 %collective-permute-start.9 = (bf16[4,16,384]{2,1,0:T(8,128)(2,1)}, bf16[4,16,384]{2,1,0:T(8,128)(2,1)S(1)}, u32[]{:S(2)}, u32[]{:S(2)}) collective-permute-start(bf16[4,16,384]{2,1,0:T(8,128)(2,1)} %get-tuple-element.74), channel_id=1, source_target_pairs={{0,4},{4,0},{1,5},{5,1},{2,6},{6,2},{3,7},{7,3},{8,12},{12,8},{9,1... | collective-permute-start | bytes 147464 | tf_op jit(solution)/shard_map/ppermute | solution.py:521
  262.7 5.0 %copy-start.7 = (bf16[256,256]{1,0:T(8,128)(2,1)}, bf16[256,256]{1,0:T(8,128)(2,1)S(1)}, u32[]{:S(2)}) copy-start(bf16[256,256]{1,0:T(8,128)(2,1)S(1)} %collective-permute-done.4.back1_ref) | copy-start | bytes 393220
  264.2 3.4 %copy-start.8 = (bf16[256,256]{1,0:T(8,128)(2,1)}, bf16[256,256]{1,0:T(8,128)(2,1)S(1)}, u32[]{:S(2)}) copy-start(bf16[256,256]{1,0:T(8,128)(2,1)S(1)} %collective-permute-done.5.back2_ref) | copy-start | bytes 393220
  271.7 2.0 collective-permute-start.8
  276.2 29.7 %all-to-all-start.1 = ((bf16[64,16,512]{2,1,0:T(8,128)(2,1)}), bf16[64,16,512]{2,1,0:T(8,128)(2,1)S(1)}, u32[]{:S(2)}, u32[]{:S(2)}) async-start(bf16[64,16,512]{2,1,0:T(8,128)(2,1)} %pad_maximum_fusion.1), calls=%async_computation.1 | async-start | bytes 2097152 | tf_op jit(solution)/shard_map/all_to_all | solution.py:629
  306.8 8.2 %copy-start.1 = (bf16[1152,128]{1,0:T(8,128)(2,1)S(1)}, bf16[1152,128]{1,0:T(8,128)(2,1)}, u32[]{:S(2)}) copy-start(bf16[1152,128]{1,0:T(8,128)(2,1)} %param.31) | copy-start | bytes 884740
  (7 other events, 8.3 us)
Sparse Core Ops, SparseCore 0:
  12.5 159.3 all-gather.5
  231.6 18.6 reduce-scatter.1
  252.8 57.2 all-gather.7

commit v6 on v5

--- a/solution.py
+++ b/solution.py
@@ -246,7 +246,7 @@
 def attn_back_kernel(
     kv_ref, gb_ref, gro_ref, r1_ref, cos_ref, sin_ref,
     q_ref, mixed_ref, p_ref, inv_ref, wo_ref, bo_ref, wq_ref, bq_ref,
-    dkv_ref, g1_ref, gr_ref, gbq_ref,
+    dkva_ref, dkvb_ref, dkvc_ref, dkvd_ref, dkve_ref, g1_ref, gr_ref, gbq_ref,
     ds_ref, dk_ref, dv_ref, kt_ref, r1t_ref, gq_ref, gm_ref, qs_ref, gs_ref,
 ):
     step = pl.program_id(0)
@@ -294,8 +294,10 @@
 
     @pl.when(step == pl.num_programs(0) - 1)
     def _():
-        dkv_ref[:, :HD] = (dk_ref[...] * (1.0 / LOG2E)).astype(BF)
-        dkv_ref[:, HD:] = dv_ref[...].astype(BF)
+        for c, dkv_ref in enumerate((dkva_ref, dkvb_ref, dkvc_ref, dkvd_ref, dkve_ref)):
+            span = slice(c * rows, (c + 1) * rows)
+            dkv_ref[:, :HD] = (dk_ref[span] * (1.0 / LOG2E)).astype(BF)
+            dkv_ref[:, HD:] = dv_ref[span].astype(BF)
 
 
 def shared_back_kernel(
@@ -326,6 +328,25 @@
         theirs_ref[rows] = term
 
 
+def payload_kernel(core_ref, mine_ref, other_ref, q_ref, q_other_ref, out_ref):
+    first = core_ref[0] == 0
+    total = mine_ref[...].astype(F32) + other_ref[...].astype(F32)
+    tensor_count = q_ref.shape[0]
+    count = out_ref.shape[0]
+    own_rows = (total.shape[0] - 2 * RANK) // count
+    queries = [(q_ref[t].astype(F32) + q_other_ref[t].astype(F32)).astype(BF) for t in range(tensor_count)]
+    blank = jnp.zeros((RANK - own_rows - 2, LANES), F32)
+    for n in range(count):
+        pieces = [total[n * own_rows : (n + 1) * own_rows]]
+        row = (2 * (n // tensor_count) * tensor_count + n % tensor_count) % RANK
+        for j in range(2):
+            at = count * own_rows + j * RANK + row
+            low, high = total[at : at + 1], total[at + tensor_count : at + tensor_count + 1]
+            pieces.append(jnp.where(first, low, high))
+        out_ref[n, :, :LANES] = jnp.concatenate(pieces + [blank], axis=0).astype(BF)
+        out_ref[n, :, LANES:] = queries[n % tensor_count]
+
+
 def input_kernel(
     x_ref, gain_ref, a_ref, wk_ref, wv_ref, gk_ref, gv_ref, gr_ref, g1_ref, gres_ref, grad_ref,
 ):
@@ -335,11 +356,13 @@
     grad_ref[...] = gres_ref[...] + rms_back(x, gain_ref[...], g1)
 
 
-def sum_hidden_kernel(ids_ref, terms_ref, gu_ref, down_ref, out_ref, acc_ref):
+def sum_hidden_kernel(ids_ref, core_ref, own_ref, other_ref, gu_ref, down_ref, out_ref, acc_ref):
     acc_ref[...] = jnp.zeros_like(acc_ref)
-    for s in range(terms_ref.shape[0] // 2):
-        acc_ref[ids_ref[s]] += terms_ref[2 * s].astype(F32) + terms_ref[2 * s + 1].astype(F32)
     adapters, rank, cols = acc_ref.shape
+    for core, terms_ref in ((core_ref[0], own_ref), (1 - core_ref[0], other_ref)):
+        part = pl.ds(pl.multiple_of(core * (cols // 2), LANES), cols // 2)
+        for s in range(terms_ref.shape[0]):
+            acc_ref[ids_ref[s], :, part] += terms_ref[s].astype(F32)
     ff = gu_ref.shape[2]
 
     def taken(first, last):
@@ -362,13 +385,13 @@
     adapters, rank, _ = acc_ref.shape
     q_ref[...] = acc_ref[:, :, LANES:].reshape(q_ref.shape)
     lane = lax.broadcasted_iota(jnp.int32, (rank, LANES), 1) // RANK
-    slots, own_rows = wide_ref.shape[:2]
+    own_rows, slots = wide_ref.shape[:2]
     for j in range(slots):
         total = jnp.zeros((rank, LANES), F32)
         for a in range(adapters):
             moved = pltpu.roll(acc_ref[a, :, :LANES], ((a - j) * RANK) % LANES, 1)
             total = jnp.where(lane == a, moved, total)
-        wide_ref[j] = total[:own_rows]
+        wide_ref[:, j] = total[:own_rows]
     mine = acc_ref[own_ref[0], :, :LANES]
     for j in range(2):
         kv_ref[j] = mine[own_rows + j : own_rows + j + 1]
@@ -454,10 +477,16 @@
     wide = jnp.take(wide, adapter_ids, axis=2).transpose(2, 1, 0, 3)
     wide = wide.reshape(seqs, shard_rows, 7 * RANK)
     wide = jnp.pad(wide, ((0, 0), (0, 0), (0, LANES - 7 * RANK)))
-    wide = jnp.repeat(wide, dp_count // seqs, axis=0)
-    shared = jnp.broadcast_to(kv_weight[:, None], (2, dp_count, shard_rows, HD))
+    shared = jnp.broadcast_to(kv_weight[:, None], (2, seqs, shard_rows, HD))
     wide = jnp.concatenate([wide, shared[0], shared[1]], axis=2)
-    a_all = lax.all_to_all(wide, DP, 0, 0, tiled=True).reshape(width, 3 * LANES)
+
+    def from_other_core(value):
+        return lax.ppermute(value, "core", [(0, 1), (1, 0)])
+
+    a_own = lax.all_to_all(wide, ("y", "x"), 0, 0, tiled=True)
+    a_other = from_other_core(a_own)
+    a_all = jnp.where(my_core == 0, jnp.stack([a_own, a_other], 1), jnp.stack([a_other, a_own], 1))
+    a_all = a_all.reshape(width, 3 * LANES)
 
     def take_rows(matrix):
         return lax.dynamic_slice_in_dim(matrix, column, RANK, matrix.ndim - 2)
@@ -516,9 +545,6 @@
 
     def moved(value, steps):
         return lax.ppermute(value, SEQ, [(c, c + steps) for c in range(parts) if 0 <= c + steps < parts])
-
-    def from_other_core(value):
-        return lax.ppermute(value, "core", [(0, 1), (1, 0)])
 
     kv_window = jnp.concatenate([moved(kv_own, d) for d in range(reach, 0, -1)] + [kv_own])
 
@@ -583,11 +609,11 @@
         kv_window, grad_branch, grad_ro, rank_one, cos, sin, queries, mixed, probs, norms,
         weights, b_heads, weights, b_heads,
     )
-    dkv, grad_one, grad_rank, grad_bq = call(
+    *dkv, grad_one, grad_rank, grad_bq = call(
         attn_back_kernel, "attention_back", tensor_count, args,
         wholes(*args[:6]) + [token_cols, token_cols, p_spec, norm_spec, o_spec, ob_spec, q_spec, qb_spec],
         [
-            (sds((span, 2 * HD), BF), None), (tok_f32, None), (sds((rows, LANES), F32), None),
+            *[(sds((rows, 2 * HD), BF), None)] * (reach + 1), (tok_f32, None), (sds((rows, LANES), F32), None),
             (sds((tensor_count, RANK, q_cols), BF), by_step(RANK, q_cols)),
         ],
         [
@@ -599,34 +625,39 @@
         2 * rows * heads_cols * (4 * span + 2 * width), 4 * width * heads_cols,
     )
 
-    backs = [moved(dkv[(reach - d) * rows : (reach - d + 1) * rows], -d) for d in range(1, reach + 1)]
-    grad_bq = (grad_bq.astype(F32) + from_other_core(grad_bq).astype(F32)).astype(BF)
+    half_cols = (f3 + q_cols) // 2
+    early, grad_one = lax.optimization_barrier((early, grad_one))
+    early_mine = lax.dynamic_slice_in_dim(early, my_core * half_cols, half_cols, 1)
+    early_theirs = lax.dynamic_slice_in_dim(early, (1 - my_core) * half_cols, half_cols, 1)
+    early = (early_mine.astype(F32) + from_other_core(early_theirs).astype(F32)).astype(BF)
+    early = lax.all_to_all(jnp.broadcast_to(early[None], (seqs, RANK, half_cols)), ("y", "x"), 0, 0, tiled=True)
+
+    backs = [moved(dkv[reach - d], -d) for d in range(1, reach + 1)]
     chips = dp_count // 2
     share = width // 2 + 2 * RANK
     args = (
-        my_core.astype(jnp.int32).reshape(1), normed_one, rank_one, b_kv, cos, sin, dkv, *backs, grad_rank, wide_ffn,
+        my_core.astype(jnp.int32).reshape(1), normed_one, rank_one, b_kv, cos, sin, dkv[reach], *backs, grad_rank, wide_ffn,
     )
     mine, theirs, grad_key, grad_value, grad_rank = call(
         functools.partial(shared_back_kernel, chips), "shared_back", 1, args,
-        [scalars()] + wholes(*args[1:6]) + [pl.BlockSpec((rows, 2 * HD), lambda *_: (reach, 0))] + wholes(*args[7:]),
+        [scalars()] + wholes(*args[1:]),
         [
             (sds((share, LANES), BF), None), (sds((share, LANES), BF), None),
             (sds((rows, HD), BF), None), (sds((rows, HD), BF), None), (rank_bf, None),
         ],
         [], 4 * rows * width * LANES, 6 * rows * width,
     )
-    mine = (mine.astype(F32) + from_other_core(theirs).astype(F32)).astype(BF)
-
     own_rows = width // devices
     planes = chips * tensor_count
-    kv_terms = mine[width // 2 :].reshape(2, RANK // (2 * tensor_count), 2, tensor_count, HD)
-    kv_terms = lax.dynamic_index_in_dim(kv_terms, my_core, 2, keepdims=False).transpose(1, 2, 0, 3)
-    kv_terms = jnp.tile(kv_terms.reshape(-1, 2, HD), (planes // (RANK // 2), 1, 1))
-    owned = jnp.concatenate(
-        [mine[: width // 2].reshape(planes, own_rows, LANES), kv_terms, jnp.zeros((planes, 2, LANES), BF)], axis=1
-    )
-    every = jnp.broadcast_to(grad_bq[None], (chips, tensor_count, RANK, q_cols)).reshape(planes, RANK, q_cols)
-    terms = lax.all_to_all(jnp.concatenate([owned, every], axis=2), PLANES, 0, 0, tiled=True)
+    theirs, early = lax.optimization_barrier((theirs, early))
+    other, grad_bq_other = from_other_core(theirs), from_other_core(grad_bq)
+    args = (my_core.astype(jnp.int32).reshape(1), mine, other, grad_bq, grad_bq_other)
+    (payload,) = call(
+        payload_kernel, "payload", 1, args, [scalars()] + wholes(*args[1:]),
+        [(sds((planes, RANK, LANES + q_cols), BF), None)], [], 0, 2 * planes * RANK * (LANES + q_cols),
+    )
+    payload, grad_key = lax.optimization_barrier((payload, grad_key))
+    terms = lax.all_to_all(payload, PLANES, 0, 0, tiled=True)
     terms = terms.reshape(seqs, tensor_count, RANK, LANES + q_cols)
 
     args = (
@@ -638,11 +669,10 @@
         [(tok_f32, None)], [], 2 * rows * width * 384, 16 * rows * width,
     )
 
-    early, grad_one = lax.optimization_barrier((early, grad_one))
-    early = lax.all_gather(early, DP, axis=0, tiled=False)
+    early_other = from_other_core(early)
+    args = (adapter_ids, my_core.astype(jnp.int32).reshape(1), early, early_other)
     gate_up_adapter_grad, down_adapter_grad, out_adapter_grad = call(
-        sum_hidden_kernel, "sum_hidden", 1, (adapter_ids, early),
-        [scalars()] + wholes(early),
+        sum_hidden_kernel, "sum_hidden", 1, args, [scalars(), scalars()] + wholes(*args[2:]),
         [(sds((2, LANES, ff_cols), F32), None), (sds((ff_cols, LANES), F32), None), (sds((q_cols, LANES), F32), None)],
         [pltpu.VMEM((adapters, RANK, f3 + q_cols), F32)], 0, 4 * LANES * f3,
     )
@@ -650,11 +680,11 @@
     wide_grad, kv_adapter_grad, q_adapter_grad = call(
         sum_wide_kernel, "sum_wide", 1, (adapter_ids, own_adapter, terms),
         [scalars(), scalars()] + wholes(terms),
-        [(sds((7, own_rows, LANES), F32), None), (sds((2, 1, HD), F32), None), (sds((LANES, q_cols), F32), None)],
+        [(sds((own_rows, 7, LANES), F32), None), (sds((2, 1, HD), F32), None), (sds((LANES, q_cols), F32), None)],
         [pltpu.VMEM((adapters, RANK, LANES + q_cols), F32)], 0, 4 * LANES * f3,
     )
     return (
-        block_output, input_grad, wide_grad, kv_adapter_grad,
+        block_output, input_grad, wide_grad.transpose(1, 0, 2), kv_adapter_grad,
         q_adapter_grad, out_adapter_grad, gate_up_adapter_grad, down_adapter_grad,
     )
 

time: 324 us -> 318 us (0.981)
  waiting for transfers between devices: 127 us -> 110 us
  starting transfers between devices: 37.5 us -> 48.2 us
    all_to_all x2 -> x3, waiting for transfers between devices: 30.6 us -> 13.1 us  [the longest x1 7.44 us: on_device(): terms = lax.all_to_all(payload, PLANES, 0, 0, tiled=True)]
    all_to_all x2 -> x3, starting transfers between devices: 15.9 us -> 22.2 us  [the longest x1 8.14 us: on_device(): terms = lax.all_to_all(payload, PLANES, 0, 0, tiled=True)]
    ppermute x2 -> x5, starting transfers between devices: 0.78 us -> 5.78 us  [from_other_core(): return lax.ppermute(value, 'core', [(0, 1), (1, 0)])]
    pallas_call x8 -> x9, Pallas kernels: 96.5 us -> 97.4 us  [call(): pl.pallas_call(kernel, name=name, grid=(steps,), in_specs=specs, out_spec...]
    unnamed x48 -> x63, local copies, waits for them, and re-layouts: 11.2 us -> 10.4 us
  transfers between devices with their start and end apart: 15 -> 18, of which waited for: 9 -> 11; matrix products, arithmetic and copies ran while one was open for 8% -> 6% of each run, Pallas kernels for 11% -> 11%
where the time goes in v6:
time: 318 us; the launch traced here: 316 us
  waiting for transfers between devices  110 us (35%)
  Pallas kernels  97.4 us (31%)
  starting transfers between devices  48.2 us (15%)
  local copies, waits for them, and re-layouts  19.6 us (6%)
  between operations  15.2 us (5%)
  other arithmetic  12.8 us (4%)
  blocking collectives  12.8 us (4%)
    pallas_call x9, Pallas kernels, call(): pl.pallas_call(kernel, name=name, grid=(steps,), in_specs=specs, out_spec...  97.4 us
    all_gather x1, waiting for transfers between devices, on_device(): weights = lax.all_gather(pack, ALL, axis=0, tiled=False)  80.7 us
    ppermute x8, starting transfers between devices, moved(): lax.ppermute(value, SEQ, [(c, c + steps) for c in range(parts) if 0 <= c...  20.1 us
    ppermute x8, waiting for transfers between devices, moved(): lax.ppermute(value, SEQ, [(c, c + steps) for c in range(parts) if 0 <= c...  14.4 us
    all_gather x1, blocking collectives, on_device(): b_all = lax.all_gather(b_own, 'tensor', axis=0, tiled=False)  12.8 us
    unnamed x63, local copies, waits for them, and re-layouts  10.4 us
    all_to_all x1, starting transfers between devices, on_device(): terms = lax.all_to_all(payload, PLANES, 0, 0, tiled=True)  8.14 us
    all_to_all x1, starting transfers between devices, on_device(): a_own = lax.all_to_all(wide, ('y', 'x'), 0, 0, tiled=True)  7.58 us
  transfers between devices with their start and end apart: 18, of which 11 were waited for; matrix products, arithmetic and copies ran while one was open for 6% of the time, Pallas kernels for 11%

profile of v6, /device:TPU:1, one launch (start us, length us, event | category | flops | bytes accessed | tf_op | source)
XLA Modules:
  0.0 316.4 jit_solution(3330722005493965896)
XLA Ops:
  16.1 7.6 %all-to-all-start = ((bf16[16,48,384]{2,1,0:T(8,128)(2,1)}), bf16[16,48,384]{2,1,0:T(8,128)(2,1)S(1)}, u32[]{:S(2)}, u32[]{:S(2)}) async-start(bf16[16,48,384]{2,1,0:T(8,128)(2,1)} %fusion.11), calls=%async_computation | async-start | bytes 1179648 | tf_op jit(solution)/shard_map/all_to_all | solution.py:486
  28.6 2.4 fusion.12
  30.9 5.6 %all-to-all-done = bf16[16,48,384]{2,1,0:T(8,128)(2,1)S(1)} async-done(((bf16[16,48,384]{2,1,0:T(8,128)(2,1)}), bf16[16,48,384]{2,1,0:T(8,128)(2,1)S(1)}, u32[]{:S(2)}, u32[]{:S(2)}) %all-to-all-start) | async-done | bytes 589856 | tf_op jit(solution)/shard_map/all_to_all | solution.py:486
  36.6 2.8 collective-permute-start
  42.6 3.4 %keys_values.1 = (bf16[256,1536]{1,0:T(8,128)(2,1)}, bf16[256,128]{1,0:T(8,128)(2,1)}, bf16[256,256]{1,0:T(8,128)(2,1)}) custom-call(bf16[256,1536]{1,0:T(8,128)(2,1)} %x_ref.5, f32[1,1536]{1,0:T(1,128)} %get-tuple-element.112.gain_ref, bf16[1536,384]{1,0:T(8,128)(2,1)} %bitcast.66, bf16[1536,384]{1,0:T(8,128)(2,1)} %bitcast.67, bf16[1536,384]{1,0:T(8,128)(2,1)} %bitcast.68, ...), custom_call_target="tpu_custom_call" | custom-call | flops 301989888 | bytes 2359296 | tf_op jit(solution)/shard_map/keys_values/pallas_call | solution.py:423
  47.5 6.1 %collective-permute-start.2 = (bf16[256,256]{1,0:T(8,128)(2,1)}, bf16[256,256]{1,0:T(8,128)(2,1)S(1)}, u32[]{:S(2)}, u32[]{:S(2)}) collective-permute-start(bf16[256,256]{1,0:T(8,128)(2,1)} %get-tuple-element.56), channel_id=1, source_target_pairs={{0,3},{1,4},{2,5},{3,6},{4,7},{8,11},{9,12},{10,13},{11,14},{12,15... | collective-permute-start | bytes 393224 | tf_op jit(solution)/shard_map/ppermute | solution.py:547
  59.5 7.4 %collective-permute-done.3 = bf16[256,256]{1,0:T(8,128)(2,1)S(1)} collective-permute-done((bf16[256,256]{1,0:T(8,128)(2,1)}, bf16[256,256]{1,0:T(8,128)(2,1)S(1)}, u32[]{:S(2)}, u32[]{:S(2)}) %collective-permute-start.3) | collective-permute-done | bytes 131104 | tf_op jit(solution)/shard_map/ppermute | solution.py:547
  69.1 12.8 %all-gather.1 = bf16[64,4224]{1,0:T(8,128)(2,1)S(1)} all-gather(bf16[16,4224]{1,0:T(8,128)(2,1)S(1)} %constant_dynamic-update-slice_fusion), channel_id=3, replica_groups=mesh['y'=4,'x'=4,'core'=2,'tensor'=4] {'tensor'}, dimensions={0}, use_global_device_ids=true | all-gather | bytes 675840 | tf_op jit(solution)/shard_map/all_gather | solution.py:552
  83.7 2.4 fusion.5.b_ref
  86.2 80.7 %all-gather.4.cloned.1.call-done = bf16[6144,4224]{1,0:T(8,128)(2,1)} async-done(((bf16[48,4224]{1,0:T(8,128)(2,1)}), bf16[6144,4224]{1,0:T(8,128)(2,1)}) %all-gather.4.cloned.1.call-update) | async-done | bytes 51904528 | tf_op jit(solution)/shard_map/all_gather | solution.py:473
  166.8 18.8 %attention.1 = (bf16[256,1536]{1,0:T(8,128)(2,1)}, bf16[256,1536]{1,0:T(8,128)(2,1)}, bf16[4,1280,768]{2,1,0:T(8,128)(2,1)}, f32[4,8,768]{2,1,0:T(8,128)}, f32[2...) custom-call(bf16[1280,256]{1,0:T(8,128)(2,1)} %copy-done.4, ...), custom_call_target="tpu_custom_call" | custom-call | flops 4429185024 | bytes 9437184 | tf_op jit(solution)/shard_map/attention/pallas_call | solution.py:423
  185.7 39.0 %feed_forward.1 = (bf16[256,1536]{1,0:T(8,128)(2,1)}, f32[256,1536]{1,0:T(8,128)}, bf16[256,1536]{1,0:T(8,128)(2,1)}, f32[128,1536]{1,0:T(8,128)}, bf16[256,128]...) custom-call(f32[256,1536]{1,0:T(8,128)} %get-tuple-element.62.res_ref, ...), custom_call_target="tpu_custom_call" | custom-call | flops 21743271936 | bytes 42467328 | tf_op jit(solution)/shard_map/feed_forward/pallas_call | solution.py:423
  226.5 20.2 %attention_back.1 = (bf16[256,256]{1,0:T(8,128)(2,1)}, bf16[256,256]{1,0:T(8,128)(2,1)}, bf16[256,256]{1,0:T(8,128)(2,1)}, bf16[256,256]{1,0:T(8,128)(2,1)}, bf1...) custom-call(bf16[1280,256]{1,0:T(8,128)(2,1)} %copy-done.4, ...), custom_call_target="tpu_custom_call" | custom-call | flops 6442450944 | bytes 9437184 | tf_op jit(solution)/shard_map/attention_back/pallas_call | solution.py:423
  251.3 6.5 %all-to-all-start.1 = ((bf16[16,16,1920]{2,1,0:T(8,128)(2,1)}), bf16[16,16,1920]{2,1,0:T(8,128)(2,1)S(1)}, u32[]{:S(2)}, u32[]{:S(2)}) async-start(bf16[16,16,1920]{2,1,0:T(8,128)(2,1)} %broadcast_in_dim.40), calls=%async_computation.2 | async-start | bytes 1966080 | tf_op jit(solution)/shard_map/all_to_all | solution.py:633
  257.8 2.8 collective-permute-start.5
  260.6 2.8 collective-permute-start.6
  266.6 2.5 collective-permute-done.6.back2_ref
  271.9 3.3 %shared_back.1 = (bf16[800,128]{1,0:T(8,128)(2,1)}, bf16[800,128]{1,0:T(8,128)(2,1)}, bf16[256,128]{1,0:T(8,128)(2,1)}, bf16[256,128]{1,0:T(8,128)(2,1)}, bf16[256,128]{1,0:T(8,128)(2,1)}) custom-call(s32[1]{0:T(128)} %bitcast.32.core_ref, bf16[256,1536]{1,0:T(8,128)(2,1)} %get-tuple-element.58.n1_ref, bf16[256,128]{1,0:T(8,128)(2,1)} %get-tuple-element.59.r1_ref, ...), custom_call_target="tpu_custom_call" | custom-call | flops 201326592 | bytes 2359296 | tf_op jit(solution)/shard_map/shared_back/pallas_call | solution.py:423
  278.4 2.2 payload.1
  280.6 8.1 %all-to-all-start.2 = ((bf16[64,16,512]{2,1,0:T(8,128)(2,1)}), bf16[64,16,512]{2,1,0:T(8,128)(2,1)S(1)}, u32[]{:S(2)}, u32[]{:S(2)}) async-start(bf16[64,16,512]{2,1,0:T(8,128)(2,1)} %payload.1), calls=%async_computation.3 | async-start | bytes 2097152 | tf_op jit(solution)/shard_map/all_to_all | solution.py:660
  289.5 4.9 %input_gradient.1 = f32[256,1536]{1,0:T(8,128)} custom-call(bf16[256,1536]{1,0:T(8,128)(2,1)} %x_ref.5, f32[1,1536]{1,0:T(1,128)} %get-tuple-element.112.gain_ref, bf16[1536,384]{1,0:T(8,128)(2,1)} %bitcast.71, bf16[1536,384]{1,0:T(8,128)(2,1)} %bitcast.72, bf16[1536,384]{1,0:T(8,128)(2,1)} %bitcast.73, bf16[256,128]{1,0:T(8,128)(2,1)} %get-tuple-element.89.gk_ref, ...), custom_call_target="tpu_custom_call" | custom-call | flops 301989888 | bytes 6291456 | tf_op jit(solution)/shard_map/input_gradient/pallas_call | solution.py:423
  295.4 3.5 %sum_hidden.1 = (f32[2,128,1152]{2,1,0:T(8,128)}, f32[1152,128]{1,0:T(8,128)}, f32[384,128]{1,0:T(8,128)}) custom-call(s32[16]{0:T(128)} %ids_ref.3, s32[1]{0:T(128)} %bitcast.32.core_ref, bf16[16,16,1920]{2,1,0:T(8,128)(2,1)} %copy-done.3, bf16[16,16,1920]{2,1,0:T(8,128)(2,1)} %copy-done.5), custom_call_target="tpu_custom_call" | custom-call | bytes 1769472 | tf_op jit(solution)/shard_map/sum_hidden/pallas_call | solution.py:423
  298.9 7.4 %all-to-all-done.2 = bf16[64,16,512]{2,1,0:T(8,128)(2,1)S(1)} async-done(((bf16[64,16,512]{2,1,0:T(8,128)(2,1)}), bf16[64,16,512]{2,1,0:T(8,128)(2,1)S(1)}, u32[]{:S(2)}, u32[]{:S(2)}) %all-to-all-start.2) | async-done | bytes 1048608 | tf_op jit(solution)/shard_map/all_to_all | solution.py:660
  307.3 2.2 sum_wide.1
  (127 shorter events, 45.8 us)
Async XLA Ops:
  7.2 17.9 %copy-start = (bf16[1152,128]{1,0:T(8,128)(2,1)S(1)}, bf16[1152,128]{1,0:T(8,128)(2,1)}, u32[]{:S(2)}) copy-start(bf16[1152,128]{1,0:T(8,128)(2,1)} %param.31) | copy-start | bytes 884740
  7.2 159.6 %all-gather.4.cloned.1.call-start = ((), (), s32[]{:S(2)}) async-start(), calls=%async_computation.5 | async-start | bytes 52310016 | tf_op jit(solution)/shard_map/all_gather | solution.py:473
  16.1 20.5 %all-to-all-start = ((bf16[16,48,384]{2,1,0:T(8,128)(2,1)}), bf16[16,48,384]{2,1,0:T(8,128)(2,1)S(1)}, u32[]{:S(2)}, u32[]{:S(2)}) async-start(bf16[16,48,384]{2,1,0:T(8,128)(2,1)} %fusion.11), calls=%async_computation | async-start | bytes 1179648 | tf_op jit(solution)/shard_map/all_to_all | solution.py:486
  23.7 223.1 %reduce-scatter.2.cloned.1.call-start = ((), (), s32[]{:S(2)}) async-start(), calls=%async_computation.4 | async-start | bytes 614400 | tf_op jit(solution)/shard_map/reduce_scatter | solution.py:606
  36.6 4.8 %collective-permute-start = (bf16[16,48,384]{2,1,0:T(8,128)(2,1)S(1)}, bf16[16,48,384]{2,1,0:T(8,128)(2,1)S(1)}, u32[]{:S(2)}, u32[]{:S(2)}) collective-permute-start(bf16[16,48,384]{2,1,0:T(8,128)(2,1)S(1)} %all-to-all-done), channel_id=1, source_target_pairs={{0,4},{4,0},{1,5},{5,1},{2,6},{6,2},{3,7},{7,3},{8,12},{12,8},{9,1... | collective-permute-start | bytes 1769480 | tf_op jit(solution)/shard_map/ppermute | solution.py:484
  45.9 23.1 %copy-start.13 = (bf16[256,256]{1,0:T(8,128)(2,1)S(1)}, bf16[256,256]{1,0:T(8,128)(2,1)}, u32[]{:S(2)}) copy-start(bf16[256,256]{1,0:T(8,128)(2,1)} %get-tuple-element.56) | copy-start | bytes 393220
  45.9 13.2 %collective-permute-start.1 = (bf16[256,256]{1,0:T(8,128)(2,1)}, bf16[256,256]{1,0:T(8,128)(2,1)S(1)}, u32[]{:S(2)}, u32[]{:S(2)}) collective-permute-start(bf16[256,256]{1,0:T(8,128)(2,1)} %get-tuple-element.56), channel_id=1, source_target_pairs={{0,4},{1,5},{2,6},{3,7},{8,12},{9,13},{10,14},{11,15},{16,20},{17,... | collective-permute-start | bytes 393224 | tf_op jit(solution)/shard_map/ppermute | solution.py:547
  47.5 12.0 %collective-permute-start.2 = (bf16[256,256]{1,0:T(8,128)(2,1)}, bf16[256,256]{1,0:T(8,128)(2,1)S(1)}, u32[]{:S(2)}, u32[]{:S(2)}) collective-permute-start(bf16[256,256]{1,0:T(8,128)(2,1)} %get-tuple-element.56), channel_id=1, source_target_pairs={{0,3},{1,4},{2,5},{3,6},{4,7},{8,11},{9,12},{10,13},{11,14},{12,15... | collective-permute-start | bytes 393224 | tf_op jit(solution)/shard_map/ppermute | solution.py:547
  55.3 11.6 %collective-permute-start.3 = (bf16[256,256]{1,0:T(8,128)(2,1)}, bf16[256,256]{1,0:T(8,128)(2,1)S(1)}, u32[]{:S(2)}, u32[]{:S(2)}) collective-permute-start(bf16[256,256]{1,0:T(8,128)(2,1)} %get-tuple-element.56), channel_id=1, source_target_pairs={{0,2},{1,3},{2,4},{3,5},{4,6},{5,7},{8,10},{9,11},{10,12},{11,13},... | collective-permute-start | bytes 393224 | tf_op jit(solution)/shard_map/ppermute | solution.py:547
  57.2 11.9 %collective-permute-start.4 = (bf16[256,256]{1,0:T(8,128)(2,1)}, bf16[256,256]{1,0:T(8,128)(2,1)S(1)}, u32[]{:S(2)}, u32[]{:S(2)}) collective-permute-start(bf16[256,256]{1,0:T(8,128)(2,1)} %get-tuple-element.56), channel_id=1, source_target_pairs={{0,1},{1,2},{2,3},{3,4},{4,5},{5,6},{6,7},{8,9},{9,10},{10,11},{11... | collective-permute-start | bytes 393224 | tf_op jit(solution)/shard_map/ppermute | solution.py:547
  247.6 1.8 collective-permute-start.9
  248.5 14.9 %copy-start.21 = (bf16[256,256]{1,0:T(8,128)(2,1)S(1)}, bf16[256,256]{1,0:T(8,128)(2,1)}, u32[]{:S(2)}) copy-start(bf16[256,256]{1,0:T(8,128)(2,1)} %get-tuple-element.76) | copy-start | bytes 393220
  248.5 16.8 %copy-start.20 = (bf16[256,256]{1,0:T(8,128)(2,1)S(1)}, bf16[256,256]{1,0:T(8,128)(2,1)}, u32[]{:S(2)}) copy-start(bf16[256,256]{1,0:T(8,128)(2,1)} %get-tuple-element.77) | copy-start | bytes 393220
  251.3 23.9 %all-to-all-start.1 = ((bf16[16,16,1920]{2,1,0:T(8,128)(2,1)}), bf16[16,16,1920]{2,1,0:T(8,128)(2,1)S(1)}, u32[]{:S(2)}, u32[]{:S(2)}) async-start(bf16[16,16,1920]{2,1,0:T(8,128)(2,1)} %broadcast_in_dim.40), calls=%async_computation.2 | async-start | bytes 1966080 | tf_op jit(solution)/shard_map/all_to_all | solution.py:633
  257.8 18.7 %copy-start.15 = (bf16[4,16,384]{2,1,0:T(8,128)(2,1)S(1)}, bf16[4,16,384]{2,1,0:T(8,128)(2,1)}, u32[]{:S(2)}) copy-start(bf16[4,16,384]{2,1,0:T(8,128)(2,1)} %get-tuple-element.87.q_ref) | copy-start | bytes 147460
  257.8 8.8 %collective-permute-start.5 = (bf16[256,256]{1,0:T(8,128)(2,1)S(1)}, bf16[256,256]{1,0:T(8,128)(2,1)S(1)}, u32[]{:S(2)}, u32[]{:S(2)}) collective-permute-start(bf16[256,256]{1,0:T(8,128)(2,1)S(1)} %copy-done.23), channel_id=1, source_target_pairs={{1,0},{2,1},{3,2},{4,3},{5,4},{6,5},{7,6},{9,8},{10,9},{11,10},{12... | collective-permute-start | bytes 393224 | tf_op jit(solution)/shard_map/ppermute | solution.py:547
  260.6 8.5 %collective-permute-start.6 = (bf16[256,256]{1,0:T(8,128)(2,1)S(1)}, bf16[256,256]{1,0:T(8,128)(2,1)S(1)}, u32[]{:S(2)}, u32[]{:S(2)}) collective-permute-start(bf16[256,256]{1,0:T(8,128)(2,1)S(1)} %copy-done.22), channel_id=1, source_target_pairs={{2,0},{3,1},{4,2},{5,3},{6,4},{7,5},{10,8},{11,9},{12,10},{13,11},... | collective-permute-start | bytes 393224 | tf_op jit(solution)/shard_map/ppermute | solution.py:547
  263.4 7.8 %collective-permute-start.7 = (bf16[256,256]{1,0:T(8,128)(2,1)S(1)}, bf16[256,256]{1,0:T(8,128)(2,1)S(1)}, u32[]{:S(2)}, u32[]{:S(2)}) collective-permute-start(bf16[256,256]{1,0:T(8,128)(2,1)S(1)} %copy-done.21), channel_id=1, source_target_pairs={{3,0},{4,1},{5,2},{6,3},{7,4},{11,8},{12,9},{13,10},{14,11},{15,12... | collective-permute-start | bytes 393224 | tf_op jit(solution)/shard_map/ppermute | solution.py:547
  265.3 5.9 %collective-permute-start.8 = (bf16[256,256]{1,0:T(8,128)(2,1)S(1)}, bf16[256,256]{1,0:T(8,128)(2,1)S(1)}, u32[]{:S(2)}, u32[]{:S(2)}) collective-permute-start(bf16[256,256]{1,0:T(8,128)(2,1)S(1)} %copy-done.20), channel_id=1, source_target_pairs={{4,0},{5,1},{6,2},{7,3},{12,8},{13,9},{14,10},{15,11},{20,16},{21,... | collective-permute-start | bytes 393224 | tf_op jit(solution)/shard_map/ppermute | solution.py:547
  275.2 2.6 collective-permute-start.10
  276.5 1.2 collective-permute-start.11
  280.6 25.7 %all-to-all-start.2 = ((bf16[64,16,512]{2,1,0:T(8,128)(2,1)}), bf16[64,16,512]{2,1,0:T(8,128)(2,1)S(1)}, u32[]{:S(2)}, u32[]{:S(2)}) async-start(bf16[64,16,512]{2,1,0:T(8,128)(2,1)} %payload.1), calls=%async_computation.3 | async-start | bytes 2097152 | tf_op jit(solution)/shard_map/all_to_all | solution.py:660
  288.8 5.6 %collective-permute-start.12 = (bf16[16,16,1920]{2,1,0:T(8,128)(2,1)S(1)}, bf16[16,16,1920]{2,1,0:T(8,128)(2,1)S(1)}, u32[]{:S(2)}, u32[]{:S(2)}) collective-permute-start(bf16[16,16,1920]{2,1,0:T(8,128)(2,1)S(1)} %all-to-all-done.1.own_ref), channel_id=1, source_target_pairs={{0,4},{4,0},{1,5},{5,1},{2,6},{6,2},{3,7},{7,3},{8,12},{12,8},{9,1... | collective-permute-start | bytes 2949128 | tf_op jit(solution)/shard_map/ppermute | solution.py:484
  289.5 20.0 %copy-start.1 = (bf16[1152,128]{1,0:T(8,128)(2,1)S(1)}, bf16[1152,128]{1,0:T(8,128)(2,1)}, u32[]{:S(2)}) copy-start(bf16[1152,128]{1,0:T(8,128)(2,1)} %param.31) | copy-start | bytes 884740
  (18 other events, 88.7 us)
Sparse Core Ops, SparseCore 0:
  12.5 154.3 all-gather.3
  226.6 18.6 reduce-scatter.1

commit v7 on v6

--- a/solution.py
+++ b/solution.py
@@ -79,15 +79,35 @@
     kv_ref[:, HD:] = (mm(n1, wv_ref[...]) + mm(r1, bkv_ref[1])).astype(BF)
 
 
-def attn_kernel(
-    kv_ref, kseg_ref, qseg_ref, n1_ref, r1_ref, cos_ref, sin_ref, x_ref, gain_ref, a_ref,
-    wq_ref, bq_ref, wo_ref, bo_ref,
-    q_ref, mixed_ref, p_ref, inv_ref, res_ref, n2_ref, r2_ref, ro_ref,
-    bias_ref, s_ref, vt_ref, acc_ref, rank_ref, qs_ref,
+def forward_kernel(
+    kv_ref, kseg_ref, qseg_ref, n1_ref, r1_ref, cos_ref, sin_ref, x_ref, cot_ref, gain_ref, a_ref,
+    wq_ref, bq_ref, wo_ref, bo_ref, b_ref, w_ref,
+    q_ref, mixed_ref, p_ref, inv_ref, out_ref, gres_ref, gb_ref, wide_ref, gro_ref, early_ref,
+    bias_ref, s_ref, vt_ref, ffn_ref, g2_ref, ro_ref, rd_ref, gr_ref, qs_ref,
+    all_mixed_ref, res_ref, n2_ref, r2_ref, r2t_ref, grd_ref, grdt_ref, wv_ref, sems,
 ):
     step = pl.program_id(0)
+    slots, tensor_count = wv_ref.shape[0], w_ref.shape[1]
+    steps = pl.num_programs(0) - tensor_count
     rows = q_ref.shape[0]
     chunks = kv_ref.shape[0] // rows
+    ff = b_ref.shape[2] // 3
+    part_cols = ff // tensor_count
+
+    def copies(at, to):
+        moves = []
+        for kind in (2, 0, 1):
+            for t in range(tensor_count):
+                source = pl.multiple_of((kind * steps + at) * part_cols, LANES)
+                target = (kind * tensor_count + t) * part_cols
+                moves.append(
+                    pltpu.make_async_copy(
+                        w_ref.at[:, t, :, pl.ds(source, part_cols)],
+                        wv_ref.at[to, :, :, pl.ds(target, part_cols)],
+                        sems.at[to, len(moves)],
+                    )
+                )
+        return moves
 
     @pl.when(step == 0)
     def _():
@@ -96,151 +116,127 @@
         allowed = (key >= query) & (key <= query + WINDOW) & (kseg_ref[...] == qseg_ref[...])
         bias_ref[...] = jnp.where(allowed, 0.0, MASKED)
         vt_ref[...] = turned(kv_ref[:, HD:])
-        acc_ref[...] = jnp.zeros_like(acc_ref)
-        rank_ref[...] = jnp.zeros_like(rank_ref)
-
-    lin = mm(n1_ref[...], flat(wq_ref)) + mm(r1_ref[...], bq_ref[0])
-    heads = q_ref.shape[1] // HD
-    for h in range(heads):
-        part = slice(h * HD, (h + 1) * HD)
-        query = (rope(lin[:, part], cos_ref[...], sin_ref[...]) * (SCALE * LOG2E)).astype(BF)
-        q_ref[:, part] = query
-        qs_ref[h * rows : (h + 1) * rows] = query
-    queries = qs_ref[...]
-    top = jnp.full((1, heads * rows), MASKED, F32)
-    for c in range(chunks):
-        span = slice(c * rows, (c + 1) * rows)
-        s = mm_nt(kv_ref[span, :HD], queries)
-        bias = bias_ref[span]
-        s = jnp.concatenate([s[:, h * rows : (h + 1) * rows] + bias for h in range(heads)], axis=1)
-        s_ref[span] = s
-        top = jnp.maximum(top, jnp.max(s, axis=0, keepdims=True))
-    total = jnp.zeros((1, heads * rows), F32)
-    for c in range(chunks):
-        span = slice(c * rows, (c + 1) * rows)
-        p = jnp.exp2(s_ref[span] - top)
-        total = total + jnp.sum(p, axis=0, keepdims=True)
-        p_ref[0, span] = p.astype(BF)
-    inv = 1.0 / total
-    inv_ref[0, 0:1] = inv
-    out = mm(vt_ref[...], p_ref[0]) * inv
-    for h in range(heads):
-        mixed_ref[:, h * HD : (h + 1) * HD] = out[:, h * rows : (h + 1) * rows].T.astype(BF)
-
-    mixed = mixed_ref[...]
-    acc_ref[...] += mm_nt(mixed, flat(wo_ref))
-    rank_ref[...] += mm_nt(mixed, bo_ref[0])
-
-    @pl.when(step == pl.num_programs(0) - 1)
-    def _():
-        ro = rank_ref[...].astype(BF)
-        ro_ref[...] = ro
-        res = x_ref[...].astype(F32) + (acc_ref[...] + mm_nt(ro, a_ref[...]))
+        ffn_ref[...] = jnp.zeros_like(ffn_ref)
+        ro_ref[...] = jnp.zeros_like(ro_ref)
+
+    @pl.when((step >= 1) & (step < 1 + slots))
+    def _():
+        for copy in copies(step - 1, step - 1):
+            copy.start()
+
+    @pl.when(step < tensor_count)
+    def _():
+        lin = mm(n1_ref[...], flat(wq_ref)) + mm(r1_ref[...], bq_ref[0])
+        heads = q_ref.shape[1] // HD
+        for h in range(heads):
+            part = slice(h * HD, (h + 1) * HD)
+            query = (rope(lin[:, part], cos_ref[...], sin_ref[...]) * (SCALE * LOG2E)).astype(BF)
+            q_ref[:, part] = query
+            qs_ref[h * rows : (h + 1) * rows] = query
+        queries = qs_ref[...]
+        top = jnp.full((1, heads * rows), MASKED, F32)
+        for c in range(chunks):
+            span = slice(c * rows, (c + 1) * rows)
+            s = mm_nt(kv_ref[span, :HD], queries)
+            bias = bias_ref[span]
+            s = jnp.concatenate([s[:, h * rows : (h + 1) * rows] + bias for h in range(heads)], axis=1)
+            s_ref[span] = s
+            top = jnp.maximum(top, jnp.max(s, axis=0, keepdims=True))
+        total = jnp.zeros((1, heads * rows), F32)
+        for c in range(chunks):
+            span = slice(c * rows, (c + 1) * rows)
+            p = jnp.exp2(s_ref[span] - top)
+            total = total + jnp.sum(p, axis=0, keepdims=True)
+            p_ref[0, span] = p.astype(BF)
+        inv = 1.0 / total
+        inv_ref[0, 0:1] = inv
+        out = mm(vt_ref[...], p_ref[0]) * inv
+        for h in range(heads):
+            mixed_ref[:, h * HD : (h + 1) * HD] = out[:, h * rows : (h + 1) * rows].T.astype(BF)
+        mixed = mixed_ref[...]
+        all_mixed_ref[step] = mixed
+        ffn_ref[...] += mm_nt(mixed, flat(wo_ref))
+        ro_ref[...] += mm_nt(mixed, bo_ref[0])
+
+    @pl.when(step == tensor_count - 1)
+    def _():
+        res = x_ref[...].astype(F32) + (ffn_ref[...] + mm_nt(ro_ref[...].astype(BF), a_ref[...]))
         res_ref[...] = res
         n2 = rms(res, gain_ref[...]).astype(BF)
         n2_ref[...] = n2
-        r2_ref[...] = mm(n2, a_ref[...]).astype(BF)
-
-
-def ffn_kernel(
-    res_ref, n2_ref, r2_ref, cot_ref, gain_ref, mixed_ref, ro_ref, a_ref, b_ref, w_ref,
-    out_ref, gres_ref, gb_ref, wide_ref, gro_ref, gbo_ref, gbh_ref,
-    ffn_ref, g2_ref, rd_ref, gr_ref, r2t_ref, grd_ref, grdt_ref, wv_ref, sems,
-):
-    step = pl.program_id(0)
-    steps = pl.num_programs(0)
-    tensor_count = w_ref.shape[1]
-    ff = b_ref.shape[2] // 3
-    part = ff // tensor_count
-    slot = lax.rem(step, 2)
-
-    def copies(at, to):
-        moves = []
-        for kind in (2, 0, 1):
-            for t in range(tensor_count):
-                source = pl.multiple_of((kind * steps + at) * part, LANES)
-                target = (kind * tensor_count + t) * part
-                moves.append(
-                    pltpu.make_async_copy(
-                        w_ref.at[:, t, :, pl.ds(source, part)],
-                        wv_ref.at[to, :, :, pl.ds(target, part)],
-                        sems.at[to, len(moves)],
-                    )
-                )
-        return moves
-
-    @pl.when(step == 0)
-    def _():
-        for copy in copies(0, 0):
-            copy.start()
+        r2 = mm(n2, a_ref[...]).astype(BF)
+        r2_ref[...] = r2
+        r2t_ref[...] = turned(r2)
+        grd = mm(cot_ref[...], a_ref[...]).astype(BF)
+        grd_ref[...] = grd
+        grdt_ref[...] = turned(grd)
         ffn_ref[...] = jnp.zeros_like(ffn_ref)
         g2_ref[...] = jnp.zeros_like(g2_ref)
         rd_ref[...] = jnp.zeros_like(rd_ref)
         gr_ref[...] = jnp.zeros_like(gr_ref)
-        r2t_ref[...] = turned(r2_ref[...])
-        grd = mm(cot_ref[...], a_ref[...]).astype(BF)
-        grd_ref[...] = grd
-        grdt_ref[...] = turned(grd)
-
-    @pl.when(step < steps - 1)
-    def _():
-        for copy in copies(step + 1, 1 - slot):
-            copy.start()
-
-    n2, r2, cot = n2_ref[...], r2_ref[...], cot_ref[...]
-    b_gu, b_d = b_ref[0, :, : 2 * ff], b_ref[0, :, 2 * ff :]
-    arrivals = copies(step, slot)
-    rows_of_weight = wv_ref.shape[1] * wv_ref.shape[2]
-    for copy in arrivals[:tensor_count]:
-        copy.wait()
-    w_d = wv_ref[slot, :, :, 2 * ff :].reshape(rows_of_weight, ff)
-    grad_hidden = (mm(cot, w_d) + mm(grd_ref[...], b_d)).astype(BF).astype(F32)
-    for copy in arrivals[tensor_count:]:
-        copy.wait()
-    w_gu = wv_ref[slot, :, :, : 2 * ff].reshape(rows_of_weight, 2 * ff)
-    lin = mm(n2, w_gu) + mm(r2, b_gu)
-    gate, up = lin[:, :ff], lin[:, ff:]
-    square = gate * gate
-    th = jnp.tanh(GELU_C * (gate + GELU_A * square * gate))
-    half = 0.5 * (1.0 + th)
-    act = gate * half
-    slope = half + 0.5 * gate * (1.0 - th * th) * (GELU_C * (1.0 + 3.0 * GELU_A * square))
-    hidden = (act * up).astype(BF)
-    grad_gate = (grad_hidden * up * slope).astype(BF)
-    grad_up = (grad_hidden * act).astype(BF)
-    grads = jnp.concatenate([grad_gate, grad_up], axis=1)
-    ffn_ref[...] += mm_nt(hidden, w_d)
-    rd_ref[...] += mm_nt(hidden, b_d)
-    g2_ref[...] += mm_nt(grads, w_gu)
-    gr_ref[...] += mm_nt(grads, b_gu)
-    terms = (
-        mm(r2t_ref[rows_of(SLOT_G)], grad_gate), mm(r2t_ref[rows_of(SLOT_U)], grad_up),
-        mm(grdt_ref[rows_of(SLOT_D)], hidden),
-    )
-    for kind, term in enumerate(terms):
-        target = pl.multiple_of((kind * steps + step) * part, LANES)
-        for t in range(tensor_count):
-            gbh_ref[t, :, pl.ds(target, part)] = term[:, t * part : (t + 1) * part].astype(BF)
-
-    @pl.when(step == steps - 1)
-    def _():
-        rd = rd_ref[...].astype(BF)
-        gr = gr_ref[...].astype(BF)
-        res = res_ref[...]
-        out_ref[...] = (res + (ffn_ref[...] + mm_nt(rd, a_ref[...]))).astype(BF)
-        grad_two = g2_ref[...] + mm_nt(gr, a_ref[...])
-        grad_res = cot_ref[...].astype(F32) + rms_back(res, gain_ref[...], grad_two)
+
+    @pl.when(step >= tensor_count)
+    def _():
+        at = step - tensor_count
+        slot = lax.rem(at, slots)
+
+        @pl.when((at >= 1) & (at + slots - 1 < steps))
+        def _():
+            for copy in copies(at + slots - 1, lax.rem(at + slots - 1, slots)):
+                copy.start()
+
+        n2, r2, cot = n2_ref[...], r2_ref[...], cot_ref[...]
+        b_gu, b_d = b_ref[0, :, : 2 * ff], b_ref[0, :, 2 * ff :]
+        arrivals = copies(at, slot)
+        weight_rows = wv_ref.shape[1] * wv_ref.shape[2]
+        for copy in arrivals[:tensor_count]:
+            copy.wait()
+        w_d = wv_ref[slot, :, :, 2 * ff :].reshape(weight_rows, ff)
+        grad_hidden = (mm(cot, w_d) + mm(grd_ref[...], b_d)).astype(BF).astype(F32)
+        for copy in arrivals[tensor_count:]:
+            copy.wait()
+        w_gu = wv_ref[slot, :, :, : 2 * ff].reshape(weight_rows, 2 * ff)
+        lin = mm(n2, w_gu) + mm(r2, b_gu)
+        gate, up = lin[:, :ff], lin[:, ff:]
+        square = gate * gate
+        th = jnp.tanh(GELU_C * (gate + GELU_A * square * gate))
+        half = 0.5 * (1.0 + th)
+        act = gate * half
+        slope = half + 0.5 * gate * (1.0 - th * th) * (GELU_C * (1.0 + 3.0 * GELU_A * square))
+        hidden = (act * up).astype(BF)
+        grad_gate = (grad_hidden * up * slope).astype(BF)
+        grad_up = (grad_hidden * act).astype(BF)
+        grads = jnp.concatenate([grad_gate, grad_up], axis=1)
+        ffn_ref[...] += mm_nt(hidden, w_d)
+        rd_ref[...] += mm_nt(hidden, b_d)
+        g2_ref[...] += mm_nt(grads, w_gu)
+        gr_ref[...] += mm_nt(grads, b_gu)
+        terms = (
+            mm(r2t_ref[rows_of(SLOT_G)], grad_gate), mm(r2t_ref[rows_of(SLOT_U)], grad_up),
+            mm(grdt_ref[rows_of(SLOT_D)], hidden),
+        )
+        for kind, term in enumerate(terms):
+            target = pl.multiple_of((kind * steps + at) * part_cols, LANES)
+            for t in range(tensor_count):
+                early_ref[t, :, pl.ds(target, part_cols)] = term[:, t * part_cols : (t + 1) * part_cols].astype(BF)
+
+    @pl.when(step == tensor_count + steps - 1)
+    def _():
+        res, n2, cot = res_ref[...], n2_ref[...], cot_ref[...]
+        out_ref[...] = (res + (ffn_ref[...] + mm_nt(rd_ref[...].astype(BF), a_ref[...]))).astype(BF)
+        grad_two = g2_ref[...] + mm_nt(gr_ref[...].astype(BF), a_ref[...])
+        grad_res = cot.astype(F32) + rms_back(res, gain_ref[...], grad_two)
         gres_ref[...] = grad_res
         grad_branch = grad_res.astype(BF)
         gb_ref[...] = grad_branch
         gro = mm(grad_branch, a_ref[...])
         gro_ref[...] = gro.astype(BF)
         grot = gro.T[rows_of(SLOT_O)].astype(BF)
-        cols = gbo_ref.shape[2]
-        for t in range(gbo_ref.shape[0]):
-            gbo_ref[t] = mm(grot, mixed_ref[:, t * cols : (t + 1) * cols]).astype(BF)
+        first = 3 * steps * part_cols
+        for t in range(tensor_count):
+            early_ref[t, :, first:] = mm(grot, all_mixed_ref[t]).astype(BF)
         wide = mm(gr_ref[...].T.astype(BF), n2) + mm(rd_ref[...].T.astype(BF), cot)
-        wide_ref[...] = wide + mm(turned(ro_ref[...]), grad_branch)
+        wide_ref[...] = wide + mm(ro_ref[...].T.astype(BF), grad_branch)
 
 
 def attn_back_kernel(
@@ -356,13 +352,11 @@
     grad_ref[...] = gres_ref[...] + rms_back(x, gain_ref[...], g1)
 
 
-def sum_hidden_kernel(ids_ref, core_ref, own_ref, other_ref, gu_ref, down_ref, out_ref, acc_ref):
+def sum_hidden_kernel(ids_ref, terms_ref, gu_ref, down_ref, out_ref, acc_ref):
     acc_ref[...] = jnp.zeros_like(acc_ref)
+    for s in range(terms_ref.shape[0] // 2):
+        acc_ref[ids_ref[s]] += terms_ref[2 * s].astype(F32) + terms_ref[2 * s + 1].astype(F32)
     adapters, rank, cols = acc_ref.shape
-    for core, terms_ref in ((core_ref[0], own_ref), (1 - core_ref[0], other_ref)):
-        part = pl.ds(pl.multiple_of(core * (cols // 2), LANES), cols // 2)
-        for s in range(terms_ref.shape[0]):
-            acc_ref[ids_ref[s], :, part] += terms_ref[s].astype(F32)
     ff = gu_ref.shape[2]
 
     def taken(first, last):
@@ -553,7 +547,7 @@
     b_heads = jnp.concatenate(
         [in_slot(b_all[:, :, f3 : f3 + q_cols], SLOT_Q), in_slot(b_all[:, :, f3 + q_cols :], SLOT_O)], axis=2
     )
-    steps = 3
+    steps, slots = ff_cols // LANES, 2
     part_cols = ff_cols // steps
     b_hidden = b_all[:, :, :f3].reshape(tensor_count, RANK, 3, steps, part_cols).transpose(3, 2, 1, 0, 4)
     b_hidden = b_hidden.reshape(steps, 3, RANK, tensor_count * part_cols)
@@ -561,48 +555,46 @@
         [in_slot(b_hidden[:, kind], slot) for kind, slot in enumerate((SLOT_G, SLOT_U, SLOT_D))], axis=2
     )
 
+    heads = q_cols // HD
+    first, last = tensor_count, tensor_count - 1
+
+    def until_last(spec):
+        return pl.BlockSpec(spec.block_shape, lambda t: spec.index_map(jnp.minimum(t, last)))
+
+    p_spec, norm_spec = by_step(span, heads * rows), by_step(8, heads * rows)
+    hidden_spec = pl.BlockSpec(
+        (1, LANES, 3 * tensor_count * part_cols), lambda t: (jnp.maximum(t - first, 0), 0, 0)
+    )
     args = (
-        kv_window, kseg, qseg, normed_one, rank_one, cos, sin, tokens, gain_two, a_all,
-        weights, b_heads, weights, b_heads,
-    )
-    heads = q_cols // HD
-    p_spec, norm_spec = by_step(span, heads * rows), by_step(8, heads * rows)
-    queries, mixed, probs, norms, residual, normed_two, rank_two, rank_out = call(
-        attn_kernel, "attention", tensor_count, args,
-        wholes(*args[:9]) + [a_spec] + head_specs,
+        kv_window, kseg, qseg, normed_one, rank_one, cos, sin, tokens, cotangent, gain_two, a_all,
+        weights, b_heads, weights, b_heads, b_hidden, weights,
+    )
+    (
+        queries, mixed, probs, norms, block_output, grad_residual, grad_branch, wide_ffn, grad_ro, early
+    ) = call(
+        forward_kernel, "forward", tensor_count + steps, args,
+        wholes(*args[:10]) + [a_spec] + [until_last(spec) for spec in head_specs]
+        + [hidden_spec, pl.BlockSpec(memory_space=pl.ANY)],
         [
-            (sds((rows, heads_cols), BF), token_cols), (sds((rows, heads_cols), BF), token_cols),
-            (sds((tensor_count, span, heads * rows), BF), p_spec),
-            (sds((tensor_count, 8, heads * rows), F32), norm_spec),
-            (tok_f32, None), (tok_bf, None), (rank_bf, None), (rank_bf, None),
+            (sds((rows, heads_cols), BF), until_last(token_cols)), (sds((rows, heads_cols), BF), until_last(token_cols)),
+            (sds((tensor_count, span, heads * rows), BF), until_last(p_spec)),
+            (sds((tensor_count, 8, heads * rows), F32), until_last(norm_spec)),
+            (tok_bf, None), (tok_f32, None), (tok_bf, None), (sds((LANES, width), F32), None), (rank_bf, None),
+            (sds((tensor_count, RANK, f3 + q_cols), BF), None),
         ],
         [
             pltpu.VMEM((span, rows), F32), pltpu.VMEM((span, heads * rows), F32), pltpu.VMEM((HD, span), BF),
-            pltpu.VMEM((rows, width), F32), pltpu.VMEM((rows, LANES), F32), pltpu.VMEM((heads * rows, HD), BF),
+            pltpu.VMEM((rows, width), F32), pltpu.VMEM((rows, width), F32), pltpu.VMEM((rows, LANES), F32),
+            pltpu.VMEM((rows, LANES), F32), pltpu.VMEM((rows, LANES), F32), pltpu.VMEM((heads * rows, HD), BF),
+            pltpu.VMEM((tensor_count, rows, q_cols), BF), pltpu.VMEM((rows, width), F32), pltpu.VMEM((rows, width), BF),
+            pltpu.VMEM((rows, LANES), BF), pltpu.VMEM((LANES, rows), BF),
+            pltpu.VMEM((rows, LANES), BF), pltpu.VMEM((LANES, rows), BF),
+            pltpu.VMEM((slots, dp_count, shard_rows, 3 * tensor_count * part_cols), BF),
+            pltpu.SemaphoreType.DMA((slots, 3 * tensor_count)),
         ],
-        4 * rows * heads_cols * (span + width), 4 * width * heads_cols,
-    )
-
-    args = (
-        residual, normed_two, rank_two, cotangent, gain_two, mixed, rank_out, a_all, b_hidden, weights,
-    )
-    block_output, grad_residual, grad_branch, wide_ffn, grad_ro, grad_bo, grad_bh = call(
-        ffn_kernel, "feed_forward", steps, args,
-        wholes(*args[:7]) + [a_spec, by_step(LANES, 3 * tensor_count * part_cols), pl.BlockSpec(memory_space=pl.ANY)],
-        [
-            (tok_bf, None), (tok_f32, None), (tok_bf, None), (sds((LANES, width), F32), None), (rank_bf, None),
-            (sds((tensor_count, RANK, q_cols), BF), None), (sds((tensor_count, RANK, f3), BF), None),
-        ],
-        [
-            pltpu.VMEM((rows, width), F32), pltpu.VMEM((rows, width), F32),
-            pltpu.VMEM((rows, LANES), F32), pltpu.VMEM((rows, LANES), F32),
-            pltpu.VMEM((LANES, rows), BF), pltpu.VMEM((rows, LANES), BF), pltpu.VMEM((LANES, rows), BF),
-            pltpu.VMEM((2, dp_count, shard_rows, 3 * tensor_count * part_cols), BF),
-            pltpu.SemaphoreType.DMA((2, 3 * tensor_count)),
-        ],
-        12 * rows * width * tensor_count * ff_cols, 6 * width * tensor_count * ff_cols,
-    )
-    early = jnp.concatenate([grad_bh, grad_bo], axis=2)
+        4 * rows * heads_cols * (span + width) + 12 * rows * width * tensor_count * ff_cols,
+        4 * width * heads_cols + 6 * width * tensor_count * ff_cols,
+    )
     early = lax.psum_scatter(early, "tensor", scatter_dimension=0, tiled=True).reshape(RANK, -1)
 
     args = (
@@ -625,12 +617,8 @@
         2 * rows * heads_cols * (4 * span + 2 * width), 4 * width * heads_cols,
     )
 
-    half_cols = (f3 + q_cols) // 2
     early, grad_one = lax.optimization_barrier((early, grad_one))
-    early_mine = lax.dynamic_slice_in_dim(early, my_core * half_cols, half_cols, 1)
-    early_theirs = lax.dynamic_slice_in_dim(early, (1 - my_core) * half_cols, half_cols, 1)
-    early = (early_mine.astype(F32) + from_other_core(early_theirs).astype(F32)).astype(BF)
-    early = lax.all_to_all(jnp.broadcast_to(early[None], (seqs, RANK, half_cols)), ("y", "x"), 0, 0, tiled=True)
+    early = lax.all_gather(early, DP, axis=0, tiled=False)
 
     backs = [moved(dkv[reach - d], -d) for d in range(1, reach + 1)]
     chips = dp_count // 2
@@ -649,7 +637,6 @@
     )
     own_rows = width // devices
     planes = chips * tensor_count
-    theirs, early = lax.optimization_barrier((theirs, early))
     other, grad_bq_other = from_other_core(theirs), from_other_core(grad_bq)
     args = (my_core.astype(jnp.int32).reshape(1), mine, other, grad_bq, grad_bq_other)
     (payload,) = call(
@@ -669,10 +656,8 @@
         [(tok_f32, None)], [], 2 * rows * width * 384, 16 * rows * width,
     )
 
-    early_other = from_other_core(early)
-    args = (adapter_ids, my_core.astype(jnp.int32).reshape(1), early, early_other)
     gate_up_adapter_grad, down_adapter_grad, out_adapter_grad = call(
-        sum_hidden_kernel, "sum_hidden", 1, args, [scalars(), scalars()] + wholes(*args[2:]),
+        sum_hidden_kernel, "sum_hidden", 1, (adapter_ids, early), [scalars()] + wholes(early),
         [(sds((2, LANES, ff_cols), F32), None), (sds((ff_cols, LANES), F32), None), (sds((q_cols, LANES), F32), None)],
         [pltpu.VMEM((adapters, RANK, f3 + q_cols), F32)], 0, 4 * LANES * f3,
     )

time: 318 us -> 311 us (0.978)
  waiting for transfers between devices: 110 us -> 121 us
  starting transfers between devices: 48.2 us -> 40.1 us
    all_to_all x1, waiting for transfers between devices: 7.44 us -> 16.9 us  [on_device(): terms = lax.all_to_all(payload, PLANES, 0, 0, tiled=True)]
    all_to_all x1 -> x0, starting transfers between devices: 6.5 us -> none  [on_device(): lax.all_to_all(jnp.broadcast_to(early[None], (seqs, RANK, half_cols)), ('...]
    pallas_call x9 -> x8, Pallas kernels: 97.4 us -> 96.1 us  [call(): pl.pallas_call(kernel, name=name, grid=(steps,), in_specs=specs, out_spec...]
    unnamed x63 -> x51, local copies, waits for them, and re-layouts: 10.4 us -> 9.41 us
  transfers between devices with their start and end apart: 18 -> 16, of which waited for: 11 -> 9; matrix products, arithmetic and copies ran while one was open for 6% -> 6% of each run, Pallas kernels for 11% -> 12%
where the time goes in v7:
time: 311 us; the launch traced here: 310 us
  waiting for transfers between devices  121 us (39%)
  Pallas kernels  96.1 us (31%)
  starting transfers between devices  40.1 us (13%)
  local copies, waits for them, and re-layouts  16.8 us (5%)
  between operations  14.9 us (5%)
  blocking collectives  11.3 us (4%)
  other arithmetic  9.85 us (3%)
    pallas_call x8, Pallas kernels, call(): pl.pallas_call(kernel, name=name, grid=(steps,), in_specs=specs, out_spec...  96.1 us
    all_gather x1, waiting for transfers between devices, on_device(): weights = lax.all_gather(pack, ALL, axis=0, tiled=False)  79.9 us
    ppermute x8, starting transfers between devices, moved(): lax.ppermute(value, SEQ, [(c, c + steps) for c in range(parts) if 0 <= c...  21.8 us
    all_to_all x1, waiting for transfers between devices, on_device(): terms = lax.all_to_all(payload, PLANES, 0, 0, tiled=True)  16.9 us
    ppermute x8, waiting for transfers between devices, moved(): lax.ppermute(value, SEQ, [(c, c + steps) for c in range(parts) if 0 <= c...  15.8 us
    all_gather x1, blocking collectives, on_device(): b_all = lax.all_gather(b_own, 'tensor', axis=0, tiled=False)  11.3 us
    unnamed x51, local copies, waits for them, and re-layouts  9.41 us
    all_to_all x1, starting transfers between devices, on_device(): a_own = lax.all_to_all(wide, ('y', 'x'), 0, 0, tiled=True)  7.58 us
  transfers between devices with their start and end apart: 16, of which 9 were waited for; matrix products, arithmetic and copies ran while one was open for 6% of the time, Pallas kernels for 12%

profile of v7, /device:TPU:1, one launch (start us, length us, event | category | flops | bytes accessed | tf_op | source)
XLA Modules:
  0.0 310.1 jit_solution(1548078346408441826)
XLA Ops:
  16.1 7.6 %all-to-all-start = ((bf16[16,48,384]{2,1,0:T(8,128)(2,1)}), bf16[16,48,384]{2,1,0:T(8,128)(2,1)S(1)}, u32[]{:S(2)}, u32[]{:S(2)}) async-start(bf16[16,48,384]{2,1,0:T(8,128)(2,1)} %fusion.11), calls=%async_computation | async-start | bytes 1179648 | tf_op jit(solution)/shard_map/all_to_all | solution.py:480
  28.6 2.4 fusion.12
  30.9 5.6 %all-to-all-done = bf16[16,48,384]{2,1,0:T(8,128)(2,1)S(1)} async-done(((bf16[16,48,384]{2,1,0:T(8,128)(2,1)}), bf16[16,48,384]{2,1,0:T(8,128)(2,1)S(1)}, u32[]{:S(2)}, u32[]{:S(2)}) %all-to-all-start) | async-done | bytes 589856 | tf_op jit(solution)/shard_map/all_to_all | solution.py:480
  36.5 2.4 collective-permute-start
  42.2 3.4 %keys_values.1 = (bf16[256,1536]{1,0:T(8,128)(2,1)}, bf16[256,128]{1,0:T(8,128)(2,1)}, bf16[256,256]{1,0:T(8,128)(2,1)}) custom-call(bf16[256,1536]{1,0:T(8,128)(2,1)} %x_ref.5, f32[1,1536]{1,0:T(1,128)} %get-tuple-element.98.gain_ref, bf16[1536,384]{1,0:T(8,128)(2,1)} %bitcast.67, bf16[1536,384]{1,0:T(8,128)(2,1)} %bitcast.68, bf16[1536,384]{1,0:T(8,128)(2,1)} %bitcast.69, ...), custom_call_target="tpu_custom_call" | custom-call | flops 301989888 | bytes 2359296 | tf_op jit(solution)/shard_map/keys_values/pallas_call | solution.py:417
  47.1 6.5 %collective-permute-start.2 = (bf16[256,256]{1,0:T(8,128)(2,1)}, bf16[256,256]{1,0:T(8,128)(2,1)S(1)}, u32[]{:S(2)}, u32[]{:S(2)}) collective-permute-start(bf16[256,256]{1,0:T(8,128)(2,1)} %get-tuple-element.49), channel_id=1, source_target_pairs={{0,3},{1,4},{2,5},{3,6},{4,7},{8,11},{9,12},{10,13},{11,14},{12,15... | collective-permute-start | bytes 393224 | tf_op jit(solution)/shard_map/ppermute | solution.py:541
  57.2 2.5 collective-permute-start.3
  59.7 10.5 %collective-permute-done.3 = bf16[256,256]{1,0:T(8,128)(2,1)S(1)} collective-permute-done((bf16[256,256]{1,0:T(8,128)(2,1)}, bf16[256,256]{1,0:T(8,128)(2,1)S(1)}, u32[]{:S(2)}, u32[]{:S(2)}) %collective-permute-start.3) | collective-permute-done | bytes 131104 | tf_op jit(solution)/shard_map/ppermute | solution.py:541
  70.3 11.3 %all-gather.1 = bf16[64,4224]{1,0:T(8,128)(2,1)S(1)} all-gather(bf16[16,4224]{1,0:T(8,128)(2,1)S(1)} %constant_dynamic-update-slice_fusion), channel_id=3, replica_groups=mesh['y'=4,'x'=4,'core'=2,'tensor'=4] {'tensor'}, dimensions={0}, use_global_device_ids=true | all-gather | bytes 675840 | tf_op jit(solution)/shard_map/all_gather | solution.py:546
  83.4 2.2 fusion.5.b_ref
  85.6 79.9 %all-gather.6.cloned.1.call-done = bf16[6144,4224]{1,0:T(8,128)(2,1)} async-done(((bf16[48,4224]{1,0:T(8,128)(2,1)}), bf16[6144,4224]{1,0:T(8,128)(2,1)}) %all-gather.6.cloned.1.call-update) | async-done | bytes 51904528 | tf_op jit(solution)/shard_map/all_gather | solution.py:467
  165.5 55.4 %forward.1 = (bf16[256,1536]{1,0:T(8,128)(2,1)}, bf16[256,1536]{1,0:T(8,128)(2,1)}, bf16[4,1280,768]{2,1,0:T(8,128)(2,1)}, f32[4,8,768]{2,1,0:T(8,128)}, bf16[25...) custom-call(bf16[1280,256]{1,0:T(8,128)(2,1)} %copy-done.3, ...), custom_call_target="tpu_custom_call" | custom-call | flops 26172456960 | bytes 51904512 | tf_op jit(solution)/shard_map/forward/pallas_call | solution.py:417
  221.2 19.9 %attention_back.1 = (bf16[256,256]{1,0:T(8,128)(2,1)}, bf16[256,256]{1,0:T(8,128)(2,1)}, bf16[256,256]{1,0:T(8,128)(2,1)}, bf16[256,256]{1,0:T(8,128)(2,1)}, bf1...) custom-call(bf16[1280,256]{1,0:T(8,128)(2,1)} %copy-done.3, ...), custom_call_target="tpu_custom_call" | custom-call | flops 6442450944 | bytes 9437184 | tf_op jit(solution)/shard_map/attention_back/pallas_call | solution.py:417
  241.3 3.7 %collective-permute-start.5 = (bf16[256,256]{1,0:T(8,128)(2,1)}, bf16[256,256]{1,0:T(8,128)(2,1)S(1)}, u32[]{:S(2)}, u32[]{:S(2)}) collective-permute-start(bf16[256,256]{1,0:T(8,128)(2,1)} %get-tuple-element.63), channel_id=1, source_target_pairs={{1,0},{2,1},{3,2},{4,3},{5,4},{6,5},{7,6},{9,8},{10,9},{11,10},{12... | collective-permute-start | bytes 393224 | tf_op jit(solution)/shard_map/ppermute | solution.py:541
  245.0 2.6 collective-permute-start.6
  247.6 1.9 collective-permute-start.7
  252.7 3.4 %collective-permute-done.7.back3_ref = bf16[256,256]{1,0:T(8,128)(2,1)S(1)} collective-permute-done((bf16[256,256]{1,0:T(8,128)(2,1)}, bf16[256,256]{1,0:T(8,128)(2,1)S(1)}, u32[]{:S(2)}, u32[]{:S(2)}) %collective-permute-start.7) | collective-permute-done | bytes 131104 | tf_op jit(solution)/shard_map/ppermute | solution.py:541
  256.8 3.3 %shared_back.1 = (bf16[800,128]{1,0:T(8,128)(2,1)}, bf16[800,128]{1,0:T(8,128)(2,1)}, bf16[256,128]{1,0:T(8,128)(2,1)}, bf16[256,128]{1,0:T(8,128)(2,1)}, bf16[256,128]{1,0:T(8,128)(2,1)}) custom-call(s32[1]{0:T(128)} %bitcast.32.core_ref, bf16[256,1536]{1,0:T(8,128)(2,1)} %get-tuple-element.51.n1_ref, bf16[256,128]{1,0:T(8,128)(2,1)} %get-tuple-element.52.r1_ref, ...), custom_call_target="tpu_custom_call" | custom-call | flops 201326592 | bytes 2359296 | tf_op jit(solution)/shard_map/shared_back/pallas_call | solution.py:417
  262.8 2.2 payload.1
  265.0 7.2 %all-to-all-start.1 = ((bf16[64,16,512]{2,1,0:T(8,128)(2,1)}), bf16[64,16,512]{2,1,0:T(8,128)(2,1)S(1)}, u32[]{:S(2)}, u32[]{:S(2)}) async-start(bf16[64,16,512]{2,1,0:T(8,128)(2,1)} %payload.1), calls=%async_computation.2 | async-start | bytes 2097152 | tf_op jit(solution)/shard_map/all_to_all | solution.py:647
  272.2 5.2 %input_gradient.1 = f32[256,1536]{1,0:T(8,128)} custom-call(bf16[256,1536]{1,0:T(8,128)(2,1)} %x_ref.5, f32[1,1536]{1,0:T(1,128)} %get-tuple-element.98.gain_ref, bf16[1536,384]{1,0:T(8,128)(2,1)} %bitcast.71, bf16[1536,384]{1,0:T(8,128)(2,1)} %bitcast.72, bf16[1536,384]{1,0:T(8,128)(2,1)} %bitcast.73, bf16[256,128]{1,0:T(8,128)(2,1)} %get-tuple-element.73.gk_ref, ...), custom_call_target="tpu_custom_call" | custom-call | flops 301989888 | bytes 6291456 | tf_op jit(solution)/shard_map/input_gradient/pallas_call | solution.py:417
  277.4 16.9 %all-to-all-done.1 = bf16[64,16,512]{2,1,0:T(8,128)(2,1)S(1)} async-done(((bf16[64,16,512]{2,1,0:T(8,128)(2,1)}), bf16[64,16,512]{2,1,0:T(8,128)(2,1)S(1)}, u32[]{:S(2)}, u32[]{:S(2)}) %all-to-all-start.1) | async-done | bytes 1048608 | tf_op jit(solution)/shard_map/all_to_all | solution.py:647
  295.3 2.2 sum_wide.1
  299.0 4.6 %sum_hidden.1 = (f32[2,128,1152]{2,1,0:T(8,128)}, f32[1152,128]{1,0:T(8,128)}, f32[384,128]{1,0:T(8,128)}) custom-call(s32[16]{0:T(128)} %ids_ref.3, bf16[32,16,3840]{2,1,0:T(8,128)(2,1)} %bitcast.76), custom_call_target="tpu_custom_call" | custom-call | bytes 1769472 | tf_op jit(solution)/shard_map/sum_hidden/pallas_call | solution.py:417
  (107 shorter events, 32.6 us)
Async XLA Ops:
  7.2 18.0 %copy-start = (bf16[1152,128]{1,0:T(8,128)(2,1)S(1)}, bf16[1152,128]{1,0:T(8,128)(2,1)}, u32[]{:S(2)}) copy-start(bf16[1152,128]{1,0:T(8,128)(2,1)} %param.31) | copy-start | bytes 884740
  7.2 158.3 %all-gather.6.cloned.1.call-start = ((), (), s32[]{:S(2)}) async-start(), calls=%async_computation.4 | async-start | bytes 52310016 | tf_op jit(solution)/shard_map/all_gather | solution.py:467
  14.9 10.1 %copy-start.12 = (bf16[384,128]{1,0:T(8,128)(2,1)S(1)}, bf16[384,128]{1,0:T(8,128)(2,1)}, u32[]{:S(2)}) copy-start(bf16[384,128]{1,0:T(8,128)(2,1)} %param.29) | copy-start | bytes 294916
  16.1 20.4 %all-to-all-start = ((bf16[16,48,384]{2,1,0:T(8,128)(2,1)}), bf16[16,48,384]{2,1,0:T(8,128)(2,1)S(1)}, u32[]{:S(2)}, u32[]{:S(2)}) async-start(bf16[16,48,384]{2,1,0:T(8,128)(2,1)} %fusion.11), calls=%async_computation | async-start | bytes 1179648 | tf_op jit(solution)/shard_map/all_to_all | solution.py:480
  23.7 217.5 %reduce-scatter.2.cloned.1.call-start = ((), (), s32[]{:S(2)}) async-start(), calls=%async_computation.3 | async-start | bytes 614400 | tf_op jit(solution)/shard_map/reduce_scatter | solution.py:598
  28.6 11.9 %copy-start.16 = (f32[2,1536]{1,0:T(2,128)S(1)}, f32[2,1536]{1,0:T(2,128)}, u32[]{:S(2)}) copy-start(f32[2,1536]{1,0:T(2,128)} %param.20) | copy-start | bytes 36868
  36.5 4.5 %collective-permute-start = (bf16[16,48,384]{2,1,0:T(8,128)(2,1)S(1)}, bf16[16,48,384]{2,1,0:T(8,128)(2,1)S(1)}, u32[]{:S(2)}, u32[]{:S(2)}) collective-permute-start(bf16[16,48,384]{2,1,0:T(8,128)(2,1)S(1)} %all-to-all-done), channel_id=1, source_target_pairs={{0,4},{4,0},{1,5},{5,1},{2,6},{6,2},{3,7},{7,3},{8,12},{12,8},{9,1... | collective-permute-start | bytes 1769480 | tf_op jit(solution)/shard_map/ppermute | solution.py:478
  42.2 4.8 %copy-start.5 = (s32[32768]{0:T(1024)S(1)}, s32[32768]{0:T(1024)}, u32[]{:S(2)}) copy-start(s32[32768]{0:T(1024)} %param.18) | copy-start | bytes 393220
  45.6 24.7 %copy-start.11 = (bf16[256,256]{1,0:T(8,128)(2,1)S(1)}, bf16[256,256]{1,0:T(8,128)(2,1)}, u32[]{:S(2)}) copy-start(bf16[256,256]{1,0:T(8,128)(2,1)} %get-tuple-element.49) | copy-start | bytes 393220
  45.6 14.1 %collective-permute-start.1 = (bf16[256,256]{1,0:T(8,128)(2,1)}, bf16[256,256]{1,0:T(8,128)(2,1)S(1)}, u32[]{:S(2)}, u32[]{:S(2)}) collective-permute-start(bf16[256,256]{1,0:T(8,128)(2,1)} %get-tuple-element.49), channel_id=1, source_target_pairs={{0,4},{1,5},{2,6},{3,7},{8,12},{9,13},{10,14},{11,15},{16,20},{17,... | collective-permute-start | bytes 393224 | tf_op jit(solution)/shard_map/ppermute | solution.py:541
  47.1 12.6 %collective-permute-start.2 = (bf16[256,256]{1,0:T(8,128)(2,1)}, bf16[256,256]{1,0:T(8,128)(2,1)S(1)}, u32[]{:S(2)}, u32[]{:S(2)}) collective-permute-start(bf16[256,256]{1,0:T(8,128)(2,1)} %get-tuple-element.49), channel_id=1, source_target_pairs={{0,3},{1,4},{2,5},{3,6},{4,7},{8,11},{9,12},{10,13},{11,14},{12,15... | collective-permute-start | bytes 393224 | tf_op jit(solution)/shard_map/ppermute | solution.py:541
  55.3 14.9 %collective-permute-start.4 = (bf16[256,256]{1,0:T(8,128)(2,1)}, bf16[256,256]{1,0:T(8,128)(2,1)S(1)}, u32[]{:S(2)}, u32[]{:S(2)}) collective-permute-start(bf16[256,256]{1,0:T(8,128)(2,1)} %get-tuple-element.49), channel_id=1, source_target_pairs={{0,1},{1,2},{2,3},{3,4},{4,5},{5,6},{6,7},{8,9},{9,10},{10,11},{11... | collective-permute-start | bytes 393224 | tf_op jit(solution)/shard_map/ppermute | solution.py:541
  57.2 13.0 %collective-permute-start.3 = (bf16[256,256]{1,0:T(8,128)(2,1)}, bf16[256,256]{1,0:T(8,128)(2,1)S(1)}, u32[]{:S(2)}, u32[]{:S(2)}) collective-permute-start(bf16[256,256]{1,0:T(8,128)(2,1)} %get-tuple-element.49), channel_id=1, source_target_pairs={{0,2},{1,3},{2,4},{3,5},{4,6},{5,7},{8,10},{9,11},{10,12},{11,13},... | collective-permute-start | bytes 393224 | tf_op jit(solution)/shard_map/ppermute | solution.py:541
  70.2 12.0 %copy-start.3 = (bf16[1280,256]{1,0:T(8,128)(2,1)}, bf16[1280,256]{1,0:T(8,128)(2,1)S(1)}, u32[]{:S(2)}) copy-start(bf16[1280,256]{1,0:T(8,128)(2,1)S(1)} %constant_dynamic-update-slice_fusion.3.kv_ref) | copy-start | bytes 1966084
  221.0 78.1 %all-gather.8.cloned.1.call-start = ((), (), s32[]{:S(2)}) async-start(), calls=%async_computation.5 | async-start | bytes 4055040 | tf_op jit(solution)/shard_map/all_gather | solution.py:621
  241.2 19.6 %copy-start.13 = (bf16[4,16,384]{2,1,0:T(8,128)(2,1)S(1)}, bf16[4,16,384]{2,1,0:T(8,128)(2,1)}, u32[]{:S(2)}) copy-start(bf16[4,16,384]{2,1,0:T(8,128)(2,1)} %get-tuple-element.71.q_ref) | copy-start | bytes 147460
  241.3 9.6 %collective-permute-start.5 = (bf16[256,256]{1,0:T(8,128)(2,1)}, bf16[256,256]{1,0:T(8,128)(2,1)S(1)}, u32[]{:S(2)}, u32[]{:S(2)}) collective-permute-start(bf16[256,256]{1,0:T(8,128)(2,1)} %get-tuple-element.63), channel_id=1, source_target_pairs={{1,0},{2,1},{3,2},{4,3},{5,4},{6,5},{7,6},{9,8},{10,9},{11,10},{12... | collective-permute-start | bytes 393224 | tf_op jit(solution)/shard_map/ppermute | solution.py:541
  245.0 7.7 %collective-permute-start.6 = (bf16[256,256]{1,0:T(8,128)(2,1)}, bf16[256,256]{1,0:T(8,128)(2,1)S(1)}, u32[]{:S(2)}, u32[]{:S(2)}) collective-permute-start(bf16[256,256]{1,0:T(8,128)(2,1)} %get-tuple-element.64), channel_id=1, source_target_pairs={{2,0},{3,1},{4,2},{5,3},{6,4},{7,5},{10,8},{11,9},{12,10},{13,11},... | collective-permute-start | bytes 393224 | tf_op jit(solution)/shard_map/ppermute | solution.py:541
  247.6 8.5 %collective-permute-start.7 = (bf16[256,256]{1,0:T(8,128)(2,1)}, bf16[256,256]{1,0:T(8,128)(2,1)S(1)}, u32[]{:S(2)}, u32[]{:S(2)}) collective-permute-start(bf16[256,256]{1,0:T(8,128)(2,1)} %get-tuple-element.65), channel_id=1, source_target_pairs={{3,0},{4,1},{5,2},{6,3},{7,4},{11,8},{12,9},{13,10},{14,11},{15,12... | collective-permute-start | bytes 393224 | tf_op jit(solution)/shard_map/ppermute | solution.py:541
  249.5 6.6 %collective-permute-start.8 = (bf16[256,256]{1,0:T(8,128)(2,1)}, bf16[256,256]{1,0:T(8,128)(2,1)S(1)}, u32[]{:S(2)}, u32[]{:S(2)}) collective-permute-start(bf16[256,256]{1,0:T(8,128)(2,1)} %get-tuple-element.66), channel_id=1, source_target_pairs={{4,0},{5,1},{6,2},{7,3},{12,8},{13,9},{14,10},{15,11},{20,16},{21,... | collective-permute-start | bytes 393224 | tf_op jit(solution)/shard_map/ppermute | solution.py:541
  250.9 5.3 %copy-start.7 = (bf16[256,256]{1,0:T(8,128)(2,1)}, bf16[256,256]{1,0:T(8,128)(2,1)S(1)}, u32[]{:S(2)}) copy-start(bf16[256,256]{1,0:T(8,128)(2,1)S(1)} %collective-permute-done.5.back1_ref) | copy-start | bytes 393220
  260.1 2.0 collective-permute-start.9
  260.8 1.2 collective-permute-start.10
  265.0 29.3 %all-to-all-start.1 = ((bf16[64,16,512]{2,1,0:T(8,128)(2,1)}), bf16[64,16,512]{2,1,0:T(8,128)(2,1)S(1)}, u32[]{:S(2)}, u32[]{:S(2)}) async-start(bf16[64,16,512]{2,1,0:T(8,128)(2,1)} %payload.1), calls=%async_computation.2 | async-start | bytes 2097152 | tf_op jit(solution)/shard_map/all_to_all | solution.py:647
  (10 other events, 17.3 us)
Sparse Core Ops, SparseCore 0:
  12.5 152.9 all-gather.5
  221.1 18.6 reduce-scatter.1
  242.3 56.6 all-gather.7

commit v8 on v7

--- a/solution.py
+++ b/solution.py
@@ -67,6 +67,15 @@
     scaled = grad * gain
     dot = jnp.mean(v * scaled, axis=-1, keepdims=True)
     return inv * scaled - v * (inv * inv * inv * dot)
+
+
+def pack_kernel(gu_ref, down_ref, q_ref, o_ref, out_ref):
+    ff, cols = gu_ref.shape[2], q_ref.shape[1]
+    out_ref[:, :ff] = gu_ref[0]
+    out_ref[:, ff : 2 * ff] = gu_ref[1]
+    out_ref[:, 2 * ff : 3 * ff] = down_ref[...]
+    out_ref[:, 3 * ff : 3 * ff + cols] = q_ref[...]
+    out_ref[:, 3 * ff + cols :] = o_ref[...]
 
 
 def shared_kernel(x_ref, gain_ref, a_ref, wk_ref, wv_ref, bkv_ref, cos_ref, sin_ref, n1_ref, r1_ref, kv_ref):
@@ -240,9 +249,9 @@
 
 
 def attn_back_kernel(
-    kv_ref, gb_ref, gro_ref, r1_ref, cos_ref, sin_ref,
+    tensor_ref, kv_ref, gb_ref, gro_ref, r1_ref, cos_ref, sin_ref,
     q_ref, mixed_ref, p_ref, inv_ref, wo_ref, bo_ref, wq_ref, bq_ref,
-    dkva_ref, dkvb_ref, dkvc_ref, dkvd_ref, dkve_ref, g1_ref, gr_ref, gbq_ref,
+    dkva_ref, dkvb_ref, dkvc_ref, dkvd_ref, dkve_ref, q0_ref, g1_ref, gr_ref,
     ds_ref, dk_ref, dv_ref, kt_ref, r1t_ref, gq_ref, gm_ref, qs_ref, gs_ref,
 ):
     step = pl.program_id(0)
@@ -284,7 +293,21 @@
         gq_ref[:, part] = rope_back(dq[:, span].T, cos_ref[...], sin_ref[...]).astype(BF)
 
     gq = gq_ref[...]
-    gbq_ref[0] = mm(r1t_ref[rows_of(SLOT_Q)], gq).astype(BF)
+    grad_bq = mm(r1t_ref[rows_of(SLOT_Q)], gq).astype(BF)
+    away = lax.rem(tensor_ref[0] + pl.num_programs(0) - step, pl.num_programs(0))
+
+    @pl.when(away == 0)
+    def _():
+        q0_ref[...] = grad_bq
+
+    for d, dkv_ref in ((1, dkvd_ref), (2, dkvc_ref), (3, dkvb_ref)):
+
+        @pl.when(away == d)
+        def _(dkv_ref=dkv_ref):
+            dkv_ref[rows : rows + RANK] = grad_bq[:, : 2 * HD]
+            dkv_ref[rows + RANK :, :HD] = grad_bq[:, 2 * HD :]
+            dkv_ref[rows + RANK :, HD:] = jnp.zeros((RANK, HD), BF)
+
     gr_ref[...] += mm_nt(gq, bq_ref[0])
     g1_ref[...] += mm_nt(gq, flat(wq_ref))
 
@@ -292,18 +315,24 @@
     def _():
         for c, dkv_ref in enumerate((dkva_ref, dkvb_ref, dkvc_ref, dkvd_ref, dkve_ref)):
             span = slice(c * rows, (c + 1) * rows)
-            dkv_ref[:, :HD] = (dk_ref[span] * (1.0 / LOG2E)).astype(BF)
-            dkv_ref[:, HD:] = dv_ref[span].astype(BF)
+            dkv_ref[:rows, :HD] = (dk_ref[span] * (1.0 / LOG2E)).astype(BF)
+            dkv_ref[:rows, HD:] = dv_ref[span].astype(BF)
 
 
 def shared_back_kernel(
     chips, core_ref, n1_ref, r1_ref, bkv_ref, cos_ref, sin_ref, own_ref, back1_ref, back2_ref, back3_ref, back4_ref,
-    gr_ref, widef_ref,
+    q0_ref, gr_ref, widef_ref,
     mine_ref, theirs_ref, gk_ref, gv_ref, grt_ref,
 ):
+    rows = own_ref.shape[0]
     gkv = own_ref[...].astype(F32)
     for back_ref in (back1_ref, back2_ref, back3_ref, back4_ref):
-        gkv = gkv + back_ref[...].astype(F32)
+        gkv = gkv + back_ref[:rows].astype(F32)
+    queries = [q0_ref[:, j * LANES : (j + 1) * LANES].astype(F32) for j in range(3)]
+    for back_ref in (back1_ref, back2_ref, back3_ref):
+        queries[0] = queries[0] + back_ref[rows : rows + RANK, :HD].astype(F32)
+        queries[1] = queries[1] + back_ref[rows : rows + RANK, HD:].astype(F32)
+        queries[2] = queries[2] + back_ref[rows + RANK :, :HD].astype(F32)
     gk = rope_back(gkv[:, :HD], cos_ref[...], sin_ref[...]).astype(BF)
     gv = gkv[:, HD:].astype(BF)
     gk_ref[...] = gk
@@ -311,7 +340,7 @@
     gr = gr_ref[...] + mm_nt(gk, bkv_ref[0]) + mm_nt(gv, bkv_ref[1])
     grt_ref[...] = gr.astype(BF)
     wide = (mm(gr.T.astype(BF), n1_ref[...]) + widef_ref[...]).T.astype(BF)
-    share = mine_ref.shape[0] - 2 * RANK
+    share = mine_ref.shape[0] - 5 * RANK
     wide = wide.reshape(chips, 2, share // chips, LANES)
     first = core_ref[0] == 0
     mine_ref[:share] = jnp.where(first, wide[:, 0], wide[:, 1]).reshape(share, LANES)
@@ -319,18 +348,25 @@
     r1t = turned(r1_ref[...])
     for j, (slot, grad) in enumerate(((SLOT_K, gk), (SLOT_V, gv))):
         term = mm(r1t[rows_of(slot)], grad).astype(BF)
-        rows = slice(share + j * RANK, share + (j + 1) * RANK)
-        mine_ref[rows] = term
-        theirs_ref[rows] = term
-
-
-def payload_kernel(core_ref, mine_ref, other_ref, q_ref, q_other_ref, out_ref):
+        part = slice(share + j * RANK, share + (j + 1) * RANK)
+        mine_ref[part] = term
+        theirs_ref[part] = term
+    for j, term in enumerate(queries):
+        part = slice(share + (2 + j) * RANK, share + (3 + j) * RANK)
+        mine_ref[part] = term.astype(BF)
+        theirs_ref[part] = term.astype(BF)
+
+
+def payload_kernel(core_ref, mine_ref, other_ref, out_ref, q_ref):
     first = core_ref[0] == 0
     total = mine_ref[...].astype(F32) + other_ref[...].astype(F32)
-    tensor_count = q_ref.shape[0]
     count = out_ref.shape[0]
-    own_rows = (total.shape[0] - 2 * RANK) // count
-    queries = [(q_ref[t].astype(F32) + q_other_ref[t].astype(F32)).astype(BF) for t in range(tensor_count)]
+    own_rows = (total.shape[0] - 5 * RANK) // count
+    queries = total[total.shape[0] - 3 * RANK :].astype(BF)
+    for n in range(q_ref.shape[0]):
+        for j in range(3):
+            q_ref[n, :, j * LANES : (j + 1) * LANES] = queries[j * RANK : (j + 1) * RANK]
+    tensor_count = RANK // 4
     blank = jnp.zeros((RANK - own_rows - 2, LANES), F32)
     for n in range(count):
         pieces = [total[n * own_rows : (n + 1) * own_rows]]
@@ -339,8 +375,7 @@
             at = count * own_rows + j * RANK + row
             low, high = total[at : at + 1], total[at + tensor_count : at + tensor_count + 1]
             pieces.append(jnp.where(first, low, high))
-        out_ref[n, :, :LANES] = jnp.concatenate(pieces + [blank], axis=0).astype(BF)
-        out_ref[n, :, LANES:] = queries[n % tensor_count]
+        out_ref[n] = jnp.concatenate(pieces + [blank], axis=0).astype(BF)
 
 
 def input_kernel(
@@ -356,20 +391,29 @@
     acc_ref[...] = jnp.zeros_like(acc_ref)
     for s in range(terms_ref.shape[0] // 2):
         acc_ref[ids_ref[s]] += terms_ref[2 * s].astype(F32) + terms_ref[2 * s + 1].astype(F32)
-    adapters, rank, cols = acc_ref.shape
-    ff = gu_ref.shape[2]
-
-    def taken(first, last):
-        return acc_ref[:, :, first:last].reshape(adapters * rank, last - first)
+    adapters, rank, _ = acc_ref.shape
+    ff, heads = gu_ref.shape[2], out_ref.shape[0]
+
+    def taken(first, count):
+        return acc_ref[:, :, first : first + count].reshape(adapters * rank, count)
 
     gu_ref[0] = taken(0, ff)
-    gu_ref[1] = taken(ff, 2 * ff)
-    down_ref[...] = taken(2 * ff, 3 * ff).T
-    out_ref[...] = taken(3 * ff, cols).T
-
-
-def sum_wide_kernel(ids_ref, own_ref, terms_ref, wide_ref, kv_ref, q_ref, acc_ref):
+    gu_ref[1] = taken(ff, ff)
+    down_ref[...] = taken(2 * ff, ff).T
+    out_ref[...] = taken(3 * ff, heads).T
+
+
+def sum_wide_kernel(ids_ref, own_ref, terms_ref, *rest):
+    q_refs, (wide_ref, kv_ref, q_ref, acc_ref, accq_ref) = rest[:-5], rest[-5:]
     acc_ref[...] = jnp.zeros_like(acc_ref)
+    accq_ref[...] = jnp.zeros_like(accq_ref)
+    y_count, x_count = len(q_refs), q_refs[0].shape[0]
+    for away_y, terms in enumerate(q_refs):
+        y = lax.rem(own_ref[1] + away_y, y_count)
+        for away_x in range(x_count):
+            x = lax.rem(own_ref[2] + away_x, x_count)
+            accq_ref[ids_ref[y * x_count + x]] += terms[away_x].astype(F32)
+    q_ref[...] = accq_ref[...].reshape(q_ref.shape)
     seqs, parts = terms_ref.shape[:2]
     for s in range(seqs):
         term = terms_ref[s, 0].astype(F32)
@@ -377,16 +421,15 @@
             term = term + terms_ref[s, part].astype(F32)
         acc_ref[ids_ref[s]] += term
     adapters, rank, _ = acc_ref.shape
-    q_ref[...] = acc_ref[:, :, LANES:].reshape(q_ref.shape)
     lane = lax.broadcasted_iota(jnp.int32, (rank, LANES), 1) // RANK
     own_rows, slots = wide_ref.shape[:2]
     for j in range(slots):
         total = jnp.zeros((rank, LANES), F32)
         for a in range(adapters):
-            moved = pltpu.roll(acc_ref[a, :, :LANES], ((a - j) * RANK) % LANES, 1)
+            moved = pltpu.roll(acc_ref[a], ((a - j) * RANK) % LANES, 1)
             total = jnp.where(lane == a, moved, total)
         wide_ref[:, j] = total[:own_rows]
-    mine = acc_ref[own_ref[0], :, :LANES]
+    mine = acc_ref[own_ref[0]]
     for j in range(2):
         kv_ref[j] = mine[own_rows + j : own_rows + j + 1]
 
@@ -460,8 +503,10 @@
     column = adapter * RANK
     f3 = 3 * ff_cols
 
-    pack = jnp.concatenate(
-        [gate_up_weight[0], gate_up_weight[1], down_weight.T, q_weight, out_weight.T], axis=1
+    args = (gate_up_weight, down_weight.T, q_weight, out_weight.T)
+    (pack,) = call(
+        pack_kernel, "pack", 1, args, wholes(*args), [(sds((shard_rows, f3 + 2 * q_cols), BF), None)], [],
+        0, 4 * shard_rows * (f3 + 2 * q_cols),
     )
     pack, wide_adapters = lax.optimization_barrier((pack, wide_adapters))
     weights = lax.all_gather(pack, ALL, axis=0, tiled=False)
@@ -497,6 +542,10 @@
     b_own = jnp.concatenate(
         [gu_rows[0], gu_rows[1], take_cols(down_adapter).T, take_rows(q_adapter), take_cols(out_adapter).T], axis=1
     )
+    b_parts = [b_own] + [
+        lax.ppermute(b_own, "tensor", [((z + d) % tensor_count, z) for z in range(tensor_count)])
+        for d in range(1, tensor_count)
+    ]
     kv_rows = take_rows(kv_adapter)
     b_kv = jnp.stack([in_slot(kv_rows[0], SLOT_K), in_slot(kv_rows[1], SLOT_V)])
 
@@ -542,8 +591,7 @@
 
     kv_window = jnp.concatenate([moved(kv_own, d) for d in range(reach, 0, -1)] + [kv_own])
 
-    b_own, kv_window = lax.optimization_barrier((b_own, kv_window))
-    b_all = lax.all_gather(b_own, "tensor", axis=0, tiled=False)
+    b_all = jnp.roll(jnp.stack(b_parts), tensor, axis=0)
     b_heads = jnp.concatenate(
         [in_slot(b_all[:, :, f3 : f3 + q_cols], SLOT_Q), in_slot(b_all[:, :, f3 + q_cols :], SLOT_O)], axis=2
     )
@@ -598,15 +646,15 @@
     early = lax.psum_scatter(early, "tensor", scatter_dimension=0, tiled=True).reshape(RANK, -1)
 
     args = (
-        kv_window, grad_branch, grad_ro, rank_one, cos, sin, queries, mixed, probs, norms,
-        weights, b_heads, weights, b_heads,
-    )
-    *dkv, grad_one, grad_rank, grad_bq = call(
+        tensor.astype(jnp.int32).reshape(1), kv_window, grad_branch, grad_ro, rank_one, cos, sin,
+        queries, mixed, probs, norms, weights, b_heads, weights, b_heads,
+    )
+    *dkv, q_own, grad_one, grad_rank = call(
         attn_back_kernel, "attention_back", tensor_count, args,
-        wholes(*args[:6]) + [token_cols, token_cols, p_spec, norm_spec, o_spec, ob_spec, q_spec, qb_spec],
+        [scalars()] + wholes(*args[1:7]) + [token_cols, token_cols, p_spec, norm_spec, o_spec, ob_spec, q_spec, qb_spec],
         [
-            *[(sds((rows, 2 * HD), BF), None)] * (reach + 1), (tok_f32, None), (sds((rows, LANES), F32), None),
-            (sds((tensor_count, RANK, q_cols), BF), by_step(RANK, q_cols)),
+            *[(sds((rows + (2 * RANK if 0 < w < reach else 0), 2 * HD), BF), None) for w in range(reach + 1)],
+            (sds((RANK, q_cols), BF), None), (tok_f32, None), (sds((rows, LANES), F32), None),
         ],
         [
             pltpu.VMEM((span, heads * rows), BF),
@@ -620,11 +668,15 @@
     early, grad_one = lax.optimization_barrier((early, grad_one))
     early = lax.all_gather(early, DP, axis=0, tiled=False)
 
-    backs = [moved(dkv[reach - d], -d) for d in range(1, reach + 1)]
+    def around(value, steps):
+        return lax.ppermute(value, SEQ, [(c, (c - steps) % parts) for c in range(parts)])
+
+    backs = [around(dkv[reach - d], d) for d in range(1, reach)] + [moved(dkv[0], -reach)]
+    core = my_core.astype(jnp.int32).reshape(1)
     chips = dp_count // 2
-    share = width // 2 + 2 * RANK
+    share = width // 2 + 5 * RANK
     args = (
-        my_core.astype(jnp.int32).reshape(1), normed_one, rank_one, b_kv, cos, sin, dkv[reach], *backs, grad_rank, wide_ffn,
+        core, normed_one, rank_one, b_kv, cos, sin, dkv[reach], *backs, q_own, grad_rank, wide_ffn,
     )
     mine, theirs, grad_key, grad_value, grad_rank = call(
         functools.partial(shared_back_kernel, chips), "shared_back", 1, args,
@@ -637,15 +689,23 @@
     )
     own_rows = width // devices
     planes = chips * tensor_count
-    other, grad_bq_other = from_other_core(theirs), from_other_core(grad_bq)
-    args = (my_core.astype(jnp.int32).reshape(1), mine, other, grad_bq, grad_bq_other)
-    (payload,) = call(
+    args = (core, mine, from_other_core(theirs))
+    payload, q_terms = call(
         payload_kernel, "payload", 1, args, [scalars()] + wholes(*args[1:]),
-        [(sds((planes, RANK, LANES + q_cols), BF), None)], [], 0, 2 * planes * RANK * (LANES + q_cols),
+        [(sds((planes, RANK, LANES), BF), None), (sds((1, RANK, q_cols), BF), None)], [],
+        0, 2 * planes * RANK * LANES,
     )
     payload, grad_key = lax.optimization_barrier((payload, grad_key))
     terms = lax.all_to_all(payload, PLANES, 0, 0, tiled=True)
-    terms = terms.reshape(seqs, tensor_count, RANK, LANES + q_cols)
+
+    def with_others(value, axis):
+        count = lax.axis_size(axis)
+        return [value] + [
+            lax.ppermute(value, axis, [((i + d) % count, i) for i in range(count)]) for d in range(1, count)
+        ]
+
+    q_terms = with_others(jnp.concatenate(with_others(q_terms, "x")), "y")
+    terms = terms.reshape(seqs, tensor_count, RANK, LANES)
 
     args = (
         tokens, gain_one, a_all, a_all, a_all, grad_key, grad_value, grad_rank, grad_one, grad_residual,
@@ -656,17 +716,18 @@
         [(tok_f32, None)], [], 2 * rows * width * 384, 16 * rows * width,
     )
 
+    terms, input_grad = lax.optimization_barrier((terms, input_grad))
+    own = jnp.stack([(dp * tensor_count + tensor) // RANK, lax.axis_index("y"), lax.axis_index("x")]).astype(jnp.int32)
+    wide_grad, kv_adapter_grad, q_adapter_grad = call(
+        sum_wide_kernel, "sum_wide", 1, (adapter_ids, own, terms, *q_terms),
+        [scalars(), scalars()] + wholes(terms, *q_terms),
+        [(sds((own_rows, 7, LANES), F32), None), (sds((2, 1, HD), F32), None), (sds((LANES, q_cols), F32), None)],
+        [pltpu.VMEM((adapters, RANK, LANES), F32), pltpu.VMEM((adapters, RANK, q_cols), F32)], 0, 4 * LANES * f3,
+    )
     gate_up_adapter_grad, down_adapter_grad, out_adapter_grad = call(
         sum_hidden_kernel, "sum_hidden", 1, (adapter_ids, early), [scalars()] + wholes(early),
         [(sds((2, LANES, ff_cols), F32), None), (sds((ff_cols, LANES), F32), None), (sds((q_cols, LANES), F32), None)],
         [pltpu.VMEM((adapters, RANK, f3 + q_cols), F32)], 0, 4 * LANES * f3,
-    )
-    own_adapter = ((dp * tensor_count + tensor) // RANK).astype(jnp.int32).reshape(1)
-    wide_grad, kv_adapter_grad, q_adapter_grad = call(
-        sum_wide_kernel, "sum_wide", 1, (adapter_ids, own_adapter, terms),
-        [scalars(), scalars()] + wholes(terms),
-        [(sds((own_rows, 7, LANES), F32), None), (sds((2, 1, HD), F32), None), (sds((LANES, q_cols), F32), None)],
-        [pltpu.VMEM((adapters, RANK, LANES + q_cols), F32)], 0, 4 * LANES * f3,
     )
     return (
         block_output, input_grad, wide_grad.transpose(1, 0, 2), kv_adapter_grad,

time: 311 us -> 302 us (0.971)
  blocking collectives: 11.3 us -> 0 us
  starting transfers between devices: 40.1 us -> 46 us
    ppermute x0 -> x12, starting transfers between devices: none -> 18.4 us  [the longest x6 8.83 us: with_others(): lax.ppermute(value, axis, [((i + d) % count, i) for i in range(count)])]
    all_to_all x1, waiting for transfers between devices: 16.9 us -> 1.81 us  [on_device(): terms = lax.all_to_all(payload, PLANES, 0, 0, tiled=True)]
    all_gather x1 -> x0, blocking collectives: 11.3 us -> none  [on_device(): b_all = lax.all_gather(b_own, 'tensor', axis=0, tiled=False)]
    all_gather x1, waiting for transfers between devices: 79.9 us -> 90.4 us  [on_device(): weights = lax.all_gather(pack, ALL, axis=0, tiled=False)]
    ppermute x8 -> x5, starting transfers between devices: 21.8 us -> 11.3 us  [moved(): lax.ppermute(value, SEQ, [(c, c + steps) for c in range(parts) if 0 <= c...]
    ppermute x0 -> x12, waiting for transfers between devices: none -> 5.9 us  [the longest x3 5.88 us: around(): lax.ppermute(value, SEQ, [(c, (c - steps) % parts) for c in range(parts)])]
    ppermute x8 -> x5, waiting for transfers between devices: 15.8 us -> 11.3 us  [moved(): lax.ppermute(value, SEQ, [(c, c + steps) for c in range(parts) if 0 <= c...]
    all_to_all x1, waiting for transfers between devices: 5.59 us -> 1.96 us  [on_device(): a_own = lax.all_to_all(wide, ('y', 'x'), 0, 0, tiled=True)]
  transfers between devices with their start and end apart: 16 -> 24, of which waited for: 9 -> 9; matrix products, arithmetic and copies ran while one was open for 6% -> 7% of each run, Pallas kernels for 12% -> 12%
where the time goes in v8:
time: 302 us; the launch traced here: 301 us
  waiting for transfers between devices  118 us (39%)
  Pallas kernels  97.5 us (32%)
  starting transfers between devices  46 us (15%)
  local copies, waits for them, and re-layouts  15.5 us (5%)
  between operations  14.9 us (5%)
  other arithmetic  9.76 us (3%)
    pallas_call x9, Pallas kernels, call(): pl.pallas_call(kernel, name=name, grid=(steps,), in_specs=specs, out_spec...  97.5 us
    all_gather x1, waiting for transfers between devices, on_device(): weights = lax.all_gather(pack, ALL, axis=0, tiled=False)  90.4 us
    ppermute x5, starting transfers between devices, moved(): lax.ppermute(value, SEQ, [(c, c + steps) for c in range(parts) if 0 <= c...  11.3 us
    ppermute x5, waiting for transfers between devices, moved(): lax.ppermute(value, SEQ, [(c, c + steps) for c in range(parts) if 0 <= c...  11.3 us
    unnamed x65, local copies, waits for them, and re-layouts  8.86 us
    ppermute x6, starting transfers between devices, with_others(): lax.ppermute(value, axis, [((i + d) % count, i) for i in range(count)])  8.83 us
    all_to_all x1, starting transfers between devices, on_device(): a_own = lax.all_to_all(wide, ('y', 'x'), 0, 0, tiled=True)  6.75 us
    ppermute x3, starting transfers between devices, on_device(): lax.ppermute(b_own, 'tensor', [((z + d) % tensor_count, z) for z in range...  6.5 us
  transfers between devices with their start and end apart: 24, of which 9 were waited for; matrix products, arithmetic and copies ran while one was open for 7% of the time, Pallas kernels for 12%

profile of v8, /device:TPU:1, one launch (start us, length us, event | category | flops | bytes accessed | tf_op | source)
XLA Modules:
  0.0 301.4 jit_solution(13370351327365696957)
XLA Ops:
  13.2 2.5 collective-permute-start.7
  15.6 3.3 %collective-permute-start.6 = (bf16[16,4224]{1,0:T(8,128)(2,1)S(1)}, bf16[16,4224]{1,0:T(8,128)(2,1)S(1)}, u32[]{:S(2)}, u32[]{:S(2)}) collective-permute-start(bf16[16,4224]{1,0:T(8,128)(2,1)S(1)} %constant_dynamic-update-slice_fusion.5), channel_id=1, source_target_pairs={{2,0},{3,1},{0,2},{1,3},{6,4},{7,5},{4,6},{5,7},{10,8},{11,9},{8,1... | collective-permute-start | bytes 405512 | tf_op jit(solution)/shard_map/ppermute | solution.py:546
  22.3 6.8 %all-to-all-start = ((bf16[16,48,384]{2,1,0:T(8,128)(2,1)}), bf16[16,48,384]{2,1,0:T(8,128)(2,1)S(1)}, u32[]{:S(2)}, u32[]{:S(2)}) async-start(bf16[16,48,384]{2,1,0:T(8,128)(2,1)} %fusion.11), calls=%async_computation | async-start | bytes 1179648 | tf_op jit(solution)/shard_map/all_to_all | solution.py:525
  31.2 2.4 fusion.12
  40.1 2.0 all-to-all-done
  42.1 2.5 collective-permute-start
  44.6 2.1 fusion.5.b_ref
  47.9 3.3 %keys_values.1 = (bf16[256,1536]{1,0:T(8,128)(2,1)}, bf16[256,128]{1,0:T(8,128)(2,1)}, bf16[256,256]{1,0:T(8,128)(2,1)}) custom-call(bf16[256,1536]{1,0:T(8,128)(2,1)} %x_ref.5, f32[1,1536]{1,0:T(1,128)} %get-tuple-element.102.gain_ref, bf16[1536,384]{1,0:T(8,128)(2,1)} %bitcast.75, bf16[1536,384]{1,0:T(8,128)(2,1)} %bitcast.76, bf16[1536,384]{1,0:T(8,128)(2,1)} %bitcast.77, ...), custom_call_target="tpu_custom_call" | custom-call | flops 301989888 | bytes 2359296 | tf_op jit(solution)/shard_map/keys_values/pallas_call | solution.py:460
  51.2 3.1 %collective-permute-start.2 = (bf16[256,256]{1,0:T(8,128)(2,1)}, bf16[256,256]{1,0:T(8,128)(2,1)S(1)}, u32[]{:S(2)}, u32[]{:S(2)}) collective-permute-start(bf16[256,256]{1,0:T(8,128)(2,1)} %get-tuple-element.51), channel_id=1, source_target_pairs={{0,3},{1,4},{2,5},{3,6},{4,7},{8,11},{9,12},{10,13},{11,14},{12,15... | collective-permute-start | bytes 393224 | tf_op jit(solution)/shard_map/ppermute | solution.py:590
  58.5 2.6 collective-permute-start.3
  61.2 10.1 %collective-permute-done.3 = bf16[256,256]{1,0:T(8,128)(2,1)S(1)} collective-permute-done((bf16[256,256]{1,0:T(8,128)(2,1)}, bf16[256,256]{1,0:T(8,128)(2,1)S(1)}, u32[]{:S(2)}, u32[]{:S(2)}) %collective-permute-start.3) | collective-permute-done | bytes 131104 | tf_op jit(solution)/shard_map/ppermute | solution.py:590
  71.4 90.4 %all-gather.5.cloned.1.call-done = bf16[6144,4224]{1,0:T(8,128)(2,1)} async-done(((bf16[48,4224]{1,0:T(8,128)(2,1)}), bf16[6144,4224]{1,0:T(8,128)(2,1)}) %all-gather.5.cloned.1.call-update) | async-done | bytes 51904528 | tf_op jit(solution)/shard_map/all_gather | solution.py:512
  161.8 55.5 %forward.1 = (bf16[256,1536]{1,0:T(8,128)(2,1)}, bf16[256,1536]{1,0:T(8,128)(2,1)}, bf16[4,1280,768]{2,1,0:T(8,128)(2,1)}, f32[4,8,768]{2,1,0:T(8,128)}, bf16[25...) custom-call(bf16[1280,256]{1,0:T(8,128)(2,1)} %copy-done.2, ...), custom_call_target="tpu_custom_call" | custom-call | flops 26172456960 | bytes 51904512 | tf_op jit(solution)/shard_map/forward/pallas_call | solution.py:460
  217.6 20.3 %attention_back.1 = (bf16[256,256]{1,0:T(8,128)(2,1)}, bf16[288,256]{1,0:T(8,128)(2,1)}, bf16[288,256]{1,0:T(8,128)(2,1)}, bf16[288,256]{1,0:T(8,128)(2,1)}, bf1...) custom-call(s32[1]{0:T(128)} %bitcast.34.tensor_ref, ...), custom_call_target="tpu_custom_call" | custom-call | flops 6442450944 | bytes 9437184 | tf_op jit(solution)/shard_map/attention_back/pallas_call | solution.py:460
  241.1 2.4 collective-permute-start.11
  244.7 2.1 collective-permute-done.9.back2_ref
  246.8 3.7 %collective-permute-done.10.back3_ref = bf16[288,256]{1,0:T(8,128)(2,1)S(1)} collective-permute-done((bf16[288,256]{1,0:T(8,128)(2,1)}, bf16[288,256]{1,0:T(8,128)(2,1)S(1)}, u32[]{:S(2)}, u32[]{:S(2)}) %collective-permute-start.10) | collective-permute-done | bytes 147488 | tf_op jit(solution)/shard_map/ppermute | solution.py:672
  251.2 3.3 %shared_back.1 = (bf16[848,128]{1,0:T(8,128)(2,1)}, bf16[848,128]{1,0:T(8,128)(2,1)}, bf16[256,128]{1,0:T(8,128)(2,1)}, bf16[256,128]{1,0:T(8,128)(2,1)}, bf16[256,128]{1,0:T(8,128)(2,1)}) custom-call(s32[1]{0:T(128)} %bitcast.33.core_ref, bf16[256,1536]{1,0:T(8,128)(2,1)} %get-tuple-element.52.n1_ref, bf16[256,128]{1,0:T(8,128)(2,1)} %get-tuple-element.53.r1_ref, ...), custom_call_target="tpu_custom_call" | custom-call | flops 201326592 | bytes 2359296 | tf_op jit(solution)/shard_map/shared_back/pallas_call | solution.py:460
  259.4 2.4 collective-permute-start.14
  263.7 6.1 %all-to-all-start.1 = ((bf16[64,16,128]{2,1,0:T(8,128)(2,1)}), bf16[64,16,128]{2,1,0:T(8,128)(2,1)S(1)}, u32[]{:S(2)}, u32[]{:S(2)}) async-start(bf16[64,16,128]{2,1,0:T(8,128)(2,1)} %get-tuple-element.74), calls=%async_computation.1 | async-start | bytes 524288 | tf_op jit(solution)/shard_map/all_to_all | solution.py:699
  271.0 2.6 collective-permute-start.17
  275.3 4.9 %input_gradient.1 = f32[256,1536]{1,0:T(8,128)} custom-call(bf16[256,1536]{1,0:T(8,128)(2,1)} %x_ref.5, f32[1,1536]{1,0:T(1,128)} %get-tuple-element.102.gain_ref, bf16[1536,384]{1,0:T(8,128)(2,1)} %bitcast.79, bf16[1536,384]{1,0:T(8,128)(2,1)} %bitcast.80, bf16[1536,384]{1,0:T(8,128)(2,1)} %bitcast.81, bf16[256,128]{1,0:T(8,128)(2,1)} %get-tuple-element.75.gk_ref, ...), custom_call_target="tpu_custom_call" | custom-call | flops 301989888 | bytes 6291456 | tf_op jit(solution)/shard_map/input_gradient/pallas_call | solution.py:460
  285.3 5.0 %all-gather.7.cloned.1.call-done = bf16[512,3840]{1,0:T(8,128)(2,1)} async-done(((bf16[16,3840]{1,0:T(8,128)(2,1)}), bf16[512,3840]{1,0:T(8,128)(2,1)}) %all-gather.7.cloned.1.call-update) | async-done | bytes 3932176 | tf_op jit(solution)/shard_map/all_gather | solution.py:669
  290.3 4.6 %sum_hidden.1 = (f32[2,128,1152]{2,1,0:T(8,128)}, f32[1152,128]{1,0:T(8,128)}, f32[384,128]{1,0:T(8,128)}) custom-call(s32[16]{0:T(128)} %ids_ref.3, bf16[32,16,3840]{2,1,0:T(8,128)(2,1)} %bitcast.83), custom_call_target="tpu_custom_call" | custom-call | bytes 1769472 | tf_op jit(solution)/shard_map/sum_hidden/pallas_call | solution.py:460
  (139 shorter events, 42.3 us)
Async XLA Ops:
  7.2 154.6 %all-gather.5.cloned.1.call-start = ((), (), s32[]{:S(2)}) async-start(), calls=%async_computation.4 | async-start | bytes 52310016 | tf_op jit(solution)/shard_map/all_gather | solution.py:512
  13.2 24.2 %collective-permute-start.7 = (bf16[16,4224]{1,0:T(8,128)(2,1)S(1)}, bf16[16,4224]{1,0:T(8,128)(2,1)S(1)}, u32[]{:S(2)}, u32[]{:S(2)}) collective-permute-start(bf16[16,4224]{1,0:T(8,128)(2,1)S(1)} %constant_dynamic-update-slice_fusion.5), channel_id=1, source_target_pairs={{3,0},{0,1},{1,2},{2,3},{7,4},{4,5},{5,6},{6,7},{11,8},{8,9},{9,10... | collective-permute-start | bytes 405512 | tf_op jit(solution)/shard_map/ppermute | solution.py:546
  15.6 21.7 %collective-permute-start.6 = (bf16[16,4224]{1,0:T(8,128)(2,1)S(1)}, bf16[16,4224]{1,0:T(8,128)(2,1)S(1)}, u32[]{:S(2)}, u32[]{:S(2)}) collective-permute-start(bf16[16,4224]{1,0:T(8,128)(2,1)S(1)} %constant_dynamic-update-slice_fusion.5), channel_id=1, source_target_pairs={{2,0},{3,1},{0,2},{1,3},{6,4},{7,5},{4,6},{5,7},{10,8},{11,9},{8,1... | collective-permute-start | bytes 405512 | tf_op jit(solution)/shard_map/ppermute | solution.py:546
  18.9 17.8 %collective-permute-start.5 = (bf16[16,4224]{1,0:T(8,128)(2,1)S(1)}, bf16[16,4224]{1,0:T(8,128)(2,1)S(1)}, u32[]{:S(2)}, u32[]{:S(2)}) collective-permute-start(bf16[16,4224]{1,0:T(8,128)(2,1)S(1)} %constant_dynamic-update-slice_fusion.5), channel_id=1, source_target_pairs={{1,0},{2,1},{3,2},{0,3},{5,4},{6,5},{7,6},{4,7},{9,8},{10,9},{11,1... | collective-permute-start | bytes 405512 | tf_op jit(solution)/shard_map/ppermute | solution.py:546
  22.3 19.8 %all-to-all-start = ((bf16[16,48,384]{2,1,0:T(8,128)(2,1)}), bf16[16,48,384]{2,1,0:T(8,128)(2,1)S(1)}, u32[]{:S(2)}, u32[]{:S(2)}) async-start(bf16[16,48,384]{2,1,0:T(8,128)(2,1)} %fusion.11), calls=%async_computation | async-start | bytes 1179648 | tf_op jit(solution)/shard_map/all_to_all | solution.py:525
  29.1 208.9 %reduce-scatter.2.cloned.1.call-start = ((), (), s32[]{:S(2)}) async-start(), calls=%async_computation.3 | async-start | bytes 614400 | tf_op jit(solution)/shard_map/reduce_scatter | solution.py:646
  42.1 4.6 %collective-permute-start = (bf16[16,48,384]{2,1,0:T(8,128)(2,1)S(1)}, bf16[16,48,384]{2,1,0:T(8,128)(2,1)S(1)}, u32[]{:S(2)}, u32[]{:S(2)}) collective-permute-start(bf16[16,48,384]{2,1,0:T(8,128)(2,1)S(1)} %all-to-all-done), channel_id=1, source_target_pairs={{0,4},{4,0},{1,5},{5,1},{2,6},{6,2},{3,7},{7,3},{8,12},{12,8},{9,1... | collective-permute-start | bytes 1769480 | tf_op jit(solution)/shard_map/ppermute | solution.py:523
  51.2 9.9 %collective-permute-start.2 = (bf16[256,256]{1,0:T(8,128)(2,1)}, bf16[256,256]{1,0:T(8,128)(2,1)S(1)}, u32[]{:S(2)}, u32[]{:S(2)}) collective-permute-start(bf16[256,256]{1,0:T(8,128)(2,1)} %get-tuple-element.51), channel_id=1, source_target_pairs={{0,3},{1,4},{2,5},{3,6},{4,7},{8,11},{9,12},{10,13},{11,14},{12,15... | collective-permute-start | bytes 393224 | tf_op jit(solution)/shard_map/ppermute | solution.py:590
  54.3 6.8 %collective-permute-start.1 = (bf16[256,256]{1,0:T(8,128)(2,1)}, bf16[256,256]{1,0:T(8,128)(2,1)S(1)}, u32[]{:S(2)}, u32[]{:S(2)}) collective-permute-start(bf16[256,256]{1,0:T(8,128)(2,1)} %get-tuple-element.51), channel_id=1, source_target_pairs={{0,4},{1,5},{2,6},{3,7},{8,12},{9,13},{10,14},{11,15},{16,20},{17,... | collective-permute-start | bytes 393224 | tf_op jit(solution)/shard_map/ppermute | solution.py:590
  56.5 14.7 %collective-permute-start.4 = (bf16[256,256]{1,0:T(8,128)(2,1)}, bf16[256,256]{1,0:T(8,128)(2,1)S(1)}, u32[]{:S(2)}, u32[]{:S(2)}) collective-permute-start(bf16[256,256]{1,0:T(8,128)(2,1)} %get-tuple-element.51), channel_id=1, source_target_pairs={{0,1},{1,2},{2,3},{3,4},{4,5},{5,6},{6,7},{8,9},{9,10},{10,11},{11... | collective-permute-start | bytes 393224 | tf_op jit(solution)/shard_map/ppermute | solution.py:590
  58.5 12.8 %collective-permute-start.3 = (bf16[256,256]{1,0:T(8,128)(2,1)}, bf16[256,256]{1,0:T(8,128)(2,1)S(1)}, u32[]{:S(2)}, u32[]{:S(2)}) collective-permute-start(bf16[256,256]{1,0:T(8,128)(2,1)} %get-tuple-element.51), channel_id=1, source_target_pairs={{0,2},{1,3},{2,4},{3,5},{4,6},{5,7},{8,10},{9,11},{10,12},{11,13},... | collective-permute-start | bytes 393224 | tf_op jit(solution)/shard_map/ppermute | solution.py:590
  217.4 73.0 %all-gather.7.cloned.1.call-start = ((), (), s32[]{:S(2)}) async-start(), calls=%async_computation.5 | async-start | bytes 4055040 | tf_op jit(solution)/shard_map/all_gather | solution.py:669
  238.0 6.7 %collective-permute-start.8 = (bf16[288,256]{1,0:T(8,128)(2,1)}, bf16[288,256]{1,0:T(8,128)(2,1)S(1)}, u32[]{:S(2)}, u32[]{:S(2)}) collective-permute-start(bf16[288,256]{1,0:T(8,128)(2,1)} %get-tuple-element.63), channel_id=1, source_target_pairs={{0,7},{1,0},{2,1},{3,2},{4,3},{5,4},{6,5},{7,6},{8,15},{9,8},{10,9... | collective-permute-start | bytes 442376 | tf_op jit(solution)/shard_map/ppermute | solution.py:672
  239.9 7.0 %collective-permute-start.9 = (bf16[288,256]{1,0:T(8,128)(2,1)}, bf16[288,256]{1,0:T(8,128)(2,1)S(1)}, u32[]{:S(2)}, u32[]{:S(2)}) collective-permute-start(bf16[288,256]{1,0:T(8,128)(2,1)} %get-tuple-element.64), channel_id=1, source_target_pairs={{0,6},{1,7},{2,0},{3,1},{4,2},{5,3},{6,4},{7,5},{8,14},{9,15},{10,... | collective-permute-start | bytes 442376 | tf_op jit(solution)/shard_map/ppermute | solution.py:672
  240.6 10.0 %collective-permute-start.10 = (bf16[288,256]{1,0:T(8,128)(2,1)}, bf16[288,256]{1,0:T(8,128)(2,1)S(1)}, u32[]{:S(2)}, u32[]{:S(2)}) collective-permute-start(bf16[288,256]{1,0:T(8,128)(2,1)} %get-tuple-element.65), channel_id=1, source_target_pairs={{0,5},{1,6},{2,7},{3,0},{4,1},{5,2},{6,3},{7,4},{8,13},{9,14},{10,... | collective-permute-start | bytes 442376 | tf_op jit(solution)/shard_map/ppermute | solution.py:672
  241.1 3.6 %collective-permute-start.11 = (bf16[256,256]{1,0:T(8,128)(2,1)}, bf16[256,256]{1,0:T(8,128)(2,1)S(1)}, u32[]{:S(2)}, u32[]{:S(2)}) collective-permute-start(bf16[256,256]{1,0:T(8,128)(2,1)} %get-tuple-element.66), channel_id=1, source_target_pairs={{4,0},{5,1},{6,2},{7,3},{12,8},{13,9},{14,10},{15,11},{20,16},{21,... | collective-permute-start | bytes 393224 | tf_op jit(solution)/shard_map/ppermute | solution.py:590
  254.6 1.7 collective-permute-start.12
  258.8 11.0 %collective-permute-start.15 = (bf16[1,16,384]{2,1,0:T(8,128)(2,1)}, bf16[1,16,384]{2,1,0:T(8,128)(2,1)S(1)}, u32[]{:S(2)}, u32[]{:S(2)}) collective-permute-start(bf16[1,16,384]{2,1,0:T(8,128)(2,1)} %get-tuple-element.84), channel_id=1, source_target_pairs={{24,0},{0,8},{8,16},{16,24},{25,1},{1,9},{9,17},{17,25},{26,2},{2,... | collective-permute-start | bytes 36872 | tf_op jit(solution)/shard_map/ppermute | solution.py:704
  259.4 10.5 %collective-permute-start.14 = (bf16[1,16,384]{2,1,0:T(8,128)(2,1)}, bf16[1,16,384]{2,1,0:T(8,128)(2,1)S(1)}, u32[]{:S(2)}, u32[]{:S(2)}) collective-permute-start(bf16[1,16,384]{2,1,0:T(8,128)(2,1)} %get-tuple-element.84), channel_id=1, source_target_pairs={{16,0},{24,8},{0,16},{8,24},{17,1},{25,9},{1,17},{9,25},{18,2},{26... | collective-permute-start | bytes 36872 | tf_op jit(solution)/shard_map/ppermute | solution.py:704
  261.8 8.0 %collective-permute-start.13 = (bf16[1,16,384]{2,1,0:T(8,128)(2,1)}, bf16[1,16,384]{2,1,0:T(8,128)(2,1)S(1)}, u32[]{:S(2)}, u32[]{:S(2)}) collective-permute-start(bf16[1,16,384]{2,1,0:T(8,128)(2,1)} %get-tuple-element.84), channel_id=1, source_target_pairs={{8,0},{16,8},{24,16},{0,24},{9,1},{17,9},{25,17},{1,25},{10,2},{18... | collective-permute-start | bytes 36872 | tf_op jit(solution)/shard_map/ppermute | solution.py:704
  263.7 18.4 %all-to-all-start.1 = ((bf16[64,16,128]{2,1,0:T(8,128)(2,1)}), bf16[64,16,128]{2,1,0:T(8,128)(2,1)S(1)}, u32[]{:S(2)}, u32[]{:S(2)}) async-start(bf16[64,16,128]{2,1,0:T(8,128)(2,1)} %get-tuple-element.74), calls=%async_computation.1 | async-start | bytes 524288 | tf_op jit(solution)/shard_map/all_to_all | solution.py:699
  269.9 12.1 %collective-permute-start.18 = (bf16[4,16,384]{2,1,0:T(8,128)(2,1)S(1)}, bf16[4,16,384]{2,1,0:T(8,128)(2,1)S(1)}, u32[]{:S(2)}, u32[]{:S(2)}) collective-permute-start(bf16[4,16,384]{2,1,0:T(8,128)(2,1)S(1)} %constant_dynamic-update-slice_fusion.10.rest_0_), channel_id=1, source_target_pairs={{96,0},{0,32},{32,64},{64,96},{97,1},{1,33},{33,65},{65,97},{98,2}... | collective-permute-start | bytes 147464 | tf_op jit(solution)/shard_map/ppermute | solution.py:704
  271.0 11.1 %collective-permute-start.17 = (bf16[4,16,384]{2,1,0:T(8,128)(2,1)S(1)}, bf16[4,16,384]{2,1,0:T(8,128)(2,1)S(1)}, u32[]{:S(2)}, u32[]{:S(2)}) collective-permute-start(bf16[4,16,384]{2,1,0:T(8,128)(2,1)S(1)} %constant_dynamic-update-slice_fusion.10.rest_0_), channel_id=1, source_target_pairs={{64,0},{96,32},{0,64},{32,96},{65,1},{97,33},{1,65},{33,97},{66,2}... | collective-permute-start | bytes 147464 | tf_op jit(solution)/shard_map/ppermute | solution.py:704
  273.6 8.5 %collective-permute-start.16 = (bf16[4,16,384]{2,1,0:T(8,128)(2,1)S(1)}, bf16[4,16,384]{2,1,0:T(8,128)(2,1)S(1)}, u32[]{:S(2)}, u32[]{:S(2)}) collective-permute-start(bf16[4,16,384]{2,1,0:T(8,128)(2,1)S(1)} %constant_dynamic-update-slice_fusion.10.rest_0_), channel_id=1, source_target_pairs={{32,0},{64,32},{96,64},{0,96},{33,1},{65,33},{97,65},{1,97},{34,2}... | collective-permute-start | bytes 147464 | tf_op jit(solution)/shard_map/ppermute | solution.py:704
  (22 other events, 184.2 us)
Sparse Core Ops, SparseCore 0:
  11.6 150.1 all-gather.4
  217.5 18.6 reduce-scatter.1
  238.7 51.5 all-gather.6

commit v9 on v8

--- a/solution.py
+++ b/solution.py
@@ -89,15 +89,15 @@
 
 
 def forward_kernel(
-    kv_ref, kseg_ref, qseg_ref, n1_ref, r1_ref, cos_ref, sin_ref, x_ref, cot_ref, gain_ref, a_ref,
-    wq_ref, bq_ref, wo_ref, bo_ref, b_ref, w_ref,
+    kv_ref, kseg_ref, qseg_ref, n1_ref, r1_ref, cos_ref, sin_ref, gain_ref, a_ref,
+    wq_ref, bq_ref, wo_ref, bo_ref, x_hbm, cot_hbm, b_hbm, w_ref,
     q_ref, mixed_ref, p_ref, inv_ref, out_ref, gres_ref, gb_ref, wide_ref, gro_ref, early_ref,
     bias_ref, s_ref, vt_ref, ffn_ref, g2_ref, ro_ref, rd_ref, gr_ref, qs_ref,
-    all_mixed_ref, res_ref, n2_ref, r2_ref, r2t_ref, grd_ref, grdt_ref, wv_ref, sems,
+    all_mixed_ref, res_ref, n2_ref, r2_ref, r2t_ref, grd_ref, grdt_ref, wv_ref, x_ref, cot_ref, b_ref, sems, late_sems,
 ):
     step = pl.program_id(0)
     slots, tensor_count = wv_ref.shape[0], w_ref.shape[1]
-    steps = pl.num_programs(0) - tensor_count
+    steps = b_ref.shape[0]
     rows = q_ref.shape[0]
     chunks = kv_ref.shape[0] // rows
     ff = b_ref.shape[2] // 3
@@ -118,8 +118,15 @@
                 )
         return moves
 
+    late = [
+        pltpu.make_async_copy(source, target, late_sems.at[j])
+        for j, (source, target) in enumerate(((x_hbm, x_ref), (cot_hbm, cot_ref), (b_hbm, b_ref)))
+    ]
+
     @pl.when(step == 0)
     def _():
+        for copy in late:
+            copy.start()
         key = lax.broadcasted_iota(jnp.int32, bias_ref.shape, 0)
         query = lax.broadcasted_iota(jnp.int32, bias_ref.shape, 1)
         allowed = (key >= query) & (key <= query + WINDOW) & (kseg_ref[...] == qseg_ref[...])
@@ -169,6 +176,8 @@
 
     @pl.when(step == tensor_count - 1)
     def _():
+        for copy in late:
+            copy.wait()
         res = x_ref[...].astype(F32) + (ffn_ref[...] + mm_nt(ro_ref[...].astype(BF), a_ref[...]))
         res_ref[...] = res
         n2 = rms(res, gain_ref[...]).astype(BF)
@@ -184,9 +193,7 @@
         rd_ref[...] = jnp.zeros_like(rd_ref)
         gr_ref[...] = jnp.zeros_like(gr_ref)
 
-    @pl.when(step >= tensor_count)
-    def _():
-        at = step - tensor_count
+    def feed_forward(at, carry):
         slot = lax.rem(at, slots)
 
         @pl.when((at >= 1) & (at + slots - 1 < steps))
@@ -195,7 +202,7 @@
                 copy.start()
 
         n2, r2, cot = n2_ref[...], r2_ref[...], cot_ref[...]
-        b_gu, b_d = b_ref[0, :, : 2 * ff], b_ref[0, :, 2 * ff :]
+        b_gu, b_d = b_ref[at, :, : 2 * ff], b_ref[at, :, 2 * ff :]
         arrivals = copies(at, slot)
         weight_rows = wv_ref.shape[1] * wv_ref.shape[2]
         for copy in arrivals[:tensor_count]:
@@ -228,9 +235,11 @@
             target = pl.multiple_of((kind * steps + at) * part_cols, LANES)
             for t in range(tensor_count):
                 early_ref[t, :, pl.ds(target, part_cols)] = term[:, t * part_cols : (t + 1) * part_cols].astype(BF)
-
-    @pl.when(step == tensor_count + steps - 1)
+        return carry
+
+    @pl.when(step == tensor_count)
     def _():
+        lax.fori_loop(0, steps, feed_forward, 0)
         res, n2, cot = res_ref[...], n2_ref[...], cot_ref[...]
         out_ref[...] = (res + (ffn_ref[...] + mm_nt(rd_ref[...].astype(BF), a_ref[...]))).astype(BF)
         grad_two = g2_ref[...] + mm_nt(gr_ref[...].astype(BF), a_ref[...])
@@ -387,9 +396,17 @@
     grad_ref[...] = gres_ref[...] + rms_back(x, gain_ref[...], g1)
 
 
-def sum_hidden_kernel(ids_ref, terms_ref, gu_ref, down_ref, out_ref, acc_ref):
+def sum_hidden_kernel(ids_ref, terms_hbm, gu_ref, down_ref, out_ref, acc_ref, terms_ref, sems):
+    share = terms_ref.shape[0] // sems.shape[0]
+    copies = []
+    for j in range(sems.shape[0]):
+        part = pl.ds(j * share, share)
+        copies.append(pltpu.make_async_copy(terms_hbm.at[part], terms_ref.at[part], sems.at[j]))
+        copies[j].start()
     acc_ref[...] = jnp.zeros_like(acc_ref)
     for s in range(terms_ref.shape[0] // 2):
+        if 2 * s % share == 0:
+            copies[2 * s // share].wait()
         acc_ref[ids_ref[s]] += terms_ref[2 * s].astype(F32) + terms_ref[2 * s + 1].astype(F32)
     adapters, rank, _ = acc_ref.shape
     ff, heads = gu_ref.shape[2], out_ref.shape[0]
@@ -604,25 +621,22 @@
     )
 
     heads = q_cols // HD
-    first, last = tensor_count, tensor_count - 1
+    last = tensor_count - 1
 
     def until_last(spec):
         return pl.BlockSpec(spec.block_shape, lambda t: spec.index_map(jnp.minimum(t, last)))
 
     p_spec, norm_spec = by_step(span, heads * rows), by_step(8, heads * rows)
-    hidden_spec = pl.BlockSpec(
-        (1, LANES, 3 * tensor_count * part_cols), lambda t: (jnp.maximum(t - first, 0), 0, 0)
-    )
     args = (
-        kv_window, kseg, qseg, normed_one, rank_one, cos, sin, tokens, cotangent, gain_two, a_all,
-        weights, b_heads, weights, b_heads, b_hidden, weights,
+        kv_window, kseg, qseg, normed_one, rank_one, cos, sin, gain_two, a_all,
+        weights, b_heads, weights, b_heads, tokens, cotangent, b_hidden, weights,
     )
     (
         queries, mixed, probs, norms, block_output, grad_residual, grad_branch, wide_ffn, grad_ro, early
     ) = call(
-        forward_kernel, "forward", tensor_count + steps, args,
-        wholes(*args[:10]) + [a_spec] + [until_last(spec) for spec in head_specs]
-        + [hidden_spec, pl.BlockSpec(memory_space=pl.ANY)],
+        forward_kernel, "forward", tensor_count + 1, args,
+        wholes(*args[:8]) + [a_spec] + [until_last(spec) for spec in head_specs]
+        + [pl.BlockSpec(memory_space=pl.ANY)] * 4,
         [
             (sds((rows, heads_cols), BF), until_last(token_cols)), (sds((rows, heads_cols), BF), until_last(token_cols)),
             (sds((tensor_count, span, heads * rows), BF), until_last(p_spec)),
@@ -638,7 +652,8 @@
             pltpu.VMEM((rows, LANES), BF), pltpu.VMEM((LANES, rows), BF),
             pltpu.VMEM((rows, LANES), BF), pltpu.VMEM((LANES, rows), BF),
             pltpu.VMEM((slots, dp_count, shard_rows, 3 * tensor_count * part_cols), BF),
-            pltpu.SemaphoreType.DMA((slots, 3 * tensor_count)),
+            pltpu.VMEM((rows, width), BF), pltpu.VMEM((rows, width), BF), pltpu.VMEM(b_hidden.shape, BF),
+            pltpu.SemaphoreType.DMA((slots, 3 * tensor_count)), pltpu.SemaphoreType.DMA((3,)),
         ],
         4 * rows * heads_cols * (span + width) + 12 * rows * width * tensor_count * ff_cols,
         4 * width * heads_cols + 6 * width * tensor_count * ff_cols,
@@ -725,9 +740,13 @@
         [pltpu.VMEM((adapters, RANK, LANES), F32), pltpu.VMEM((adapters, RANK, q_cols), F32)], 0, 4 * LANES * f3,
     )
     gate_up_adapter_grad, down_adapter_grad, out_adapter_grad = call(
-        sum_hidden_kernel, "sum_hidden", 1, (adapter_ids, early), [scalars()] + wholes(early),
+        sum_hidden_kernel, "sum_hidden", 1, (adapter_ids, early),
+        [scalars(), pl.BlockSpec(memory_space=pl.ANY)],
         [(sds((2, LANES, ff_cols), F32), None), (sds((ff_cols, LANES), F32), None), (sds((q_cols, LANES), F32), None)],
-        [pltpu.VMEM((adapters, RANK, f3 + q_cols), F32)], 0, 4 * LANES * f3,
+        [
+            pltpu.VMEM((adapters, RANK, f3 + q_cols), F32), pltpu.VMEM(early.shape, BF), pltpu.SemaphoreType.DMA((8,)),
+        ],
+        0, 4 * LANES * f3,
     )
     return (
         block_output, input_grad, wide_grad.transpose(1, 0, 2), kv_adapter_grad,

time: 302 us -> 300 us (level)
  no operation moved by 1% of the time
where the time goes in v9:
time: 300 us; the launch traced here: 299 us
  waiting for transfers between devices  118 us (39%)
  Pallas kernels  95.3 us (32%)
  starting transfers between devices  45.9 us (15%)
  local copies, waits for them, and re-layouts  15.5 us (5%)
  between operations  15 us (5%)
  other arithmetic  9.76 us (3%)
    pallas_call x9, Pallas kernels, call(): pl.pallas_call(kernel, name=name, grid=(steps,), in_specs=specs, out_spec...  95.3 us
    all_gather x1, waiting for transfers between devices, on_device(): weights = lax.all_gather(pack, ALL, axis=0, tiled=False)  90.4 us
    ppermute x5, starting transfers between devices, moved(): lax.ppermute(value, SEQ, [(c, c + steps) for c in range(parts) if 0 <= c...  11.3 us
    ppermute x5, waiting for transfers between devices, moved(): lax.ppermute(value, SEQ, [(c, c + steps) for c in range(parts) if 0 <= c...  11.3 us
    unnamed x65, local copies, waits for them, and re-layouts  8.86 us
    ppermute x6, starting transfers between devices, with_others(): lax.ppermute(value, axis, [((i + d) % count, i) for i in range(count)])  8.84 us
    all_to_all x1, starting transfers between devices, on_device(): a_own = lax.all_to_all(wide, ('y', 'x'), 0, 0, tiled=True)  6.75 us
    ppermute x3, starting transfers between devices, on_device(): lax.ppermute(b_own, 'tensor', [((z + d) % tensor_count, z) for z in range...  6.5 us
  transfers between devices with their start and end apart: 24, of which 9 were waited for; matrix products, arithmetic and copies ran while one was open for 7% of the time, Pallas kernels for 12%

profile of v9, /device:TPU:1, one launch (start us, length us, event | category | flops | bytes accessed | tf_op | source)
XLA Modules:
  0.0 299.2 jit_solution(5013127241532016463)
XLA Ops:
  13.2 2.5 collective-permute-start.7
  15.6 3.3 %collective-permute-start.6 = (bf16[16,4224]{1,0:T(8,128)(2,1)S(1)}, bf16[16,4224]{1,0:T(8,128)(2,1)S(1)}, u32[]{:S(2)}, u32[]{:S(2)}) collective-permute-start(bf16[16,4224]{1,0:T(8,128)(2,1)S(1)} %constant_dynamic-update-slice_fusion.5), channel_id=1, source_target_pairs={{2,0},{3,1},{0,2},{1,3},{6,4},{7,5},{4,6},{5,7},{10,8},{11,9},{8,1... | collective-permute-start | bytes 405512 | tf_op jit(solution)/shard_map/ppermute | solution.py:563
  22.3 6.8 %all-to-all-start = ((bf16[16,48,384]{2,1,0:T(8,128)(2,1)}), bf16[16,48,384]{2,1,0:T(8,128)(2,1)S(1)}, u32[]{:S(2)}, u32[]{:S(2)}) async-start(bf16[16,48,384]{2,1,0:T(8,128)(2,1)} %fusion.11), calls=%async_computation | async-start | bytes 1179648 | tf_op jit(solution)/shard_map/all_to_all | solution.py:542
  31.2 2.4 fusion.12
  42.1 2.5 collective-permute-start
  44.6 2.1 fusion.5.b_hbm
  47.9 3.3 %keys_values.1 = (bf16[256,1536]{1,0:T(8,128)(2,1)}, bf16[256,128]{1,0:T(8,128)(2,1)}, bf16[256,256]{1,0:T(8,128)(2,1)}) custom-call(bf16[256,1536]{1,0:T(8,128)(2,1)} %x_ref.3, f32[1,1536]{1,0:T(1,128)} %get-tuple-element.102.gain_ref, bf16[1536,384]{1,0:T(8,128)(2,1)} %bitcast.75, bf16[1536,384]{1,0:T(8,128)(2,1)} %bitcast.76, bf16[1536,384]{1,0:T(8,128)(2,1)} %bitcast.77, ...), custom_call_target="tpu_custom_call" | custom-call | flops 301989888 | bytes 2359296 | tf_op jit(solution)/shard_map/keys_values/pallas_call | solution.py:477
  51.2 3.1 %collective-permute-start.2 = (bf16[256,256]{1,0:T(8,128)(2,1)}, bf16[256,256]{1,0:T(8,128)(2,1)S(1)}, u32[]{:S(2)}, u32[]{:S(2)}) collective-permute-start(bf16[256,256]{1,0:T(8,128)(2,1)} %get-tuple-element.51), channel_id=1, source_target_pairs={{0,3},{1,4},{2,5},{3,6},{4,7},{8,11},{9,12},{10,13},{11,14},{12,15... | collective-permute-start | bytes 393224 | tf_op jit(solution)/shard_map/ppermute | solution.py:607
  58.5 2.6 collective-permute-start.3
  61.2 10.1 %collective-permute-done.3 = bf16[256,256]{1,0:T(8,128)(2,1)S(1)} collective-permute-done((bf16[256,256]{1,0:T(8,128)(2,1)}, bf16[256,256]{1,0:T(8,128)(2,1)S(1)}, u32[]{:S(2)}, u32[]{:S(2)}) %collective-permute-start.3) | collective-permute-done | bytes 131104 | tf_op jit(solution)/shard_map/ppermute | solution.py:607
  71.3 90.4 %all-gather.5.cloned.1.call-done = bf16[6144,4224]{1,0:T(8,128)(2,1)} async-done(((bf16[48,4224]{1,0:T(8,128)(2,1)}), bf16[6144,4224]{1,0:T(8,128)(2,1)}) %all-gather.5.cloned.1.call-update) | async-done | bytes 51904528 | tf_op jit(solution)/shard_map/all_gather | solution.py:529
  161.8 53.3 %forward.1 = (bf16[256,1536]{1,0:T(8,128)(2,1)}, bf16[256,1536]{1,0:T(8,128)(2,1)}, bf16[4,1280,768]{2,1,0:T(8,128)(2,1)}, f32[4,8,768]{2,1,0:T(8,128)}, bf16[25...) custom-call(bf16[1280,256]{1,0:T(8,128)(2,1)} %copy-done.2, ...), custom_call_target="tpu_custom_call" | custom-call | flops 26172456960 | bytes 51904512 | tf_op jit(solution)/shard_map/forward/pallas_call | solution.py:477
  215.4 20.3 %attention_back.1 = (bf16[256,256]{1,0:T(8,128)(2,1)}, bf16[288,256]{1,0:T(8,128)(2,1)}, bf16[288,256]{1,0:T(8,128)(2,1)}, bf16[288,256]{1,0:T(8,128)(2,1)}, bf1...) custom-call(s32[1]{0:T(128)} %bitcast.34.tensor_ref, ...), custom_call_target="tpu_custom_call" | custom-call | flops 6442450944 | bytes 9437184 | tf_op jit(solution)/shard_map/attention_back/pallas_call | solution.py:477
  238.9 2.4 collective-permute-start.11
  242.5 2.1 collective-permute-done.9.back2_ref
  244.6 3.7 %collective-permute-done.10.back3_ref = bf16[288,256]{1,0:T(8,128)(2,1)S(1)} collective-permute-done((bf16[288,256]{1,0:T(8,128)(2,1)}, bf16[288,256]{1,0:T(8,128)(2,1)S(1)}, u32[]{:S(2)}, u32[]{:S(2)}) %collective-permute-start.10) | collective-permute-done | bytes 147488 | tf_op jit(solution)/shard_map/ppermute | solution.py:687
  249.0 3.3 %shared_back.1 = (bf16[848,128]{1,0:T(8,128)(2,1)}, bf16[848,128]{1,0:T(8,128)(2,1)}, bf16[256,128]{1,0:T(8,128)(2,1)}, bf16[256,128]{1,0:T(8,128)(2,1)}, bf16[256,128]{1,0:T(8,128)(2,1)}) custom-call(s32[1]{0:T(128)} %bitcast.33.core_ref, bf16[256,1536]{1,0:T(8,128)(2,1)} %get-tuple-element.52.n1_ref, bf16[256,128]{1,0:T(8,128)(2,1)} %get-tuple-element.53.r1_ref, ...), custom_call_target="tpu_custom_call" | custom-call | flops 201326592 | bytes 2359296 | tf_op jit(solution)/shard_map/shared_back/pallas_call | solution.py:477
  257.1 2.4 collective-permute-start.14
  261.5 6.1 %all-to-all-start.1 = ((bf16[64,16,128]{2,1,0:T(8,128)(2,1)}), bf16[64,16,128]{2,1,0:T(8,128)(2,1)S(1)}, u32[]{:S(2)}, u32[]{:S(2)}) async-start(bf16[64,16,128]{2,1,0:T(8,128)(2,1)} %get-tuple-element.74), calls=%async_computation.1 | async-start | bytes 524288 | tf_op jit(solution)/shard_map/all_to_all | solution.py:714
  268.8 2.6 collective-permute-start.17
  273.1 4.9 %input_gradient.1 = f32[256,1536]{1,0:T(8,128)} custom-call(bf16[256,1536]{1,0:T(8,128)(2,1)} %x_ref.3, f32[1,1536]{1,0:T(1,128)} %get-tuple-element.102.gain_ref, bf16[1536,384]{1,0:T(8,128)(2,1)} %bitcast.79, bf16[1536,384]{1,0:T(8,128)(2,1)} %bitcast.80, bf16[1536,384]{1,0:T(8,128)(2,1)} %bitcast.81, bf16[256,128]{1,0:T(8,128)(2,1)} %get-tuple-element.75.gk_ref, ...), custom_call_target="tpu_custom_call" | custom-call | flops 301989888 | bytes 6291456 | tf_op jit(solution)/shard_map/input_gradient/pallas_call | solution.py:477
  278.0 2.2 all-to-all-done.1
  283.5 4.6 %all-gather.7.cloned.1.call-done = bf16[512,3840]{1,0:T(8,128)(2,1)} async-done(((bf16[16,3840]{1,0:T(8,128)(2,1)}), bf16[512,3840]{1,0:T(8,128)(2,1)}) %all-gather.7.cloned.1.call-update) | async-done | bytes 3932176 | tf_op jit(solution)/shard_map/all_gather | solution.py:684
  288.1 4.5 %sum_hidden.1 = (f32[2,128,1152]{2,1,0:T(8,128)}, f32[1152,128]{1,0:T(8,128)}, f32[384,128]{1,0:T(8,128)}) custom-call(s32[16]{0:T(128)} %ids_ref.3, bf16[32,16,3840]{2,1,0:T(8,128)(2,1)} %bitcast.83), custom_call_target="tpu_custom_call" | custom-call | bytes 1769472 | tf_op jit(solution)/shard_map/sum_hidden/pallas_call | solution.py:477
  (139 shorter events, 42.6 us)
Async XLA Ops:
  7.2 154.6 %all-gather.5.cloned.1.call-start = ((), (), s32[]{:S(2)}) async-start(), calls=%async_computation.4 | async-start | bytes 52310016 | tf_op jit(solution)/shard_map/all_gather | solution.py:529
  13.2 24.2 %collective-permute-start.7 = (bf16[16,4224]{1,0:T(8,128)(2,1)S(1)}, bf16[16,4224]{1,0:T(8,128)(2,1)S(1)}, u32[]{:S(2)}, u32[]{:S(2)}) collective-permute-start(bf16[16,4224]{1,0:T(8,128)(2,1)S(1)} %constant_dynamic-update-slice_fusion.5), channel_id=1, source_target_pairs={{3,0},{0,1},{1,2},{2,3},{7,4},{4,5},{5,6},{6,7},{11,8},{8,9},{9,10... | collective-permute-start | bytes 405512 | tf_op jit(solution)/shard_map/ppermute | solution.py:563
  15.6 21.7 %collective-permute-start.6 = (bf16[16,4224]{1,0:T(8,128)(2,1)S(1)}, bf16[16,4224]{1,0:T(8,128)(2,1)S(1)}, u32[]{:S(2)}, u32[]{:S(2)}) collective-permute-start(bf16[16,4224]{1,0:T(8,128)(2,1)S(1)} %constant_dynamic-update-slice_fusion.5), channel_id=1, source_target_pairs={{2,0},{3,1},{0,2},{1,3},{6,4},{7,5},{4,6},{5,7},{10,8},{11,9},{8,1... | collective-permute-start | bytes 405512 | tf_op jit(solution)/shard_map/ppermute | solution.py:563
  18.9 17.8 %collective-permute-start.5 = (bf16[16,4224]{1,0:T(8,128)(2,1)S(1)}, bf16[16,4224]{1,0:T(8,128)(2,1)S(1)}, u32[]{:S(2)}, u32[]{:S(2)}) collective-permute-start(bf16[16,4224]{1,0:T(8,128)(2,1)S(1)} %constant_dynamic-update-slice_fusion.5), channel_id=1, source_target_pairs={{1,0},{2,1},{3,2},{0,3},{5,4},{6,5},{7,6},{4,7},{9,8},{10,9},{11,1... | collective-permute-start | bytes 405512 | tf_op jit(solution)/shard_map/ppermute | solution.py:563
  22.3 19.8 %all-to-all-start = ((bf16[16,48,384]{2,1,0:T(8,128)(2,1)}), bf16[16,48,384]{2,1,0:T(8,128)(2,1)S(1)}, u32[]{:S(2)}, u32[]{:S(2)}) async-start(bf16[16,48,384]{2,1,0:T(8,128)(2,1)} %fusion.11), calls=%async_computation | async-start | bytes 1179648 | tf_op jit(solution)/shard_map/all_to_all | solution.py:542
  29.0 206.7 %reduce-scatter.2.cloned.1.call-start = ((), (), s32[]{:S(2)}) async-start(), calls=%async_computation.3 | async-start | bytes 614400 | tf_op jit(solution)/shard_map/reduce_scatter | solution.py:661
  42.1 4.6 %collective-permute-start = (bf16[16,48,384]{2,1,0:T(8,128)(2,1)S(1)}, bf16[16,48,384]{2,1,0:T(8,128)(2,1)S(1)}, u32[]{:S(2)}, u32[]{:S(2)}) collective-permute-start(bf16[16,48,384]{2,1,0:T(8,128)(2,1)S(1)} %all-to-all-done), channel_id=1, source_target_pairs={{0,4},{4,0},{1,5},{5,1},{2,6},{6,2},{3,7},{7,3},{8,12},{12,8},{9,1... | collective-permute-start | bytes 1769480 | tf_op jit(solution)/shard_map/ppermute | solution.py:540
  51.2 9.9 %collective-permute-start.2 = (bf16[256,256]{1,0:T(8,128)(2,1)}, bf16[256,256]{1,0:T(8,128)(2,1)S(1)}, u32[]{:S(2)}, u32[]{:S(2)}) collective-permute-start(bf16[256,256]{1,0:T(8,128)(2,1)} %get-tuple-element.51), channel_id=1, source_target_pairs={{0,3},{1,4},{2,5},{3,6},{4,7},{8,11},{9,12},{10,13},{11,14},{12,15... | collective-permute-start | bytes 393224 | tf_op jit(solution)/shard_map/ppermute | solution.py:607
  54.3 6.8 %collective-permute-start.1 = (bf16[256,256]{1,0:T(8,128)(2,1)}, bf16[256,256]{1,0:T(8,128)(2,1)S(1)}, u32[]{:S(2)}, u32[]{:S(2)}) collective-permute-start(bf16[256,256]{1,0:T(8,128)(2,1)} %get-tuple-element.51), channel_id=1, source_target_pairs={{0,4},{1,5},{2,6},{3,7},{8,12},{9,13},{10,14},{11,15},{16,20},{17,... | collective-permute-start | bytes 393224 | tf_op jit(solution)/shard_map/ppermute | solution.py:607
  56.5 14.7 %collective-permute-start.4 = (bf16[256,256]{1,0:T(8,128)(2,1)}, bf16[256,256]{1,0:T(8,128)(2,1)S(1)}, u32[]{:S(2)}, u32[]{:S(2)}) collective-permute-start(bf16[256,256]{1,0:T(8,128)(2,1)} %get-tuple-element.51), channel_id=1, source_target_pairs={{0,1},{1,2},{2,3},{3,4},{4,5},{5,6},{6,7},{8,9},{9,10},{10,11},{11... | collective-permute-start | bytes 393224 | tf_op jit(solution)/shard_map/ppermute | solution.py:607
  58.5 12.8 %collective-permute-start.3 = (bf16[256,256]{1,0:T(8,128)(2,1)}, bf16[256,256]{1,0:T(8,128)(2,1)S(1)}, u32[]{:S(2)}, u32[]{:S(2)}) collective-permute-start(bf16[256,256]{1,0:T(8,128)(2,1)} %get-tuple-element.51), channel_id=1, source_target_pairs={{0,2},{1,3},{2,4},{3,5},{4,6},{5,7},{8,10},{9,11},{10,12},{11,13},... | collective-permute-start | bytes 393224 | tf_op jit(solution)/shard_map/ppermute | solution.py:607
  215.1 72.9 %all-gather.7.cloned.1.call-start = ((), (), s32[]{:S(2)}) async-start(), calls=%async_computation.5 | async-start | bytes 4055040 | tf_op jit(solution)/shard_map/all_gather | solution.py:684
  235.8 6.7 %collective-permute-start.8 = (bf16[288,256]{1,0:T(8,128)(2,1)}, bf16[288,256]{1,0:T(8,128)(2,1)S(1)}, u32[]{:S(2)}, u32[]{:S(2)}) collective-permute-start(bf16[288,256]{1,0:T(8,128)(2,1)} %get-tuple-element.63), channel_id=1, source_target_pairs={{0,7},{1,0},{2,1},{3,2},{4,3},{5,4},{6,5},{7,6},{8,15},{9,8},{10,9... | collective-permute-start | bytes 442376 | tf_op jit(solution)/shard_map/ppermute | solution.py:687
  237.7 7.0 %collective-permute-start.9 = (bf16[288,256]{1,0:T(8,128)(2,1)}, bf16[288,256]{1,0:T(8,128)(2,1)S(1)}, u32[]{:S(2)}, u32[]{:S(2)}) collective-permute-start(bf16[288,256]{1,0:T(8,128)(2,1)} %get-tuple-element.64), channel_id=1, source_target_pairs={{0,6},{1,7},{2,0},{3,1},{4,2},{5,3},{6,4},{7,5},{8,14},{9,15},{10,... | collective-permute-start | bytes 442376 | tf_op jit(solution)/shard_map/ppermute | solution.py:687
  238.3 10.0 %collective-permute-start.10 = (bf16[288,256]{1,0:T(8,128)(2,1)}, bf16[288,256]{1,0:T(8,128)(2,1)S(1)}, u32[]{:S(2)}, u32[]{:S(2)}) collective-permute-start(bf16[288,256]{1,0:T(8,128)(2,1)} %get-tuple-element.65), channel_id=1, source_target_pairs={{0,5},{1,6},{2,7},{3,0},{4,1},{5,2},{6,3},{7,4},{8,13},{9,14},{10,... | collective-permute-start | bytes 442376 | tf_op jit(solution)/shard_map/ppermute | solution.py:687
  238.9 3.6 %collective-permute-start.11 = (bf16[256,256]{1,0:T(8,128)(2,1)}, bf16[256,256]{1,0:T(8,128)(2,1)S(1)}, u32[]{:S(2)}, u32[]{:S(2)}) collective-permute-start(bf16[256,256]{1,0:T(8,128)(2,1)} %get-tuple-element.66), channel_id=1, source_target_pairs={{4,0},{5,1},{6,2},{7,3},{12,8},{13,9},{14,10},{15,11},{20,16},{21,... | collective-permute-start | bytes 393224 | tf_op jit(solution)/shard_map/ppermute | solution.py:607
  252.4 1.7 collective-permute-start.12
  256.6 11.0 %collective-permute-start.15 = (bf16[1,16,384]{2,1,0:T(8,128)(2,1)}, bf16[1,16,384]{2,1,0:T(8,128)(2,1)S(1)}, u32[]{:S(2)}, u32[]{:S(2)}) collective-permute-start(bf16[1,16,384]{2,1,0:T(8,128)(2,1)} %get-tuple-element.84), channel_id=1, source_target_pairs={{24,0},{0,8},{8,16},{16,24},{25,1},{1,9},{9,17},{17,25},{26,2},{2,... | collective-permute-start | bytes 36872 | tf_op jit(solution)/shard_map/ppermute | solution.py:719
  257.1 10.5 %collective-permute-start.14 = (bf16[1,16,384]{2,1,0:T(8,128)(2,1)}, bf16[1,16,384]{2,1,0:T(8,128)(2,1)S(1)}, u32[]{:S(2)}, u32[]{:S(2)}) collective-permute-start(bf16[1,16,384]{2,1,0:T(8,128)(2,1)} %get-tuple-element.84), channel_id=1, source_target_pairs={{16,0},{24,8},{0,16},{8,24},{17,1},{25,9},{1,17},{9,25},{18,2},{26... | collective-permute-start | bytes 36872 | tf_op jit(solution)/shard_map/ppermute | solution.py:719
  259.5 8.1 %collective-permute-start.13 = (bf16[1,16,384]{2,1,0:T(8,128)(2,1)}, bf16[1,16,384]{2,1,0:T(8,128)(2,1)S(1)}, u32[]{:S(2)}, u32[]{:S(2)}) collective-permute-start(bf16[1,16,384]{2,1,0:T(8,128)(2,1)} %get-tuple-element.84), channel_id=1, source_target_pairs={{8,0},{16,8},{24,16},{0,24},{9,1},{17,9},{25,17},{1,25},{10,2},{18... | collective-permute-start | bytes 36872 | tf_op jit(solution)/shard_map/ppermute | solution.py:719
  261.5 18.7 %all-to-all-start.1 = ((bf16[64,16,128]{2,1,0:T(8,128)(2,1)}), bf16[64,16,128]{2,1,0:T(8,128)(2,1)S(1)}, u32[]{:S(2)}, u32[]{:S(2)}) async-start(bf16[64,16,128]{2,1,0:T(8,128)(2,1)} %get-tuple-element.74), calls=%async_computation.1 | async-start | bytes 524288 | tf_op jit(solution)/shard_map/all_to_all | solution.py:714
  267.7 12.5 %collective-permute-start.18 = (bf16[4,16,384]{2,1,0:T(8,128)(2,1)S(1)}, bf16[4,16,384]{2,1,0:T(8,128)(2,1)S(1)}, u32[]{:S(2)}, u32[]{:S(2)}) collective-permute-start(bf16[4,16,384]{2,1,0:T(8,128)(2,1)S(1)} %constant_dynamic-update-slice_fusion.10.rest_0_), channel_id=1, source_target_pairs={{96,0},{0,32},{32,64},{64,96},{97,1},{1,33},{33,65},{65,97},{98,2}... | collective-permute-start | bytes 147464 | tf_op jit(solution)/shard_map/ppermute | solution.py:719
  268.8 11.4 %collective-permute-start.17 = (bf16[4,16,384]{2,1,0:T(8,128)(2,1)S(1)}, bf16[4,16,384]{2,1,0:T(8,128)(2,1)S(1)}, u32[]{:S(2)}, u32[]{:S(2)}) collective-permute-start(bf16[4,16,384]{2,1,0:T(8,128)(2,1)S(1)} %constant_dynamic-update-slice_fusion.10.rest_0_), channel_id=1, source_target_pairs={{64,0},{96,32},{0,64},{32,96},{65,1},{97,33},{1,65},{33,97},{66,2}... | collective-permute-start | bytes 147464 | tf_op jit(solution)/shard_map/ppermute | solution.py:719
  271.4 8.8 %collective-permute-start.16 = (bf16[4,16,384]{2,1,0:T(8,128)(2,1)S(1)}, bf16[4,16,384]{2,1,0:T(8,128)(2,1)S(1)}, u32[]{:S(2)}, u32[]{:S(2)}) collective-permute-start(bf16[4,16,384]{2,1,0:T(8,128)(2,1)S(1)} %constant_dynamic-update-slice_fusion.10.rest_0_), channel_id=1, source_target_pairs={{32,0},{64,32},{96,64},{0,96},{33,1},{65,33},{97,65},{1,97},{34,2}... | collective-permute-start | bytes 147464 | tf_op jit(solution)/shard_map/ppermute | solution.py:719
  (22 other events, 184.2 us)
Sparse Core Ops, SparseCore 0:
  11.6 150.1 all-gather.4
  215.3 18.6 reduce-scatter.1
  236.5 51.5 all-gather.6

commit v10 on v9

--- a/solution.py
+++ b/solution.py
@@ -396,28 +396,43 @@
     grad_ref[...] = gres_ref[...] + rms_back(x, gain_ref[...], g1)
 
 
-def sum_hidden_kernel(ids_ref, terms_hbm, gu_ref, down_ref, out_ref, acc_ref, terms_ref, sems):
-    share = terms_ref.shape[0] // sems.shape[0]
-    copies = []
-    for j in range(sems.shape[0]):
-        part = pl.ds(j * share, share)
-        copies.append(pltpu.make_async_copy(terms_hbm.at[part], terms_ref.at[part], sems.at[j]))
-        copies[j].start()
+def sum_hidden_kernel(
+    ids_ref, terms_hbm, gu_hbm, down_hbm, out_hbm, terms_ref, acc_ref, gu_ref, down_ref, out_ref, sems, out_sems,
+):
+    adapters, rank, cols = acc_ref.shape
+    ff = gu_ref.shape[2]
+    groups = (slice(2 * ff, cols), slice(0, ff), slice(ff, 2 * ff))
+    arrivals = []
+    for j, group in enumerate(groups):
+        part = pl.ds(group.start, group.stop - group.start)
+        arrivals.append(pltpu.make_async_copy(terms_hbm.at[:, :, part], terms_ref.at[:, :, part], sems.at[j]))
+        arrivals[j].start()
     acc_ref[...] = jnp.zeros_like(acc_ref)
-    for s in range(terms_ref.shape[0] // 2):
-        if 2 * s % share == 0:
-            copies[2 * s // share].wait()
-        acc_ref[ids_ref[s]] += terms_ref[2 * s].astype(F32) + terms_ref[2 * s + 1].astype(F32)
-    adapters, rank, _ = acc_ref.shape
-    ff, heads = gu_ref.shape[2], out_ref.shape[0]
-
-    def taken(first, count):
-        return acc_ref[:, :, first : first + count].reshape(adapters * rank, count)
-
-    gu_ref[0] = taken(0, ff)
-    gu_ref[1] = taken(ff, ff)
-    down_ref[...] = taken(2 * ff, ff).T
-    out_ref[...] = taken(3 * ff, heads).T
+
+    def added(group):
+        for s in range(terms_ref.shape[0] // 2):
+            pair = terms_ref[2 * s, :, group].astype(F32) + terms_ref[2 * s + 1, :, group].astype(F32)
+            acc_ref[ids_ref[s], :, group] += pair
+
+    sent = [
+        pltpu.make_async_copy(down_ref, down_hbm, out_sems.at[0]),
+        pltpu.make_async_copy(out_ref, out_hbm, out_sems.at[1]),
+        pltpu.make_async_copy(gu_ref.at[0], gu_hbm.at[0], out_sems.at[2]),
+        pltpu.make_async_copy(gu_ref.at[1], gu_hbm.at[1], out_sems.at[3]),
+    ]
+    arrivals[0].wait()
+    added(groups[0])
+    down_ref[...] = acc_ref[:, :, 2 * ff : 3 * ff].reshape(adapters * rank, ff).T
+    sent[0].start()
+    out_ref[...] = acc_ref[:, :, 3 * ff :].reshape(adapters * rank, cols - 3 * ff).T
+    sent[1].start()
+    for j in range(2):
+        arrivals[1 + j].wait()
+        added(groups[1 + j])
+        gu_ref[j] = acc_ref[:, :, groups[1 + j]].reshape(adapters * rank, ff)
+        sent[2 + j].start()
+    for copy in sent:
+        copy.wait()
 
 
 def sum_wide_kernel(ids_ref, own_ref, terms_ref, *rest):
@@ -559,10 +574,6 @@
     b_own = jnp.concatenate(
         [gu_rows[0], gu_rows[1], take_cols(down_adapter).T, take_rows(q_adapter), take_cols(out_adapter).T], axis=1
     )
-    b_parts = [b_own] + [
-        lax.ppermute(b_own, "tensor", [((z + d) % tensor_count, z) for z in range(tensor_count)])
-        for d in range(1, tensor_count)
-    ]
     kv_rows = take_rows(kv_adapter)
     b_kv = jnp.stack([in_slot(kv_rows[0], SLOT_K), in_slot(kv_rows[1], SLOT_V)])
 
@@ -608,6 +619,11 @@
 
     kv_window = jnp.concatenate([moved(kv_own, d) for d in range(reach, 0, -1)] + [kv_own])
 
+    b_own, kv_own = lax.optimization_barrier((b_own, kv_own))
+    b_parts = [b_own] + [
+        lax.ppermute(b_own, "tensor", [((z + d) % tensor_count, z) for z in range(tensor_count)])
+        for d in range(1, tensor_count)
+    ]
     b_all = jnp.roll(jnp.stack(b_parts), tensor, axis=0)
     b_heads = jnp.concatenate(
         [in_slot(b_all[:, :, f3 : f3 + q_cols], SLOT_Q), in_slot(b_all[:, :, f3 + q_cols :], SLOT_O)], axis=2
@@ -739,13 +755,14 @@
         [(sds((own_rows, 7, LANES), F32), None), (sds((2, 1, HD), F32), None), (sds((LANES, q_cols), F32), None)],
         [pltpu.VMEM((adapters, RANK, LANES), F32), pltpu.VMEM((adapters, RANK, q_cols), F32)], 0, 4 * LANES * f3,
     )
+    shapes = [(2, LANES, ff_cols), (ff_cols, LANES), (q_cols, LANES)]
     gate_up_adapter_grad, down_adapter_grad, out_adapter_grad = call(
         sum_hidden_kernel, "sum_hidden", 1, (adapter_ids, early),
         [scalars(), pl.BlockSpec(memory_space=pl.ANY)],
-        [(sds((2, LANES, ff_cols), F32), None), (sds((ff_cols, LANES), F32), None), (sds((q_cols, LANES), F32), None)],
-        [
-            pltpu.VMEM((adapters, RANK, f3 + q_cols), F32), pltpu.VMEM(early.shape, BF), pltpu.SemaphoreType.DMA((8,)),
-        ],
+        [(sds(shape, F32), pl.BlockSpec(memory_space=pl.ANY)) for shape in shapes],
+        [pltpu.VMEM(early.shape, BF), pltpu.VMEM((adapters, RANK, f3 + q_cols), F32)]
+        + [pltpu.VMEM(shape, F32) for shape in shapes]
+        + [pltpu.SemaphoreType.DMA((3,)), pltpu.SemaphoreType.DMA((4,))],
         0, 4 * LANES * f3,
     )
     return (

time: 300 us -> 300 us (level)
    ppermute x3, waiting for transfers between devices: 0.01 us -> 6.68 us  [on_device(): lax.ppermute(b_own, 'tensor', [((z + d) % tensor_count, z) for z in range...]
    all_gather x1, waiting for transfers between devices: 90.4 us -> 85 us  [on_device(): weights = lax.all_gather(pack, ALL, axis=0, tiled=False)]
    ppermute x3, starting transfers between devices: 6.5 us -> 1.86 us  [on_device(): lax.ppermute(b_own, 'tensor', [((z + d) % tensor_count, z) for z in range...]
    ppermute x5, starting transfers between devices: 11.3 us -> 15.6 us  [moved(): lax.ppermute(value, SEQ, [(c, c + steps) for c in range(parts) if 0 <= c...]
    unnamed x65 -> x63, local copies, waits for them, and re-layouts: 8.86 us -> 7.69 us
  transfers between devices with their start and end apart: 24 -> 24, of which waited for: 9 -> 11; matrix products, arithmetic and copies ran while one was open for 7% -> 7% of each run, Pallas kernels for 12% -> 12%
where the time goes in v10:
time: 300 us; the launch traced here: 299 us
  waiting for transfers between devices  118 us (39%)
  Pallas kernels  94.8 us (32%)
  starting transfers between devices  46.6 us (16%)
  between operations  15 us (5%)
  local copies, waits for them, and re-layouts  14.3 us (5%)
  other arithmetic  9.73 us (3%)
    pallas_call x9, Pallas kernels, call(): pl.pallas_call(kernel, name=name, grid=(steps,), in_specs=specs, out_spec...  94.8 us
    all_gather x1, waiting for transfers between devices, on_device(): weights = lax.all_gather(pack, ALL, axis=0, tiled=False)  85 us
    ppermute x5, starting transfers between devices, moved(): lax.ppermute(value, SEQ, [(c, c + steps) for c in range(parts) if 0 <= c...  15.6 us
    ppermute x5, waiting for transfers between devices, moved(): lax.ppermute(value, SEQ, [(c, c + steps) for c in range(parts) if 0 <= c...  9.42 us
    ppermute x6, starting transfers between devices, with_others(): lax.ppermute(value, axis, [((i + d) % count, i) for i in range(count)])  8.83 us
    all_to_all x1, starting transfers between devices, on_device(): a_own = lax.all_to_all(wide, ('y', 'x'), 0, 0, tiled=True)  7.72 us
    unnamed x63, local copies, waits for them, and re-layouts  7.69 us
    ppermute x3, waiting for transfers between devices, on_device(): lax.ppermute(b_own, 'tensor', [((z + d) % tensor_count, z) for z in range...  6.68 us
  transfers between devices with their start and end apart: 24, of which 11 were waited for; matrix products, arithmetic and copies ran while one was open for 7% of the time, Pallas kernels for 12%

profile of v10, /device:TPU:1, one launch (start us, length us, event | category | flops | bytes accessed | tf_op | source)
XLA Modules:
  0.0 298.7 jit_solution(11705954991723869155)
XLA Ops:
  11.7 7.7 %all-to-all-start = ((bf16[16,48,384]{2,1,0:T(8,128)(2,1)}), bf16[16,48,384]{2,1,0:T(8,128)(2,1)S(1)}, u32[]{:S(2)}, u32[]{:S(2)}) async-start(bf16[16,48,384]{2,1,0:T(8,128)(2,1)} %fusion.11), calls=%async_computation | async-start | bytes 1179648 | tf_op jit(solution)/shard_map/all_to_all | solution.py:557
  25.0 2.4 fusion.12
  27.4 3.1 %all-to-all-done = bf16[16,48,384]{2,1,0:T(8,128)(2,1)S(1)} async-done(((bf16[16,48,384]{2,1,0:T(8,128)(2,1)}), bf16[16,48,384]{2,1,0:T(8,128)(2,1)S(1)}, u32[]{:S(2)}, u32[]{:S(2)}) %all-to-all-start) | async-done | bytes 589856 | tf_op jit(solution)/shard_map/all_to_all | solution.py:557
  30.5 2.5 collective-permute-start
  37.4 3.4 %keys_values.1 = (bf16[256,1536]{1,0:T(8,128)(2,1)}, bf16[256,128]{1,0:T(8,128)(2,1)}, bf16[256,256]{1,0:T(8,128)(2,1)}) custom-call(bf16[256,1536]{1,0:T(8,128)(2,1)} %x_ref.3, f32[1,1536]{1,0:T(1,128)} %get-tuple-element.104.gain_ref, bf16[1536,384]{1,0:T(8,128)(2,1)} %bitcast.75, bf16[1536,384]{1,0:T(8,128)(2,1)} %bitcast.76, bf16[1536,384]{1,0:T(8,128)(2,1)} %bitcast.77, ...), custom_call_target="tpu_custom_call" | custom-call | flops 301989888 | bytes 2359296 | tf_op jit(solution)/shard_map/keys_values/pallas_call | solution.py:492
  40.7 4.4 %collective-permute-start.4 = (bf16[256,256]{1,0:T(8,128)(2,1)}, bf16[256,256]{1,0:T(8,128)(2,1)S(1)}, u32[]{:S(2)}, u32[]{:S(2)}) collective-permute-start(bf16[256,256]{1,0:T(8,128)(2,1)} %get-tuple-element.52), channel_id=1, source_target_pairs={{0,1},{1,2},{2,3},{3,4},{4,5},{5,6},{6,7},{8,9},{9,10},{10,11},{11... | collective-permute-start | bytes 393224 | tf_op jit(solution)/shard_map/ppermute | solution.py:618
  45.2 5.6 %collective-permute-start.3 = (bf16[256,256]{1,0:T(8,128)(2,1)}, bf16[256,256]{1,0:T(8,128)(2,1)S(1)}, u32[]{:S(2)}, u32[]{:S(2)}) collective-permute-start(bf16[256,256]{1,0:T(8,128)(2,1)} %get-tuple-element.52), channel_id=1, source_target_pairs={{0,2},{1,3},{2,4},{3,5},{4,6},{5,7},{8,10},{9,11},{10,12},{11,13},... | collective-permute-start | bytes 393224 | tf_op jit(solution)/shard_map/ppermute | solution.py:618
  54.1 2.2 collective-permute-done.1
  56.3 6.0 %collective-permute-done.2 = bf16[256,256]{1,0:T(8,128)(2,1)S(1)} collective-permute-done((bf16[256,256]{1,0:T(8,128)(2,1)}, bf16[256,256]{1,0:T(8,128)(2,1)S(1)}, u32[]{:S(2)}, u32[]{:S(2)}) %collective-permute-start.2) | collective-permute-done | bytes 131104 | tf_op jit(solution)/shard_map/ppermute | solution.py:618
  64.2 6.7 %collective-permute-done.5 = bf16[16,4224]{1,0:T(8,128)(2,1)S(1)} collective-permute-done((bf16[16,4224]{1,0:T(8,128)(2,1)S(1)}, bf16[16,4224]{1,0:T(8,128)(2,1)S(1)}, u32[]{:S(2)}, u32[]{:S(2)}) %collective-permute-start.5) | collective-permute-done | bytes 135200 | tf_op jit(solution)/shard_map/ppermute | solution.py:624
  74.7 2.2 fusion.5.b_hbm
  76.9 85.0 %all-gather.5.cloned.1.call-done = bf16[6144,4224]{1,0:T(8,128)(2,1)} async-done(((bf16[48,4224]{1,0:T(8,128)(2,1)}), bf16[6144,4224]{1,0:T(8,128)(2,1)}) %all-gather.5.cloned.1.call-update) | async-done | bytes 51904528 | tf_op jit(solution)/shard_map/all_gather | solution.py:544
  161.9 53.3 %forward.1 = (bf16[256,1536]{1,0:T(8,128)(2,1)}, bf16[256,1536]{1,0:T(8,128)(2,1)}, bf16[4,1280,768]{2,1,0:T(8,128)(2,1)}, f32[4,8,768]{2,1,0:T(8,128)}, bf16[25...) custom-call(bf16[1280,256]{1,0:T(8,128)(2,1)} %copy-done.2, ...), custom_call_target="tpu_custom_call" | custom-call | flops 26172456960 | bytes 51904512 | tf_op jit(solution)/shard_map/forward/pallas_call | solution.py:492
  215.5 20.3 %attention_back.1 = (bf16[256,256]{1,0:T(8,128)(2,1)}, bf16[288,256]{1,0:T(8,128)(2,1)}, bf16[288,256]{1,0:T(8,128)(2,1)}, bf16[288,256]{1,0:T(8,128)(2,1)}, bf1...) custom-call(s32[1]{0:T(128)} %bitcast.34.tensor_ref, ...), custom_call_target="tpu_custom_call" | custom-call | flops 6442450944 | bytes 9437184 | tf_op jit(solution)/shard_map/attention_back/pallas_call | solution.py:492
  238.9 2.4 collective-permute-start.11
  242.5 2.1 collective-permute-done.9.back2_ref
  244.7 3.8 %collective-permute-done.10.back3_ref = bf16[288,256]{1,0:T(8,128)(2,1)S(1)} collective-permute-done((bf16[288,256]{1,0:T(8,128)(2,1)}, bf16[288,256]{1,0:T(8,128)(2,1)S(1)}, u32[]{:S(2)}, u32[]{:S(2)}) %collective-permute-start.10) | collective-permute-done | bytes 147488 | tf_op jit(solution)/shard_map/ppermute | solution.py:703
  249.1 3.3 %shared_back.1 = (bf16[848,128]{1,0:T(8,128)(2,1)}, bf16[848,128]{1,0:T(8,128)(2,1)}, bf16[256,128]{1,0:T(8,128)(2,1)}, bf16[256,128]{1,0:T(8,128)(2,1)}, bf16[256,128]{1,0:T(8,128)(2,1)}) custom-call(s32[1]{0:T(128)} %bitcast.33.core_ref, bf16[256,1536]{1,0:T(8,128)(2,1)} %get-tuple-element.53.n1_ref, bf16[256,128]{1,0:T(8,128)(2,1)} %get-tuple-element.54.r1_ref, ...), custom_call_target="tpu_custom_call" | custom-call | flops 201326592 | bytes 2359296 | tf_op jit(solution)/shard_map/shared_back/pallas_call | solution.py:492
  257.2 2.4 collective-permute-start.14
  261.5 6.2 %all-to-all-start.1 = ((bf16[64,16,128]{2,1,0:T(8,128)(2,1)}), bf16[64,16,128]{2,1,0:T(8,128)(2,1)S(1)}, u32[]{:S(2)}, u32[]{:S(2)}) async-start(bf16[64,16,128]{2,1,0:T(8,128)(2,1)} %get-tuple-element.76), calls=%async_computation.1 | async-start | bytes 524288 | tf_op jit(solution)/shard_map/all_to_all | solution.py:730
  268.8 2.6 collective-permute-start.17
  273.1 4.9 %input_gradient.1 = f32[256,1536]{1,0:T(8,128)} custom-call(bf16[256,1536]{1,0:T(8,128)(2,1)} %x_ref.3, f32[1,1536]{1,0:T(1,128)} %get-tuple-element.104.gain_ref, bf16[1536,384]{1,0:T(8,128)(2,1)} %bitcast.79, bf16[1536,384]{1,0:T(8,128)(2,1)} %bitcast.80, bf16[1536,384]{1,0:T(8,128)(2,1)} %bitcast.81, bf16[256,128]{1,0:T(8,128)(2,1)} %get-tuple-element.77.gk_ref, ...), custom_call_target="tpu_custom_call" | custom-call | flops 301989888 | bytes 6291456 | tf_op jit(solution)/shard_map/input_gradient/pallas_call | solution.py:492
  283.2 4.9 %all-gather.7.cloned.1.call-done = bf16[512,3840]{1,0:T(8,128)(2,1)} async-done(((bf16[16,3840]{1,0:T(8,128)(2,1)}), bf16[512,3840]{1,0:T(8,128)(2,1)}) %all-gather.7.cloned.1.call-update) | async-done | bytes 3932176 | tf_op jit(solution)/shard_map/all_gather | solution.py:700
  288.2 4.0 %sum_hidden.1 = (f32[2,128,1152]{2,1,0:T(8,128)}, f32[1152,128]{1,0:T(8,128)}, f32[384,128]{1,0:T(8,128)}) custom-call(s32[16]{0:T(128)} %ids_ref.3, bf16[32,16,3840]{2,1,0:T(8,128)(2,1)} %bitcast.83), custom_call_target="tpu_custom_call" | custom-call | bytes 1769472 | tf_op jit(solution)/shard_map/sum_hidden/pallas_call | solution.py:492
  (137 shorter events, 42.3 us)
Async XLA Ops:
  7.2 154.6 %all-gather.5.cloned.1.call-start = ((), (), s32[]{:S(2)}) async-start(), calls=%async_computation.4 | async-start | bytes 52310016 | tf_op jit(solution)/shard_map/all_gather | solution.py:544
  11.7 18.8 %all-to-all-start = ((bf16[16,48,384]{2,1,0:T(8,128)(2,1)}), bf16[16,48,384]{2,1,0:T(8,128)(2,1)S(1)}, u32[]{:S(2)}, u32[]{:S(2)}) async-start(bf16[16,48,384]{2,1,0:T(8,128)(2,1)} %fusion.11), calls=%async_computation | async-start | bytes 1179648 | tf_op jit(solution)/shard_map/all_to_all | solution.py:557
  19.4 216.3 %reduce-scatter.2.cloned.1.call-start = ((), (), s32[]{:S(2)}) async-start(), calls=%async_computation.3 | async-start | bytes 614400 | tf_op jit(solution)/shard_map/reduce_scatter | solution.py:677
  30.5 5.7 %collective-permute-start = (bf16[16,48,384]{2,1,0:T(8,128)(2,1)S(1)}, bf16[16,48,384]{2,1,0:T(8,128)(2,1)S(1)}, u32[]{:S(2)}, u32[]{:S(2)}) collective-permute-start(bf16[16,48,384]{2,1,0:T(8,128)(2,1)S(1)} %all-to-all-done), channel_id=1, source_target_pairs={{0,4},{4,0},{1,5},{5,1},{2,6},{6,2},{3,7},{7,3},{8,12},{12,8},{9,1... | collective-permute-start | bytes 1769480 | tf_op jit(solution)/shard_map/ppermute | solution.py:555
  40.7 23.4 %collective-permute-start.4 = (bf16[256,256]{1,0:T(8,128)(2,1)}, bf16[256,256]{1,0:T(8,128)(2,1)S(1)}, u32[]{:S(2)}, u32[]{:S(2)}) collective-permute-start(bf16[256,256]{1,0:T(8,128)(2,1)} %get-tuple-element.52), channel_id=1, source_target_pairs={{0,1},{1,2},{2,3},{3,4},{4,5},{5,6},{6,7},{8,9},{9,10},{10,11},{11... | collective-permute-start | bytes 393224 | tf_op jit(solution)/shard_map/ppermute | solution.py:618
  45.2 19.0 %collective-permute-start.3 = (bf16[256,256]{1,0:T(8,128)(2,1)}, bf16[256,256]{1,0:T(8,128)(2,1)S(1)}, u32[]{:S(2)}, u32[]{:S(2)}) collective-permute-start(bf16[256,256]{1,0:T(8,128)(2,1)} %get-tuple-element.52), channel_id=1, source_target_pairs={{0,2},{1,3},{2,4},{3,5},{4,6},{5,7},{8,10},{9,11},{10,12},{11,13},... | collective-permute-start | bytes 393224 | tf_op jit(solution)/shard_map/ppermute | solution.py:618
  50.7 11.6 %collective-permute-start.2 = (bf16[256,256]{1,0:T(8,128)(2,1)}, bf16[256,256]{1,0:T(8,128)(2,1)S(1)}, u32[]{:S(2)}, u32[]{:S(2)}) collective-permute-start(bf16[256,256]{1,0:T(8,128)(2,1)} %get-tuple-element.52), channel_id=1, source_target_pairs={{0,3},{1,4},{2,5},{3,6},{4,7},{8,11},{9,12},{10,13},{11,14},{12,15... | collective-permute-start | bytes 393224 | tf_op jit(solution)/shard_map/ppermute | solution.py:618
  52.7 3.6 %collective-permute-start.1 = (bf16[256,256]{1,0:T(8,128)(2,1)}, bf16[256,256]{1,0:T(8,128)(2,1)S(1)}, u32[]{:S(2)}, u32[]{:S(2)}) collective-permute-start(bf16[256,256]{1,0:T(8,128)(2,1)} %get-tuple-element.52), channel_id=1, source_target_pairs={{0,4},{1,5},{2,6},{3,7},{8,12},{9,13},{10,14},{11,15},{16,20},{17,... | collective-permute-start | bytes 393224 | tf_op jit(solution)/shard_map/ppermute | solution.py:618
  54.0 17.0 %collective-permute-start.7 = (bf16[16,4224]{1,0:T(8,128)(2,1)S(1)}, bf16[16,4224]{1,0:T(8,128)(2,1)S(1)}, u32[]{:S(2)}, u32[]{:S(2)}) collective-permute-start(bf16[16,4224]{1,0:T(8,128)(2,1)S(1)} %constant_dynamic-update-slice_fusion.5), channel_id=1, source_target_pairs={{3,0},{0,1},{1,2},{2,3},{7,4},{4,5},{5,6},{6,7},{11,8},{8,9},{9,10... | collective-permute-start | bytes 405512 | tf_op jit(solution)/shard_map/ppermute | solution.py:624
  56.3 14.6 %collective-permute-start.6 = (bf16[16,4224]{1,0:T(8,128)(2,1)S(1)}, bf16[16,4224]{1,0:T(8,128)(2,1)S(1)}, u32[]{:S(2)}, u32[]{:S(2)}) collective-permute-start(bf16[16,4224]{1,0:T(8,128)(2,1)S(1)} %constant_dynamic-update-slice_fusion.5), channel_id=1, source_target_pairs={{2,0},{3,1},{0,2},{1,3},{6,4},{7,5},{4,6},{5,7},{10,8},{11,9},{8,1... | collective-permute-start | bytes 405512 | tf_op jit(solution)/shard_map/ppermute | solution.py:624
  62.3 8.6 %collective-permute-start.5 = (bf16[16,4224]{1,0:T(8,128)(2,1)S(1)}, bf16[16,4224]{1,0:T(8,128)(2,1)S(1)}, u32[]{:S(2)}, u32[]{:S(2)}) collective-permute-start(bf16[16,4224]{1,0:T(8,128)(2,1)S(1)} %constant_dynamic-update-slice_fusion.5), channel_id=1, source_target_pairs={{1,0},{2,1},{3,2},{0,3},{5,4},{6,5},{7,6},{4,7},{9,8},{10,9},{11,1... | collective-permute-start | bytes 405512 | tf_op jit(solution)/shard_map/ppermute | solution.py:624
  215.2 73.0 %all-gather.7.cloned.1.call-start = ((), (), s32[]{:S(2)}) async-start(), calls=%async_computation.5 | async-start | bytes 4055040 | tf_op jit(solution)/shard_map/all_gather | solution.py:700
  235.8 6.7 %collective-permute-start.8 = (bf16[288,256]{1,0:T(8,128)(2,1)}, bf16[288,256]{1,0:T(8,128)(2,1)S(1)}, u32[]{:S(2)}, u32[]{:S(2)}) collective-permute-start(bf16[288,256]{1,0:T(8,128)(2,1)} %get-tuple-element.65), channel_id=1, source_target_pairs={{0,7},{1,0},{2,1},{3,2},{4,3},{5,4},{6,5},{7,6},{8,15},{9,8},{10,9... | collective-permute-start | bytes 442376 | tf_op jit(solution)/shard_map/ppermute | solution.py:703
  237.7 7.0 %collective-permute-start.9 = (bf16[288,256]{1,0:T(8,128)(2,1)}, bf16[288,256]{1,0:T(8,128)(2,1)S(1)}, u32[]{:S(2)}, u32[]{:S(2)}) collective-permute-start(bf16[288,256]{1,0:T(8,128)(2,1)} %get-tuple-element.66), channel_id=1, source_target_pairs={{0,6},{1,7},{2,0},{3,1},{4,2},{5,3},{6,4},{7,5},{8,14},{9,15},{10,... | collective-permute-start | bytes 442376 | tf_op jit(solution)/shard_map/ppermute | solution.py:703
  238.4 10.0 %collective-permute-start.10 = (bf16[288,256]{1,0:T(8,128)(2,1)}, bf16[288,256]{1,0:T(8,128)(2,1)S(1)}, u32[]{:S(2)}, u32[]{:S(2)}) collective-permute-start(bf16[288,256]{1,0:T(8,128)(2,1)} %get-tuple-element.67), channel_id=1, source_target_pairs={{0,5},{1,6},{2,7},{3,0},{4,1},{5,2},{6,3},{7,4},{8,13},{9,14},{10,... | collective-permute-start | bytes 442376 | tf_op jit(solution)/shard_map/ppermute | solution.py:703
  238.9 3.6 %collective-permute-start.11 = (bf16[256,256]{1,0:T(8,128)(2,1)}, bf16[256,256]{1,0:T(8,128)(2,1)S(1)}, u32[]{:S(2)}, u32[]{:S(2)}) collective-permute-start(bf16[256,256]{1,0:T(8,128)(2,1)} %get-tuple-element.68), channel_id=1, source_target_pairs={{4,0},{5,1},{6,2},{7,3},{12,8},{13,9},{14,10},{15,11},{20,16},{21,... | collective-permute-start | bytes 393224 | tf_op jit(solution)/shard_map/ppermute | solution.py:618
  252.4 1.7 collective-permute-start.12
  256.7 11.0 %collective-permute-start.15 = (bf16[1,16,384]{2,1,0:T(8,128)(2,1)}, bf16[1,16,384]{2,1,0:T(8,128)(2,1)S(1)}, u32[]{:S(2)}, u32[]{:S(2)}) collective-permute-start(bf16[1,16,384]{2,1,0:T(8,128)(2,1)} %get-tuple-element.86), channel_id=1, source_target_pairs={{24,0},{0,8},{8,16},{16,24},{25,1},{1,9},{9,17},{17,25},{26,2},{2,... | collective-permute-start | bytes 36872 | tf_op jit(solution)/shard_map/ppermute | solution.py:735
  257.2 10.5 %collective-permute-start.14 = (bf16[1,16,384]{2,1,0:T(8,128)(2,1)}, bf16[1,16,384]{2,1,0:T(8,128)(2,1)S(1)}, u32[]{:S(2)}, u32[]{:S(2)}) collective-permute-start(bf16[1,16,384]{2,1,0:T(8,128)(2,1)} %get-tuple-element.86), channel_id=1, source_target_pairs={{16,0},{24,8},{0,16},{8,24},{17,1},{25,9},{1,17},{9,25},{18,2},{26... | collective-permute-start | bytes 36872 | tf_op jit(solution)/shard_map/ppermute | solution.py:735
  259.6 8.1 %collective-permute-start.13 = (bf16[1,16,384]{2,1,0:T(8,128)(2,1)}, bf16[1,16,384]{2,1,0:T(8,128)(2,1)S(1)}, u32[]{:S(2)}, u32[]{:S(2)}) collective-permute-start(bf16[1,16,384]{2,1,0:T(8,128)(2,1)} %get-tuple-element.86), channel_id=1, source_target_pairs={{8,0},{16,8},{24,16},{0,24},{9,1},{17,9},{25,17},{1,25},{10,2},{18... | collective-permute-start | bytes 36872 | tf_op jit(solution)/shard_map/ppermute | solution.py:735
  261.5 18.4 %all-to-all-start.1 = ((bf16[64,16,128]{2,1,0:T(8,128)(2,1)}), bf16[64,16,128]{2,1,0:T(8,128)(2,1)S(1)}, u32[]{:S(2)}, u32[]{:S(2)}) async-start(bf16[64,16,128]{2,1,0:T(8,128)(2,1)} %get-tuple-element.76), calls=%async_computation.1 | async-start | bytes 524288 | tf_op jit(solution)/shard_map/all_to_all | solution.py:730
  267.7 12.2 %collective-permute-start.18 = (bf16[4,16,384]{2,1,0:T(8,128)(2,1)S(1)}, bf16[4,16,384]{2,1,0:T(8,128)(2,1)S(1)}, u32[]{:S(2)}, u32[]{:S(2)}) collective-permute-start(bf16[4,16,384]{2,1,0:T(8,128)(2,1)S(1)} %constant_dynamic-update-slice_fusion.10.rest_0_), channel_id=1, source_target_pairs={{96,0},{0,32},{32,64},{64,96},{97,1},{1,33},{33,65},{65,97},{98,2}... | collective-permute-start | bytes 147464 | tf_op jit(solution)/shard_map/ppermute | solution.py:735
  268.8 11.1 %collective-permute-start.17 = (bf16[4,16,384]{2,1,0:T(8,128)(2,1)S(1)}, bf16[4,16,384]{2,1,0:T(8,128)(2,1)S(1)}, u32[]{:S(2)}, u32[]{:S(2)}) collective-permute-start(bf16[4,16,384]{2,1,0:T(8,128)(2,1)S(1)} %constant_dynamic-update-slice_fusion.10.rest_0_), channel_id=1, source_target_pairs={{64,0},{96,32},{0,64},{32,96},{65,1},{97,33},{1,65},{33,97},{66,2}... | collective-permute-start | bytes 147464 | tf_op jit(solution)/shard_map/ppermute | solution.py:735
  271.4 8.5 %collective-permute-start.16 = (bf16[4,16,384]{2,1,0:T(8,128)(2,1)S(1)}, bf16[4,16,384]{2,1,0:T(8,128)(2,1)S(1)}, u32[]{:S(2)}, u32[]{:S(2)}) collective-permute-start(bf16[4,16,384]{2,1,0:T(8,128)(2,1)S(1)} %constant_dynamic-update-slice_fusion.10.rest_0_), channel_id=1, source_target_pairs={{32,0},{64,32},{96,64},{0,96},{33,1},{65,33},{97,65},{1,97},{34,2}... | collective-permute-start | bytes 147464 | tf_op jit(solution)/shard_map/ppermute | solution.py:735
  (21 other events, 105.1 us)
Sparse Core Ops, SparseCore 0:
  11.6 150.2 all-gather.4
  215.3 18.6 reduce-scatter.1
  236.5 51.5 all-gather.6

commit v11 on v10

--- a/solution.py
+++ b/solution.py
@@ -91,9 +91,9 @@
 def forward_kernel(
     kv_ref, kseg_ref, qseg_ref, n1_ref, r1_ref, cos_ref, sin_ref, gain_ref, a_ref,
     wq_ref, bq_ref, wo_ref, bo_ref, x_hbm, cot_hbm, b_hbm, w_ref,
-    q_ref, mixed_ref, p_ref, inv_ref, out_ref, gres_ref, gb_ref, wide_ref, gro_ref, early_ref,
+    q_ref, mixed_ref, p_ref, inv_ref, out_ref, gres_ref, gb_ref, n2_ref, ranks_ref, gro_ref, early_ref,
     bias_ref, s_ref, vt_ref, ffn_ref, g2_ref, ro_ref, rd_ref, gr_ref, qs_ref,
-    all_mixed_ref, res_ref, n2_ref, r2_ref, r2t_ref, grd_ref, grdt_ref, wv_ref, x_ref, cot_ref, b_ref, sems, late_sems,
+    all_mixed_ref, res_ref, r2_ref, r2t_ref, grd_ref, grdt_ref, wv_ref, x_ref, cot_ref, b_ref, sems, late_sems,
 ):
     step = pl.program_id(0)
     slots, tensor_count = wv_ref.shape[0], w_ref.shape[1]
@@ -240,7 +240,7 @@
     @pl.when(step == tensor_count)
     def _():
         lax.fori_loop(0, steps, feed_forward, 0)
-        res, n2, cot = res_ref[...], n2_ref[...], cot_ref[...]
+        res, cot = res_ref[...], cot_ref[...]
         out_ref[...] = (res + (ffn_ref[...] + mm_nt(rd_ref[...].astype(BF), a_ref[...]))).astype(BF)
         grad_two = g2_ref[...] + mm_nt(gr_ref[...].astype(BF), a_ref[...])
         grad_res = cot.astype(F32) + rms_back(res, gain_ref[...], grad_two)
@@ -253,14 +253,14 @@
         first = 3 * steps * part_cols
         for t in range(tensor_count):
             early_ref[t, :, first:] = mm(grot, all_mixed_ref[t]).astype(BF)
-        wide = mm(gr_ref[...].T.astype(BF), n2) + mm(rd_ref[...].T.astype(BF), cot)
-        wide_ref[...] = wide + mm(ro_ref[...].T.astype(BF), grad_branch)
+        for j, rank in enumerate((gr_ref, rd_ref, ro_ref)):
+            ranks_ref[j] = rank[...].astype(BF)
 
 
 def attn_back_kernel(
-    tensor_ref, kv_ref, gb_ref, gro_ref, r1_ref, cos_ref, sin_ref,
+    tensor_ref, kv_ref, gb_ref, gro_ref, r1_ref, cos_ref, sin_ref, ranks_ref, n2_ref, cot_ref,
     q_ref, mixed_ref, p_ref, inv_ref, wo_ref, bo_ref, wq_ref, bq_ref,
-    dkva_ref, dkvb_ref, dkvc_ref, dkvd_ref, dkve_ref, q0_ref, g1_ref, gr_ref,
+    dkva_ref, dkvb_ref, dkvc_ref, dkvd_ref, dkve_ref, q0_ref, g1_ref, gr_ref, wide_ref,
     ds_ref, dk_ref, dv_ref, kt_ref, r1t_ref, gq_ref, gm_ref, qs_ref, gs_ref,
 ):
     step = pl.program_id(0)
@@ -322,6 +322,8 @@
 
     @pl.when(step == pl.num_programs(0) - 1)
     def _():
+        wide = mm(turned(ranks_ref[0]), n2_ref[...]) + mm(turned(ranks_ref[1]), cot_ref[...])
+        wide_ref[...] = wide + mm(turned(ranks_ref[2]), gb_ref[...])
         for c, dkv_ref in enumerate((dkva_ref, dkvb_ref, dkvc_ref, dkvd_ref, dkve_ref)):
             span = slice(c * rows, (c + 1) * rows)
             dkv_ref[:rows, :HD] = (dk_ref[span] * (1.0 / LOG2E)).astype(BF)
@@ -648,7 +650,7 @@
         weights, b_heads, weights, b_heads, tokens, cotangent, b_hidden, weights,
     )
     (
-        queries, mixed, probs, norms, block_output, grad_residual, grad_branch, wide_ffn, grad_ro, early
+        queries, mixed, probs, norms, block_output, grad_residual, grad_branch, normed_two, ranks, grad_ro, early
     ) = call(
         forward_kernel, "forward", tensor_count + 1, args,
         wholes(*args[:8]) + [a_spec] + [until_last(spec) for spec in head_specs]
@@ -657,14 +659,14 @@
             (sds((rows, heads_cols), BF), until_last(token_cols)), (sds((rows, heads_cols), BF), until_last(token_cols)),
             (sds((tensor_count, span, heads * rows), BF), until_last(p_spec)),
             (sds((tensor_count, 8, heads * rows), F32), until_last(norm_spec)),
-            (tok_bf, None), (tok_f32, None), (tok_bf, None), (sds((LANES, width), F32), None), (rank_bf, None),
-            (sds((tensor_count, RANK, f3 + q_cols), BF), None),
+            (tok_bf, None), (tok_f32, None), (tok_bf, None), (tok_bf, None), (sds((3, rows, LANES), BF), None),
+            (rank_bf, None), (sds((tensor_count, RANK, f3 + q_cols), BF), None),
         ],
         [
             pltpu.VMEM((span, rows), F32), pltpu.VMEM((span, heads * rows), F32), pltpu.VMEM((HD, span), BF),
             pltpu.VMEM((rows, width), F32), pltpu.VMEM((rows, width), F32), pltpu.VMEM((rows, LANES), F32),
             pltpu.VMEM((rows, LANES), F32), pltpu.VMEM((rows, LANES), F32), pltpu.VMEM((heads * rows, HD), BF),
-            pltpu.VMEM((tensor_count, rows, q_cols), BF), pltpu.VMEM((rows, width), F32), pltpu.VMEM((rows, width), BF),
+            pltpu.VMEM((tensor_count, rows, q_cols), BF), pltpu.VMEM((rows, width), F32),
             pltpu.VMEM((rows, LANES), BF), pltpu.VMEM((LANES, rows), BF),
             pltpu.VMEM((rows, LANES), BF), pltpu.VMEM((LANES, rows), BF),
             pltpu.VMEM((slots, dp_count, shard_rows, 3 * tensor_count * part_cols), BF),
@@ -678,14 +680,15 @@
 
     args = (
         tensor.astype(jnp.int32).reshape(1), kv_window, grad_branch, grad_ro, rank_one, cos, sin,
-        queries, mixed, probs, norms, weights, b_heads, weights, b_heads,
-    )
-    *dkv, q_own, grad_one, grad_rank = call(
+        ranks, normed_two, cotangent, queries, mixed, probs, norms, weights, b_heads, weights, b_heads,
+    )
+    *dkv, q_own, grad_one, grad_rank, wide_ffn = call(
         attn_back_kernel, "attention_back", tensor_count, args,
-        [scalars()] + wholes(*args[1:7]) + [token_cols, token_cols, p_spec, norm_spec, o_spec, ob_spec, q_spec, qb_spec],
+        [scalars()] + wholes(*args[1:10]) + [token_cols, token_cols, p_spec, norm_spec, o_spec, ob_spec, q_spec, qb_spec],
         [
             *[(sds((rows + (2 * RANK if 0 < w < reach else 0), 2 * HD), BF), None) for w in range(reach + 1)],
             (sds((RANK, q_cols), BF), None), (tok_f32, None), (sds((rows, LANES), F32), None),
+            (sds((LANES, width), F32), None),
         ],
         [
             pltpu.VMEM((span, heads * rows), BF),

time: 300 us -> 299 us (level)
  no operation moved by 1% of the time
where the time goes in v11:
time: 299 us
  waiting for transfers between devices  117 us (39%)
  Pallas kernels  95.8 us (32%)
  starting transfers between devices  46.5 us (16%)
  between operations  15 us (5%)
  local copies, waits for them, and re-layouts  14.3 us (5%)
  other arithmetic  9.73 us (3%)
    pallas_call x9, Pallas kernels, call(): pl.pallas_call(kernel, name=name, grid=(steps,), in_specs=specs, out_spec...  95.8 us
    all_gather x1, waiting for transfers between devices, on_device(): weights = lax.all_gather(pack, ALL, axis=0, tiled=False)  85.1 us
    ppermute x5, starting transfers between devices, moved(): lax.ppermute(value, SEQ, [(c, c + steps) for c in range(parts) if 0 <= c...  15.6 us
    ppermute x5, waiting for transfers between devices, moved(): lax.ppermute(value, SEQ, [(c, c + steps) for c in range(parts) if 0 <= c...  9.38 us
    ppermute x6, starting transfers between devices, with_others(): lax.ppermute(value, axis, [((i + d) % count, i) for i in range(count)])  8.83 us
    all_to_all x1, starting transfers between devices, on_device(): a_own = lax.all_to_all(wide, ('y', 'x'), 0, 0, tiled=True)  7.72 us
    unnamed x63, local copies, waits for them, and re-layouts  7.69 us
    ppermute x3, waiting for transfers between devices, on_device(): lax.ppermute(b_own, 'tensor', [((z + d) % tensor_count, z) for z in range...  6.69 us
  transfers between devices with their start and end apart: 24, of which 11 were waited for; matrix products, arithmetic and copies ran while one was open for 7% of the time, Pallas kernels for 12%

profile of v11, /device:TPU:1, one launch (start us, length us, event | category | flops | bytes accessed | tf_op | source)
XLA Modules:
  0.0 298.5 jit_solution(2149992237199541968)
XLA Ops:
  11.7 7.7 %all-to-all-start = ((bf16[16,48,384]{2,1,0:T(8,128)(2,1)}), bf16[16,48,384]{2,1,0:T(8,128)(2,1)S(1)}, u32[]{:S(2)}, u32[]{:S(2)}) async-start(bf16[16,48,384]{2,1,0:T(8,128)(2,1)} %fusion.11), calls=%async_computation | async-start | bytes 1179648 | tf_op jit(solution)/shard_map/all_to_all | solution.py:559
  25.0 2.4 fusion.12
  27.4 3.1 %all-to-all-done = bf16[16,48,384]{2,1,0:T(8,128)(2,1)S(1)} async-done(((bf16[16,48,384]{2,1,0:T(8,128)(2,1)}), bf16[16,48,384]{2,1,0:T(8,128)(2,1)S(1)}, u32[]{:S(2)}, u32[]{:S(2)}) %all-to-all-start) | async-done | bytes 589856 | tf_op jit(solution)/shard_map/all_to_all | solution.py:559
  30.5 2.5 collective-permute-start
  37.4 3.4 %keys_values.1 = (bf16[256,1536]{1,0:T(8,128)(2,1)}, bf16[256,128]{1,0:T(8,128)(2,1)}, bf16[256,256]{1,0:T(8,128)(2,1)}) custom-call(bf16[256,1536]{1,0:T(8,128)(2,1)} %x_ref.3, f32[1,1536]{1,0:T(1,128)} %get-tuple-element.108.gain_ref, bf16[1536,384]{1,0:T(8,128)(2,1)} %bitcast.75, bf16[1536,384]{1,0:T(8,128)(2,1)} %bitcast.76, bf16[1536,384]{1,0:T(8,128)(2,1)} %bitcast.77, ...), custom_call_target="tpu_custom_call" | custom-call | flops 301989888 | bytes 2359296 | tf_op jit(solution)/shard_map/keys_values/pallas_call | solution.py:494
  40.7 4.4 %collective-permute-start.4 = (bf16[256,256]{1,0:T(8,128)(2,1)}, bf16[256,256]{1,0:T(8,128)(2,1)S(1)}, u32[]{:S(2)}, u32[]{:S(2)}) collective-permute-start(bf16[256,256]{1,0:T(8,128)(2,1)} %get-tuple-element.54), channel_id=1, source_target_pairs={{0,1},{1,2},{2,3},{3,4},{4,5},{5,6},{6,7},{8,9},{9,10},{10,11},{11... | collective-permute-start | bytes 393224 | tf_op jit(solution)/shard_map/ppermute | solution.py:620
  45.2 5.5 %collective-permute-start.3 = (bf16[256,256]{1,0:T(8,128)(2,1)}, bf16[256,256]{1,0:T(8,128)(2,1)S(1)}, u32[]{:S(2)}, u32[]{:S(2)}) collective-permute-start(bf16[256,256]{1,0:T(8,128)(2,1)} %get-tuple-element.54), channel_id=1, source_target_pairs={{0,2},{1,3},{2,4},{3,5},{4,6},{5,7},{8,10},{9,11},{10,12},{11,13},... | collective-permute-start | bytes 393224 | tf_op jit(solution)/shard_map/ppermute | solution.py:620
  54.0 2.3 collective-permute-done.1
  56.3 5.9 %collective-permute-done.2 = bf16[256,256]{1,0:T(8,128)(2,1)S(1)} collective-permute-done((bf16[256,256]{1,0:T(8,128)(2,1)}, bf16[256,256]{1,0:T(8,128)(2,1)S(1)}, u32[]{:S(2)}, u32[]{:S(2)}) %collective-permute-start.2) | collective-permute-done | bytes 131104 | tf_op jit(solution)/shard_map/ppermute | solution.py:620
  64.1 6.7 %collective-permute-done.5 = bf16[16,4224]{1,0:T(8,128)(2,1)S(1)} collective-permute-done((bf16[16,4224]{1,0:T(8,128)(2,1)S(1)}, bf16[16,4224]{1,0:T(8,128)(2,1)S(1)}, u32[]{:S(2)}, u32[]{:S(2)}) %collective-permute-start.5) | collective-permute-done | bytes 135200 | tf_op jit(solution)/shard_map/ppermute | solution.py:626
  74.6 2.2 fusion.5.b_hbm
  76.8 85.1 %all-gather.5.cloned.1.call-done = bf16[6144,4224]{1,0:T(8,128)(2,1)} async-done(((bf16[48,4224]{1,0:T(8,128)(2,1)}), bf16[6144,4224]{1,0:T(8,128)(2,1)}) %all-gather.5.cloned.1.call-update) | async-done | bytes 51904528 | tf_op jit(solution)/shard_map/all_gather | solution.py:546
  161.8 53.0 %forward.1 = (bf16[256,1536]{1,0:T(8,128)(2,1)}, bf16[256,1536]{1,0:T(8,128)(2,1)}, bf16[4,1280,768]{2,1,0:T(8,128)(2,1)}, f32[4,8,768]{2,1,0:T(8,128)}, bf16[25...) custom-call(bf16[1280,256]{1,0:T(8,128)(2,1)} %copy-done.2, ...), custom_call_target="tpu_custom_call" | custom-call | flops 26172456960 | bytes 51904512 | tf_op jit(solution)/shard_map/forward/pallas_call | solution.py:494
  215.2 21.6 %attention_back.1 = (bf16[256,256]{1,0:T(8,128)(2,1)}, bf16[288,256]{1,0:T(8,128)(2,1)}, bf16[288,256]{1,0:T(8,128)(2,1)}, bf16[288,256]{1,0:T(8,128)(2,1)}, bf1...) custom-call(s32[1]{0:T(128)} %bitcast.34.tensor_ref, ...), custom_call_target="tpu_custom_call" | custom-call | flops 6442450944 | bytes 9437184 | tf_op jit(solution)/shard_map/attention_back/pallas_call | solution.py:494
  240.0 2.4 collective-permute-start.11
  243.6 2.1 collective-permute-done.9.back2_ref
  245.7 3.8 %collective-permute-done.10.back3_ref = bf16[288,256]{1,0:T(8,128)(2,1)S(1)} collective-permute-done((bf16[288,256]{1,0:T(8,128)(2,1)}, bf16[288,256]{1,0:T(8,128)(2,1)S(1)}, u32[]{:S(2)}, u32[]{:S(2)}) %collective-permute-start.10) | collective-permute-done | bytes 147488 | tf_op jit(solution)/shard_map/ppermute | solution.py:706
  250.1 3.3 %shared_back.1 = (bf16[848,128]{1,0:T(8,128)(2,1)}, bf16[848,128]{1,0:T(8,128)(2,1)}, bf16[256,128]{1,0:T(8,128)(2,1)}, bf16[256,128]{1,0:T(8,128)(2,1)}, bf16[256,128]{1,0:T(8,128)(2,1)}) custom-call(s32[1]{0:T(128)} %bitcast.33.core_ref, bf16[256,1536]{1,0:T(8,128)(2,1)} %get-tuple-element.55.n1_ref, bf16[256,128]{1,0:T(8,128)(2,1)} %get-tuple-element.56.r1_ref, ...), custom_call_target="tpu_custom_call" | custom-call | flops 201326592 | bytes 2359296 | tf_op jit(solution)/shard_map/shared_back/pallas_call | solution.py:494
  258.2 2.4 collective-permute-start.14
  262.6 6.1 %all-to-all-start.1 = ((bf16[64,16,128]{2,1,0:T(8,128)(2,1)}), bf16[64,16,128]{2,1,0:T(8,128)(2,1)S(1)}, u32[]{:S(2)}, u32[]{:S(2)}) async-start(bf16[64,16,128]{2,1,0:T(8,128)(2,1)} %get-tuple-element.80), calls=%async_computation.1 | async-start | bytes 524288 | tf_op jit(solution)/shard_map/all_to_all | solution.py:733
  269.8 2.6 collective-permute-start.17
  274.1 4.9 %input_gradient.1 = f32[256,1536]{1,0:T(8,128)} custom-call(bf16[256,1536]{1,0:T(8,128)(2,1)} %x_ref.3, f32[1,1536]{1,0:T(1,128)} %get-tuple-element.108.gain_ref, bf16[1536,384]{1,0:T(8,128)(2,1)} %bitcast.79, bf16[1536,384]{1,0:T(8,128)(2,1)} %bitcast.80, bf16[1536,384]{1,0:T(8,128)(2,1)} %bitcast.81, bf16[256,128]{1,0:T(8,128)(2,1)} %get-tuple-element.81.gk_ref, ...), custom_call_target="tpu_custom_call" | custom-call | flops 301989888 | bytes 6291456 | tf_op jit(solution)/shard_map/input_gradient/pallas_call | solution.py:494
  284.3 3.7 %all-gather.7.cloned.1.call-done = bf16[512,3840]{1,0:T(8,128)(2,1)} async-done(((bf16[16,3840]{1,0:T(8,128)(2,1)}), bf16[512,3840]{1,0:T(8,128)(2,1)}) %all-gather.7.cloned.1.call-update) | async-done | bytes 3932176 | tf_op jit(solution)/shard_map/all_gather | solution.py:703
  288.0 4.0 %sum_hidden.1 = (f32[2,128,1152]{2,1,0:T(8,128)}, f32[1152,128]{1,0:T(8,128)}, f32[384,128]{1,0:T(8,128)}) custom-call(s32[16]{0:T(128)} %ids_ref.3, bf16[32,16,3840]{2,1,0:T(8,128)(2,1)} %bitcast.83), custom_call_target="tpu_custom_call" | custom-call | bytes 1769472 | tf_op jit(solution)/shard_map/sum_hidden/pallas_call | solution.py:494
  (137 shorter events, 42.4 us)
Async XLA Ops:
  7.2 154.6 %all-gather.5.cloned.1.call-start = ((), (), s32[]{:S(2)}) async-start(), calls=%async_computation.4 | async-start | bytes 52310016 | tf_op jit(solution)/shard_map/all_gather | solution.py:546
  11.7 18.8 %all-to-all-start = ((bf16[16,48,384]{2,1,0:T(8,128)(2,1)}), bf16[16,48,384]{2,1,0:T(8,128)(2,1)S(1)}, u32[]{:S(2)}, u32[]{:S(2)}) async-start(bf16[16,48,384]{2,1,0:T(8,128)(2,1)} %fusion.11), calls=%async_computation | async-start | bytes 1179648 | tf_op jit(solution)/shard_map/all_to_all | solution.py:559
  19.4 217.4 %reduce-scatter.2.cloned.1.call-start = ((), (), s32[]{:S(2)}) async-start(), calls=%async_computation.3 | async-start | bytes 614400 | tf_op jit(solution)/shard_map/reduce_scatter | solution.py:679
  30.5 5.7 %collective-permute-start = (bf16[16,48,384]{2,1,0:T(8,128)(2,1)S(1)}, bf16[16,48,384]{2,1,0:T(8,128)(2,1)S(1)}, u32[]{:S(2)}, u32[]{:S(2)}) collective-permute-start(bf16[16,48,384]{2,1,0:T(8,128)(2,1)S(1)} %all-to-all-done), channel_id=1, source_target_pairs={{0,4},{4,0},{1,5},{5,1},{2,6},{6,2},{3,7},{7,3},{8,12},{12,8},{9,1... | collective-permute-start | bytes 1769480 | tf_op jit(solution)/shard_map/ppermute | solution.py:557
  40.7 23.3 %collective-permute-start.4 = (bf16[256,256]{1,0:T(8,128)(2,1)}, bf16[256,256]{1,0:T(8,128)(2,1)S(1)}, u32[]{:S(2)}, u32[]{:S(2)}) collective-permute-start(bf16[256,256]{1,0:T(8,128)(2,1)} %get-tuple-element.54), channel_id=1, source_target_pairs={{0,1},{1,2},{2,3},{3,4},{4,5},{5,6},{6,7},{8,9},{9,10},{10,11},{11... | collective-permute-start | bytes 393224 | tf_op jit(solution)/shard_map/ppermute | solution.py:620
  45.2 18.9 %collective-permute-start.3 = (bf16[256,256]{1,0:T(8,128)(2,1)}, bf16[256,256]{1,0:T(8,128)(2,1)S(1)}, u32[]{:S(2)}, u32[]{:S(2)}) collective-permute-start(bf16[256,256]{1,0:T(8,128)(2,1)} %get-tuple-element.54), channel_id=1, source_target_pairs={{0,2},{1,3},{2,4},{3,5},{4,6},{5,7},{8,10},{9,11},{10,12},{11,13},... | collective-permute-start | bytes 393224 | tf_op jit(solution)/shard_map/ppermute | solution.py:620
  50.7 11.6 %collective-permute-start.2 = (bf16[256,256]{1,0:T(8,128)(2,1)}, bf16[256,256]{1,0:T(8,128)(2,1)S(1)}, u32[]{:S(2)}, u32[]{:S(2)}) collective-permute-start(bf16[256,256]{1,0:T(8,128)(2,1)} %get-tuple-element.54), channel_id=1, source_target_pairs={{0,3},{1,4},{2,5},{3,6},{4,7},{8,11},{9,12},{10,13},{11,14},{12,15... | collective-permute-start | bytes 393224 | tf_op jit(solution)/shard_map/ppermute | solution.py:620
  52.6 3.7 %collective-permute-start.1 = (bf16[256,256]{1,0:T(8,128)(2,1)}, bf16[256,256]{1,0:T(8,128)(2,1)S(1)}, u32[]{:S(2)}, u32[]{:S(2)}) collective-permute-start(bf16[256,256]{1,0:T(8,128)(2,1)} %get-tuple-element.54), channel_id=1, source_target_pairs={{0,4},{1,5},{2,6},{3,7},{8,12},{9,13},{10,14},{11,15},{16,20},{17,... | collective-permute-start | bytes 393224 | tf_op jit(solution)/shard_map/ppermute | solution.py:620
  53.9 16.9 %collective-permute-start.7 = (bf16[16,4224]{1,0:T(8,128)(2,1)S(1)}, bf16[16,4224]{1,0:T(8,128)(2,1)S(1)}, u32[]{:S(2)}, u32[]{:S(2)}) collective-permute-start(bf16[16,4224]{1,0:T(8,128)(2,1)S(1)} %constant_dynamic-update-slice_fusion.5), channel_id=1, source_target_pairs={{3,0},{0,1},{1,2},{2,3},{7,4},{4,5},{5,6},{6,7},{11,8},{8,9},{9,10... | collective-permute-start | bytes 405512 | tf_op jit(solution)/shard_map/ppermute | solution.py:626
  56.3 14.5 %collective-permute-start.6 = (bf16[16,4224]{1,0:T(8,128)(2,1)S(1)}, bf16[16,4224]{1,0:T(8,128)(2,1)S(1)}, u32[]{:S(2)}, u32[]{:S(2)}) collective-permute-start(bf16[16,4224]{1,0:T(8,128)(2,1)S(1)} %constant_dynamic-update-slice_fusion.5), channel_id=1, source_target_pairs={{2,0},{3,1},{0,2},{1,3},{6,4},{7,5},{4,6},{5,7},{10,8},{11,9},{8,1... | collective-permute-start | bytes 405512 | tf_op jit(solution)/shard_map/ppermute | solution.py:626
  62.2 8.6 %collective-permute-start.5 = (bf16[16,4224]{1,0:T(8,128)(2,1)S(1)}, bf16[16,4224]{1,0:T(8,128)(2,1)S(1)}, u32[]{:S(2)}, u32[]{:S(2)}) collective-permute-start(bf16[16,4224]{1,0:T(8,128)(2,1)S(1)} %constant_dynamic-update-slice_fusion.5), channel_id=1, source_target_pairs={{1,0},{2,1},{3,2},{0,3},{5,4},{6,5},{7,6},{4,7},{9,8},{10,9},{11,1... | collective-permute-start | bytes 405512 | tf_op jit(solution)/shard_map/ppermute | solution.py:626
  214.9 73.1 %all-gather.7.cloned.1.call-start = ((), (), s32[]{:S(2)}) async-start(), calls=%async_computation.5 | async-start | bytes 4055040 | tf_op jit(solution)/shard_map/all_gather | solution.py:703
  236.9 6.7 %collective-permute-start.8 = (bf16[288,256]{1,0:T(8,128)(2,1)}, bf16[288,256]{1,0:T(8,128)(2,1)S(1)}, u32[]{:S(2)}, u32[]{:S(2)}) collective-permute-start(bf16[288,256]{1,0:T(8,128)(2,1)} %get-tuple-element.69), channel_id=1, source_target_pairs={{0,7},{1,0},{2,1},{3,2},{4,3},{5,4},{6,5},{7,6},{8,15},{9,8},{10,9... | collective-permute-start | bytes 442376 | tf_op jit(solution)/shard_map/ppermute | solution.py:706
  238.8 6.9 %collective-permute-start.9 = (bf16[288,256]{1,0:T(8,128)(2,1)}, bf16[288,256]{1,0:T(8,128)(2,1)S(1)}, u32[]{:S(2)}, u32[]{:S(2)}) collective-permute-start(bf16[288,256]{1,0:T(8,128)(2,1)} %get-tuple-element.70), channel_id=1, source_target_pairs={{0,6},{1,7},{2,0},{3,1},{4,2},{5,3},{6,4},{7,5},{8,14},{9,15},{10,... | collective-permute-start | bytes 442376 | tf_op jit(solution)/shard_map/ppermute | solution.py:706
  239.4 10.0 %collective-permute-start.10 = (bf16[288,256]{1,0:T(8,128)(2,1)}, bf16[288,256]{1,0:T(8,128)(2,1)S(1)}, u32[]{:S(2)}, u32[]{:S(2)}) collective-permute-start(bf16[288,256]{1,0:T(8,128)(2,1)} %get-tuple-element.71), channel_id=1, source_target_pairs={{0,5},{1,6},{2,7},{3,0},{4,1},{5,2},{6,3},{7,4},{8,13},{9,14},{10,... | collective-permute-start | bytes 442376 | tf_op jit(solution)/shard_map/ppermute | solution.py:706
  240.0 3.6 %collective-permute-start.11 = (bf16[256,256]{1,0:T(8,128)(2,1)}, bf16[256,256]{1,0:T(8,128)(2,1)S(1)}, u32[]{:S(2)}, u32[]{:S(2)}) collective-permute-start(bf16[256,256]{1,0:T(8,128)(2,1)} %get-tuple-element.72), channel_id=1, source_target_pairs={{4,0},{5,1},{6,2},{7,3},{12,8},{13,9},{14,10},{15,11},{20,16},{21,... | collective-permute-start | bytes 393224 | tf_op jit(solution)/shard_map/ppermute | solution.py:620
  253.5 1.7 collective-permute-start.12
  257.8 11.0 %collective-permute-start.15 = (bf16[1,16,384]{2,1,0:T(8,128)(2,1)}, bf16[1,16,384]{2,1,0:T(8,128)(2,1)S(1)}, u32[]{:S(2)}, u32[]{:S(2)}) collective-permute-start(bf16[1,16,384]{2,1,0:T(8,128)(2,1)} %get-tuple-element.90), channel_id=1, source_target_pairs={{24,0},{0,8},{8,16},{16,24},{25,1},{1,9},{9,17},{17,25},{26,2},{2,... | collective-permute-start | bytes 36872 | tf_op jit(solution)/shard_map/ppermute | solution.py:738
  258.2 10.5 %collective-permute-start.14 = (bf16[1,16,384]{2,1,0:T(8,128)(2,1)}, bf16[1,16,384]{2,1,0:T(8,128)(2,1)S(1)}, u32[]{:S(2)}, u32[]{:S(2)}) collective-permute-start(bf16[1,16,384]{2,1,0:T(8,128)(2,1)} %get-tuple-element.90), channel_id=1, source_target_pairs={{16,0},{24,8},{0,16},{8,24},{17,1},{25,9},{1,17},{9,25},{18,2},{26... | collective-permute-start | bytes 36872 | tf_op jit(solution)/shard_map/ppermute | solution.py:738
  260.7 8.0 %collective-permute-start.13 = (bf16[1,16,384]{2,1,0:T(8,128)(2,1)}, bf16[1,16,384]{2,1,0:T(8,128)(2,1)S(1)}, u32[]{:S(2)}, u32[]{:S(2)}) collective-permute-start(bf16[1,16,384]{2,1,0:T(8,128)(2,1)} %get-tuple-element.90), channel_id=1, source_target_pairs={{8,0},{16,8},{24,16},{0,24},{9,1},{17,9},{25,17},{1,25},{10,2},{18... | collective-permute-start | bytes 36872 | tf_op jit(solution)/shard_map/ppermute | solution.py:738
  262.6 18.4 %all-to-all-start.1 = ((bf16[64,16,128]{2,1,0:T(8,128)(2,1)}), bf16[64,16,128]{2,1,0:T(8,128)(2,1)S(1)}, u32[]{:S(2)}, u32[]{:S(2)}) async-start(bf16[64,16,128]{2,1,0:T(8,128)(2,1)} %get-tuple-element.80), calls=%async_computation.1 | async-start | bytes 524288 | tf_op jit(solution)/shard_map/all_to_all | solution.py:733
  268.7 12.3 %collective-permute-start.18 = (bf16[4,16,384]{2,1,0:T(8,128)(2,1)S(1)}, bf16[4,16,384]{2,1,0:T(8,128)(2,1)S(1)}, u32[]{:S(2)}, u32[]{:S(2)}) collective-permute-start(bf16[4,16,384]{2,1,0:T(8,128)(2,1)S(1)} %constant_dynamic-update-slice_fusion.10.rest_0_), channel_id=1, source_target_pairs={{96,0},{0,32},{32,64},{64,96},{97,1},{1,33},{33,65},{65,97},{98,2}... | collective-permute-start | bytes 147464 | tf_op jit(solution)/shard_map/ppermute | solution.py:738
  269.8 11.2 %collective-permute-start.17 = (bf16[4,16,384]{2,1,0:T(8,128)(2,1)S(1)}, bf16[4,16,384]{2,1,0:T(8,128)(2,1)S(1)}, u32[]{:S(2)}, u32[]{:S(2)}) collective-permute-start(bf16[4,16,384]{2,1,0:T(8,128)(2,1)S(1)} %constant_dynamic-update-slice_fusion.10.rest_0_), channel_id=1, source_target_pairs={{64,0},{96,32},{0,64},{32,96},{65,1},{97,33},{1,65},{33,97},{66,2}... | collective-permute-start | bytes 147464 | tf_op jit(solution)/shard_map/ppermute | solution.py:738
  272.4 8.6 %collective-permute-start.16 = (bf16[4,16,384]{2,1,0:T(8,128)(2,1)S(1)}, bf16[4,16,384]{2,1,0:T(8,128)(2,1)S(1)}, u32[]{:S(2)}, u32[]{:S(2)}) collective-permute-start(bf16[4,16,384]{2,1,0:T(8,128)(2,1)S(1)} %constant_dynamic-update-slice_fusion.10.rest_0_), channel_id=1, source_target_pairs={{32,0},{64,32},{96,64},{0,96},{33,1},{65,33},{97,65},{1,97},{34,2}... | collective-permute-start | bytes 147464 | tf_op jit(solution)/shard_map/ppermute | solution.py:738
  (21 other events, 105.0 us)
Sparse Core Ops, SparseCore 0:
  11.6 150.2 all-gather.4
  215.0 18.6 reduce-scatter.1
  237.0 50.9 all-gather.6

commit v12 on v11

--- a/solution.py
+++ b/solution.py
@@ -738,7 +738,6 @@
             lax.ppermute(value, axis, [((i + d) % count, i) for i in range(count)]) for d in range(1, count)
         ]
 
-    q_terms = with_others(jnp.concatenate(with_others(q_terms, "x")), "y")
     terms = terms.reshape(seqs, tensor_count, RANK, LANES)
 
     args = (
@@ -750,6 +749,8 @@
         [(tok_f32, None)], [], 2 * rows * width * 384, 16 * rows * width,
     )
 
+    q_terms, input_grad = lax.optimization_barrier((q_terms, input_grad))
+    q_terms = with_others(jnp.concatenate(with_others(q_terms, "x")), "y")
     terms, input_grad = lax.optimization_barrier((terms, input_grad))
     own = jnp.stack([(dp * tensor_count + tensor) // RANK, lax.axis_index("y"), lax.axis_index("x")]).astype(jnp.int32)
     wide_grad, kv_adapter_grad, q_adapter_grad = call(

time: 299 us -> 300 us (level)
    all_gather x1, waiting for transfers between devices: 3.7 us -> 0.01 us  [on_device(): early = lax.all_gather(early, DP, axis=0, tiled=False)]
    ppermute x6, waiting for transfers between devices: 0.02 us -> 3.7 us  [with_others(): lax.ppermute(value, axis, [((i + d) % count, i) for i in range(count)])]
    unnamed x63 -> x65, local copies, waits for them, and re-layouts: 7.69 us -> 6.27 us
  transfers between devices with their start and end apart: 24 -> 24, of which waited for: 11 -> 12; matrix products, arithmetic and copies ran while one was open for 7% -> 6% of each run, Pallas kernels for 12% -> 12%
where the time goes in v12:
time: 300 us; the launch traced here: 297 us
  waiting for transfers between devices  115 us (38%)
  Pallas kernels  95.8 us (32%)
  starting transfers between devices  48.1 us (16%)
  between operations  14.9 us (5%)
  local copies, waits for them, and re-layouts  12.9 us (4%)
  other arithmetic  9.82 us (3%)
    pallas_call x9, Pallas kernels, call(): pl.pallas_call(kernel, name=name, grid=(steps,), in_specs=specs, out_spec...  95.8 us
    all_gather x1, waiting for transfers between devices, on_device(): weights = lax.all_gather(pack, ALL, axis=0, tiled=False)  85.1 us
    ppermute x5, starting transfers between devices, moved(): lax.ppermute(value, SEQ, [(c, c + steps) for c in range(parts) if 0 <= c...  15.6 us
    ppermute x6, starting transfers between devices, with_others(): lax.ppermute(value, axis, [((i + d) % count, i) for i in range(count)])  9.44 us
    ppermute x5, waiting for transfers between devices, moved(): lax.ppermute(value, SEQ, [(c, c + steps) for c in range(parts) if 0 <= c...  9.38 us
    all_to_all x1, starting transfers between devices, on_device(): a_own = lax.all_to_all(wide, ('y', 'x'), 0, 0, tiled=True)  7.72 us
    all_to_all x1, starting transfers between devices, on_device(): terms = lax.all_to_all(payload, PLANES, 0, 0, tiled=True)  7.12 us
    ppermute x3, waiting for transfers between devices, on_device(): lax.ppermute(b_own, 'tensor', [((z + d) % tensor_count, z) for z in range...  6.68 us
  transfers between devices with their start and end apart: 24, of which 12 were waited for; matrix products, arithmetic and copies ran while one was open for 6% of the time, Pallas kernels for 12%

profile of v12, /device:TPU:1, one launch (start us, length us, event | category | flops | bytes accessed | tf_op | source)
XLA Modules:
  0.0 296.8 jit_solution(15288850733224362889)
XLA Ops:
  11.7 7.7 %all-to-all-start = ((bf16[16,48,384]{2,1,0:T(8,128)(2,1)}), bf16[16,48,384]{2,1,0:T(8,128)(2,1)S(1)}, u32[]{:S(2)}, u32[]{:S(2)}) async-start(bf16[16,48,384]{2,1,0:T(8,128)(2,1)} %fusion.11), calls=%async_computation | async-start | bytes 1179648 | tf_op jit(solution)/shard_map/all_to_all | solution.py:559
  25.0 2.4 fusion.12
  27.4 3.1 %all-to-all-done = bf16[16,48,384]{2,1,0:T(8,128)(2,1)S(1)} async-done(((bf16[16,48,384]{2,1,0:T(8,128)(2,1)}), bf16[16,48,384]{2,1,0:T(8,128)(2,1)S(1)}, u32[]{:S(2)}, u32[]{:S(2)}) %all-to-all-start) | async-done | bytes 589856 | tf_op jit(solution)/shard_map/all_to_all | solution.py:559
  30.5 2.5 collective-permute-start
  37.4 3.4 %keys_values.1 = (bf16[256,1536]{1,0:T(8,128)(2,1)}, bf16[256,128]{1,0:T(8,128)(2,1)}, bf16[256,256]{1,0:T(8,128)(2,1)}) custom-call(bf16[256,1536]{1,0:T(8,128)(2,1)} %x_ref.3, f32[1,1536]{1,0:T(1,128)} %get-tuple-element.112.gain_ref, bf16[1536,384]{1,0:T(8,128)(2,1)} %bitcast.75, bf16[1536,384]{1,0:T(8,128)(2,1)} %bitcast.76, bf16[1536,384]{1,0:T(8,128)(2,1)} %bitcast.77, ...), custom_call_target="tpu_custom_call" | custom-call | flops 301989888 | bytes 2359296 | tf_op jit(solution)/shard_map/keys_values/pallas_call | solution.py:494
  40.7 4.4 %collective-permute-start.4 = (bf16[256,256]{1,0:T(8,128)(2,1)}, bf16[256,256]{1,0:T(8,128)(2,1)S(1)}, u32[]{:S(2)}, u32[]{:S(2)}) collective-permute-start(bf16[256,256]{1,0:T(8,128)(2,1)} %get-tuple-element.56), channel_id=1, source_target_pairs={{0,1},{1,2},{2,3},{3,4},{4,5},{5,6},{6,7},{8,9},{9,10},{10,11},{11... | collective-permute-start | bytes 393224 | tf_op jit(solution)/shard_map/ppermute | solution.py:620
  45.2 5.5 %collective-permute-start.3 = (bf16[256,256]{1,0:T(8,128)(2,1)}, bf16[256,256]{1,0:T(8,128)(2,1)S(1)}, u32[]{:S(2)}, u32[]{:S(2)}) collective-permute-start(bf16[256,256]{1,0:T(8,128)(2,1)} %get-tuple-element.56), channel_id=1, source_target_pairs={{0,2},{1,3},{2,4},{3,5},{4,6},{5,7},{8,10},{9,11},{10,12},{11,13},... | collective-permute-start | bytes 393224 | tf_op jit(solution)/shard_map/ppermute | solution.py:620
  54.0 2.3 collective-permute-done.1
  56.3 5.9 %collective-permute-done.2 = bf16[256,256]{1,0:T(8,128)(2,1)S(1)} collective-permute-done((bf16[256,256]{1,0:T(8,128)(2,1)}, bf16[256,256]{1,0:T(8,128)(2,1)S(1)}, u32[]{:S(2)}, u32[]{:S(2)}) %collective-permute-start.2) | collective-permute-done | bytes 131104 | tf_op jit(solution)/shard_map/ppermute | solution.py:620
  64.1 6.7 %collective-permute-done.5 = bf16[16,4224]{1,0:T(8,128)(2,1)S(1)} collective-permute-done((bf16[16,4224]{1,0:T(8,128)(2,1)S(1)}, bf16[16,4224]{1,0:T(8,128)(2,1)S(1)}, u32[]{:S(2)}, u32[]{:S(2)}) %collective-permute-start.5) | collective-permute-done | bytes 135200 | tf_op jit(solution)/shard_map/ppermute | solution.py:626
  74.6 2.2 fusion.5.b_hbm
  76.8 85.1 %all-gather.5.cloned.1.call-done = bf16[6144,4224]{1,0:T(8,128)(2,1)} async-done(((bf16[48,4224]{1,0:T(8,128)(2,1)}), bf16[6144,4224]{1,0:T(8,128)(2,1)}) %all-gather.5.cloned.1.call-update) | async-done | bytes 51904528 | tf_op jit(solution)/shard_map/all_gather | solution.py:546
  161.9 53.1 %forward.1 = (bf16[256,1536]{1,0:T(8,128)(2,1)}, bf16[256,1536]{1,0:T(8,128)(2,1)}, bf16[4,1280,768]{2,1,0:T(8,128)(2,1)}, f32[4,8,768]{2,1,0:T(8,128)}, bf16[25...) custom-call(bf16[1280,256]{1,0:T(8,128)(2,1)} %copy-done.2, ...), custom_call_target="tpu_custom_call" | custom-call | flops 26172456960 | bytes 51904512 | tf_op jit(solution)/shard_map/forward/pallas_call | solution.py:494
  215.2 21.6 %attention_back.1 = (bf16[256,256]{1,0:T(8,128)(2,1)}, bf16[288,256]{1,0:T(8,128)(2,1)}, bf16[288,256]{1,0:T(8,128)(2,1)}, bf16[288,256]{1,0:T(8,128)(2,1)}, bf1...) custom-call(s32[1]{0:T(128)} %bitcast.34.tensor_ref, ...), custom_call_target="tpu_custom_call" | custom-call | flops 6442450944 | bytes 9437184 | tf_op jit(solution)/shard_map/attention_back/pallas_call | solution.py:494
  240.0 2.4 collective-permute-start.11
  243.6 2.1 collective-permute-done.9.back2_ref
  245.8 3.8 %collective-permute-done.10.back3_ref = bf16[288,256]{1,0:T(8,128)(2,1)S(1)} collective-permute-done((bf16[288,256]{1,0:T(8,128)(2,1)}, bf16[288,256]{1,0:T(8,128)(2,1)S(1)}, u32[]{:S(2)}, u32[]{:S(2)}) %collective-permute-start.10) | collective-permute-done | bytes 147488 | tf_op jit(solution)/shard_map/ppermute | solution.py:706
  250.2 3.3 %shared_back.1 = (bf16[848,128]{1,0:T(8,128)(2,1)}, bf16[848,128]{1,0:T(8,128)(2,1)}, bf16[256,128]{1,0:T(8,128)(2,1)}, bf16[256,128]{1,0:T(8,128)(2,1)}, bf16[256,128]{1,0:T(8,128)(2,1)}) custom-call(s32[1]{0:T(128)} %bitcast.33.core_ref, bf16[256,1536]{1,0:T(8,128)(2,1)} %get-tuple-element.57.n1_ref, bf16[256,128]{1,0:T(8,128)(2,1)} %get-tuple-element.58.r1_ref, ...), custom_call_target="tpu_custom_call" | custom-call | flops 201326592 | bytes 2359296 | tf_op jit(solution)/shard_map/shared_back/pallas_call | solution.py:494
  257.8 7.1 %all-to-all-start.1 = ((bf16[64,16,128]{2,1,0:T(8,128)(2,1)}), bf16[64,16,128]{2,1,0:T(8,128)(2,1)S(1)}, u32[]{:S(2)}, u32[]{:S(2)}) async-start(bf16[64,16,128]{2,1,0:T(8,128)(2,1)} %get-tuple-element.82), calls=%async_computation.1 | async-start | bytes 524288 | tf_op jit(solution)/shard_map/all_to_all | solution.py:733
  264.9 4.8 %input_gradient.1 = f32[256,1536]{1,0:T(8,128)} custom-call(bf16[256,1536]{1,0:T(8,128)(2,1)} %x_ref.3, f32[1,1536]{1,0:T(1,128)} %get-tuple-element.112.gain_ref, bf16[1536,384]{1,0:T(8,128)(2,1)} %bitcast.79, bf16[1536,384]{1,0:T(8,128)(2,1)} %bitcast.80, bf16[1536,384]{1,0:T(8,128)(2,1)} %bitcast.81, bf16[256,128]{1,0:T(8,128)(2,1)} %get-tuple-element.84.gk_ref, ...), custom_call_target="tpu_custom_call" | custom-call | flops 301989888 | bytes 6291456 | tf_op jit(solution)/shard_map/input_gradient/pallas_call | solution.py:494
  270.8 2.4 collective-permute-start.14
  277.5 2.9 collective-permute-start.17
  284.3 1.9 sum_wide.1
  286.2 4.0 %sum_hidden.1 = (f32[2,128,1152]{2,1,0:T(8,128)}, f32[1152,128]{1,0:T(8,128)}, f32[384,128]{1,0:T(8,128)}) custom-call(s32[16]{0:T(128)} %ids_ref.3, bf16[32,16,3840]{2,1,0:T(8,128)(2,1)} %bitcast.83), custom_call_target="tpu_custom_call" | custom-call | bytes 1769472 | tf_op jit(solution)/shard_map/sum_hidden/pallas_call | solution.py:494
  (139 shorter events, 41.2 us)
Async XLA Ops:
  7.2 154.7 %all-gather.5.cloned.1.call-start = ((), (), s32[]{:S(2)}) async-start(), calls=%async_computation.4 | async-start | bytes 52310016 | tf_op jit(solution)/shard_map/all_gather | solution.py:546
  11.7 18.8 %all-to-all-start = ((bf16[16,48,384]{2,1,0:T(8,128)(2,1)}), bf16[16,48,384]{2,1,0:T(8,128)(2,1)S(1)}, u32[]{:S(2)}, u32[]{:S(2)}) async-start(bf16[16,48,384]{2,1,0:T(8,128)(2,1)} %fusion.11), calls=%async_computation | async-start | bytes 1179648 | tf_op jit(solution)/shard_map/all_to_all | solution.py:559
  19.4 217.4 %reduce-scatter.2.cloned.1.call-start = ((), (), s32[]{:S(2)}) async-start(), calls=%async_computation.3 | async-start | bytes 614400 | tf_op jit(solution)/shard_map/reduce_scatter | solution.py:679
  30.5 5.7 %collective-permute-start = (bf16[16,48,384]{2,1,0:T(8,128)(2,1)S(1)}, bf16[16,48,384]{2,1,0:T(8,128)(2,1)S(1)}, u32[]{:S(2)}, u32[]{:S(2)}) collective-permute-start(bf16[16,48,384]{2,1,0:T(8,128)(2,1)S(1)} %all-to-all-done), channel_id=1, source_target_pairs={{0,4},{4,0},{1,5},{5,1},{2,6},{6,2},{3,7},{7,3},{8,12},{12,8},{9,1... | collective-permute-start | bytes 1769480 | tf_op jit(solution)/shard_map/ppermute | solution.py:557
  40.7 23.3 %collective-permute-start.4 = (bf16[256,256]{1,0:T(8,128)(2,1)}, bf16[256,256]{1,0:T(8,128)(2,1)S(1)}, u32[]{:S(2)}, u32[]{:S(2)}) collective-permute-start(bf16[256,256]{1,0:T(8,128)(2,1)} %get-tuple-element.56), channel_id=1, source_target_pairs={{0,1},{1,2},{2,3},{3,4},{4,5},{5,6},{6,7},{8,9},{9,10},{10,11},{11... | collective-permute-start | bytes 393224 | tf_op jit(solution)/shard_map/ppermute | solution.py:620
  45.2 18.9 %collective-permute-start.3 = (bf16[256,256]{1,0:T(8,128)(2,1)}, bf16[256,256]{1,0:T(8,128)(2,1)S(1)}, u32[]{:S(2)}, u32[]{:S(2)}) collective-permute-start(bf16[256,256]{1,0:T(8,128)(2,1)} %get-tuple-element.56), channel_id=1, source_target_pairs={{0,2},{1,3},{2,4},{3,5},{4,6},{5,7},{8,10},{9,11},{10,12},{11,13},... | collective-permute-start | bytes 393224 | tf_op jit(solution)/shard_map/ppermute | solution.py:620
  50.7 11.6 %collective-permute-start.2 = (bf16[256,256]{1,0:T(8,128)(2,1)}, bf16[256,256]{1,0:T(8,128)(2,1)S(1)}, u32[]{:S(2)}, u32[]{:S(2)}) collective-permute-start(bf16[256,256]{1,0:T(8,128)(2,1)} %get-tuple-element.56), channel_id=1, source_target_pairs={{0,3},{1,4},{2,5},{3,6},{4,7},{8,11},{9,12},{10,13},{11,14},{12,15... | collective-permute-start | bytes 393224 | tf_op jit(solution)/shard_map/ppermute | solution.py:620
  52.6 3.7 %collective-permute-start.1 = (bf16[256,256]{1,0:T(8,128)(2,1)}, bf16[256,256]{1,0:T(8,128)(2,1)S(1)}, u32[]{:S(2)}, u32[]{:S(2)}) collective-permute-start(bf16[256,256]{1,0:T(8,128)(2,1)} %get-tuple-element.56), channel_id=1, source_target_pairs={{0,4},{1,5},{2,6},{3,7},{8,12},{9,13},{10,14},{11,15},{16,20},{17,... | collective-permute-start | bytes 393224 | tf_op jit(solution)/shard_map/ppermute | solution.py:620
  53.9 16.9 %collective-permute-start.7 = (bf16[16,4224]{1,0:T(8,128)(2,1)S(1)}, bf16[16,4224]{1,0:T(8,128)(2,1)S(1)}, u32[]{:S(2)}, u32[]{:S(2)}) collective-permute-start(bf16[16,4224]{1,0:T(8,128)(2,1)S(1)} %constant_dynamic-update-slice_fusion.5), channel_id=1, source_target_pairs={{3,0},{0,1},{1,2},{2,3},{7,4},{4,5},{5,6},{6,7},{11,8},{8,9},{9,10... | collective-permute-start | bytes 405512 | tf_op jit(solution)/shard_map/ppermute | solution.py:626
  56.3 14.5 %collective-permute-start.6 = (bf16[16,4224]{1,0:T(8,128)(2,1)S(1)}, bf16[16,4224]{1,0:T(8,128)(2,1)S(1)}, u32[]{:S(2)}, u32[]{:S(2)}) collective-permute-start(bf16[16,4224]{1,0:T(8,128)(2,1)S(1)} %constant_dynamic-update-slice_fusion.5), channel_id=1, source_target_pairs={{2,0},{3,1},{0,2},{1,3},{6,4},{7,5},{4,6},{5,7},{10,8},{11,9},{8,1... | collective-permute-start | bytes 405512 | tf_op jit(solution)/shard_map/ppermute | solution.py:626
  62.3 8.6 %collective-permute-start.5 = (bf16[16,4224]{1,0:T(8,128)(2,1)S(1)}, bf16[16,4224]{1,0:T(8,128)(2,1)S(1)}, u32[]{:S(2)}, u32[]{:S(2)}) collective-permute-start(bf16[16,4224]{1,0:T(8,128)(2,1)S(1)} %constant_dynamic-update-slice_fusion.5), channel_id=1, source_target_pairs={{1,0},{2,1},{3,2},{0,3},{5,4},{6,5},{7,6},{4,7},{9,8},{10,9},{11,1... | collective-permute-start | bytes 405512 | tf_op jit(solution)/shard_map/ppermute | solution.py:626
  215.0 71.3 %all-gather.7.cloned.1.call-start = ((), (), s32[]{:S(2)}) async-start(), calls=%async_computation.5 | async-start | bytes 4055040 | tf_op jit(solution)/shard_map/all_gather | solution.py:703
  236.9 6.7 %collective-permute-start.8 = (bf16[288,256]{1,0:T(8,128)(2,1)}, bf16[288,256]{1,0:T(8,128)(2,1)S(1)}, u32[]{:S(2)}, u32[]{:S(2)}) collective-permute-start(bf16[288,256]{1,0:T(8,128)(2,1)} %get-tuple-element.71), channel_id=1, source_target_pairs={{0,7},{1,0},{2,1},{3,2},{4,3},{5,4},{6,5},{7,6},{8,15},{9,8},{10,9... | collective-permute-start | bytes 442376 | tf_op jit(solution)/shard_map/ppermute | solution.py:706
  238.8 7.0 %collective-permute-start.9 = (bf16[288,256]{1,0:T(8,128)(2,1)}, bf16[288,256]{1,0:T(8,128)(2,1)S(1)}, u32[]{:S(2)}, u32[]{:S(2)}) collective-permute-start(bf16[288,256]{1,0:T(8,128)(2,1)} %get-tuple-element.72), channel_id=1, source_target_pairs={{0,6},{1,7},{2,0},{3,1},{4,2},{5,3},{6,4},{7,5},{8,14},{9,15},{10,... | collective-permute-start | bytes 442376 | tf_op jit(solution)/shard_map/ppermute | solution.py:706
  239.5 10.0 %collective-permute-start.10 = (bf16[288,256]{1,0:T(8,128)(2,1)}, bf16[288,256]{1,0:T(8,128)(2,1)S(1)}, u32[]{:S(2)}, u32[]{:S(2)}) collective-permute-start(bf16[288,256]{1,0:T(8,128)(2,1)} %get-tuple-element.73), channel_id=1, source_target_pairs={{0,5},{1,6},{2,7},{3,0},{4,1},{5,2},{6,3},{7,4},{8,13},{9,14},{10,... | collective-permute-start | bytes 442376 | tf_op jit(solution)/shard_map/ppermute | solution.py:706
  240.0 3.6 %collective-permute-start.11 = (bf16[256,256]{1,0:T(8,128)(2,1)}, bf16[256,256]{1,0:T(8,128)(2,1)S(1)}, u32[]{:S(2)}, u32[]{:S(2)}) collective-permute-start(bf16[256,256]{1,0:T(8,128)(2,1)} %get-tuple-element.74), channel_id=1, source_target_pairs={{4,0},{5,1},{6,2},{7,3},{12,8},{13,9},{14,10},{15,11},{20,16},{21,... | collective-permute-start | bytes 393224 | tf_op jit(solution)/shard_map/ppermute | solution.py:620
  253.5 1.7 collective-permute-start.12
  257.8 24.0 %all-to-all-start.1 = ((bf16[64,16,128]{2,1,0:T(8,128)(2,1)}), bf16[64,16,128]{2,1,0:T(8,128)(2,1)S(1)}, u32[]{:S(2)}, u32[]{:S(2)}) async-start(bf16[64,16,128]{2,1,0:T(8,128)(2,1)} %get-tuple-element.82), calls=%async_computation.1 | async-start | bytes 524288 | tf_op jit(solution)/shard_map/all_to_all | solution.py:733
  269.8 6.5 %collective-permute-start.15 = (bf16[1,16,384]{2,1,0:T(8,128)(2,1)S(1)}, bf16[1,16,384]{2,1,0:T(8,128)(2,1)S(1)}, u32[]{:S(2)}, u32[]{:S(2)}) collective-permute-start(bf16[1,16,384]{2,1,0:T(8,128)(2,1)S(1)} %copy-done.20), channel_id=1, source_target_pairs={{24,0},{0,8},{8,16},{16,24},{25,1},{1,9},{9,17},{17,25},{26,2},{2,... | collective-permute-start | bytes 36872 | tf_op jit(solution)/shard_map/ppermute | solution.py:738
  270.8 5.5 %collective-permute-start.14 = (bf16[1,16,384]{2,1,0:T(8,128)(2,1)S(1)}, bf16[1,16,384]{2,1,0:T(8,128)(2,1)S(1)}, u32[]{:S(2)}, u32[]{:S(2)}) collective-permute-start(bf16[1,16,384]{2,1,0:T(8,128)(2,1)S(1)} %copy-done.20), channel_id=1, source_target_pairs={{16,0},{24,8},{0,16},{8,24},{17,1},{25,9},{1,17},{9,25},{18,2},{26... | collective-permute-start | bytes 36872 | tf_op jit(solution)/shard_map/ppermute | solution.py:738
  273.2 3.1 %collective-permute-start.13 = (bf16[1,16,384]{2,1,0:T(8,128)(2,1)S(1)}, bf16[1,16,384]{2,1,0:T(8,128)(2,1)S(1)}, u32[]{:S(2)}, u32[]{:S(2)}) collective-permute-start(bf16[1,16,384]{2,1,0:T(8,128)(2,1)S(1)} %copy-done.20), channel_id=1, source_target_pairs={{8,0},{16,8},{24,16},{0,24},{9,1},{17,9},{25,17},{1,25},{10,2},{18... | collective-permute-start | bytes 36872 | tf_op jit(solution)/shard_map/ppermute | solution.py:738
  276.3 5.5 %collective-permute-start.18 = (bf16[4,16,384]{2,1,0:T(8,128)(2,1)S(1)}, bf16[4,16,384]{2,1,0:T(8,128)(2,1)S(1)}, u32[]{:S(2)}, u32[]{:S(2)}) collective-permute-start(bf16[4,16,384]{2,1,0:T(8,128)(2,1)S(1)} %constant_dynamic-update-slice_fusion.10.rest_0_), channel_id=1, source_target_pairs={{96,0},{0,32},{32,64},{64,96},{97,1},{1,33},{33,65},{65,97},{98,2}... | collective-permute-start | bytes 147464 | tf_op jit(solution)/shard_map/ppermute | solution.py:738
  277.5 5.4 %collective-permute-start.17 = (bf16[4,16,384]{2,1,0:T(8,128)(2,1)S(1)}, bf16[4,16,384]{2,1,0:T(8,128)(2,1)S(1)}, u32[]{:S(2)}, u32[]{:S(2)}) collective-permute-start(bf16[4,16,384]{2,1,0:T(8,128)(2,1)S(1)} %constant_dynamic-update-slice_fusion.10.rest_0_), channel_id=1, source_target_pairs={{64,0},{96,32},{0,64},{32,96},{65,1},{97,33},{1,65},{33,97},{66,2}... | collective-permute-start | bytes 147464 | tf_op jit(solution)/shard_map/ppermute | solution.py:738
  280.4 3.2 %collective-permute-start.16 = (bf16[4,16,384]{2,1,0:T(8,128)(2,1)S(1)}, bf16[4,16,384]{2,1,0:T(8,128)(2,1)S(1)}, u32[]{:S(2)}, u32[]{:S(2)}) collective-permute-start(bf16[4,16,384]{2,1,0:T(8,128)(2,1)S(1)} %constant_dynamic-update-slice_fusion.10.rest_0_), channel_id=1, source_target_pairs={{32,0},{64,32},{96,64},{0,96},{33,1},{65,33},{97,65},{1,97},{34,2}... | collective-permute-start | bytes 147464 | tf_op jit(solution)/shard_map/ppermute | solution.py:738
  (22 other events, 109.1 us)
Sparse Core Ops, SparseCore 0:
  11.6 150.2 all-gather.4
  215.1 18.6 reduce-scatter.1
  237.0 47.5 all-gather.6
